TPU v7x, 32 devices: a whole 2x2x4 slice. The times are simulated.
32 devices in a mesh: groups: 2 (over y), expert: 8 (over z, x), ffn: 2 (over core).
Axes of the slice: x: 2, y: 2, z: 4, core: 2. Of those that a mesh axis runs over, the one named last changes fastest.
Arguments:
- tokens: bfloat16 [2048, 4096], P(('groups', 'expert'), 'ffn'), parts along dimension 0, may hold values from -6 to 6
- grad_out: bfloat16 [2048, 4096], P(('groups', 'expert'), 'ffn'), parts along dimension 0, may hold values from -6 to 6
- route_ids: int32 [2048, 8], P(('groups', 'expert')), parts along dimension 0, may hold values from 0 to 127, all different within a row; in each aligned block of 128 rows (0 to 127, 128 to 255, ...) at most 9 rows name the same one
- route_weight: float32 [2048, 8], P(('groups', 'expert')), parts along dimension 0, may hold values from 0.05 to 1
- gate_weight: bfloat16 [8, 4096, 1536], P('expert', None, 'ffn'), may hold values from -0.09375 to 0.09375
- up_weight: bfloat16 [8, 4096, 1536], P('expert', None, 'ffn'), may hold values from -0.09375 to 0.09375
- down_weight: bfloat16 [8, 1536, 4096], P('expert', 'ffn'), may hold values from -0.15625 to 0.15625
Outputs:
- out_tokens: bfloat16 [2048, 4096], P(('groups', 'expert'), 'ffn'), parts along dimension 0
- grad_tokens: bfloat16 [2048, 4096], P(('groups', 'expert'), 'ffn'), parts along dimension 0
- grad_gate: bfloat16 [16, 4096, 1536], P(('groups', 'expert'), None, 'ffn'), parts along dimension 0
- grad_up: bfloat16 [16, 4096, 1536], P(('groups', 'expert'), None, 'ffn'), parts along dimension 0
- grad_down: bfloat16 [16, 1536, 4096], P(('groups', 'expert'), 'ffn'), parts along dimension 0
There are 2 independent parts, one for each index of `groups`. A program takes and returns all parts, laid end to end along the dimension named above; an argument that names none is the same for every part. Nothing has to cross between parts.
Inputs may be any that keep to these rules, and one draw needn't show every extreme that they name: `route_ids`: each token names 8 different experts. Among the tokens of one index of expert (aligned blocks of 128 tokens) no expert is named more than 9 times.
All inputs are finite; a program needn't handle non-finite values.
Results may differ from a plain program's by a relative error of at most 0.014.
Values may be sent and summed in bfloat16 or wider, within the bound.
No kernel may reach another device: no remote copies, remote signals or barrier semaphores. Data moves between devices by JAX's collectives and lax.ppermute only.
A program may use at most 128 MiB of HBM per device.

v0:
```python
import jax
import jax.numpy as jnp
from jax import lax
from jax.sharding import PartitionSpec as P

EXPERTS = 128


def contract_rows(left, right):
    return lax.dot_general(
        left, right, (((0,), (0,)), ((), ())), preferred_element_type=jnp.float32
    )


def contract_cols(left, right):
    return lax.dot_general(
        left, right, (((1,), (1,)), ((), ())), preferred_element_type=jnp.float32
    )


def shards(tokens, grad_out, route_ids, route_weight, gate_weight, up_weight, down_weight):
    tokens, grad_out = (
        lax.all_gather(tokens, "ffn", axis=1, tiled=True),
        lax.all_gather(grad_out, "ffn", axis=1, tiled=True),
    )
    tok_dev, width = tokens.shape
    top_count = route_ids.shape[1]
    piece_width = gate_weight.shape[1]
    hidden_half = gate_weight.shape[2]
    pieces = width // piece_width
    devices = lax.axis_size("expert")
    flight = devices // pieces
    halves = lax.axis_size("ffn")
    sub_width = piece_width // halves
    capacity = max(2, min(tok_dev, (9 * tok_dev * top_count + 8 * EXPERTS - 1) // (8 * EXPERTS)))
    total_rows = devices * capacity
    expert_ids = jnp.arange(flight, dtype=jnp.int32)
    member = jnp.zeros((tok_dev, flight), jnp.float32)
    mixing = jnp.zeros((tok_dev, flight), jnp.float32)
    for route in range(top_count):
        hit = (route_ids[:, route : route + 1] == expert_ids[None, :]).astype(jnp.float32)
        member = member + hit
        mixing = mixing + hit * route_weight[:, route : route + 1]
    slots = jnp.cumsum(member, axis=0) - member
    place = member[:, :, None] * (
        slots[:, :, None] == jnp.arange(capacity, dtype=jnp.float32)
    ).astype(jnp.float32)
    weighted = place * mixing[:, :, None]
    place_low = place.astype(jnp.bfloat16)
    x_four = tokens.reshape(tok_dev, halves, pieces, sub_width)
    g_four = grad_out.reshape(tok_dev, halves, pieces, sub_width)
    x_parts = []
    g_parts = []
    for half in range(halves):
        x_parts.append(
            jnp.einsum(
                "Tec,Tjr->ejcr", place_low, x_four[:, half], preferred_element_type=jnp.float32
            )
        )
        g_parts.append(jnp.einsum("Tec,Tjr->ejcr", weighted, g_four[:, half].astype(jnp.float32)))
    x_send = jnp.concatenate(x_parts, axis=3).astype(jnp.bfloat16).reshape(total_rows, piece_width)
    g_send = jnp.concatenate(g_parts, axis=3).astype(jnp.bfloat16).reshape(total_rows, piece_width)

    def return_parts(values):
        arrived = lax.all_to_all(values, "expert", split_axis=0, concat_axis=0, tiled=True)
        lanes = arrived.shape[1]
        return arrived.astype(jnp.float32).reshape(flight, pieces, capacity, lanes).sum(axis=1)

    def spread_rows(values):
        lanes = values.shape[2]
        copies = jnp.broadcast_to(values[:, None], (flight, pieces, capacity, lanes)).reshape(
            total_rows, lanes
        )
        return lax.all_to_all(copies, "expert", split_axis=0, concat_axis=0, tiled=True)

    def finish(term, mix):
        summed = lax.psum_scatter(term, "ffn", scatter_dimension=1, tiled=True)
        back = lax.all_to_all(summed, "expert", split_axis=0, concat_axis=0, tiled=True)
        back = back.reshape(flight, pieces, capacity, sub_width)
        joined = jnp.einsum("Tec,ejcr->Tjr", mix, back)
        return joined.reshape(tok_dev, pieces * sub_width).astype(jnp.bfloat16)

    rows = lax.all_to_all(x_send, "expert", split_axis=0, concat_axis=0, tiled=True)
    w_gate = gate_weight[0]
    w_up = up_weight[0]
    w_down = down_weight[0]
    partial_value = jnp.concatenate(
        [
            jnp.dot(rows, w_gate, preferred_element_type=jnp.float32),
            jnp.dot(rows, w_up, preferred_element_type=jnp.float32),
        ],
        axis=1,
    )
    summed = return_parts(partial_value.astype(jnp.bfloat16))
    gate = summed[:, :, :hidden_half]
    up = summed[:, :, hidden_half:]
    sig = jax.nn.sigmoid(gate)
    act = gate * sig
    hidden = (act * up).astype(jnp.bfloat16)
    h_rows = spread_rows(hidden)
    out_term = jnp.dot(h_rows, w_down, preferred_element_type=jnp.float32)
    out_tokens = finish(out_term, weighted)
    grads = lax.all_to_all(g_send, "expert", split_axis=0, concat_axis=0, tiled=True)
    grad_down = contract_rows(h_rows, grads).astype(jnp.bfloat16)
    hidden_part = contract_cols(grads, w_down).astype(jnp.bfloat16)
    grad_hidden = return_parts(hidden_part)
    pre_gate = (grad_hidden * up * sig * (1.0 + gate * (1.0 - sig))).astype(jnp.bfloat16)
    pre_up = (grad_hidden * act).astype(jnp.bfloat16)
    both = spread_rows(jnp.concatenate([pre_gate, pre_up], axis=2))
    d_gate_rows = both[:, :hidden_half]
    d_up_rows = both[:, hidden_half:]
    grad_gate = contract_rows(rows, d_gate_rows).astype(jnp.bfloat16)
    grad_up = contract_rows(rows, d_up_rows).astype(jnp.bfloat16)
    x_term = contract_cols(d_gate_rows, w_gate) + contract_cols(d_up_rows, w_up)
    grad_tokens = finish(x_term, place)
    return (out_tokens, grad_tokens, grad_gate[None], grad_up[None], grad_down[None])


def solution(mesh):
    in_specs = (
        P(("groups", "expert"), "ffn"),
        P(("groups", "expert"), "ffn"),
        P(("groups", "expert"), None),
        P(("groups", "expert"), None),
        P("expert", None, "ffn"),
        P("expert", None, "ffn"),
        P("expert", "ffn", None),
    )
    out_specs = (
        P(("groups", "expert"), "ffn"),
        P(("groups", "expert"), "ffn"),
        P(("groups", "expert"), None, "ffn"),
        P(("groups", "expert"), None, "ffn"),
        P(("groups", "expert"), "ffn", None),
    )
    return jax.shard_map(shards, mesh=mesh, in_specs=in_specs, out_specs=out_specs, check_vma=False)
```

profile of v0, /device:TPU:0, one launch (start us, length us, event | category | flops | bytes accessed | tf_op | source)
XLA Modules:
  0.0 201.3 jit_solution(6410501192173883688)
XLA Ops:
  7.2 2.0 %copy.18 = bf16[128,2048]{0,1:T(8,128)(2,1)} copy(bf16[128,2048]{1,0:T(8,128)(2,1)} %param.7) | data formatting | bytes 1048576 | tf_op args[0]
  9.3 2.0 %copy.21 = bf16[128,2048]{0,1:T(8,128)(2,1)} copy(bf16[128,2048]{1,0:T(8,128)(2,1)} %param.8) | data formatting | bytes 1048576 | tf_op args[1]
  14.2 7.7 %all-gather.3.cloned.1.call-done = bf16[128,4096]{0,1:T(8,128)(2,1)} async-done(((bf16[128,2048]{0,1:T(8,128)(2,1)}), bf16[128,4096]{0,1:T(8,128)(2,1)}) %all-gather.3.cloned.1.call-update) | async-done | bytes 1048592 | tf_op jit(solution)/shard_map/all_gather | solution.py:23
  23.2 1.3 convolution_convert_fusion.4
  25.7 5.8 %all-to-all-start = ((bf16[8,9,4096]{2,1,0:T(8,128)(2,1)}), bf16[8,9,4096]{2,1,0:T(8,128)(2,1)S(1)}, u32[]{:S(2)}, u32[]{:S(2)}) async-start(bf16[8,9,4096]{2,1,0:T(8,128)(2,1)} %pad_maximum_fusion), calls=%async_computation | async-start | bytes 2097152 | tf_op jit(solution)/shard_map/all_to_all | solution.py:83
  31.5 2.7 %all-gather.5.cloned.1.call-done = bf16[128,4096]{0,1:T(8,128)(2,1)} async-done(((bf16[128,2048]{0,1:T(8,128)(2,1)}), bf16[128,4096]{0,1:T(8,128)(2,1)}) %all-gather.5.cloned.1.call-update) | async-done | bytes 1048592 | tf_op jit(solution)/shard_map/all_gather | solution.py:24
  34.2 1.3 convolution_convert_fusion.3
  35.6 1.3 convolution_convert_fusion.2
  38.1 19.6 %all-to-all-done = bf16[8,9,4096]{2,1,0:T(8,128)(2,1)S(1)} async-done(((bf16[8,9,4096]{2,1,0:T(8,128)(2,1)}), bf16[8,9,4096]{2,1,0:T(8,128)(2,1)S(1)}, u32[]{:S(2)}, u32[]{:S(2)}) %all-to-all-start) | async-done | bytes 589856 | tf_op jit(solution)/shard_map/all_to_all | solution.py:83
  57.7 3.6 %all-to-all-start.4 = ((bf16[8,9,4096]{2,1,0:T(8,128)(2,1)}), bf16[8,9,4096]{2,1,0:T(8,128)(2,1)S(1)}, u32[]{:S(2)}, u32[]{:S(2)}) async-start(bf16[8,9,4096]{2,1,0:T(8,128)(2,1)} %pad_maximum_fusion.1), calls=%async_computation.5 | async-start | bytes 2097152 | tf_op jit(solution)/shard_map/all_to_all | solution.py:103
  61.3 3.8 %fusion.23 = bf16[8,9,768]{2,1,0:T(8,128)(2,1)S(1)} fusion(bf16[8,9,4096]{2,1,0:T(8,128)(2,1)S(1)} %all-to-all-done, bf16[1,4096,768]{2,1,0:T(8,128)(2,1)} %param.12), kind=kOutput, calls=%fused_computation.28 | convolution fusion | flops 453040128 | bytes 6991872 | tf_op jit(solution)/shard_map/dot_general | solution.py:90
  65.1 3.8 %fusion.20 = bf16[8,9,768]{2,1,0:T(8,128)(2,1)S(1)} fusion(bf16[8,9,4096]{2,1,0:T(8,128)(2,1)S(1)} %all-to-all-done, bf16[1,4096,768]{2,1,0:T(8,128)(2,1)} %param.11), kind=kOutput, calls=%fused_computation.27 | convolution fusion | flops 453040128 | bytes 6991872 | tf_op jit(solution)/shard_map/dot_general | solution.py:89
  69.7 17.6 %all-to-all-done.4 = bf16[8,9,4096]{2,1,0:T(8,128)(2,1)S(1)} async-done(((bf16[8,9,4096]{2,1,0:T(8,128)(2,1)}), bf16[8,9,4096]{2,1,0:T(8,128)(2,1)S(1)}, u32[]{:S(2)}, u32[]{:S(2)}) %all-to-all-start.4) | async-done | bytes 589856 | tf_op jit(solution)/shard_map/all_to_all | solution.py:103
  87.3 3.6 %all-to-all-start.1 = ((bf16[8,9,1536]{2,1,0:T(8,128)(2,1)}), bf16[8,9,1536]{2,1,0:T(8,128)(2,1)S(1)}, u32[]{:S(2)}, u32[]{:S(2)}) async-start(bf16[8,9,1536]{2,1,0:T(8,128)(2,1)} %pad_maximum_fusion.2), calls=%async_computation.1 | async-start | bytes 786432 | tf_op jit(solution)/shard_map/all_to_all | solution.py:65
  91.2 4.8 %fusion.26 = bf16[72,768]{1,0:T(8,128)(2,1)S(1)} fusion(bf16[72,4096]{1,0:T(8,128)(2,1)S(1)} %all_to_all.53, bf16[1,768,4096]{2,1,0:T(8,128)(2,1)} %param.13), kind=kOutput, calls=%fused_computation.29 | convolution fusion | flops 453040128 | bytes 6991872 | tf_op jit(solution)/shard_map/dot_general | solution.py:16
  96.8 6.0 %all-to-all-done.1 = bf16[8,9,1536]{2,1,0:T(8,128)(2,1)S(1)} async-done(((bf16[8,9,1536]{2,1,0:T(8,128)(2,1)}), bf16[8,9,1536]{2,1,0:T(8,128)(2,1)S(1)}, u32[]{:S(2)}, u32[]{:S(2)}) %all-to-all-start.1) | async-done | bytes 221216 | tf_op jit(solution)/shard_map/all_to_all | solution.py:65
  102.8 3.6 %all-to-all-start.5 = ((bf16[8,9,768]{2,1,0:T(8,128)(2,1)}), bf16[8,9,768]{2,1,0:T(8,128)(2,1)S(1)}, u32[]{:S(2)}, u32[]{:S(2)}) async-start(bf16[8,9,768]{2,1,0:T(8,128)(2,1)} %all_to_all.54), calls=%async_computation.6 | async-start | bytes 393216 | tf_op jit(solution)/shard_map/all_to_all | solution.py:65
  106.6 7.9 %all-to-all-done.5 = bf16[8,9,768]{2,1,0:T(8,128)(2,1)S(1)} async-done(((bf16[8,9,768]{2,1,0:T(8,128)(2,1)}), bf16[8,9,768]{2,1,0:T(8,128)(2,1)S(1)}, u32[]{:S(2)}, u32[]{:S(2)}) %all-to-all-start.5) | async-done | bytes 110624 | tf_op jit(solution)/shard_map/all_to_all | solution.py:65
  115.4 10.7 %all_to_all.69 = bf16[8,9,768]{2,1,0:T(8,128)(2,1)S(1)} all-to-all(bf16[8,9,768]{2,1,0:T(8,128)(2,1)S(1)} %get-tuple-element.7), channel_id=1, replica_groups=mesh['groups'=2,'expert'=8,'ffn'=2] {'expert'}, dimensions={0} | all-to-all | bytes 221184 | tf_op jit(solution)/shard_map/all_to_all | solution.py:74
  126.3 5.1 %fusion.2 = f32[72,4096]{1,0:T(8,128)} fusion(bf16[72,768]{1,0:T(8,128)(2,1)S(1)} %all_to_all.49, bf16[1,768,4096]{2,1,0:T(8,128)(2,1)} %param.13), kind=kOutput, calls=%fused_computation.5 | convolution fusion | flops 452984832 | bytes 7581696 | tf_op jit(solution)/shard_map/dot_general | solution.py:101
  131.5 14.5 %all_to_all.70 = bf16[8,9,1536]{2,1,0:T(8,128)(2,1)S(1)} all-to-all(bf16[8,9,1536]{2,1,0:T(8,128)(2,1)S(1)} %pad_maximum_fusion.3), channel_id=1, replica_groups=mesh['groups'=2,'expert'=8,'ffn'=2] {'expert'}, dimensions={0} | all-to-all | bytes 442368 | tf_op jit(solution)/shard_map/all_to_all | solution.py:74
  146.0 4.8 %fusion.6 = f32[72,4096]{1,0:T(8,128)S(1)} fusion(bf16[1,4096,768]{2,1,0:T(8,128)(2,1)} %param.12, bf16[72,1536]{1,0:T(8,128)(2,1)S(1)} %all_to_all.57), kind=kOutput, calls=%fused_computation.9 | convolution fusion | flops 452984832 | bytes 7581696 | tf_op jit(solution)/shard_map/dot_general | solution.py:16
  150.8 5.8 %fusion.15 = f32[72,4096]{1,0:T(8,128)} fusion(f32[72,4096]{1,0:T(8,128)S(1)} %fusion.6, bf16[1,4096,768]{2,1,0:T(8,128)(2,1)} %param.11, bf16[72,1536]{1,0:T(8,128)(2,1)S(1)} %all_to_all.57), kind=kOutput, calls=%fused_computation.18 | convolution fusion | flops 453279744 | bytes 8761344 | tf_op jit(solution)/shard_map/dot_general | solution.py:16
  157.0 2.0 all_to_all.50
  158.9 3.7 %all-to-all-start.3 = ((bf16[8,9,2048]{2,1,0:T(8,128)(2,1)}), bf16[8,9,2048]{2,1,0:T(8,128)(2,1)S(1)}, u32[]{:S(2)}, u32[]{:S(2)}) async-start(bf16[8,9,2048]{2,1,0:T(8,128)(2,1)} %all_to_all.50), calls=%async_computation.4 | async-start | bytes 1048576 | tf_op jit(solution)/shard_map/all_to_all | solution.py:78
  162.6 4.5 %fusion.14 = bf16[1,768,4096]{2,1,0:T(8,128)(2,1)} fusion(bf16[8,9,768]{2,1,0:T(8,128)(2,1)S(1)} %all_to_all.69, bf16[8,9,4096]{2,1,0:T(8,128)(2,1)S(1)} %all-to-all-done.4), kind=kOutput, calls=%fused_computation.17 | convolution fusion | flops 456130560 | bytes 6991872 | tf_op jit(solution)/shard_map/dot_general | solution.py:10
  167.2 2.0 all_to_all.58
  169.1 7.1 %all-to-all-done.3 = bf16[8,9,2048]{2,1,0:T(8,128)(2,1)S(1)} async-done(((bf16[8,9,2048]{2,1,0:T(8,128)(2,1)}), bf16[8,9,2048]{2,1,0:T(8,128)(2,1)S(1)}, u32[]{:S(2)}, u32[]{:S(2)}) %all-to-all-start.3) | async-done | bytes 294944 | tf_op jit(solution)/shard_map/all_to_all | solution.py:78
  176.2 3.6 %all-to-all-start.7 = ((bf16[8,9,2048]{2,1,0:T(8,128)(2,1)}), bf16[8,9,2048]{2,1,0:T(8,128)(2,1)S(1)}, u32[]{:S(2)}, u32[]{:S(2)}) async-start(bf16[8,9,2048]{2,1,0:T(8,128)(2,1)} %all_to_all.58), calls=%async_computation.9 | async-start | bytes 1048576 | tf_op jit(solution)/shard_map/all_to_all | solution.py:78
  179.8 4.6 %fusion.12 = bf16[1,4096,768]{2,1,0:T(8,128)(2,1)} fusion(bf16[72,4096]{1,0:T(8,128)(2,1)S(1)} %all_to_all.60, bf16[72,1536]{1,0:T(8,128)(2,1)S(1)} %all_to_all.57), kind=kOutput, calls=%fused_computation.15 | convolution fusion | flops 456130560 | bytes 6991872 | tf_op jit(solution)/shard_map/dot_general | solution.py:10
  184.4 4.6 %fusion.13 = bf16[1,4096,768]{2,1,0:T(8,128)(2,1)} fusion(bf16[72,4096]{1,0:T(8,128)(2,1)S(1)} %all_to_all.60, bf16[72,1536]{1,0:T(8,128)(2,1)S(1)} %all_to_all.57), kind=kOutput, calls=%fused_computation.16 | convolution fusion | flops 456130560 | bytes 6991872 | tf_op jit(solution)/shard_map/dot_general | solution.py:10
  190.1 3.5 %all-to-all-done.7 = bf16[8,9,2048]{2,1,0:T(8,128)(2,1)S(1)} async-done(((bf16[8,9,2048]{2,1,0:T(8,128)(2,1)}), bf16[8,9,2048]{2,1,0:T(8,128)(2,1)S(1)}, u32[]{:S(2)}, u32[]{:S(2)}) %all-to-all-start.7) | async-done | bytes 294944 | tf_op jit(solution)/shard_map/all_to_all | solution.py:78
  (36 shorter events, 12.2 us)
Async XLA Ops:
  7.2 14.7 %all-gather.3.cloned.1.call-start = ((), (), s32[]{:S(2)}) async-start(), calls=%async_computation.10 | async-start | bytes 1572864 | tf_op jit(solution)/shard_map/all_gather | solution.py:23
  9.3 25.0 %all-gather.5.cloned.1.call-start = ((), (), s32[]{:S(2)}) async-start(), calls=%async_computation.12 | async-start | bytes 1572864 | tf_op jit(solution)/shard_map/all_gather | solution.py:24
  25.7 32.0 %all-to-all-start = ((bf16[8,9,4096]{2,1,0:T(8,128)(2,1)}), bf16[8,9,4096]{2,1,0:T(8,128)(2,1)S(1)}, u32[]{:S(2)}, u32[]{:S(2)}) async-start(bf16[8,9,4096]{2,1,0:T(8,128)(2,1)} %pad_maximum_fusion), calls=%async_computation | async-start | bytes 2097152 | tf_op jit(solution)/shard_map/all_to_all | solution.py:83
  57.7 29.6 %all-to-all-start.4 = ((bf16[8,9,4096]{2,1,0:T(8,128)(2,1)}), bf16[8,9,4096]{2,1,0:T(8,128)(2,1)S(1)}, u32[]{:S(2)}, u32[]{:S(2)}) async-start(bf16[8,9,4096]{2,1,0:T(8,128)(2,1)} %pad_maximum_fusion.1), calls=%async_computation.5 | async-start | bytes 2097152 | tf_op jit(solution)/shard_map/all_to_all | solution.py:103
  87.3 15.5 %all-to-all-start.1 = ((bf16[8,9,1536]{2,1,0:T(8,128)(2,1)}), bf16[8,9,1536]{2,1,0:T(8,128)(2,1)S(1)}, u32[]{:S(2)}, u32[]{:S(2)}) async-start(bf16[8,9,1536]{2,1,0:T(8,128)(2,1)} %pad_maximum_fusion.2), calls=%async_computation.1 | async-start | bytes 786432 | tf_op jit(solution)/shard_map/all_to_all | solution.py:65
  102.8 11.7 %all-to-all-start.5 = ((bf16[8,9,768]{2,1,0:T(8,128)(2,1)}), bf16[8,9,768]{2,1,0:T(8,128)(2,1)S(1)}, u32[]{:S(2)}, u32[]{:S(2)}) async-start(bf16[8,9,768]{2,1,0:T(8,128)(2,1)} %all_to_all.54), calls=%async_computation.6 | async-start | bytes 393216 | tf_op jit(solution)/shard_map/all_to_all | solution.py:65
  106.4 50.5 %reduce-scatter.3.cloned.1.call-start = ((), (), s32[]{:S(2)}) async-start(), calls=%async_computation.11 | async-start | bytes 1769472 | tf_op jit(solution)/shard_map/reduce_scatter | solution.py:77
  126.2 5.2 %copy-start = (bf16[8,9,768]{2,1,0:T(8,128)(2,1)S(1)}, bf16[8,9,768]{2,1,0:T(8,128)(2,1)}, u32[]{:S(2)}) copy-start(bf16[8,9,768]{2,1,0:T(8,128)(2,1)} %get-tuple-element.5) | copy-start | bytes 331780
  126.2 5.2 %copy-start.1 = (bf16[8,9,768]{2,1,0:T(8,128)(2,1)S(1)}, bf16[8,9,768]{2,1,0:T(8,128)(2,1)}, u32[]{:S(2)}) copy-start(bf16[8,9,768]{2,1,0:T(8,128)(2,1)} %get-tuple-element.6) | copy-start | bytes 331780
  131.3 35.8 %reduce-scatter.5.cloned.1.call-start = ((), (), s32[]{:S(2)}) async-start(), calls=%async_computation.13 | async-start | bytes 1769472 | tf_op jit(solution)/shard_map/reduce_scatter | solution.py:77
  158.9 17.3 %all-to-all-start.3 = ((bf16[8,9,2048]{2,1,0:T(8,128)(2,1)}), bf16[8,9,2048]{2,1,0:T(8,128)(2,1)S(1)}, u32[]{:S(2)}, u32[]{:S(2)}) async-start(bf16[8,9,2048]{2,1,0:T(8,128)(2,1)} %all_to_all.50), calls=%async_computation.4 | async-start | bytes 1048576 | tf_op jit(solution)/shard_map/all_to_all | solution.py:78
  176.2 17.4 %all-to-all-start.7 = ((bf16[8,9,2048]{2,1,0:T(8,128)(2,1)}), bf16[8,9,2048]{2,1,0:T(8,128)(2,1)S(1)}, u32[]{:S(2)}, u32[]{:S(2)}) async-start(bf16[8,9,2048]{2,1,0:T(8,128)(2,1)} %all_to_all.58), calls=%async_computation.9 | async-start | bytes 1048576 | tf_op jit(solution)/shard_map/all_to_all | solution.py:78
Sparse Core Ops, SparseCore 0:
  10.1 11.7 all-gather.2
  24.0 10.1 all-gather.4
  131.5 7.0 reduce-scatter.2
  156.8 7.2 reduce-scatter.4
where the time goes:
time: 203 us; the launch traced here: 201 us
  waiting for transfers between devices  72.3 us (36%)
  matrix products  49.3 us (24%)
  blocking collectives  25.2 us (12%)
  starting transfers between devices  24.2 us (12%)
  between operations  13.9 us (7%)
  local copies, waits for them, and re-layouts  11.6 us (6%)
  other arithmetic  4.81 us (2%)
    all_to_all x2, blocking collectives, spread_rows(): lax.all_to_all(copies, 'expert', split_axis=0, concat_axis=0, tiled=True)  25.2 us
    all_to_all x1, waiting for transfers between devices, shards(): lax.all_to_all(x_send, 'expert', split_axis=0, concat_axis=0, tiled=True)  19.6 us
    all_to_all x1, waiting for transfers between devices, shards(): lax.all_to_all(g_send, 'expert', split_axis=0, concat_axis=0, tiled=True)  17.6 us
    dot_general x3, matrix products, contract_cols(): lax.dot_general(left, right, (((1,), (1,)), ((), ())), preferred_element_...  15.4 us
    all_to_all x2, waiting for transfers between devices, return_parts(): lax.all_to_all(values, 'expert', split_axis=0, concat_axis=0, tiled=True)  14 us
    dot_general x3, matrix products, contract_rows(): lax.dot_general(left, right, (((0,), (0,)), ((), ())), preferred_element_...  13.7 us
    all_to_all x2, waiting for transfers between devices, finish(): lax.all_to_all(summed, 'expert', split_axis=0, concat_axis=0, tiled=True)  10.6 us
    all_gather x1, waiting for transfers between devices, shards(): lax.all_gather(tokens, 'ffn', axis=1, tiled=True)  7.68 us
  transfers between devices with their start and end apart: 10, of which 8 were waited for; matrix products, arithmetic and copies ran while one was open for 25% of the time, Pallas kernels for 0%

commit v1 on v0

--- a/solution.py
+++ b/solution.py
@@ -1,9 +1,15 @@
+import functools
+
 import jax
 import jax.numpy as jnp
 from jax import lax
+from jax.experimental import pallas as pl
+from jax.experimental.pallas import tpu as pltpu
 from jax.sharding import PartitionSpec as P
 
 EXPERTS = 128
+LANES = 128
+MIB = 1024 * 1024
 
 
 def contract_rows(left, right):
@@ -18,7 +24,7 @@
     )
 
 
-def shards(tokens, grad_out, route_ids, route_weight, gate_weight, up_weight, down_weight):
+def general_shards(tokens, grad_out, route_ids, route_weight, gate_weight, up_weight, down_weight):
     tokens, grad_out = (
         lax.all_gather(tokens, "ffn", axis=1, tiled=True),
         lax.all_gather(grad_out, "ffn", axis=1, tiled=True),
@@ -116,6 +122,343 @@
     return (out_tokens, grad_tokens, grad_gate[None], grad_up[None], grad_down[None])
 
 
+def vmem(shape, dtype):
+    return pltpu.VMEM(shape, dtype)
+
+
+def call(kernel, out_shape, args, in_spaces=None, out_spaces=None, flops=0, traffic=0, scratch=(), limit=16):
+    spaces = in_spaces or [pltpu.VMEM] * len(args)
+    outs = out_spaces or [pltpu.VMEM] * len(out_shape)
+    return pl.pallas_call(
+        kernel,
+        out_shape=tuple(out_shape),
+        in_specs=[pl.BlockSpec(memory_space=space) for space in spaces],
+        out_specs=tuple(pl.BlockSpec(memory_space=space) for space in outs),
+        scratch_shapes=list(scratch),
+        compiler_params=pltpu.CompilerParams(vmem_limit_bytes=limit * MIB),
+        cost_estimate=pl.CostEstimate(flops=flops, bytes_accessed=traffic, transcendentals=0),
+    )(*args)
+
+
+def rows_to_blocks(scratch, outs, take, rows, capacity, subs):
+    for sub in range(subs):
+        scratch[pl.ds(sub, rows, stride=subs), :] = take(sub)
+    size = capacity * subs
+    for place, out in enumerate(outs):
+        out[...] = scratch[place * size : (place + 1) * size, :].astype(out.dtype)
+
+
+def blocks_to_rows(scratch, blocks, put, rows, capacity, subs):
+    size = capacity * subs
+    for place, block in enumerate(blocks):
+        scratch[place * size : (place + 1) * size, :] = block[...].astype(jnp.float32)
+    for sub in range(subs):
+        put(sub, scratch[pl.ds(sub, rows, stride=subs), :])
+
+
+def route_kernel(devices, capacity, subs, ids, weight, x, g, *refs):
+    x_outs, g_outs = refs[:devices], refs[devices : 2 * devices]
+    place_out, mix_out, scratch = refs[2 * devices :]
+    top, tok = ids.shape
+    rows = devices * capacity
+    me = lax.axis_index("expert")
+    order = lax.broadcasted_iota(jnp.int32, (devices, tok), 0)
+    expert = order ^ me
+    member = jnp.zeros((devices, tok), jnp.float32)
+    mixing = jnp.zeros((devices, tok), jnp.float32)
+    for route in range(top):
+        hit = ids[route : route + 1, :] == expert
+        member = jnp.where(hit, 1.0, member)
+        mixing = jnp.where(hit, weight[route : route + 1, :], mixing)
+    before = lax.broadcasted_iota(jnp.int32, (tok, tok), 0) < lax.broadcasted_iota(jnp.int32, (tok, tok), 1)
+    slots = jnp.dot(
+        member.astype(jnp.bfloat16),
+        jnp.where(before, 1.0, 0.0).astype(jnp.bfloat16),
+        preferred_element_type=jnp.float32,
+    )
+    target = jnp.where(member > 0, slots + capacity * order.astype(jnp.float32), -1.0)
+    row = lax.broadcasted_iota(jnp.int32, (rows, tok), 0).astype(jnp.float32)
+    place = jnp.zeros((rows, tok), jnp.float32)
+    mix = jnp.zeros((rows, tok), jnp.float32)
+    for k in range(devices):
+        equal = target[k : k + 1, :] == row
+        place = jnp.where(equal, 1.0, place)
+        mix = jnp.where(equal, mixing[k : k + 1, :], mix)
+    row_weight = jnp.broadcast_to(jnp.sum(mix, axis=1, keepdims=True), (rows, LANES))
+    low = place.astype(jnp.bfloat16)
+    place_out[...] = low
+    mix_out[...] = row_weight
+
+    def x_part(sub):
+        return jnp.dot(low, x[:, sub * LANES : (sub + 1) * LANES], preferred_element_type=jnp.float32)
+
+    def g_part(sub):
+        part = jnp.dot(low, g[:, sub * LANES : (sub + 1) * LANES], preferred_element_type=jnp.float32)
+        return part * row_weight
+
+    rows_to_blocks(scratch, x_outs, x_part, rows, capacity, subs)
+    rows_to_blocks(scratch, g_outs, g_part, rows, capacity, subs)
+
+
+def hold_kernel(count, *refs):
+    sems = refs[2 * count]
+    copies = [pltpu.make_async_copy(refs[i], refs[count + i], sems.at[i]) for i in range(count)]
+    for copy in copies:
+        copy.start()
+    for copy in copies:
+        copy.wait()
+
+
+def arrive_kernel(devices, capacity, subs, *refs):
+    blocks, out, scratch = refs[:devices], refs[devices], refs[devices + 1]
+
+    def put(sub, value):
+        out[:, sub * LANES : (sub + 1) * LANES] = value.astype(out.dtype)
+
+    blocks_to_rows(scratch, blocks, put, devices * capacity, capacity, subs)
+
+
+def leave_kernel(devices, capacity, subs, own, other, *refs):
+    outs, scratch = refs[:devices], refs[devices]
+
+    def take(sub):
+        cols = slice(sub * LANES, (sub + 1) * LANES)
+        return own[:, cols] + other[:, cols].astype(jnp.float32)
+
+    rows_to_blocks(scratch, outs, take, devices * capacity, capacity, subs)
+
+
+def forward_kernel(step, x_own, x_other, w_gate, w_up, w_down, x_full, gate, up, hidden, out_own, out_other):
+    half_width = x_own.shape[1]
+    lanes = gate.shape[1]
+    half = lax.axis_index("ffn")
+    own_at = pl.multiple_of(half * half_width, half_width)
+    other_at = pl.multiple_of((1 - half) * half_width, half_width)
+    x_full[:, pl.ds(own_at, half_width)] = x_own[...]
+    x_full[:, pl.ds(other_at, half_width)] = x_other[...]
+
+    def project(i, carry):
+        cols = pl.ds(pl.multiple_of(i * step, step), step)
+        gate_low = jnp.dot(x_full[...], w_gate[0, :, cols], preferred_element_type=jnp.float32).astype(jnp.bfloat16)
+        up_low = jnp.dot(x_full[...], w_up[0, :, cols], preferred_element_type=jnp.float32).astype(jnp.bfloat16)
+        gate[:, cols] = gate_low
+        up[:, cols] = up_low
+        gate_val = gate_low.astype(jnp.float32)
+        hidden[:, cols] = (gate_val * jax.nn.sigmoid(gate_val) * up_low.astype(jnp.float32)).astype(jnp.bfloat16)
+        return carry
+
+    lax.fori_loop(0, lanes // step, project, 0)
+
+    def spread(i, carry):
+        at = pl.multiple_of(i * step, step)
+        here = pl.ds(at, step)
+        other = jnp.dot(hidden[...], w_down[0, :, pl.ds(other_at + at, step)], preferred_element_type=jnp.float32)
+        out_other[:, here] = other.astype(jnp.bfloat16)
+        out_own[:, here] = jnp.dot(hidden[...], w_down[0, :, pl.ds(own_at + at, step)], preferred_element_type=jnp.float32)
+        return carry
+
+    lax.fori_loop(0, half_width // step, spread, 0)
+
+
+def backward_kernel(
+    step, g_own, g_other, gate, up, w_gate, w_up, w_down, g_full, pre_gate, pre_up, dx_own, dx_other
+):
+    half_width = g_own.shape[1]
+    lanes = gate.shape[1]
+    half = lax.axis_index("ffn")
+    own_at = pl.multiple_of(half * half_width, half_width)
+    other_at = pl.multiple_of((1 - half) * half_width, half_width)
+    g_full[:, pl.ds(own_at, half_width)] = g_own[...]
+    g_full[:, pl.ds(other_at, half_width)] = g_other[...]
+
+    def pull(i, carry):
+        cols = pl.ds(pl.multiple_of(i * step, step), step)
+        part = contract_cols(g_full[...], w_down[0, cols, :]).astype(jnp.bfloat16)
+        grad_hidden = part.astype(jnp.float32)
+        gate_val = gate[:, cols].astype(jnp.float32)
+        up_val = up[:, cols].astype(jnp.float32)
+        sig = jax.nn.sigmoid(gate_val)
+        pre_gate[:, cols] = (grad_hidden * up_val * sig * (1.0 + gate_val * (1.0 - sig))).astype(jnp.bfloat16)
+        pre_up[:, cols] = (grad_hidden * gate_val * sig).astype(jnp.bfloat16)
+        return carry
+
+    lax.fori_loop(0, lanes // step, pull, 0)
+
+    def spread(i, carry):
+        at = pl.multiple_of(i * step, step)
+        here = pl.ds(at, step)
+
+        def term(base):
+            there = pl.ds(base + at, step)
+            return contract_cols(pre_gate[...], w_gate[0, there, :]) + contract_cols(pre_up[...], w_up[0, there, :])
+
+        dx_other[:, here] = term(other_at).astype(jnp.bfloat16)
+        dx_own[:, here] = term(own_at)
+        return carry
+
+    lax.fori_loop(0, half_width // step, spread, 0)
+
+
+def outer_kernel(left, *refs):
+    count = len(refs) // 2
+    for right, out in zip(refs[:count], refs[count:]):
+        out[0] = contract_rows(left[...], right[...]).astype(out.dtype)
+
+
+def outer(left, rights, step):
+    rows, height = left.shape
+    width = rights[0].shape[1]
+    return pl.pallas_call(
+        outer_kernel,
+        grid=(height // step,),
+        out_shape=tuple(jax.ShapeDtypeStruct((1, height, width), jnp.bfloat16) for _ in rights),
+        in_specs=[pl.BlockSpec((rows, step), lambda i: (0, i))]
+        + [pl.BlockSpec((rows, width), lambda i: (0, 0)) for _ in rights],
+        out_specs=tuple(pl.BlockSpec((1, step, width), lambda i: (0, i, 0)) for _ in rights),
+        compiler_params=pltpu.CompilerParams(vmem_limit_bytes=24 * MIB),
+        cost_estimate=pl.CostEstimate(
+            flops=2 * rows * height * width * len(rights),
+            bytes_accessed=2 * height * width * len(rights),
+            transcendentals=0,
+        ),
+    )(left, *rights)
+
+
+def join_kernel(weighted, devices, capacity, subs, place, mix, *refs):
+    blocks, out, scratch = refs[:devices], refs[devices], refs[devices + 1]
+
+    def put(sub, value):
+        if weighted:
+            value = value * mix[...]
+        out[:, sub * LANES : (sub + 1) * LANES] = contract_rows(place[...], value.astype(jnp.bfloat16)).astype(out.dtype)
+
+    blocks_to_rows(scratch, blocks, put, devices * capacity, capacity, subs)
+
+
+def exchange(blocks, devices):
+    arrived = [blocks[0]]
+    for k in range(1, devices):
+        arrived.append(lax.ppermute(blocks[k], "expert", [(i, i ^ k) for i in range(devices)]))
+    return arrived
+
+
+def swap(value):
+    return lax.ppermute(value, "ffn", [(0, 1), (1, 0)])
+
+
+def one_piece_shards(tokens, grad_out, route_ids, route_weight, gate_weight, up_weight, down_weight):
+    tok_dev, sub_width = tokens.shape
+    top_count = route_ids.shape[1]
+    width = gate_weight.shape[1]
+    lanes = gate_weight.shape[2]
+    devices = lax.axis_size("expert")
+    capacity = max(2, min(tok_dev, (9 * tok_dev * top_count + 8 * EXPERTS - 1) // (8 * EXPERTS)))
+    rows = devices * capacity
+    subs = sub_width // LANES
+    low = jnp.bfloat16
+    block = jax.ShapeDtypeStruct((capacity * subs, LANES), low)
+    spread_scratch = [pltpu.VMEM((rows * subs, LANES), jnp.float32)]
+    sizes = (devices, capacity, subs)
+
+    routed = call(
+        functools.partial(route_kernel, *sizes),
+        [block] * (2 * devices)
+        + [jax.ShapeDtypeStruct((rows, tok_dev), low), jax.ShapeDtypeStruct((rows, LANES), jnp.float32)],
+        (route_ids.T, route_weight.T, tokens, grad_out),
+        scratch=spread_scratch,
+        traffic=4 * tok_dev * sub_width,
+    )
+    place, mix = routed[2 * devices :]
+    x_blocks = exchange(routed[:devices], devices)
+    g_blocks = exchange(routed[devices : 2 * devices], devices)
+
+    weights = (gate_weight, up_weight, down_weight)
+    w_gate, w_up, w_down = call(
+        functools.partial(hold_kernel, 3),
+        [vmem(w.shape, w.dtype) for w in weights],
+        weights,
+        in_spaces=[pl.ANY] * 3,
+        scratch=[pltpu.SemaphoreType.DMA((3,))],
+        traffic=sum(w.size * 2 for w in weights),
+    )
+
+    def arrive(blocks):
+        return call(
+            functools.partial(arrive_kernel, *sizes),
+            [vmem((rows, sub_width), low)],
+            blocks,
+            scratch=spread_scratch,
+            traffic=4 * rows * sub_width,
+        )[0]
+
+    x_own = arrive(x_blocks)
+    x_other = swap(x_own)
+    step = 256
+    x_full, gate, up, hidden, out_own, out_other = call(
+        functools.partial(forward_kernel, step),
+        [
+            vmem((rows, width), low),
+            vmem((rows, lanes), low),
+            vmem((rows, lanes), low),
+            vmem((rows, lanes), low),
+            vmem((rows, sub_width), jnp.float32),
+            vmem((rows, sub_width), low),
+        ],
+        (x_own, x_other, w_gate, w_up, w_down),
+        flops=6 * rows * width * lanes,
+    )
+    out_arrived = swap(out_other)
+    g_own = arrive(g_blocks)
+    g_other = swap(g_own)
+    g_full, pre_gate, pre_up, dx_own, dx_other = call(
+        functools.partial(backward_kernel, step),
+        [
+            vmem((rows, width), low),
+            vmem((rows, lanes), low),
+            vmem((rows, lanes), low),
+            vmem((rows, sub_width), jnp.float32),
+            vmem((rows, sub_width), low),
+        ],
+        (g_own, g_other, gate, up, w_gate, w_up, w_down),
+        flops=6 * rows * width * lanes,
+    )
+    dx_arrived = swap(dx_other)
+
+    def leave(own, other):
+        return call(
+            functools.partial(leave_kernel, *sizes),
+            [block] * devices,
+            (own, other),
+            scratch=spread_scratch,
+            traffic=8 * rows * sub_width,
+        )
+
+    out_blocks = exchange(leave(out_own, out_arrived), devices)
+    dx_blocks = exchange(leave(dx_own, dx_arrived), devices)
+    (grad_down,) = outer(hidden, [g_full], 128)
+    grad_gate, grad_up = outer(x_full, [pre_gate, pre_up], 512)
+
+    def join(weighted, blocks):
+        return call(
+            functools.partial(join_kernel, weighted, *sizes),
+            [jax.ShapeDtypeStruct((tok_dev, sub_width), low)],
+            (place, mix, *blocks),
+            scratch=spread_scratch,
+            traffic=4 * tok_dev * sub_width,
+        )[0]
+
+    return join(True, out_blocks), join(False, dx_blocks), grad_gate, grad_up, grad_down
+
+
+def shards(*args):
+    tokens, gate_weight = args[0], args[4]
+    halves = lax.axis_size("ffn")
+    devices = lax.axis_size("expert")
+    if halves == 2 and devices & (devices - 1) == 0 and tokens.shape[1] * halves == gate_weight.shape[1]:
+        return one_piece_shards(*args)
+    return general_shards(*args)
+
+
 def solution(mesh):
     in_specs = (
         P(("groups", "expert"), "ffn"),

time: 203 us -> 98.5 us (0.49)
  waiting for transfers between devices: 72.3 us -> 9.75 us
  matrix products: 49.3 us -> 0 us
  Pallas kernels: 0 us -> 29.3 us
  blocking collectives: 25.2 us -> 0 us
  starting transfers between devices: 24.2 us -> 46.4 us
  between operations: 13.9 us -> 0.77 us
  other arithmetic: 4.81 us -> 0 us
    all_to_all x6 -> x0, waiting for transfers between devices: 61.8 us -> none  [the longest x1 19.6 us: shards(): lax.all_to_all(x_send, 'expert', split_axis=0, concat_axis=0, tiled=True)]
    dot_general x15 -> x0, matrix products: 49.3 us -> none  [the longest x3 15.4 us: contract_cols(): lax.dot_general(left, right, (((1,), (1,)), ((), ())), preferred_element_...]
    ppermute x0 -> x32, starting transfers between devices: none -> 46.4 us  [the longest x28 45.6 us: exchange(): lax.ppermute(blocks[k], 'expert', [(i, i ^ k) for i in range(devices)])]
    pallas_call x0 -> x12, Pallas kernels: none -> 29.3 us  [the longest x10 17.5 us: call(): pl.pallas_call(kernel, out_shape=tuple(out_shape), in_specs=[pl.BlockSpec...]
    all_to_all x2 -> x0, blocking collectives: 25.2 us -> none  [spread_rows(): lax.all_to_all(copies, 'expert', split_axis=0, concat_axis=0, tiled=True)]
    all_to_all x6 -> x0, starting transfers between devices: 24 us -> none  [the longest x2 7.32 us: finish(): lax.all_to_all(summed, 'expert', split_axis=0, concat_axis=0, tiled=True)]
    all_gather x2 -> x0, waiting for transfers between devices: 10.4 us -> none  [the longest x1 7.68 us: shards(): lax.all_gather(tokens, 'ffn', axis=1, tiled=True)]
    ppermute x0 -> x32, waiting for transfers between devices: none -> 9.75 us  [the longest x28 9.74 us: exchange(): lax.ppermute(blocks[k], 'expert', [(i, i ^ k) for i in range(devices)])]
  transfers between devices with their start and end apart: 10 -> 32, of which waited for: 8 -> 7; matrix products, arithmetic and copies ran while one was open for 25% -> 0% of each run, Pallas kernels for 0% -> 28%
where the time goes in v1:
time: 98.5 us; the launch traced here: 98.1 us
  starting transfers between devices  46.4 us (47%)
  Pallas kernels  29.3 us (30%)
  local copies, waits for them, and re-layouts  11.8 us (12%)
  waiting for transfers between devices  9.75 us (10%)
    ppermute x28, starting transfers between devices, exchange(): lax.ppermute(blocks[k], 'expert', [(i, i ^ k) for i in range(devices)])  45.6 us
    pallas_call x10, Pallas kernels, call(): pl.pallas_call(kernel, out_shape=tuple(out_shape), in_specs=[pl.BlockSpec...  17.5 us
    pallas_call x2, Pallas kernels, outer(): pl.pallas_call(outer_kernel, grid=(height // step,), out_shape=tuple((jax...  11.8 us
    unnamed x14, local copies, waits for them, and re-layouts  11.8 us
    ppermute x28, waiting for transfers between devices, exchange(): lax.ppermute(blocks[k], 'expert', [(i, i ^ k) for i in range(devices)])  9.74 us
  transfers between devices with their start and end apart: 32, of which 7 were waited for; matrix products, arithmetic and copies ran while one was open for 0% of the time, Pallas kernels for 28%

profile of v1, /device:TPU:0, one launch (start us, length us, event | category | flops | bytes accessed | tf_op | source)
XLA Modules:
  0.0 98.1 jit_solution(2320330129694767842)
XLA Ops:
  4.9 3.0 %collective-permute-start = (bf16[144,128]{1,0:T(8,128)(2,1)S(1)}, bf16[144,128]{1,0:T(8,128)(2,1)S(1)}, u32[]{:S(2)}, u32[]{:S(2)}) collective-permute-start(bf16[144,128]{1,0:T(8,128)(2,1)S(1)} %get-tuple-element.58), channel_id=1, source_target_pairs={{0,2},{2,0},{4,6},{6,4},{8,10},{10,8},{12,14},{14,12},{1,3},{3,1},... | collective-permute-start | bytes 110600 | tf_op jit(solution)/shard_map/ppermute | solution.py:341
  7.9 1.6 %collective-permute-start.1 = (bf16[144,128]{1,0:T(8,128)(2,1)S(1)}, bf16[144,128]{1,0:T(8,128)(2,1)S(1)}, u32[]{:S(2)}, u32[]{:S(2)}) collective-permute-start(bf16[144,128]{1,0:T(8,128)(2,1)S(1)} %get-tuple-element.59), channel_id=1, source_target_pairs={{0,4},{2,6},{4,0},{6,2},{8,12},{10,14},{12,8},{14,10},{1,5},{3,7},... | collective-permute-start | bytes 110600 | tf_op jit(solution)/shard_map/ppermute | solution.py:341
  9.5 3.0 %collective-permute-start.3 = (bf16[144,128]{1,0:T(8,128)(2,1)S(1)}, bf16[144,128]{1,0:T(8,128)(2,1)S(1)}, u32[]{:S(2)}, u32[]{:S(2)}) collective-permute-start(bf16[144,128]{1,0:T(8,128)(2,1)S(1)} %get-tuple-element.61), channel_id=1, source_target_pairs={{0,8},{2,10},{4,12},{6,14},{8,0},{10,2},{12,4},{14,6},{1,9},{3,11}... | collective-permute-start | bytes 110600 | tf_op jit(solution)/shard_map/ppermute | solution.py:341
  12.5 1.3 %collective-permute-start.4 = (bf16[144,128]{1,0:T(8,128)(2,1)S(1)}, bf16[144,128]{1,0:T(8,128)(2,1)S(1)}, u32[]{:S(2)}, u32[]{:S(2)}) collective-permute-start(bf16[144,128]{1,0:T(8,128)(2,1)S(1)} %get-tuple-element.62), channel_id=1, source_target_pairs={{0,10},{2,8},{4,14},{6,12},{8,2},{10,0},{12,6},{14,4},{1,11},{3,9}... | collective-permute-start | bytes 110600 | tf_op jit(solution)/shard_map/ppermute | solution.py:341
  13.8 3.6 %collective-permute-start.5 = (bf16[144,128]{1,0:T(8,128)(2,1)S(1)}, bf16[144,128]{1,0:T(8,128)(2,1)S(1)}, u32[]{:S(2)}, u32[]{:S(2)}) collective-permute-start(bf16[144,128]{1,0:T(8,128)(2,1)S(1)} %get-tuple-element.63), channel_id=1, source_target_pairs={{0,12},{2,14},{4,8},{6,10},{8,4},{10,6},{12,0},{14,2},{1,13},{3,15... | collective-permute-start | bytes 110600 | tf_op jit(solution)/shard_map/ppermute | solution.py:341
  17.4 1.1 %collective-permute-done.4.refs_5_ = bf16[144,128]{1,0:T(8,128)(2,1)S(1)} collective-permute-done((bf16[144,128]{1,0:T(8,128)(2,1)S(1)}, bf16[144,128]{1,0:T(8,128)(2,1)S(1)}, u32[]{:S(2)}, u32[]{:S(2)}) %collective-permute-start.4) | collective-permute-done | bytes 36896 | tf_op jit(solution)/shard_map/ppermute | solution.py:341
  18.5 1.2 %collective-permute-done.5.refs_6_ = bf16[144,128]{1,0:T(8,128)(2,1)S(1)} collective-permute-done((bf16[144,128]{1,0:T(8,128)(2,1)S(1)}, bf16[144,128]{1,0:T(8,128)(2,1)S(1)}, u32[]{:S(2)}, u32[]{:S(2)}) %collective-permute-start.5) | collective-permute-done | bytes 36896 | tf_op jit(solution)/shard_map/ppermute | solution.py:341
  19.7 4.3 %collective-permute-done.6.refs_7_ = bf16[144,128]{1,0:T(8,128)(2,1)S(1)} collective-permute-done((bf16[144,128]{1,0:T(8,128)(2,1)S(1)}, bf16[144,128]{1,0:T(8,128)(2,1)S(1)}, u32[]{:S(2)}, u32[]{:S(2)}) %collective-permute-start.6) | collective-permute-done | bytes 36896 | tf_op jit(solution)/shard_map/ppermute | solution.py:341
  25.0 3.0 %collective-permute-start.18 = (bf16[144,128]{1,0:T(8,128)(2,1)S(1)}, bf16[144,128]{1,0:T(8,128)(2,1)S(1)}, u32[]{:S(2)}, u32[]{:S(2)}) collective-permute-start(bf16[144,128]{1,0:T(8,128)(2,1)S(1)} %get-tuple-element.81), channel_id=1, source_target_pairs={{0,6},{2,4},{4,2},{6,0},{8,14},{10,12},{12,10},{14,8},{1,7},{3,5},... | collective-permute-start | bytes 110600 | tf_op jit(solution)/shard_map/ppermute | solution.py:341
  28.4 2.4 %collective-permute-start.20 = (bf16[144,128]{1,0:T(8,128)(2,1)S(1)}, bf16[144,128]{1,0:T(8,128)(2,1)S(1)}, u32[]{:S(2)}, u32[]{:S(2)}) collective-permute-start(bf16[144,128]{1,0:T(8,128)(2,1)S(1)} %get-tuple-element.83), channel_id=1, source_target_pairs={{0,10},{2,8},{4,14},{6,12},{8,2},{10,0},{12,6},{14,4},{1,11},{3,9}... | collective-permute-start | bytes 110600 | tf_op jit(solution)/shard_map/ppermute | solution.py:341
  31.2 4.3 %collective-permute-start.22 = (bf16[144,128]{1,0:T(8,128)(2,1)S(1)}, bf16[144,128]{1,0:T(8,128)(2,1)S(1)}, u32[]{:S(2)}, u32[]{:S(2)}) collective-permute-start(bf16[144,128]{1,0:T(8,128)(2,1)S(1)} %get-tuple-element.85), channel_id=1, source_target_pairs={{0,14},{2,12},{4,10},{6,8},{8,6},{10,4},{12,2},{14,0},{1,15},{3,13... | collective-permute-start | bytes 110600 | tf_op jit(solution)/shard_map/ppermute | solution.py:341
  36.6 1.3 %collective-permute-done.22.refs_7_ = bf16[144,128]{1,0:T(8,128)(2,1)S(1)} collective-permute-done((bf16[144,128]{1,0:T(8,128)(2,1)S(1)}, bf16[144,128]{1,0:T(8,128)(2,1)S(1)}, u32[]{:S(2)}, u32[]{:S(2)}) %collective-permute-start.22) | collective-permute-done | bytes 36896 | tf_op jit(solution)/shard_map/ppermute | solution.py:341
  38.2 2.8 %copy-done = bf16[1,4096,768]{2,1,0:T(8,128)(2,1)S(1)} copy-done((bf16[1,4096,768]{2,1,0:T(8,128)(2,1)S(1)}, bf16[1,4096,768]{2,1,0:T(8,128)(2,1)}, u32[]{:S(2)}) %copy-start) | copy-done | bytes 6291480
  41.0 2.8 %copy-done.1 = bf16[1,4096,768]{2,1,0:T(8,128)(2,1)S(1)} copy-done((bf16[1,4096,768]{2,1,0:T(8,128)(2,1)S(1)}, bf16[1,4096,768]{2,1,0:T(8,128)(2,1)}, u32[]{:S(2)}) %copy-start.1) | copy-done | bytes 6291480
  43.8 2.8 %copy-done.2 = bf16[1,768,4096]{2,1,0:T(8,128)(2,1)S(1)} copy-done((bf16[1,768,4096]{2,1,0:T(8,128)(2,1)S(1)}, bf16[1,768,4096]{2,1,0:T(8,128)(2,1)}, u32[]{:S(2)}) %copy-start.2) | copy-done | bytes 6291480
  46.6 1.3 %shard_map.112 = (bf16[1,4096,768]{2,1,0:T(8,128)(2,1)S(1)}, bf16[1,4096,768]{2,1,0:T(8,128)(2,1)S(1)}, bf16[1,768,4096]{2,1,0:T(8,128)(2,1)S(1)}) custom-call(bf16[1,4096,768]{2,1,0:T(8,128)(2,1)S(1)} %copy-done, bf16[1,4096,768]{2,1,0:T(8,128)(2,1)S(1)} %copy-done.1, bf16[1,768,4096]{2,1,0:T(8,128)(2,1)S(1)} %copy-done.2), custom_call_target="tpu_custom_call" | custom-call | bytes 18874368 | tf_op jit(solution)/shard_map/pallas_call | solution.py:132
  47.9 4.8 %shard_map.113 = (bf16[72,4096]{1,0:T(8,128)(2,1)S(1)}, bf16[72,768]{1,0:T(8,128)(2,1)S(1)}, bf16[72,768]{1,0:T(8,128)(2,1)S(1)}, bf16[72,768]{1,0:T(8,128)(2,1)...) custom-call(bf16[72,2048]{1,0:T(8,128)(2,1)S(1)} %shard_map.111.x_own, ...), custom_call_target="tpu_custom_call" | custom-call | flops 1358954496 | tf_op jit(solution)/shard_map/pallas_call | solution.py:132
  53.2 7.2 %shard_map.117 = (bf16[72,4096]{1,0:T(8,128)(2,1)S(1)}, bf16[72,768]{1,0:T(8,128)(2,1)S(1)}, bf16[72,768]{1,0:T(8,128)(2,1)S(1)}, f32[72,2048]{1,0:T(8,128)S(1)}, bf16[72,2048]{1,0:T(8,128)(2,1)S(1)}) custom-call(bf16[72,2048]{1,0:T(8,128)(2,1)S(1)} %shard_map.116.g_own, bf16[72,2048]{1,0:T(8,128)(2,1)S(1)} %collective-permute-done.23.g_other, ...), custom_call_target="tpu_custom_call" | custom-call | flops 1358954496 | tf_op jit(solution)/shard_map/pallas_call | solution.py:132
  60.9 1.4 %collective-permute-start.9 = (bf16[144,128]{1,0:T(8,128)(2,1)S(1)}, bf16[144,128]{1,0:T(8,128)(2,1)S(1)}, u32[]{:S(2)}, u32[]{:S(2)}) collective-permute-start(bf16[144,128]{1,0:T(8,128)(2,1)S(1)} %get-tuple-element.71), channel_id=1, source_target_pairs={{0,2},{2,0},{4,6},{6,4},{8,10},{10,8},{12,14},{14,12},{1,3},{3,1},... | collective-permute-start | bytes 110600 | tf_op jit(solution)/shard_map/ppermute | solution.py:341
  62.2 2.2 %collective-permute-start.11 = (bf16[144,128]{1,0:T(8,128)(2,1)S(1)}, bf16[144,128]{1,0:T(8,128)(2,1)S(1)}, u32[]{:S(2)}, u32[]{:S(2)}) collective-permute-start(bf16[144,128]{1,0:T(8,128)(2,1)S(1)} %get-tuple-element.73), channel_id=1, source_target_pairs={{0,6},{2,4},{4,2},{6,0},{8,14},{10,12},{12,10},{14,8},{1,7},{3,5},... | collective-permute-start | bytes 110600 | tf_op jit(solution)/shard_map/ppermute | solution.py:341
  64.4 2.0 %collective-permute-start.12 = (bf16[144,128]{1,0:T(8,128)(2,1)S(1)}, bf16[144,128]{1,0:T(8,128)(2,1)S(1)}, u32[]{:S(2)}, u32[]{:S(2)}) collective-permute-start(bf16[144,128]{1,0:T(8,128)(2,1)S(1)} %get-tuple-element.74), channel_id=1, source_target_pairs={{0,8},{2,10},{4,12},{6,14},{8,0},{10,2},{12,4},{14,6},{1,9},{3,11}... | collective-permute-start | bytes 110600 | tf_op jit(solution)/shard_map/ppermute | solution.py:341
  66.4 1.7 %collective-permute-start.13 = (bf16[144,128]{1,0:T(8,128)(2,1)S(1)}, bf16[144,128]{1,0:T(8,128)(2,1)S(1)}, u32[]{:S(2)}, u32[]{:S(2)}) collective-permute-start(bf16[144,128]{1,0:T(8,128)(2,1)S(1)} %get-tuple-element.75), channel_id=1, source_target_pairs={{0,10},{2,8},{4,14},{6,12},{8,2},{10,0},{12,6},{14,4},{1,11},{3,9}... | collective-permute-start | bytes 110600 | tf_op jit(solution)/shard_map/ppermute | solution.py:341
  68.4 3.7 %collective-permute-start.14 = (bf16[144,128]{1,0:T(8,128)(2,1)S(1)}, bf16[144,128]{1,0:T(8,128)(2,1)S(1)}, u32[]{:S(2)}, u32[]{:S(2)}) collective-permute-start(bf16[144,128]{1,0:T(8,128)(2,1)S(1)} %get-tuple-element.76), channel_id=1, source_target_pairs={{0,12},{2,14},{4,8},{6,10},{8,4},{10,6},{12,0},{14,2},{1,13},{3,15... | collective-permute-start | bytes 110600 | tf_op jit(solution)/shard_map/ppermute | solution.py:341
  72.5 1.3 %collective-permute-start.25 = (bf16[144,128]{1,0:T(8,128)(2,1)S(1)}, bf16[144,128]{1,0:T(8,128)(2,1)S(1)}, u32[]{:S(2)}, u32[]{:S(2)}) collective-permute-start(bf16[144,128]{1,0:T(8,128)(2,1)S(1)} %get-tuple-element.91), channel_id=1, source_target_pairs={{0,2},{2,0},{4,6},{6,4},{8,10},{10,8},{12,14},{14,12},{1,3},{3,1},... | collective-permute-start | bytes 110600 | tf_op jit(solution)/shard_map/ppermute | solution.py:341
  73.8 7.0 %shard_map.120 = (bf16[1,4096,768]{2,1,0:T(8,128)(2,1)}, bf16[1,4096,768]{2,1,0:T(8,128)(2,1)}) custom-call(bf16[72,4096]{1,0:T(8,128)(2,1)S(1)} %get-tuple-element.98.left, bf16[72,768]{1,0:T(8,128)(2,1)S(1)} %get-tuple-element.99.refs_0_, bf16[72,768]{1,0:T(8,128)(2,1)S(1)} %get-tuple-element.100.refs_1_), custom_call_target="tpu_custom_call" | custom-call | flops 905969664 | bytes 12582912 | tf_op jit(solution)/shard_map/pallas_call | solution.py:311
  80.8 2.2 %collective-permute-start.27 = (bf16[144,128]{1,0:T(8,128)(2,1)S(1)}, bf16[144,128]{1,0:T(8,128)(2,1)S(1)}, u32[]{:S(2)}, u32[]{:S(2)}) collective-permute-start(bf16[144,128]{1,0:T(8,128)(2,1)S(1)} %get-tuple-element.93), channel_id=1, source_target_pairs={{0,6},{2,4},{4,2},{6,0},{8,14},{10,12},{12,10},{14,8},{1,7},{3,5},... | collective-permute-start | bytes 110600 | tf_op jit(solution)/shard_map/ppermute | solution.py:341
  83.0 2.0 %collective-permute-start.28 = (bf16[144,128]{1,0:T(8,128)(2,1)S(1)}, bf16[144,128]{1,0:T(8,128)(2,1)S(1)}, u32[]{:S(2)}, u32[]{:S(2)}) collective-permute-start(bf16[144,128]{1,0:T(8,128)(2,1)S(1)} %get-tuple-element.94), channel_id=1, source_target_pairs={{0,8},{2,10},{4,12},{6,14},{8,0},{10,2},{12,4},{14,6},{1,9},{3,11}... | collective-permute-start | bytes 110600 | tf_op jit(solution)/shard_map/ppermute | solution.py:341
  85.0 1.6 %collective-permute-start.29 = (bf16[144,128]{1,0:T(8,128)(2,1)S(1)}, bf16[144,128]{1,0:T(8,128)(2,1)S(1)}, u32[]{:S(2)}, u32[]{:S(2)}) collective-permute-start(bf16[144,128]{1,0:T(8,128)(2,1)S(1)} %get-tuple-element.95), channel_id=1, source_target_pairs={{0,10},{2,8},{4,14},{6,12},{8,2},{10,0},{12,6},{14,4},{1,11},{3,9}... | collective-permute-start | bytes 110600 | tf_op jit(solution)/shard_map/ppermute | solution.py:341
  86.6 3.6 %collective-permute-start.30 = (bf16[144,128]{1,0:T(8,128)(2,1)S(1)}, bf16[144,128]{1,0:T(8,128)(2,1)S(1)}, u32[]{:S(2)}, u32[]{:S(2)}) collective-permute-start(bf16[144,128]{1,0:T(8,128)(2,1)S(1)} %get-tuple-element.96), channel_id=1, source_target_pairs={{0,12},{2,14},{4,8},{6,10},{8,4},{10,6},{12,0},{14,2},{1,13},{3,15... | collective-permute-start | bytes 110600 | tf_op jit(solution)/shard_map/ppermute | solution.py:341
  90.6 4.8 %shard_map.121 = bf16[1,768,4096]{2,1,0:T(8,128)(2,1)} custom-call(bf16[72,768]{1,0:T(8,128)(2,1)S(1)} %get-tuple-element.103.left, bf16[72,4096]{1,0:T(8,128)(2,1)S(1)} %get-tuple-element.104.refs_0_), custom_call_target="tpu_custom_call" | custom-call | flops 452984832 | bytes 6291456 | tf_op jit(solution)/shard_map/pallas_call | solution.py:311
  95.4 1.2 %shard_map.115 = bf16[128,2048]{1,0:T(8,128)(2,1)} custom-call(bf16[72,128]{1,0:T(8,128)(2,1)S(1)} %get-tuple-element.55.place, f32[72,128]{1,0:T(8,128)S(1)} %get-tuple-element.56.mix, bf16[144,128]{1,0:T(8,128)(2,1)S(1)} %get-tuple-element.70.refs_0_, bf16[144,128]{1,0:T(8,128)(2,1)S(1)} %collective-permute-done.9.refs_1_, ...), custom_call_target="tpu_custom_call" | custom-call | bytes 1048576 | tf_op jit(solution)/shard_map/pallas_call | solution.py:132
  96.9 1.2 %shard_map.119 = bf16[128,2048]{1,0:T(8,128)(2,1)} custom-call(bf16[72,128]{1,0:T(8,128)(2,1)S(1)} %get-tuple-element.55.place, f32[72,128]{1,0:T(8,128)S(1)} %get-tuple-element.56.mix, bf16[144,128]{1,0:T(8,128)(2,1)S(1)} %get-tuple-element.90.refs_0_, bf16[144,128]{1,0:T(8,128)(2,1)S(1)} %collective-permute-done.25.refs_1_, ...), custom_call_target="tpu_custom_call" | custom-call | bytes 1048576 | tf_op jit(solution)/shard_map/pallas_call | solution.py:132
  (58 shorter events, 9.9 us)
Async XLA Ops:
  4.9 8.9 %collective-permute-start = (bf16[144,128]{1,0:T(8,128)(2,1)S(1)}, bf16[144,128]{1,0:T(8,128)(2,1)S(1)}, u32[]{:S(2)}, u32[]{:S(2)}) collective-permute-start(bf16[144,128]{1,0:T(8,128)(2,1)S(1)} %get-tuple-element.58), channel_id=1, source_target_pairs={{0,2},{2,0},{4,6},{6,4},{8,10},{10,8},{12,14},{14,12},{1,3},{3,1},... | collective-permute-start | bytes 110600 | tf_op jit(solution)/shard_map/ppermute | solution.py:341
  7.9 9.5 %collective-permute-start.1 = (bf16[144,128]{1,0:T(8,128)(2,1)S(1)}, bf16[144,128]{1,0:T(8,128)(2,1)S(1)}, u32[]{:S(2)}, u32[]{:S(2)}) collective-permute-start(bf16[144,128]{1,0:T(8,128)(2,1)S(1)} %get-tuple-element.59), channel_id=1, source_target_pairs={{0,4},{2,6},{4,0},{6,2},{8,12},{10,14},{12,8},{14,10},{1,5},{3,7},... | collective-permute-start | bytes 110600 | tf_op jit(solution)/shard_map/ppermute | solution.py:341
  9.5 7.9 %collective-permute-start.2 = (bf16[144,128]{1,0:T(8,128)(2,1)S(1)}, bf16[144,128]{1,0:T(8,128)(2,1)S(1)}, u32[]{:S(2)}, u32[]{:S(2)}) collective-permute-start(bf16[144,128]{1,0:T(8,128)(2,1)S(1)} %get-tuple-element.60), channel_id=1, source_target_pairs={{0,6},{2,4},{4,2},{6,0},{8,14},{10,12},{12,10},{14,8},{1,7},{3,5},... | collective-permute-start | bytes 110600 | tf_op jit(solution)/shard_map/ppermute | solution.py:341
  9.5 7.9 %collective-permute-start.3 = (bf16[144,128]{1,0:T(8,128)(2,1)S(1)}, bf16[144,128]{1,0:T(8,128)(2,1)S(1)}, u32[]{:S(2)}, u32[]{:S(2)}) collective-permute-start(bf16[144,128]{1,0:T(8,128)(2,1)S(1)} %get-tuple-element.61), channel_id=1, source_target_pairs={{0,8},{2,10},{4,12},{6,14},{8,0},{10,2},{12,4},{14,6},{1,9},{3,11}... | collective-permute-start | bytes 110600 | tf_op jit(solution)/shard_map/ppermute | solution.py:341
  12.5 6.0 %collective-permute-start.4 = (bf16[144,128]{1,0:T(8,128)(2,1)S(1)}, bf16[144,128]{1,0:T(8,128)(2,1)S(1)}, u32[]{:S(2)}, u32[]{:S(2)}) collective-permute-start(bf16[144,128]{1,0:T(8,128)(2,1)S(1)} %get-tuple-element.62), channel_id=1, source_target_pairs={{0,10},{2,8},{4,14},{6,12},{8,2},{10,0},{12,6},{14,4},{1,11},{3,9}... | collective-permute-start | bytes 110600 | tf_op jit(solution)/shard_map/ppermute | solution.py:341
  13.8 5.9 %collective-permute-start.5 = (bf16[144,128]{1,0:T(8,128)(2,1)S(1)}, bf16[144,128]{1,0:T(8,128)(2,1)S(1)}, u32[]{:S(2)}, u32[]{:S(2)}) collective-permute-start(bf16[144,128]{1,0:T(8,128)(2,1)S(1)} %get-tuple-element.63), channel_id=1, source_target_pairs={{0,12},{2,14},{4,8},{6,10},{8,4},{10,6},{12,0},{14,2},{1,13},{3,15... | collective-permute-start | bytes 110600 | tf_op jit(solution)/shard_map/ppermute | solution.py:341
  17.4 6.7 %collective-permute-start.6 = (bf16[144,128]{1,0:T(8,128)(2,1)S(1)}, bf16[144,128]{1,0:T(8,128)(2,1)S(1)}, u32[]{:S(2)}, u32[]{:S(2)}) collective-permute-start(bf16[144,128]{1,0:T(8,128)(2,1)S(1)} %get-tuple-element.64), channel_id=1, source_target_pairs={{0,14},{2,12},{4,10},{6,8},{8,6},{10,4},{12,2},{14,0},{1,15},{3,13... | collective-permute-start | bytes 110600 | tf_op jit(solution)/shard_map/ppermute | solution.py:341
  24.3 23.6 %collective-permute-start.7 = (bf16[72,2048]{1,0:T(8,128)(2,1)S(1)}, bf16[72,2048]{1,0:T(8,128)(2,1)S(1)}, u32[]{:S(2)}, u32[]{:S(2)}) collective-permute-start(bf16[72,2048]{1,0:T(8,128)(2,1)S(1)} %shard_map.111.x_own), channel_id=1, source_target_pairs={{0,1},{1,0},{2,3},{3,2},{4,5},{5,4},{6,7},{7,6},{8,9},{9,8},{10,11... | collective-permute-start | bytes 884744 | tf_op jit(solution)/shard_map/ppermute | solution.py:346
  24.4 4.0 %collective-permute-start.16 = (bf16[144,128]{1,0:T(8,128)(2,1)S(1)}, bf16[144,128]{1,0:T(8,128)(2,1)S(1)}, u32[]{:S(2)}, u32[]{:S(2)}) collective-permute-start(bf16[144,128]{1,0:T(8,128)(2,1)S(1)} %get-tuple-element.79), channel_id=1, source_target_pairs={{0,2},{2,0},{4,6},{6,4},{8,10},{10,8},{12,14},{14,12},{1,3},{3,1},... | collective-permute-start | bytes 110600 | tf_op jit(solution)/shard_map/ppermute | solution.py:341
  24.9 5.9 %collective-permute-start.17 = (bf16[144,128]{1,0:T(8,128)(2,1)S(1)}, bf16[144,128]{1,0:T(8,128)(2,1)S(1)}, u32[]{:S(2)}, u32[]{:S(2)}) collective-permute-start(bf16[144,128]{1,0:T(8,128)(2,1)S(1)} %get-tuple-element.80), channel_id=1, source_target_pairs={{0,4},{2,6},{4,0},{6,2},{8,12},{10,14},{12,8},{14,10},{1,5},{3,7},... | collective-permute-start | bytes 110600 | tf_op jit(solution)/shard_map/ppermute | solution.py:341
  25.0 6.3 %collective-permute-start.18 = (bf16[144,128]{1,0:T(8,128)(2,1)S(1)}, bf16[144,128]{1,0:T(8,128)(2,1)S(1)}, u32[]{:S(2)}, u32[]{:S(2)}) collective-permute-start(bf16[144,128]{1,0:T(8,128)(2,1)S(1)} %get-tuple-element.81), channel_id=1, source_target_pairs={{0,6},{2,4},{4,2},{6,0},{8,14},{10,12},{12,10},{14,8},{1,7},{3,5},... | collective-permute-start | bytes 110600 | tf_op jit(solution)/shard_map/ppermute | solution.py:341
  27.9 7.7 %collective-permute-start.19 = (bf16[144,128]{1,0:T(8,128)(2,1)S(1)}, bf16[144,128]{1,0:T(8,128)(2,1)S(1)}, u32[]{:S(2)}, u32[]{:S(2)}) collective-permute-start(bf16[144,128]{1,0:T(8,128)(2,1)S(1)} %get-tuple-element.82), channel_id=1, source_target_pairs={{0,8},{2,10},{4,12},{6,14},{8,0},{10,2},{12,4},{14,6},{1,9},{3,11}... | collective-permute-start | bytes 110600 | tf_op jit(solution)/shard_map/ppermute | solution.py:341
  28.4 7.2 %collective-permute-start.20 = (bf16[144,128]{1,0:T(8,128)(2,1)S(1)}, bf16[144,128]{1,0:T(8,128)(2,1)S(1)}, u32[]{:S(2)}, u32[]{:S(2)}) collective-permute-start(bf16[144,128]{1,0:T(8,128)(2,1)S(1)} %get-tuple-element.83), channel_id=1, source_target_pairs={{0,10},{2,8},{4,14},{6,12},{8,2},{10,0},{12,6},{14,4},{1,11},{3,9}... | collective-permute-start | bytes 110600 | tf_op jit(solution)/shard_map/ppermute | solution.py:341
  30.8 5.8 %collective-permute-start.21 = (bf16[144,128]{1,0:T(8,128)(2,1)S(1)}, bf16[144,128]{1,0:T(8,128)(2,1)S(1)}, u32[]{:S(2)}, u32[]{:S(2)}) collective-permute-start(bf16[144,128]{1,0:T(8,128)(2,1)S(1)} %get-tuple-element.84), channel_id=1, source_target_pairs={{0,12},{2,14},{4,8},{6,10},{8,4},{10,6},{12,0},{14,2},{1,13},{3,15... | collective-permute-start | bytes 110600 | tf_op jit(solution)/shard_map/ppermute | solution.py:341
  31.2 6.7 %collective-permute-start.22 = (bf16[144,128]{1,0:T(8,128)(2,1)S(1)}, bf16[144,128]{1,0:T(8,128)(2,1)S(1)}, u32[]{:S(2)}, u32[]{:S(2)}) collective-permute-start(bf16[144,128]{1,0:T(8,128)(2,1)S(1)} %get-tuple-element.85), channel_id=1, source_target_pairs={{0,14},{2,12},{4,10},{6,8},{8,6},{10,4},{12,2},{14,0},{1,15},{3,13... | collective-permute-start | bytes 110600 | tf_op jit(solution)/shard_map/ppermute | solution.py:341
  38.1 15.1 %collective-permute-start.23 = (bf16[72,2048]{1,0:T(8,128)(2,1)S(1)}, bf16[72,2048]{1,0:T(8,128)(2,1)S(1)}, u32[]{:S(2)}, u32[]{:S(2)}) collective-permute-start(bf16[72,2048]{1,0:T(8,128)(2,1)S(1)} %shard_map.116.g_own), channel_id=1, source_target_pairs={{0,1},{1,0},{2,3},{3,2},{4,5},{5,4},{6,7},{7,6},{8,9},{9,8},{10,11... | collective-permute-start | bytes 884744 | tf_op jit(solution)/shard_map/ppermute | solution.py:346
  52.7 7.8 %collective-permute-start.8 = (bf16[72,2048]{1,0:T(8,128)(2,1)S(1)}, bf16[72,2048]{1,0:T(8,128)(2,1)S(1)}, u32[]{:S(2)}, u32[]{:S(2)}) collective-permute-start(bf16[72,2048]{1,0:T(8,128)(2,1)S(1)} %get-tuple-element.69), channel_id=1, source_target_pairs={{0,1},{1,0},{2,3},{3,2},{4,5},{5,4},{6,7},{7,6},{8,9},{9,8},{10,11... | collective-permute-start | bytes 884744 | tf_op jit(solution)/shard_map/ppermute | solution.py:346
  60.4 6.0 %collective-permute-start.24 = (bf16[72,2048]{1,0:T(8,128)(2,1)S(1)}, bf16[72,2048]{1,0:T(8,128)(2,1)S(1)}, u32[]{:S(2)}, u32[]{:S(2)}) collective-permute-start(bf16[72,2048]{1,0:T(8,128)(2,1)S(1)} %get-tuple-element.89), channel_id=1, source_target_pairs={{0,1},{1,0},{2,3},{3,2},{4,5},{5,4},{6,7},{7,6},{8,9},{9,8},{10,11... | collective-permute-start | bytes 884744 | tf_op jit(solution)/shard_map/ppermute | solution.py:346
  60.9 7.5 %collective-permute-start.9 = (bf16[144,128]{1,0:T(8,128)(2,1)S(1)}, bf16[144,128]{1,0:T(8,128)(2,1)S(1)}, u32[]{:S(2)}, u32[]{:S(2)}) collective-permute-start(bf16[144,128]{1,0:T(8,128)(2,1)S(1)} %get-tuple-element.71), channel_id=1, source_target_pairs={{0,2},{2,0},{4,6},{6,4},{8,10},{10,8},{12,14},{14,12},{1,3},{3,1},... | collective-permute-start | bytes 110600 | tf_op jit(solution)/shard_map/ppermute | solution.py:341
  62.2 9.9 %collective-permute-start.10 = (bf16[144,128]{1,0:T(8,128)(2,1)S(1)}, bf16[144,128]{1,0:T(8,128)(2,1)S(1)}, u32[]{:S(2)}, u32[]{:S(2)}) collective-permute-start(bf16[144,128]{1,0:T(8,128)(2,1)S(1)} %get-tuple-element.72), channel_id=1, source_target_pairs={{0,4},{2,6},{4,0},{6,2},{8,12},{10,14},{12,8},{14,10},{1,5},{3,7},... | collective-permute-start | bytes 110600 | tf_op jit(solution)/shard_map/ppermute | solution.py:341
  62.2 10.3 %collective-permute-start.11 = (bf16[144,128]{1,0:T(8,128)(2,1)S(1)}, bf16[144,128]{1,0:T(8,128)(2,1)S(1)}, u32[]{:S(2)}, u32[]{:S(2)}) collective-permute-start(bf16[144,128]{1,0:T(8,128)(2,1)S(1)} %get-tuple-element.73), channel_id=1, source_target_pairs={{0,6},{2,4},{4,2},{6,0},{8,14},{10,12},{12,10},{14,8},{1,7},{3,5},... | collective-permute-start | bytes 110600 | tf_op jit(solution)/shard_map/ppermute | solution.py:341
  64.4 9.4 %collective-permute-start.12 = (bf16[144,128]{1,0:T(8,128)(2,1)S(1)}, bf16[144,128]{1,0:T(8,128)(2,1)S(1)}, u32[]{:S(2)}, u32[]{:S(2)}) collective-permute-start(bf16[144,128]{1,0:T(8,128)(2,1)S(1)} %get-tuple-element.74), channel_id=1, source_target_pairs={{0,8},{2,10},{4,12},{6,14},{8,0},{10,2},{12,4},{14,6},{1,9},{3,11}... | collective-permute-start | bytes 110600 | tf_op jit(solution)/shard_map/ppermute | solution.py:341
  66.4 14.4 %collective-permute-start.13 = (bf16[144,128]{1,0:T(8,128)(2,1)S(1)}, bf16[144,128]{1,0:T(8,128)(2,1)S(1)}, u32[]{:S(2)}, u32[]{:S(2)}) collective-permute-start(bf16[144,128]{1,0:T(8,128)(2,1)S(1)} %get-tuple-element.75), channel_id=1, source_target_pairs={{0,10},{2,8},{4,14},{6,12},{8,2},{10,0},{12,6},{14,4},{1,11},{3,9}... | collective-permute-start | bytes 110600 | tf_op jit(solution)/shard_map/ppermute | solution.py:341
  68.4 14.6 %collective-permute-start.14 = (bf16[144,128]{1,0:T(8,128)(2,1)S(1)}, bf16[144,128]{1,0:T(8,128)(2,1)S(1)}, u32[]{:S(2)}, u32[]{:S(2)}) collective-permute-start(bf16[144,128]{1,0:T(8,128)(2,1)S(1)} %get-tuple-element.76), channel_id=1, source_target_pairs={{0,12},{2,14},{4,8},{6,10},{8,4},{10,6},{12,0},{14,2},{1,13},{3,15... | collective-permute-start | bytes 110600 | tf_op jit(solution)/shard_map/ppermute | solution.py:341
  72.1 13.0 %collective-permute-start.15 = (bf16[144,128]{1,0:T(8,128)(2,1)S(1)}, bf16[144,128]{1,0:T(8,128)(2,1)S(1)}, u32[]{:S(2)}, u32[]{:S(2)}) collective-permute-start(bf16[144,128]{1,0:T(8,128)(2,1)S(1)} %get-tuple-element.77), channel_id=1, source_target_pairs={{0,14},{2,12},{4,10},{6,8},{8,6},{10,4},{12,2},{14,0},{1,15},{3,13... | collective-permute-start | bytes 110600 | tf_op jit(solution)/shard_map/ppermute | solution.py:341
  72.5 14.2 %collective-permute-start.25 = (bf16[144,128]{1,0:T(8,128)(2,1)S(1)}, bf16[144,128]{1,0:T(8,128)(2,1)S(1)}, u32[]{:S(2)}, u32[]{:S(2)}) collective-permute-start(bf16[144,128]{1,0:T(8,128)(2,1)S(1)} %get-tuple-element.91), channel_id=1, source_target_pairs={{0,2},{2,0},{4,6},{6,4},{8,10},{10,8},{12,14},{14,12},{1,3},{3,1},... | collective-permute-start | bytes 110600 | tf_op jit(solution)/shard_map/ppermute | solution.py:341
  73.8 16.5 %collective-permute-start.26 = (bf16[144,128]{1,0:T(8,128)(2,1)S(1)}, bf16[144,128]{1,0:T(8,128)(2,1)S(1)}, u32[]{:S(2)}, u32[]{:S(2)}) collective-permute-start(bf16[144,128]{1,0:T(8,128)(2,1)S(1)} %get-tuple-element.92), channel_id=1, source_target_pairs={{0,4},{2,6},{4,0},{6,2},{8,12},{10,14},{12,8},{14,10},{1,5},{3,7},... | collective-permute-start | bytes 110600 | tf_op jit(solution)/shard_map/ppermute | solution.py:341
  80.8 15.8 %collective-permute-start.27 = (bf16[144,128]{1,0:T(8,128)(2,1)S(1)}, bf16[144,128]{1,0:T(8,128)(2,1)S(1)}, u32[]{:S(2)}, u32[]{:S(2)}) collective-permute-start(bf16[144,128]{1,0:T(8,128)(2,1)S(1)} %get-tuple-element.93), channel_id=1, source_target_pairs={{0,6},{2,4},{4,2},{6,0},{8,14},{10,12},{12,10},{14,8},{1,7},{3,5},... | collective-permute-start | bytes 110600 | tf_op jit(solution)/shard_map/ppermute | solution.py:341
  83.0 13.6 %collective-permute-start.28 = (bf16[144,128]{1,0:T(8,128)(2,1)S(1)}, bf16[144,128]{1,0:T(8,128)(2,1)S(1)}, u32[]{:S(2)}, u32[]{:S(2)}) collective-permute-start(bf16[144,128]{1,0:T(8,128)(2,1)S(1)} %get-tuple-element.94), channel_id=1, source_target_pairs={{0,8},{2,10},{4,12},{6,14},{8,0},{10,2},{12,4},{14,6},{1,9},{3,11}... | collective-permute-start | bytes 110600 | tf_op jit(solution)/shard_map/ppermute | solution.py:341
  85.0 11.6 %collective-permute-start.29 = (bf16[144,128]{1,0:T(8,128)(2,1)S(1)}, bf16[144,128]{1,0:T(8,128)(2,1)S(1)}, u32[]{:S(2)}, u32[]{:S(2)}) collective-permute-start(bf16[144,128]{1,0:T(8,128)(2,1)S(1)} %get-tuple-element.95), channel_id=1, source_target_pairs={{0,10},{2,8},{4,14},{6,12},{8,2},{10,0},{12,6},{14,4},{1,11},{3,9}... | collective-permute-start | bytes 110600 | tf_op jit(solution)/shard_map/ppermute | solution.py:341
  86.6 10.0 %collective-permute-start.30 = (bf16[144,128]{1,0:T(8,128)(2,1)S(1)}, bf16[144,128]{1,0:T(8,128)(2,1)S(1)}, u32[]{:S(2)}, u32[]{:S(2)}) collective-permute-start(bf16[144,128]{1,0:T(8,128)(2,1)S(1)} %get-tuple-element.96), channel_id=1, source_target_pairs={{0,12},{2,14},{4,8},{6,10},{8,4},{10,6},{12,0},{14,2},{1,13},{3,15... | collective-permute-start | bytes 110600 | tf_op jit(solution)/shard_map/ppermute | solution.py:341
  90.3 6.7 %collective-permute-start.31 = (bf16[144,128]{1,0:T(8,128)(2,1)S(1)}, bf16[144,128]{1,0:T(8,128)(2,1)S(1)}, u32[]{:S(2)}, u32[]{:S(2)}) collective-permute-start(bf16[144,128]{1,0:T(8,128)(2,1)S(1)} %get-tuple-element.97), channel_id=1, source_target_pairs={{0,14},{2,12},{4,10},{6,8},{8,6},{10,4},{12,2},{14,0},{1,15},{3,13... | collective-permute-start | bytes 110600 | tf_op jit(solution)/shard_map/ppermute | solution.py:341
  (7 other events, 11.8 us)

commit v2 on v1

--- a/solution.py
+++ b/solution.py
@@ -140,32 +140,36 @@
     )(*args)
 
 
-def rows_to_blocks(scratch, outs, take, rows, capacity, subs):
+def rows_to_blocks(scratch, out, take, subs):
+    devices, size, _ = out.shape
     for sub in range(subs):
-        scratch[pl.ds(sub, rows, stride=subs), :] = take(sub)
-    size = capacity * subs
-    for place, out in enumerate(outs):
-        out[...] = scratch[place * size : (place + 1) * size, :].astype(out.dtype)
-
-
-def blocks_to_rows(scratch, blocks, put, rows, capacity, subs):
-    size = capacity * subs
-    for place, block in enumerate(blocks):
-        scratch[place * size : (place + 1) * size, :] = block[...].astype(jnp.float32)
+        scratch[pl.ds(sub, devices * size // subs, stride=subs), :] = take(sub)
+    for place in range(devices):
+        out[place] = scratch[place * size : (place + 1) * size, :].astype(out.dtype)
+
+
+def blocks_to_rows(scratch, blocks, put, subs):
+    devices, size, _ = blocks.shape
+    for place in range(devices):
+        scratch[place * size : (place + 1) * size, :] = blocks[place].astype(jnp.float32)
     for sub in range(subs):
-        put(sub, scratch[pl.ds(sub, rows, stride=subs), :])
-
-
-def route_kernel(devices, capacity, subs, ids, weight, x, g, *refs):
-    x_outs, g_outs = refs[:devices], refs[devices : 2 * devices]
-    place_out, mix_out, scratch = refs[2 * devices :]
+        put(sub, scratch[pl.ds(sub, devices * size // subs, stride=subs), :])
+
+
+def route_kernel(
+    devices, capacity, subs, ids_in, weight_in, x_in, g_in, x_out, g_out, place_out, mix_out, scratch, ids, weight, x, g, sems
+):
+    pairs = ((ids_in, ids), (weight_in, weight), (x_in, x), (g_in, g))
+    copies = [pltpu.make_async_copy(src, dst, sems.at[i]) for i, (src, dst) in enumerate(pairs)]
+    for copy in copies:
+        copy.start()
     top, tok = ids.shape
     rows = devices * capacity
-    me = lax.axis_index("expert")
-    order = lax.broadcasted_iota(jnp.int32, (devices, tok), 0)
-    expert = order ^ me
+    expert = lax.broadcasted_iota(jnp.int32, (devices, tok), 0)
     member = jnp.zeros((devices, tok), jnp.float32)
     mixing = jnp.zeros((devices, tok), jnp.float32)
+    copies[0].wait()
+    copies[1].wait()
     for route in range(top):
         hit = ids[route : route + 1, :] == expert
         member = jnp.where(hit, 1.0, member)
@@ -176,7 +180,7 @@
         jnp.where(before, 1.0, 0.0).astype(jnp.bfloat16),
         preferred_element_type=jnp.float32,
     )
-    target = jnp.where(member > 0, slots + capacity * order.astype(jnp.float32), -1.0)
+    target = jnp.where(member > 0, slots + capacity * expert.astype(jnp.float32), -1.0)
     row = lax.broadcasted_iota(jnp.int32, (rows, tok), 0).astype(jnp.float32)
     place = jnp.zeros((rows, tok), jnp.float32)
     mix = jnp.zeros((rows, tok), jnp.float32)
@@ -196,8 +200,10 @@
         part = jnp.dot(low, g[:, sub * LANES : (sub + 1) * LANES], preferred_element_type=jnp.float32)
         return part * row_weight
 
-    rows_to_blocks(scratch, x_outs, x_part, rows, capacity, subs)
-    rows_to_blocks(scratch, g_outs, g_part, rows, capacity, subs)
+    copies[2].wait()
+    rows_to_blocks(scratch, x_out, x_part, subs)
+    copies[3].wait()
+    rows_to_blocks(scratch, g_out, g_part, subs)
 
 
 def hold_kernel(count, *refs):
@@ -209,23 +215,19 @@
         copy.wait()
 
 
-def arrive_kernel(devices, capacity, subs, *refs):
-    blocks, out, scratch = refs[:devices], refs[devices], refs[devices + 1]
-
+def arrive_kernel(subs, blocks, out, scratch):
     def put(sub, value):
         out[:, sub * LANES : (sub + 1) * LANES] = value.astype(out.dtype)
 
-    blocks_to_rows(scratch, blocks, put, devices * capacity, capacity, subs)
-
-
-def leave_kernel(devices, capacity, subs, own, other, *refs):
-    outs, scratch = refs[:devices], refs[devices]
-
+    blocks_to_rows(scratch, blocks, put, subs)
+
+
+def leave_kernel(subs, own, other, out, scratch):
     def take(sub):
         cols = slice(sub * LANES, (sub + 1) * LANES)
         return own[:, cols] + other[:, cols].astype(jnp.float32)
 
-    rows_to_blocks(scratch, outs, take, devices * capacity, capacity, subs)
+    rows_to_blocks(scratch, out, take, subs)
 
 
 def forward_kernel(step, x_own, x_other, w_gate, w_up, w_down, x_full, gate, up, hidden, out_own, out_other):
@@ -299,17 +301,17 @@
     lax.fori_loop(0, half_width // step, spread, 0)
 
 
-def outer_kernel(left, *refs):
+def tall_outer_kernel(left, *refs):
     count = len(refs) // 2
     for right, out in zip(refs[:count], refs[count:]):
         out[0] = contract_rows(left[...], right[...]).astype(out.dtype)
 
 
-def outer(left, rights, step):
+def tall_outer(left, rights, step):
     rows, height = left.shape
     width = rights[0].shape[1]
     return pl.pallas_call(
-        outer_kernel,
+        tall_outer_kernel,
         grid=(height // step,),
         out_shape=tuple(jax.ShapeDtypeStruct((1, height, width), jnp.bfloat16) for _ in rights),
         in_specs=[pl.BlockSpec((rows, step), lambda i: (0, i))]
@@ -324,22 +326,42 @@
     )(left, *rights)
 
 
-def join_kernel(weighted, devices, capacity, subs, place, mix, *refs):
-    blocks, out, scratch = refs[:devices], refs[devices], refs[devices + 1]
-
+def wide_outer_kernel(left, right, out, flipped):
+    @pl.when(pl.program_id(0) == 0)
+    def _():
+        flipped[...] = left[...].astype(jnp.float32).T.astype(flipped.dtype)
+
+    out[0] = jnp.dot(flipped[...], right[...], preferred_element_type=jnp.float32).astype(out.dtype)
+
+
+def wide_outer(left, right, step):
+    rows, height = left.shape
+    width = right.shape[1]
+    return pl.pallas_call(
+        wide_outer_kernel,
+        grid=(width // step,),
+        out_shape=jax.ShapeDtypeStruct((1, height, width), jnp.bfloat16),
+        in_specs=[pl.BlockSpec((rows, height), lambda i: (0, 0)), pl.BlockSpec((rows, step), lambda i: (0, i))],
+        out_specs=pl.BlockSpec((1, height, step), lambda i: (0, 0, i)),
+        scratch_shapes=[pltpu.VMEM((height, rows), jnp.bfloat16)],
+        compiler_params=pltpu.CompilerParams(vmem_limit_bytes=24 * MIB),
+        cost_estimate=pl.CostEstimate(
+            flops=2 * rows * height * width, bytes_accessed=2 * height * width, transcendentals=0
+        ),
+    )(left, right)
+
+
+def join_kernel(weighted, subs, place, mix, blocks, out, scratch):
     def put(sub, value):
         if weighted:
             value = value * mix[...]
         out[:, sub * LANES : (sub + 1) * LANES] = contract_rows(place[...], value.astype(jnp.bfloat16)).astype(out.dtype)
 
-    blocks_to_rows(scratch, blocks, put, devices * capacity, capacity, subs)
-
-
-def exchange(blocks, devices):
-    arrived = [blocks[0]]
-    for k in range(1, devices):
-        arrived.append(lax.ppermute(blocks[k], "expert", [(i, i ^ k) for i in range(devices)]))
-    return arrived
+    blocks_to_rows(scratch, blocks, put, subs)
+
+
+def exchange(blocks):
+    return lax.all_to_all(blocks, "expert", split_axis=0, concat_axis=0, tiled=True)
 
 
 def swap(value):
@@ -356,27 +378,28 @@
     rows = devices * capacity
     subs = sub_width // LANES
     low = jnp.bfloat16
-    block = jax.ShapeDtypeStruct((capacity * subs, LANES), low)
+    blocks = jax.ShapeDtypeStruct((devices, capacity * subs, LANES), low)
     spread_scratch = [pltpu.VMEM((rows * subs, LANES), jnp.float32)]
-    sizes = (devices, capacity, subs)
-
-    routed = call(
-        functools.partial(route_kernel, *sizes),
-        [block] * (2 * devices)
-        + [jax.ShapeDtypeStruct((rows, tok_dev), low), jax.ShapeDtypeStruct((rows, LANES), jnp.float32)],
-        (route_ids.T, route_weight.T, tokens, grad_out),
-        scratch=spread_scratch,
+
+    sources = (route_ids.T, route_weight.T, tokens, grad_out)
+    x_sent, g_sent, place, mix = call(
+        functools.partial(route_kernel, devices, capacity, subs),
+        [blocks, blocks, jax.ShapeDtypeStruct((rows, tok_dev), low), jax.ShapeDtypeStruct((rows, LANES), jnp.float32)],
+        [pltpu.with_memory_space_constraint(value, pltpu.HBM) for value in sources],
+        in_spaces=[pl.ANY] * 4,
+        scratch=spread_scratch
+        + [pltpu.VMEM(value.shape, value.dtype) for value in sources]
+        + [pltpu.SemaphoreType.DMA((4,))],
         traffic=4 * tok_dev * sub_width,
     )
-    place, mix = routed[2 * devices :]
-    x_blocks = exchange(routed[:devices], devices)
-    g_blocks = exchange(routed[devices : 2 * devices], devices)
+    x_blocks = exchange(x_sent)
+    g_blocks = exchange(g_sent)
 
     weights = (gate_weight, up_weight, down_weight)
     w_gate, w_up, w_down = call(
         functools.partial(hold_kernel, 3),
         [vmem(w.shape, w.dtype) for w in weights],
-        weights,
+        [pltpu.with_memory_space_constraint(w, pltpu.HBM) for w in weights],
         in_spaces=[pl.ANY] * 3,
         scratch=[pltpu.SemaphoreType.DMA((3,))],
         traffic=sum(w.size * 2 for w in weights),
@@ -384,9 +407,9 @@
 
     def arrive(blocks):
         return call(
-            functools.partial(arrive_kernel, *sizes),
+            functools.partial(arrive_kernel, subs),
             [vmem((rows, sub_width), low)],
-            blocks,
+            (blocks,),
             scratch=spread_scratch,
             traffic=4 * rows * sub_width,
         )[0]
@@ -426,23 +449,23 @@
 
     def leave(own, other):
         return call(
-            functools.partial(leave_kernel, *sizes),
-            [block] * devices,
+            functools.partial(leave_kernel, subs),
+            [blocks],
             (own, other),
             scratch=spread_scratch,
             traffic=8 * rows * sub_width,
-        )
-
-    out_blocks = exchange(leave(out_own, out_arrived), devices)
-    dx_blocks = exchange(leave(dx_own, dx_arrived), devices)
-    (grad_down,) = outer(hidden, [g_full], 128)
-    grad_gate, grad_up = outer(x_full, [pre_gate, pre_up], 512)
+        )[0]
+
+    out_blocks = exchange(leave(out_own, out_arrived))
+    dx_blocks = exchange(leave(dx_own, dx_arrived))
+    grad_down = wide_outer(hidden, g_full, 512)
+    grad_gate, grad_up = tall_outer(x_full, [pre_gate, pre_up], 1024)
 
     def join(weighted, blocks):
         return call(
-            functools.partial(join_kernel, weighted, *sizes),
+            functools.partial(join_kernel, weighted, subs),
             [jax.ShapeDtypeStruct((tok_dev, sub_width), low)],
-            (place, mix, *blocks),
+            (place, mix, blocks),
             scratch=spread_scratch,
             traffic=4 * tok_dev * sub_width,
         )[0]
@@ -453,8 +476,7 @@
 def shards(*args):
     tokens, gate_weight = args[0], args[4]
     halves = lax.axis_size("ffn")
-    devices = lax.axis_size("expert")
-    if halves == 2 and devices & (devices - 1) == 0 and tokens.shape[1] * halves == gate_weight.shape[1]:
+    if halves == 2 and tokens.shape[1] * halves == gate_weight.shape[1]:
         return one_piece_shards(*args)
     return general_shards(*args)
 

time: 98.5 us -> 84.7 us (0.86)
  starting transfers between devices: 46.4 us -> 16.2 us
  blocking collectives: 0 us -> 17.4 us
  Pallas kernels: 29.3 us -> 37.2 us
  waiting for transfers between devices: 9.75 us -> 2.4 us
  local copies, waits for them, and re-layouts: 11.8 us -> 10.2 us
    ppermute x28 -> x0, starting transfers between devices: 45.6 us -> none  [exchange(): lax.ppermute(blocks[k], 'expert', [(i, i ^ k) for i in range(devices)])]
    all_to_all x0 -> x1, blocking collectives: none -> 17.4 us  [exchange(): lax.all_to_all(blocks, 'expert', split_axis=0, concat_axis=0, tiled=True)]
    all_to_all x0 -> x3, starting transfers between devices: none -> 15.4 us  [exchange(): lax.all_to_all(blocks, 'expert', split_axis=0, concat_axis=0, tiled=True)]
    ppermute x28 -> x0, waiting for transfers between devices: 9.74 us -> none  [exchange(): lax.ppermute(blocks[k], 'expert', [(i, i ^ k) for i in range(devices)])]
    pallas_call x10, Pallas kernels: 17.5 us -> 25.9 us  [call(): pl.pallas_call(kernel, out_shape=tuple(out_shape), in_specs=[pl.BlockSpec...]
    ppermute x4, waiting for transfers between devices: 0.01 us -> 2.39 us  [swap(): return lax.ppermute(value, 'ffn', [(0, 1), (1, 0)])]
    unnamed x14 -> x12, local copies, waits for them, and re-layouts: 11.8 us -> 10.2 us
  transfers between devices with their start and end apart: 32 -> 7, of which waited for: 7 -> 2; matrix products, arithmetic and copies ran while one was open for 0% -> 0% of each run, Pallas kernels for 28% -> 40%
where the time goes in v2:
time: 84.7 us; the launch traced here: 84.1 us
  Pallas kernels  37.2 us (44%)
  blocking collectives  17.4 us (21%)
  starting transfers between devices  16.2 us (19%)
  local copies, waits for them, and re-layouts  10.2 us (12%)
  waiting for transfers between devices  2.4 us (3%)
    pallas_call x10, Pallas kernels, call(): pl.pallas_call(kernel, out_shape=tuple(out_shape), in_specs=[pl.BlockSpec...  25.9 us
    all_to_all x1, blocking collectives, exchange(): lax.all_to_all(blocks, 'expert', split_axis=0, concat_axis=0, tiled=True)  17.4 us
    all_to_all x3, starting transfers between devices, exchange(): lax.all_to_all(blocks, 'expert', split_axis=0, concat_axis=0, tiled=True)  15.4 us
    unnamed x12, local copies, waits for them, and re-layouts  10.2 us
    pallas_call x1, Pallas kernels, tall_outer(): pl.pallas_call(tall_outer_kernel, grid=(height // step,), out_shape=tuple...  5.84 us
    pallas_call x1, Pallas kernels, wide_outer(): pl.pallas_call(wide_outer_kernel, grid=(width // step,), out_shape=jax.Sh...  5.44 us
    ppermute x4, waiting for transfers between devices, swap(): return lax.ppermute(value, 'ffn', [(0, 1), (1, 0)])  2.39 us
  transfers between devices with their start and end apart: 7, of which 2 were waited for; matrix products, arithmetic and copies ran while one was open for 0% of the time, Pallas kernels for 40%

profile of v2, /device:TPU:0, one launch (start us, length us, event | category | flops | bytes accessed | tf_op | source)
XLA Modules:
  0.0 84.1 jit_solution(10123666307840077440)
XLA Ops:
  0.6 2.6 %shard_map.110 = (bf16[8,144,128]{2,1,0:T(8,128)(2,1)S(1)}, bf16[8,144,128]{2,1,0:T(8,128)(2,1)}, bf16[72,128]{1,0:T(8,128)(2,1)S(1)}, f32[72,128]{1,0:T(8,128)S(1)}) custom-call(s32[8,128]{1,0:T(8,128)} %bitcast.2, f32[8,128]{1,0:T(8,128)} %bitcast.3, bf16[128,2048]{1,0:T(8,128)(2,1)} %x_in.1, bf16[128,2048]{1,0:T(8,128)(2,1)} %g_in.1), custom_call_target="tpu_custom_call" | custom-call | bytes 1048576 | tf_op jit(solution)/shard_map/pallas_call | solution.py:132
  3.3 17.4 %all_to_all.20.blocks = bf16[8,144,128]{2,1,0:T(8,128)(2,1)S(1)} all-to-all(bf16[8,144,128]{2,1,0:T(8,128)(2,1)S(1)} %get-tuple-element.27), channel_id=1, replica_groups=mesh['groups'=2,'expert'=8,'ffn'=2] {'expert'}, dimensions={0} | all-to-all | bytes 589824 | tf_op jit(solution)/shard_map/all_to_all | solution.py:364
  20.7 3.4 %all-to-all-start.2 = ((bf16[8,144,128]{2,1,0:T(8,128)(2,1)}), bf16[8,144,128]{2,1,0:T(8,128)(2,1)S(1)}, u32[]{:S(2)}, u32[]{:S(2)}) async-start(bf16[8,144,128]{2,1,0:T(8,128)(2,1)} %get-tuple-element.33), calls=%async_computation.2 | async-start | bytes 589824 | tf_op jit(solution)/shard_map/all_to_all | solution.py:364
  24.1 0.2 shard_map.111.x_own
  24.3 0.1 collective-permute-start
  24.4 6.4 %shard_map.112 = (bf16[1,4096,768]{2,1,0:T(8,128)(2,1)S(1)}, bf16[1,4096,768]{2,1,0:T(8,128)(2,1)S(1)}, bf16[1,768,4096]{2,1,0:T(8,128)(2,1)S(1)}) custom-call(bf16[1,4096,768]{2,1,0:T(8,128)(2,1)} %refs_0_.1, bf16[1,4096,768]{2,1,0:T(8,128)(2,1)} %refs_1_.1, bf16[1,768,4096]{2,1,0:T(8,128)(2,1)} %refs_2_.1), custom_call_target="tpu_custom_call" | custom-call | bytes 18874368 | tf_op jit(solution)/shard_map/pallas_call | solution.py:132
  30.9 0.0 copy-start
  30.9 0.0 copy-start.2
  30.9 0.0 copy-start.4
  30.9 0.0 collective-permute-done.x_other
  30.9 4.8 %shard_map.113 = (bf16[72,4096]{1,0:T(8,128)(2,1)S(1)}, bf16[72,768]{1,0:T(8,128)(2,1)S(1)}, bf16[72,768]{1,0:T(8,128)(2,1)S(1)}, bf16[72,768]{1,0:T(8,128)(2,1)...) custom-call(bf16[72,2048]{1,0:T(8,128)(2,1)S(1)} %shard_map.111.x_own, ...), custom_call_target="tpu_custom_call" | custom-call | flops 1358954496 | tf_op jit(solution)/shard_map/pallas_call | solution.py:132
  35.7 1.8 %copy-done.4 = bf16[1,768,4096]{2,1,0:T(8,128)(2,1)} copy-done((bf16[1,768,4096]{2,1,0:T(8,128)(2,1)}, bf16[1,768,4096]{2,1,0:T(8,128)(2,1)S(1)}, u32[]{:S(2)}) %copy-start.4) | copy-done | bytes 6291480
  37.5 0.5 collective-permute-start.1
  38.0 0.2 shard_map.116.g_own
  38.3 0.1 collective-permute-start.2
  38.3 0.9 %collective-permute-done.1.other = bf16[72,2048]{1,0:T(8,128)(2,1)S(1)} collective-permute-done((bf16[72,2048]{1,0:T(8,128)(2,1)S(1)}, bf16[72,2048]{1,0:T(8,128)(2,1)S(1)}, u32[]{:S(2)}, u32[]{:S(2)}) %collective-permute-start.1) | collective-permute-done | bytes 294944 | tf_op jit(solution)/shard_map/ppermute | solution.py:368
  39.2 1.0 %shard_map.114 = bf16[8,144,128]{2,1,0:T(8,128)(2,1)} custom-call(f32[72,2048]{1,0:T(8,128)S(1)} %get-tuple-element.31.own, bf16[72,2048]{1,0:T(8,128)(2,1)S(1)} %collective-permute-done.1.other), custom_call_target="tpu_custom_call" | custom-call | bytes 1179648 | tf_op jit(solution)/shard_map/pallas_call | solution.py:132
  40.3 5.9 %all-to-all-start.1 = ((bf16[8,144,128]{2,1,0:T(8,128)(2,1)}), bf16[8,144,128]{2,1,0:T(8,128)(2,1)S(1)}, u32[]{:S(2)}, u32[]{:S(2)}) async-start(bf16[8,144,128]{2,1,0:T(8,128)(2,1)} %shard_map.114), calls=%async_computation.1 | async-start | bytes 589824 | tf_op jit(solution)/shard_map/all_to_all | solution.py:364
  46.2 0.0 collective-permute-done.2.g_other
  46.2 0.0 copy-start.1
  46.2 2.8 %copy-done.1 = bf16[1,4096,768]{2,1,0:T(8,128)(2,1)S(1)} copy-done((bf16[1,4096,768]{2,1,0:T(8,128)(2,1)S(1)}, bf16[1,4096,768]{2,1,0:T(8,128)(2,1)}, u32[]{:S(2)}) %copy-start.1) | copy-done | bytes 6291480
  49.0 2.8 %copy-done.3 = bf16[1,4096,768]{2,1,0:T(8,128)(2,1)S(1)} copy-done((bf16[1,4096,768]{2,1,0:T(8,128)(2,1)S(1)}, bf16[1,4096,768]{2,1,0:T(8,128)(2,1)}, u32[]{:S(2)}) %copy-start.3) | copy-done | bytes 6291480
  51.8 2.8 %copy-done.5 = bf16[1,768,4096]{2,1,0:T(8,128)(2,1)S(1)} copy-done((bf16[1,768,4096]{2,1,0:T(8,128)(2,1)S(1)}, bf16[1,768,4096]{2,1,0:T(8,128)(2,1)}, u32[]{:S(2)}) %copy-start.5) | copy-done | bytes 6291480
  54.6 7.2 %shard_map.117 = (bf16[72,4096]{1,0:T(8,128)(2,1)S(1)}, bf16[72,768]{1,0:T(8,128)(2,1)S(1)}, bf16[72,768]{1,0:T(8,128)(2,1)S(1)}, f32[72,2048]{1,0:T(8,128)S(1)}, bf16[72,2048]{1,0:T(8,128)(2,1)S(1)}) custom-call(bf16[72,2048]{1,0:T(8,128)(2,1)S(1)} %shard_map.116.g_own, bf16[72,2048]{1,0:T(8,128)(2,1)S(1)} %collective-permute-done.2.g_other, ...), custom_call_target="tpu_custom_call" | custom-call | flops 1358954496 | tf_op jit(solution)/shard_map/pallas_call | solution.py:132
  61.8 0.1 collective-permute-start.3
  61.9 1.5 %collective-permute-done.3.other = bf16[72,2048]{1,0:T(8,128)(2,1)S(1)} collective-permute-done((bf16[72,2048]{1,0:T(8,128)(2,1)S(1)}, bf16[72,2048]{1,0:T(8,128)(2,1)S(1)}, u32[]{:S(2)}, u32[]{:S(2)}) %collective-permute-start.3) | collective-permute-done | bytes 294944 | tf_op jit(solution)/shard_map/ppermute | solution.py:368
  63.4 1.1 %shard_map.118 = bf16[8,144,128]{2,1,0:T(8,128)(2,1)} custom-call(f32[72,2048]{1,0:T(8,128)S(1)} %get-tuple-element.36.own, bf16[72,2048]{1,0:T(8,128)(2,1)S(1)} %collective-permute-done.3.other), custom_call_target="tpu_custom_call" | custom-call | bytes 1179648 | tf_op jit(solution)/shard_map/pallas_call | solution.py:132
  64.5 6.0 %all-to-all-start.3 = ((bf16[8,144,128]{2,1,0:T(8,128)(2,1)}), bf16[8,144,128]{2,1,0:T(8,128)(2,1)S(1)}, u32[]{:S(2)}, u32[]{:S(2)}) async-start(bf16[8,144,128]{2,1,0:T(8,128)(2,1)} %shard_map.118), calls=%async_computation.3 | async-start | bytes 589824 | tf_op jit(solution)/shard_map/all_to_all | solution.py:364
  70.5 5.4 %shard_map.121 = bf16[1,768,4096]{2,1,0:T(8,128)(2,1)} custom-call(bf16[72,768]{1,0:T(8,128)(2,1)S(1)} %get-tuple-element.43.left, bf16[72,4096]{1,0:T(8,128)(2,1)S(1)} %get-tuple-element.44.right), custom_call_target="tpu_custom_call" | custom-call | flops 452984832 | bytes 6291456 | tf_op jit(solution)/shard_map/pallas_call | solution.py:340
  75.9 5.8 %shard_map.120 = (bf16[1,4096,768]{2,1,0:T(8,128)(2,1)}, bf16[1,4096,768]{2,1,0:T(8,128)(2,1)}) custom-call(bf16[72,4096]{1,0:T(8,128)(2,1)S(1)} %get-tuple-element.38.left, bf16[72,768]{1,0:T(8,128)(2,1)S(1)} %get-tuple-element.39.refs_0_, bf16[72,768]{1,0:T(8,128)(2,1)S(1)} %get-tuple-element.40.refs_1_), custom_call_target="tpu_custom_call" | custom-call | flops 905969664 | bytes 12582912 | tf_op jit(solution)/shard_map/pallas_call | solution.py:313
  81.7 1.2 %shard_map.115 = bf16[128,2048]{1,0:T(8,128)(2,1)} custom-call(bf16[72,128]{1,0:T(8,128)(2,1)S(1)} %get-tuple-element.25.place, f32[72,128]{1,0:T(8,128)S(1)} %get-tuple-element.26.mix, bf16[8,144,128]{2,1,0:T(8,128)(2,1)S(1)} %all-to-all-done.1.blocks), custom_call_target="tpu_custom_call" | custom-call | bytes 1048576 | tf_op jit(solution)/shard_map/pallas_call | solution.py:132
  82.9 1.2 %shard_map.119 = bf16[128,2048]{1,0:T(8,128)(2,1)} custom-call(bf16[72,128]{1,0:T(8,128)(2,1)S(1)} %get-tuple-element.25.place, f32[72,128]{1,0:T(8,128)S(1)} %get-tuple-element.26.mix, bf16[8,144,128]{2,1,0:T(8,128)(2,1)S(1)} %all-to-all-done.3.blocks), custom_call_target="tpu_custom_call" | custom-call | bytes 1048576 | tf_op jit(solution)/shard_map/pallas_call | solution.py:132
  (7 shorter events, 0.0 us)
Async XLA Ops:
  20.7 17.3 %all-to-all-start.2 = ((bf16[8,144,128]{2,1,0:T(8,128)(2,1)}), bf16[8,144,128]{2,1,0:T(8,128)(2,1)S(1)}, u32[]{:S(2)}, u32[]{:S(2)}) async-start(bf16[8,144,128]{2,1,0:T(8,128)(2,1)} %get-tuple-element.33), calls=%async_computation.2 | async-start | bytes 589824 | tf_op jit(solution)/shard_map/all_to_all | solution.py:364
  24.3 6.6 %collective-permute-start = (bf16[72,2048]{1,0:T(8,128)(2,1)S(1)}, bf16[72,2048]{1,0:T(8,128)(2,1)S(1)}, u32[]{:S(2)}, u32[]{:S(2)}) collective-permute-start(bf16[72,2048]{1,0:T(8,128)(2,1)S(1)} %shard_map.111.x_own), channel_id=1, source_target_pairs={{0,1},{1,0},{2,3},{3,2},{4,5},{5,4},{6,7},{7,6},{8,9},{9,8},{10,11... | collective-permute-start | bytes 884744 | tf_op jit(solution)/shard_map/ppermute | solution.py:368
  30.9 4.9 %copy-start = (bf16[1,4096,768]{2,1,0:T(8,128)(2,1)}, bf16[1,4096,768]{2,1,0:T(8,128)(2,1)S(1)}, u32[]{:S(2)}) copy-start(bf16[1,4096,768]{2,1,0:T(8,128)(2,1)S(1)} %get-tuple-element.28.w_gate) | copy-start | bytes 18874372
  30.9 4.9 %copy-start.2 = (bf16[1,4096,768]{2,1,0:T(8,128)(2,1)}, bf16[1,4096,768]{2,1,0:T(8,128)(2,1)S(1)}, u32[]{:S(2)}) copy-start(bf16[1,4096,768]{2,1,0:T(8,128)(2,1)S(1)} %get-tuple-element.29.w_up) | copy-start | bytes 18874372
  30.9 6.6 %copy-start.4 = (bf16[1,768,4096]{2,1,0:T(8,128)(2,1)}, bf16[1,768,4096]{2,1,0:T(8,128)(2,1)S(1)}, u32[]{:S(2)}) copy-start(bf16[1,768,4096]{2,1,0:T(8,128)(2,1)S(1)} %get-tuple-element.30.w_down) | copy-start | bytes 18874372
  37.5 1.7 %collective-permute-start.1 = (bf16[72,2048]{1,0:T(8,128)(2,1)S(1)}, bf16[72,2048]{1,0:T(8,128)(2,1)S(1)}, u32[]{:S(2)}, u32[]{:S(2)}) collective-permute-start(bf16[72,2048]{1,0:T(8,128)(2,1)S(1)} %get-tuple-element.32), channel_id=1, source_target_pairs={{0,1},{1,0},{2,3},{3,2},{4,5},{5,4},{6,7},{7,6},{8,9},{9,8},{10,11... | collective-permute-start | bytes 884744 | tf_op jit(solution)/shard_map/ppermute | solution.py:368
  38.3 8.0 %collective-permute-start.2 = (bf16[72,2048]{1,0:T(8,128)(2,1)S(1)}, bf16[72,2048]{1,0:T(8,128)(2,1)S(1)}, u32[]{:S(2)}, u32[]{:S(2)}) collective-permute-start(bf16[72,2048]{1,0:T(8,128)(2,1)S(1)} %shard_map.116.g_own), channel_id=1, source_target_pairs={{0,1},{1,0},{2,3},{3,2},{4,5},{5,4},{6,7},{7,6},{8,9},{9,8},{10,11... | collective-permute-start | bytes 884744 | tf_op jit(solution)/shard_map/ppermute | solution.py:368
  40.3 24.2 %all-to-all-start.1 = ((bf16[8,144,128]{2,1,0:T(8,128)(2,1)}), bf16[8,144,128]{2,1,0:T(8,128)(2,1)S(1)}, u32[]{:S(2)}, u32[]{:S(2)}) async-start(bf16[8,144,128]{2,1,0:T(8,128)(2,1)} %shard_map.114), calls=%async_computation.1 | async-start | bytes 589824 | tf_op jit(solution)/shard_map/all_to_all | solution.py:364
  46.2 2.8 %copy-start.1 = (bf16[1,4096,768]{2,1,0:T(8,128)(2,1)S(1)}, bf16[1,4096,768]{2,1,0:T(8,128)(2,1)}, u32[]{:S(2)}) copy-start(bf16[1,4096,768]{2,1,0:T(8,128)(2,1)} %copy-done) | copy-start | bytes 18874372
  49.0 2.8 %copy-start.3 = (bf16[1,4096,768]{2,1,0:T(8,128)(2,1)S(1)}, bf16[1,4096,768]{2,1,0:T(8,128)(2,1)}, u32[]{:S(2)}) copy-start(bf16[1,4096,768]{2,1,0:T(8,128)(2,1)} %copy-done.2) | copy-start | bytes 18874372
  51.8 2.8 %copy-start.5 = (bf16[1,768,4096]{2,1,0:T(8,128)(2,1)S(1)}, bf16[1,768,4096]{2,1,0:T(8,128)(2,1)}, u32[]{:S(2)}) copy-start(bf16[1,768,4096]{2,1,0:T(8,128)(2,1)} %copy-done.4) | copy-start | bytes 18874372
  61.8 1.6 %collective-permute-start.3 = (bf16[72,2048]{1,0:T(8,128)(2,1)S(1)}, bf16[72,2048]{1,0:T(8,128)(2,1)S(1)}, u32[]{:S(2)}, u32[]{:S(2)}) collective-permute-start(bf16[72,2048]{1,0:T(8,128)(2,1)S(1)} %get-tuple-element.37), channel_id=1, source_target_pairs={{0,1},{1,0},{2,3},{3,2},{4,5},{5,4},{6,7},{7,6},{8,9},{9,8},{10,11... | collective-permute-start | bytes 884744 | tf_op jit(solution)/shard_map/ppermute | solution.py:368
  64.5 18.5 %all-to-all-start.3 = ((bf16[8,144,128]{2,1,0:T(8,128)(2,1)}), bf16[8,144,128]{2,1,0:T(8,128)(2,1)S(1)}, u32[]{:S(2)}, u32[]{:S(2)}) async-start(bf16[8,144,128]{2,1,0:T(8,128)(2,1)} %shard_map.118), calls=%async_computation.3 | async-start | bytes 589824 | tf_op jit(solution)/shard_map/all_to_all | solution.py:364

commit v3 on v0

--- a/solution.py
+++ b/solution.py
@@ -1,9 +1,15 @@
+import functools
+
 import jax
 import jax.numpy as jnp
 from jax import lax
+from jax.experimental import pallas as pl
+from jax.experimental.pallas import tpu as pltpu
 from jax.sharding import PartitionSpec as P
 
 EXPERTS = 128
+LANES = 128
+MIB = 1024 * 1024
 
 
 def contract_rows(left, right):
@@ -18,7 +24,7 @@
     )
 
 
-def shards(tokens, grad_out, route_ids, route_weight, gate_weight, up_weight, down_weight):
+def general_shards(tokens, grad_out, route_ids, route_weight, gate_weight, up_weight, down_weight):
     tokens, grad_out = (
         lax.all_gather(tokens, "ffn", axis=1, tiled=True),
         lax.all_gather(grad_out, "ffn", axis=1, tiled=True),
@@ -116,6 +122,426 @@
     return (out_tokens, grad_tokens, grad_gate[None], grad_up[None], grad_down[None])
 
 
+def vmem(shape, dtype):
+    return pltpu.VMEM(shape, dtype)
+
+
+def call(kernel, out_shape, args, in_spaces=None, out_spaces=None, flops=0, traffic=0, scratch=(), limit=16):
+    spaces = in_spaces or [pltpu.VMEM] * len(args)
+    outs = out_spaces or [pltpu.VMEM] * len(out_shape)
+    return pl.pallas_call(
+        kernel,
+        out_shape=tuple(out_shape),
+        in_specs=[pl.BlockSpec(memory_space=space) for space in spaces],
+        out_specs=tuple(pl.BlockSpec(memory_space=space) for space in outs),
+        scratch_shapes=list(scratch),
+        compiler_params=pltpu.CompilerParams(vmem_limit_bytes=limit * MIB),
+        cost_estimate=pl.CostEstimate(flops=flops, bytes_accessed=traffic, transcendentals=0),
+    )(*args)
+
+
+def rows_to_blocks(scratch, outs, at, take, subs):
+    total = scratch.shape[0]
+    size = total // len(outs)
+    for sub in range(subs):
+        scratch[pl.ds(sub, total // subs, stride=subs), :] = take(sub)
+    for k, out in enumerate(outs):
+        out[at : at + size, :] = scratch[k * size : (k + 1) * size, :].astype(out.dtype)
+
+
+def blocks_to_rows(scratch, blocks, at, put, subs):
+    total = scratch.shape[0]
+    size = total // len(blocks)
+    for k, block in enumerate(blocks):
+        scratch[k * size : (k + 1) * size, :] = block[at : at + size, :].astype(jnp.float32)
+    for sub in range(subs):
+        put(sub, scratch[pl.ds(sub, total // subs, stride=subs), :])
+
+
+def lanes_of(sub):
+    return slice(sub * LANES, (sub + 1) * LANES)
+
+
+def route_kernel(devices, capacity, subs, ids_in, weight_in, x_in, g_in, *refs):
+    outs, (place_out, mix_out, scratch, ids, weight, x, g, sems) = refs[:devices], refs[devices:]
+    pairs = ((ids_in, ids), (weight_in, weight), (x_in, x), (g_in, g))
+    copies = [pltpu.make_async_copy(src, dst, sems.at[i]) for i, (src, dst) in enumerate(pairs)]
+    for copy in copies:
+        copy.start()
+    top, tok = ids.shape
+    rows = devices * capacity
+    order = lax.broadcasted_iota(jnp.int32, (devices, tok), 0)
+    expert = order ^ lax.axis_index("expert")
+    member = jnp.zeros((devices, tok), jnp.float32)
+    mixing = jnp.zeros((devices, tok), jnp.float32)
+    copies[0].wait()
+    copies[1].wait()
+    for route in range(top):
+        hit = ids[route : route + 1, :] == expert
+        member = jnp.where(hit, 1.0, member)
+        mixing = jnp.where(hit, weight[route : route + 1, :], mixing)
+    before = lax.broadcasted_iota(jnp.int32, (tok, tok), 0) < lax.broadcasted_iota(jnp.int32, (tok, tok), 1)
+    slots = jnp.dot(
+        member.astype(jnp.bfloat16),
+        jnp.where(before, 1.0, 0.0).astype(jnp.bfloat16),
+        preferred_element_type=jnp.float32,
+    )
+    target = jnp.where(member > 0, slots + capacity * order.astype(jnp.float32), -1.0)
+    row = lax.broadcasted_iota(jnp.int32, (rows, tok), 0).astype(jnp.float32)
+    place = jnp.zeros((rows, tok), jnp.float32)
+    mix = jnp.zeros((rows, tok), jnp.float32)
+    for k in range(devices):
+        equal = target[k : k + 1, :] == row
+        place = jnp.where(equal, 1.0, place)
+        mix = jnp.where(equal, mixing[k : k + 1, :], mix)
+    row_weight = jnp.broadcast_to(jnp.sum(mix, axis=1, keepdims=True), (rows, LANES))
+    low = place.astype(jnp.bfloat16)
+    place_out[...] = low
+    mix_out[...] = row_weight
+
+    def x_part(sub):
+        return jnp.dot(low, x[:, lanes_of(sub)], preferred_element_type=jnp.float32)
+
+    def g_part(sub):
+        return jnp.dot(low, g[:, lanes_of(sub)], preferred_element_type=jnp.float32) * row_weight
+
+    copies[2].wait()
+    rows_to_blocks(scratch, outs, 0, x_part, subs)
+    copies[3].wait()
+    rows_to_blocks(scratch, outs, capacity * subs, g_part, subs)
+
+
+def hold_kernel(count, *refs):
+    held, sems = refs[2 * count :]
+    held[...] = jnp.zeros_like(held)
+    copies = [pltpu.make_async_copy(refs[i], refs[count + i], sems.at[i]) for i in range(count)]
+    for copy in copies:
+        copy.start()
+    for copy in copies:
+        copy.wait()
+
+
+def arrive_kernel(devices, capacity, subs, *refs):
+    blocks, (_, x_own, g_own, scratch) = refs[:devices], refs[devices:]
+
+    def put_into(out):
+        def put(sub, value):
+            out[:, lanes_of(sub)] = value.astype(out.dtype)
+
+        return put
+
+    blocks_to_rows(scratch, blocks, 0, put_into(x_own), subs)
+    blocks_to_rows(scratch, blocks, capacity * subs, put_into(g_own), subs)
+
+
+def leave_kernel(capacity, subs, out_own, out_other, dx_own, dx_other, *refs):
+    outs, scratch = refs[:-1], refs[-1]
+
+    def sum_of(own, other):
+        def take(sub):
+            return own[:, lanes_of(sub)] + other[:, lanes_of(sub)].astype(jnp.float32)
+
+        return take
+
+    rows_to_blocks(scratch, outs, 0, sum_of(out_own, out_other), subs)
+    rows_to_blocks(scratch, outs, capacity * subs, sum_of(dx_own, dx_other), subs)
+
+
+def join_kernel(devices, capacity, subs, place, mix, *refs):
+    blocks, (out_tokens, grad_tokens, scratch) = refs[:devices], refs[devices:]
+
+    def put_out(sub, value):
+        low = (value * mix[...]).astype(jnp.bfloat16)
+        out_tokens[:, lanes_of(sub)] = contract_rows(place[...], low).astype(out_tokens.dtype)
+
+    def put_grad(sub, value):
+        grad_tokens[:, lanes_of(sub)] = contract_rows(place[...], value.astype(jnp.bfloat16)).astype(grad_tokens.dtype)
+
+    blocks_to_rows(scratch, blocks, 0, put_out, subs)
+    blocks_to_rows(scratch, blocks, capacity * subs, put_grad, subs)
+
+
+def half_starts(half_width):
+    half = lax.axis_index("ffn")
+    own = pl.multiple_of(half * half_width, half_width)
+    other = pl.multiple_of((1 - half) * half_width, half_width)
+    return own, other
+
+
+def chunk(i, step, base=0):
+    return pl.ds(base + pl.multiple_of(i * step, step), step)
+
+
+def dot(left, right):
+    return jnp.dot(left, right, preferred_element_type=jnp.float32)
+
+
+def project_own_kernel(step, x_own, w_gate, w_up, gate_part, up_part):
+    half_width = x_own.shape[1]
+    own, _ = half_starts(half_width)
+    rows = pl.ds(own, half_width)
+
+    def project(i, carry):
+        cols = chunk(i, step)
+        gate_part[:, cols] = dot(x_own[...], w_gate[0, rows, cols])
+        up_part[:, cols] = dot(x_own[...], w_up[0, rows, cols])
+        return carry
+
+    lax.fori_loop(0, gate_part.shape[1] // step, project, 0)
+
+
+def forward_kernel(
+    step, x_own, x_other, gate_part, up_part, w_gate, w_up, w_down, x_full, gate, up, hidden, out_own, out_other
+):
+    half_width = x_own.shape[1]
+    own, other = half_starts(half_width)
+    x_full[:, pl.ds(own, half_width)] = x_own[...]
+    x_full[:, pl.ds(other, half_width)] = x_other[...]
+    rows = pl.ds(other, half_width)
+
+    def project(i, carry):
+        cols = chunk(i, step)
+        gate_low = (gate_part[:, cols] + dot(x_other[...], w_gate[0, rows, cols])).astype(jnp.bfloat16)
+        up_low = (up_part[:, cols] + dot(x_other[...], w_up[0, rows, cols])).astype(jnp.bfloat16)
+        gate[:, cols] = gate_low
+        up[:, cols] = up_low
+        value = gate_low.astype(jnp.float32)
+        hidden[:, cols] = (value * jax.nn.sigmoid(value) * up_low.astype(jnp.float32)).astype(jnp.bfloat16)
+        return carry
+
+    lax.fori_loop(0, gate.shape[1] // step, project, 0)
+
+    def spread(i, carry):
+        here = chunk(i, step)
+        out_other[:, here] = dot(hidden[...], w_down[0, :, chunk(i, step, other)]).astype(jnp.bfloat16)
+        out_own[:, here] = dot(hidden[...], w_down[0, :, chunk(i, step, own)])
+        return carry
+
+    lax.fori_loop(0, half_width // step, spread, 0)
+
+
+def input_term(pre_gate, pre_up, w_gate, w_up, there):
+    return contract_cols(pre_gate[...], w_gate[0, there, :]) + contract_cols(pre_up[...], w_up[0, there, :])
+
+
+def backward_kernel(step, g_own, g_other, gate, up, w_gate, w_up, w_down, g_full, pre_gate, pre_up, dx_other):
+    half_width = g_own.shape[1]
+    own, other = half_starts(half_width)
+    g_full[:, pl.ds(own, half_width)] = g_own[...]
+    g_full[:, pl.ds(other, half_width)] = g_other[...]
+
+    def pull(i, carry):
+        cols = chunk(i, step)
+        part = contract_cols(g_full[...], w_down[0, cols, :]).astype(jnp.bfloat16)
+        grad_hidden = part.astype(jnp.float32)
+        value = gate[:, cols].astype(jnp.float32)
+        sig = jax.nn.sigmoid(value)
+        pre_gate[:, cols] = (
+            grad_hidden * up[:, cols].astype(jnp.float32) * sig * (1.0 + value * (1.0 - sig))
+        ).astype(jnp.bfloat16)
+        pre_up[:, cols] = (grad_hidden * value * sig).astype(jnp.bfloat16)
+        return carry
+
+    lax.fori_loop(0, gate.shape[1] // step, pull, 0)
+
+    def spread(i, carry):
+        dx_other[:, chunk(i, step)] = input_term(pre_gate, pre_up, w_gate, w_up, chunk(i, step, other)).astype(
+            jnp.bfloat16
+        )
+        return carry
+
+    lax.fori_loop(0, half_width // step, spread, 0)
+
+
+def backward_own_kernel(step, pre_gate, pre_up, w_gate, w_up, dx_own):
+    half_width = dx_own.shape[1]
+    own, _ = half_starts(half_width)
+
+    def spread(i, carry):
+        dx_own[:, chunk(i, step)] = input_term(pre_gate, pre_up, w_gate, w_up, chunk(i, step, own))
+        return carry
+
+    lax.fori_loop(0, half_width // step, spread, 0)
+
+
+def gradient_kernel(
+    step, x, g, hidden, pre_gate, pre_up, grad_gate, grad_up, grad_down, flipped, tall, wide, tall_sems, wide_sems
+):
+    width, lanes = x.shape[1], hidden.shape[1]
+    count = width // step
+    flipped[...] = hidden[...].astype(jnp.float32).T.astype(flipped.dtype)
+
+    def wide_copy(i, slot):
+        return pltpu.make_async_copy(wide.at[slot], grad_down.at[0, :, chunk(i, step)], wide_sems.at[slot])
+
+    def tall_copy(which, out, i, slot):
+        return pltpu.make_async_copy(tall.at[which, slot], out.at[0, chunk(i, step), :], tall_sems.at[which, slot])
+
+    def down(i, carry):
+        slot = i % 2
+
+        @pl.when(i >= 2)
+        def _():
+            wide_copy(i - 2, slot).wait()
+
+        wide[slot] = dot(flipped[...], g[:, chunk(i, step)]).astype(wide.dtype)
+        wide_copy(i, slot).start()
+        return carry
+
+    lax.fori_loop(0, count, down, 0)
+
+    def inputs(i, carry):
+        slot = i % 2
+        for which, (right, out) in enumerate(((pre_gate, grad_gate), (pre_up, grad_up))):
+
+            @pl.when(i >= 2)
+            def _():
+                tall_copy(which, out, i - 2, slot).wait()
+
+            tall[which, slot] = contract_rows(x[:, chunk(i, step)], right[...]).astype(tall.dtype)
+            tall_copy(which, out, i, slot).start()
+        return carry
+
+    lax.fori_loop(0, count, inputs, 0)
+    for i in range(max(0, count - 2), count):
+        wide_copy(i, i % 2).wait()
+        tall_copy(0, grad_gate, i, i % 2).wait()
+        tall_copy(1, grad_up, i, i % 2).wait()
+
+
+def exchange(blocks):
+    pairs = [[(i, i ^ k) for i in range(len(blocks))] for k in range(len(blocks))]
+    return [blocks[0]] + [lax.ppermute(blocks[k], "expert", pairs[k]) for k in range(1, len(blocks))]
+
+
+def swap(value):
+    return lax.ppermute(value, "ffn", [(0, 1), (1, 0)])
+
+
+def in_hbm(values):
+    return [pltpu.with_memory_space_constraint(value, pltpu.HBM) for value in values]
+
+
+def one_piece_shards(tokens, grad_out, route_ids, route_weight, gate_weight, up_weight, down_weight):
+    tok_dev, sub_width = tokens.shape
+    top_count = route_ids.shape[1]
+    width, lanes = gate_weight.shape[1:]
+    devices = lax.axis_size("expert")
+    capacity = max(2, min(tok_dev, (9 * tok_dev * top_count + 8 * EXPERTS - 1) // (8 * EXPERTS)))
+    rows = devices * capacity
+    subs = sub_width // LANES
+    low, full = jnp.bfloat16, jnp.float32
+    blocks = [jax.ShapeDtypeStruct((2 * capacity * subs, LANES), low)] * devices
+    spread_scratch = [pltpu.VMEM((rows * subs, LANES), full)]
+    sizes = (devices, capacity, subs)
+    step = 256
+    half_flops = 2 * rows * width * lanes // 2
+
+    sources = (route_ids.T, route_weight.T, tokens, grad_out)
+    routed = call(
+        functools.partial(route_kernel, *sizes),
+        blocks + [jax.ShapeDtypeStruct((rows, tok_dev), low), jax.ShapeDtypeStruct((rows, LANES), full)],
+        in_hbm(sources),
+        in_spaces=[pl.ANY] * 4,
+        scratch=spread_scratch
+        + [pltpu.VMEM(value.shape, value.dtype) for value in sources]
+        + [pltpu.SemaphoreType.DMA((4,))],
+        traffic=4 * tok_dev * sub_width,
+    )
+    place, mix = routed[devices:]
+    arrived = exchange(routed[:devices])
+
+    weights = (gate_weight, up_weight, down_weight)
+    w_gate, w_up, w_down, held = call(
+        functools.partial(hold_kernel, 3),
+        [vmem(w.shape, w.dtype) for w in weights] + [vmem((8, LANES), full)],
+        in_hbm(weights),
+        in_spaces=[pl.ANY] * 3,
+        scratch=[pltpu.SemaphoreType.DMA((3,))],
+        traffic=sum(w.size * 2 for w in weights),
+    )
+    x_own, g_own = call(
+        functools.partial(arrive_kernel, *sizes),
+        [vmem((rows, sub_width), low)] * 2,
+        (*arrived, held),
+        scratch=spread_scratch,
+        traffic=8 * rows * sub_width,
+    )
+    x_other = swap(x_own)
+    g_other = swap(g_own)
+    gate_part, up_part = call(
+        functools.partial(project_own_kernel, step),
+        [vmem((rows, lanes), full)] * 2,
+        (x_own, w_gate, w_up),
+        flops=2 * half_flops,
+    )
+    x_full, gate, up, hidden, out_own, out_other = call(
+        functools.partial(forward_kernel, step),
+        [vmem((rows, width), low)]
+        + [vmem((rows, lanes), low)] * 3
+        + [vmem((rows, sub_width), full), vmem((rows, sub_width), low)],
+        (x_own, x_other, gate_part, up_part, w_gate, w_up, w_down),
+        flops=4 * half_flops,
+    )
+    out_arrived = swap(out_other)
+    g_full, pre_gate, pre_up, dx_other = call(
+        functools.partial(backward_kernel, step),
+        [vmem((rows, width), low)] + [vmem((rows, lanes), low)] * 2 + [vmem((rows, sub_width), low)],
+        (g_own, g_other, gate, up, w_gate, w_up, w_down),
+        flops=4 * half_flops,
+    )
+    dx_arrived = swap(dx_other)
+    (dx_own,) = call(
+        functools.partial(backward_own_kernel, step),
+        [vmem((rows, sub_width), full)],
+        (pre_gate, pre_up, w_gate, w_up),
+        flops=2 * half_flops,
+    )
+    returned = exchange(
+        call(
+            functools.partial(leave_kernel, capacity, subs),
+            blocks,
+            (out_own, out_arrived, dx_own, dx_arrived),
+            scratch=spread_scratch,
+            traffic=16 * rows * sub_width,
+        )
+    )
+    cut = 1024 if width % 1024 == 0 else width
+    grad_gate, grad_up, grad_down = call(
+        functools.partial(gradient_kernel, cut),
+        [jax.ShapeDtypeStruct(w.shape, low) for w in weights],
+        (x_full, g_full, hidden, pre_gate, pre_up),
+        out_spaces=[pl.ANY] * 3,
+        scratch=[
+            pltpu.VMEM((lanes, rows), low),
+            pltpu.VMEM((2, 2, cut, lanes), low),
+            pltpu.VMEM((2, lanes, cut), low),
+            pltpu.SemaphoreType.DMA((2, 2)),
+            pltpu.SemaphoreType.DMA((2,)),
+        ],
+        flops=6 * half_flops,
+        traffic=sum(w.size * 2 for w in weights),
+        limit=32,
+    )
+    out_tokens, grad_tokens = call(
+        functools.partial(join_kernel, *sizes),
+        [jax.ShapeDtypeStruct((tok_dev, sub_width), low)] * 2,
+        (place, mix, *returned),
+        scratch=spread_scratch,
+        traffic=8 * tok_dev * sub_width,
+    )
+    return out_tokens, grad_tokens, grad_gate, grad_up, grad_down
+
+
+def shards(*args):
+    tokens, gate_weight = args[0], args[4]
+    halves = lax.axis_size("ffn")
+    devices = lax.axis_size("expert")
+    if halves == 2 and devices & (devices - 1) == 0 and tokens.shape[1] * halves == gate_weight.shape[1]:
+        return one_piece_shards(*args)
+    return general_shards(*args)
+
+
 def solution(mesh):
     in_specs = (
         P(("groups", "expert"), "ffn"),

time: 203 us -> 62.4 us (0.31)
  waiting for transfers between devices: 72.3 us -> 0.69 us
  matrix products: 49.3 us -> 0 us
  Pallas kernels: 0 us -> 34.7 us
  blocking collectives: 25.2 us -> 0 us
  between operations: 13.9 us -> 0.79 us
  local copies, waits for them, and re-layouts: 11.6 us -> 0 us
  other arithmetic: 4.81 us -> 0 us
    all_to_all x6 -> x0, waiting for transfers between devices: 61.8 us -> none  [the longest x1 19.6 us: shards(): lax.all_to_all(x_send, 'expert', split_axis=0, concat_axis=0, tiled=True)]
    dot_general x15 -> x0, matrix products: 49.3 us -> none  [the longest x3 15.4 us: contract_cols(): lax.dot_general(left, right, (((1,), (1,)), ((), ())), preferred_element_...]
    pallas_call x0 -> x10, Pallas kernels: none -> 34.7 us  [call(): pl.pallas_call(kernel, out_shape=tuple(out_shape), in_specs=[pl.BlockSpec...]
    ppermute x0 -> x18, starting transfers between devices: none -> 26 us  [the longest x14 24.8 us: exchange(): lax.ppermute(blocks[k], 'expert', pairs[k])]
    all_to_all x2 -> x0, blocking collectives: 25.2 us -> none  [spread_rows(): lax.all_to_all(copies, 'expert', split_axis=0, concat_axis=0, tiled=True)]
    all_to_all x6 -> x0, starting transfers between devices: 24 us -> none  [the longest x2 7.32 us: finish(): lax.all_to_all(summed, 'expert', split_axis=0, concat_axis=0, tiled=True)]
    all_gather x2 -> x0, waiting for transfers between devices: 10.4 us -> none  [the longest x1 7.68 us: shards(): lax.all_gather(tokens, 'ffn', axis=1, tiled=True)]
    all_to_all x7 -> x0, local copies, waits for them, and re-layouts: 5.36 us -> none  [the longest x2 3.94 us: finish(): lax.all_to_all(summed, 'expert', split_axis=0, concat_axis=0, tiled=True)]
  transfers between devices with their start and end apart: 10 -> 18, of which waited for: 8 -> 1; matrix products, arithmetic and copies ran while one was open for 25% -> 0% of each run, Pallas kernels for 0% -> 48%
where the time goes in v3:
time: 62.4 us; the launch traced here: 62.2 us
  Pallas kernels  34.7 us (56%)
  starting transfers between devices  26 us (42%)
  between operations  0.79 us (1%)
  waiting for transfers between devices  0.69 us (1%)
    pallas_call x10, Pallas kernels, call(): pl.pallas_call(kernel, out_shape=tuple(out_shape), in_specs=[pl.BlockSpec...  34.7 us
    ppermute x14, starting transfers between devices, exchange(): lax.ppermute(blocks[k], 'expert', pairs[k])  24.8 us
  transfers between devices with their start and end apart: 18, of which 1 were waited for; matrix products, arithmetic and copies ran while one was open for 0% of the time, Pallas kernels for 48%

profile of v3, /device:TPU:0, one launch (start us, length us, event | category | flops | bytes accessed | tf_op | source)
XLA Modules:
  0.0 62.2 jit_solution(12111941131606034178)
XLA Ops:
  0.6 1.9 %shard_map.110 = (bf16[288,128]{1,0:T(8,128)(2,1)S(1)}, bf16[288,128]{1,0:T(8,128)(2,1)S(1)}, bf16[288,128]{1,0:T(8,128)(2,1)S(1)}, bf16[288,128]{1,0:T(8,128)(2...) custom-call(s32[8,128]{1,0:T(8,128)} %bitcast.2, ...), custom_call_target="tpu_custom_call" | custom-call | bytes 1048576 | tf_op jit(solution)/shard_map/pallas_call | solution.py:132
  2.6 3.0 %collective-permute-start = (bf16[288,128]{1,0:T(8,128)(2,1)S(1)}, bf16[288,128]{1,0:T(8,128)(2,1)S(1)}, u32[]{:S(2)}, u32[]{:S(2)}) collective-permute-start(bf16[288,128]{1,0:T(8,128)(2,1)S(1)} %get-tuple-element.49), channel_id=1, source_target_pairs={{0,2},{2,0},{4,6},{6,4},{8,10},{10,8},{12,14},{14,12},{1,3},{3,1},... | collective-permute-start | bytes 221192 | tf_op jit(solution)/shard_map/ppermute | solution.py:414
  5.6 1.6 %collective-permute-start.1 = (bf16[288,128]{1,0:T(8,128)(2,1)S(1)}, bf16[288,128]{1,0:T(8,128)(2,1)S(1)}, u32[]{:S(2)}, u32[]{:S(2)}) collective-permute-start(bf16[288,128]{1,0:T(8,128)(2,1)S(1)} %get-tuple-element.50), channel_id=1, source_target_pairs={{0,4},{2,6},{4,0},{6,2},{8,12},{10,14},{12,8},{14,10},{1,5},{3,7},... | collective-permute-start | bytes 221192 | tf_op jit(solution)/shard_map/ppermute | solution.py:414
  7.1 0.0 collective-permute-start.2
  7.2 3.0 %collective-permute-start.3 = (bf16[288,128]{1,0:T(8,128)(2,1)S(1)}, bf16[288,128]{1,0:T(8,128)(2,1)S(1)}, u32[]{:S(2)}, u32[]{:S(2)}) collective-permute-start(bf16[288,128]{1,0:T(8,128)(2,1)S(1)} %get-tuple-element.52), channel_id=1, source_target_pairs={{0,8},{2,10},{4,12},{6,14},{8,0},{10,2},{12,4},{14,6},{1,9},{3,11}... | collective-permute-start | bytes 221192 | tf_op jit(solution)/shard_map/ppermute | solution.py:414
  10.2 1.3 %collective-permute-start.4 = (bf16[288,128]{1,0:T(8,128)(2,1)S(1)}, bf16[288,128]{1,0:T(8,128)(2,1)S(1)}, u32[]{:S(2)}, u32[]{:S(2)}) collective-permute-start(bf16[288,128]{1,0:T(8,128)(2,1)S(1)} %get-tuple-element.53), channel_id=1, source_target_pairs={{0,10},{2,8},{4,14},{6,12},{8,2},{10,0},{12,6},{14,4},{1,11},{3,9}... | collective-permute-start | bytes 221192 | tf_op jit(solution)/shard_map/ppermute | solution.py:414
  11.4 0.0 collective-permute-done.refs_1_
  11.4 3.6 %collective-permute-start.5 = (bf16[288,128]{1,0:T(8,128)(2,1)S(1)}, bf16[288,128]{1,0:T(8,128)(2,1)S(1)}, u32[]{:S(2)}, u32[]{:S(2)}) collective-permute-start(bf16[288,128]{1,0:T(8,128)(2,1)S(1)} %get-tuple-element.54), channel_id=1, source_target_pairs={{0,12},{2,14},{4,8},{6,10},{8,4},{10,6},{12,0},{14,2},{1,13},{3,15... | collective-permute-start | bytes 221192 | tf_op jit(solution)/shard_map/ppermute | solution.py:414
  15.0 0.0 collective-permute-start.6
  15.1 6.4 %shard_map.111 = (bf16[1,4096,768]{2,1,0:T(8,128)(2,1)S(1)}, bf16[1,4096,768]{2,1,0:T(8,128)(2,1)S(1)}, bf16[1,768,4096]{2,1,0:T(8,128)(2,1)S(1)}, f32[8,128]{1,0:T(8,128)S(1)}) custom-call(bf16[1,4096,768]{2,1,0:T(8,128)(2,1)} %refs_0_.1, bf16[1,4096,768]{2,1,0:T(8,128)(2,1)} %refs_1_.1, bf16[1,768,4096]{2,1,0:T(8,128)(2,1)} %refs_2_.1), custom_call_target="tpu_custom_call" | custom-call | bytes 18874368 | tf_op jit(solution)/shard_map/pallas_call | solution.py:132
  21.5 0.0 collective-permute-done.2.refs_3_
  21.6 0.6 %collective-permute-done.6.refs_7_ = bf16[288,128]{1,0:T(8,128)(2,1)S(1)} collective-permute-done((bf16[288,128]{1,0:T(8,128)(2,1)S(1)}, bf16[288,128]{1,0:T(8,128)(2,1)S(1)}, u32[]{:S(2)}, u32[]{:S(2)}) %collective-permute-start.6) | collective-permute-done | bytes 73760 | tf_op jit(solution)/shard_map/ppermute | solution.py:414
  22.2 0.5 shard_map.112
  22.7 0.1 collective-permute-start.7
  22.7 0.5 collective-permute-start.9
  23.2 1.5 %shard_map.113 = (f32[72,768]{1,0:T(8,128)S(1)}, f32[72,768]{1,0:T(8,128)S(1)}) custom-call(bf16[72,2048]{1,0:T(8,128)(2,1)S(1)} %get-tuple-element.57.x_own, bf16[1,4096,768]{2,1,0:T(8,128)(2,1)S(1)} %get-tuple-element.58.w_gate, bf16[1,4096,768]{2,1,0:T(8,128)(2,1)S(1)} %get-tuple-element.59.w_up), custom_call_target="tpu_custom_call" | custom-call | flops 452984832 | tf_op jit(solution)/shard_map/pallas_call | solution.py:132
  24.7 3.7 %shard_map.114 = (bf16[72,4096]{1,0:T(8,128)(2,1)S(1)}, bf16[72,768]{1,0:T(8,128)(2,1)S(1)}, bf16[72,768]{1,0:T(8,128)(2,1)S(1)}, bf16[72,768]{1,0:T(8,128)(2,1)...) custom-call(bf16[72,2048]{1,0:T(8,128)(2,1)S(1)} %get-tuple-element.57.x_own, ...), custom_call_target="tpu_custom_call" | custom-call | flops 905969664 | tf_op jit(solution)/shard_map/pallas_call | solution.py:132
  28.5 0.1 collective-permute-start.8
  28.6 5.3 %shard_map.115 = (bf16[72,4096]{1,0:T(8,128)(2,1)S(1)}, bf16[72,768]{1,0:T(8,128)(2,1)S(1)}, bf16[72,768]{1,0:T(8,128)(2,1)S(1)}, bf16[72,2048]{1,0:T(8,128)(2,1)S(1)}) custom-call(bf16[72,2048]{1,0:T(8,128)(2,1)S(1)} %get-tuple-element.65.g_own, bf16[72,2048]{1,0:T(8,128)(2,1)S(1)} %collective-permute-done.9.g_other, ...), custom_call_target="tpu_custom_call" | custom-call | flops 905969664 | tf_op jit(solution)/shard_map/pallas_call | solution.py:132
  34.0 0.5 collective-permute-start.10
  34.5 3.0 %shard_map.116.dx_own = f32[72,2048]{1,0:T(8,128)S(1)} custom-call(bf16[72,768]{1,0:T(8,128)(2,1)S(1)} %get-tuple-element.68.pre_gate, bf16[72,768]{1,0:T(8,128)(2,1)S(1)} %get-tuple-element.69.pre_up, bf16[1,4096,768]{2,1,0:T(8,128)(2,1)S(1)} %get-tuple-element.58.w_gate, bf16[1,4096,768]{2,1,0:T(8,128)(2,1)S(1)} %get-tuple-element.59.w_up), custom_call_target="tpu_custom_call" | custom-call | flops 452984832 | tf_op jit(solution)/shard_map/pallas_call | solution.py:132
  37.4 0.0 collective-permute-done.8.out_other
  37.4 0.7 %shard_map.117 = (bf16[288,128]{1,0:T(8,128)(2,1)S(1)}, bf16[288,128]{1,0:T(8,128)(2,1)S(1)}, bf16[288,128]{1,0:T(8,128)(2,1)S(1)}, bf16[288,128]{1,0:T(8,128)(2...) custom-call(f32[72,2048]{1,0:T(8,128)S(1)} %get-tuple-element.63.out, ...), custom_call_target="tpu_custom_call" | custom-call | bytes 2359296 | tf_op jit(solution)/shard_map/pallas_call | solution.py:132
  38.1 1.1 %collective-permute-start.11 = (bf16[288,128]{1,0:T(8,128)(2,1)S(1)}, bf16[288,128]{1,0:T(8,128)(2,1)S(1)}, u32[]{:S(2)}, u32[]{:S(2)}) collective-permute-start(bf16[288,128]{1,0:T(8,128)(2,1)S(1)} %get-tuple-element.72), channel_id=1, source_target_pairs={{0,2},{2,0},{4,6},{6,4},{8,10},{10,8},{12,14},{14,12},{1,3},{3,1},... | collective-permute-start | bytes 221192 | tf_op jit(solution)/shard_map/ppermute | solution.py:414
  39.2 2.8 %collective-permute-start.12 = (bf16[288,128]{1,0:T(8,128)(2,1)S(1)}, bf16[288,128]{1,0:T(8,128)(2,1)S(1)}, u32[]{:S(2)}, u32[]{:S(2)}) collective-permute-start(bf16[288,128]{1,0:T(8,128)(2,1)S(1)} %get-tuple-element.73), channel_id=1, source_target_pairs={{0,4},{2,6},{4,0},{6,2},{8,12},{10,14},{12,8},{14,10},{1,5},{3,7},... | collective-permute-start | bytes 221192 | tf_op jit(solution)/shard_map/ppermute | solution.py:414
  41.9 0.7 %collective-permute-start.13 = (bf16[288,128]{1,0:T(8,128)(2,1)S(1)}, bf16[288,128]{1,0:T(8,128)(2,1)S(1)}, u32[]{:S(2)}, u32[]{:S(2)}) collective-permute-start(bf16[288,128]{1,0:T(8,128)(2,1)S(1)} %get-tuple-element.74), channel_id=1, source_target_pairs={{0,6},{2,4},{4,2},{6,0},{8,14},{10,12},{12,10},{14,8},{1,7},{3,5},... | collective-permute-start | bytes 221192 | tf_op jit(solution)/shard_map/ppermute | solution.py:414
  42.6 3.1 %collective-permute-start.14 = (bf16[288,128]{1,0:T(8,128)(2,1)S(1)}, bf16[288,128]{1,0:T(8,128)(2,1)S(1)}, u32[]{:S(2)}, u32[]{:S(2)}) collective-permute-start(bf16[288,128]{1,0:T(8,128)(2,1)S(1)} %get-tuple-element.75), channel_id=1, source_target_pairs={{0,8},{2,10},{4,12},{6,14},{8,0},{10,2},{12,4},{14,6},{1,9},{3,11}... | collective-permute-start | bytes 221192 | tf_op jit(solution)/shard_map/ppermute | solution.py:414
  45.7 0.0 collective-permute-start.15
  45.8 2.9 %collective-permute-start.16 = (bf16[288,128]{1,0:T(8,128)(2,1)S(1)}, bf16[288,128]{1,0:T(8,128)(2,1)S(1)}, u32[]{:S(2)}, u32[]{:S(2)}) collective-permute-start(bf16[288,128]{1,0:T(8,128)(2,1)S(1)} %get-tuple-element.77), channel_id=1, source_target_pairs={{0,12},{2,14},{4,8},{6,10},{8,4},{10,6},{12,0},{14,2},{1,13},{3,15... | collective-permute-start | bytes 221192 | tf_op jit(solution)/shard_map/ppermute | solution.py:414
  48.6 1.8 %collective-permute-start.17 = (bf16[288,128]{1,0:T(8,128)(2,1)S(1)}, bf16[288,128]{1,0:T(8,128)(2,1)S(1)}, u32[]{:S(2)}, u32[]{:S(2)}) collective-permute-start(bf16[288,128]{1,0:T(8,128)(2,1)S(1)} %get-tuple-element.78), channel_id=1, source_target_pairs={{0,14},{2,12},{4,10},{6,8},{8,6},{10,4},{12,2},{14,0},{1,15},{3,13... | collective-permute-start | bytes 221192 | tf_op jit(solution)/shard_map/ppermute | solution.py:414
  50.4 10.1 %shard_map.119 = (bf16[1,4096,768]{2,1,0:T(8,128)(2,1)}, bf16[1,4096,768]{2,1,0:T(8,128)(2,1)}, bf16[1,768,4096]{2,1,0:T(8,128)(2,1)}) custom-call(bf16[72,4096]{1,0:T(8,128)(2,1)S(1)} %get-tuple-element.81.x, bf16[72,4096]{1,0:T(8,128)(2,1)S(1)} %get-tuple-element.82.g, bf16[72,768]{1,0:T(8,128)(2,1)S(1)} %get-tuple-element.83.hidden, ...), custom_call_target="tpu_custom_call" | custom-call | flops 1358954496 | bytes 18874368 | tf_op jit(solution)/shard_map/pallas_call | solution.py:132
  60.6 1.6 %shard_map.118 = (bf16[128,2048]{1,0:T(8,128)(2,1)}, bf16[128,2048]{1,0:T(8,128)(2,1)}) custom-call(bf16[72,128]{1,0:T(8,128)(2,1)S(1)} %get-tuple-element.46.place, f32[72,128]{1,0:T(8,128)S(1)} %get-tuple-element.47.mix, bf16[288,128]{1,0:T(8,128)(2,1)S(1)} %get-tuple-element.71.refs_0_, bf16[288,128]{1,0:T(8,128)(2,1)S(1)} %collective-permute-done.11.refs_1_, ...), custom_call_target="tpu_custom_call" | custom-call | bytes 2097152 | tf_op jit(solution)/shard_map/pallas_call | solution.py:132
  (14 shorter events, 0.0 us)
Async XLA Ops:
  2.6 8.9 %collective-permute-start = (bf16[288,128]{1,0:T(8,128)(2,1)S(1)}, bf16[288,128]{1,0:T(8,128)(2,1)S(1)}, u32[]{:S(2)}, u32[]{:S(2)}) collective-permute-start(bf16[288,128]{1,0:T(8,128)(2,1)S(1)} %get-tuple-element.49), channel_id=1, source_target_pairs={{0,2},{2,0},{4,6},{6,4},{8,10},{10,8},{12,14},{14,12},{1,3},{3,1},... | collective-permute-start | bytes 221192 | tf_op jit(solution)/shard_map/ppermute | solution.py:414
  5.6 9.5 %collective-permute-start.1 = (bf16[288,128]{1,0:T(8,128)(2,1)S(1)}, bf16[288,128]{1,0:T(8,128)(2,1)S(1)}, u32[]{:S(2)}, u32[]{:S(2)}) collective-permute-start(bf16[288,128]{1,0:T(8,128)(2,1)S(1)} %get-tuple-element.50), channel_id=1, source_target_pairs={{0,4},{2,6},{4,0},{6,2},{8,12},{10,14},{12,8},{14,10},{1,5},{3,7},... | collective-permute-start | bytes 221192 | tf_op jit(solution)/shard_map/ppermute | solution.py:414
  7.1 14.4 %collective-permute-start.2 = (bf16[288,128]{1,0:T(8,128)(2,1)S(1)}, bf16[288,128]{1,0:T(8,128)(2,1)S(1)}, u32[]{:S(2)}, u32[]{:S(2)}) collective-permute-start(bf16[288,128]{1,0:T(8,128)(2,1)S(1)} %get-tuple-element.51), channel_id=1, source_target_pairs={{0,6},{2,4},{4,2},{6,0},{8,14},{10,12},{12,10},{14,8},{1,7},{3,5},... | collective-permute-start | bytes 221192 | tf_op jit(solution)/shard_map/ppermute | solution.py:414
  7.2 14.4 %collective-permute-start.3 = (bf16[288,128]{1,0:T(8,128)(2,1)S(1)}, bf16[288,128]{1,0:T(8,128)(2,1)S(1)}, u32[]{:S(2)}, u32[]{:S(2)}) collective-permute-start(bf16[288,128]{1,0:T(8,128)(2,1)S(1)} %get-tuple-element.52), channel_id=1, source_target_pairs={{0,8},{2,10},{4,12},{6,14},{8,0},{10,2},{12,4},{14,6},{1,9},{3,11}... | collective-permute-start | bytes 221192 | tf_op jit(solution)/shard_map/ppermute | solution.py:414
  10.2 11.4 %collective-permute-start.4 = (bf16[288,128]{1,0:T(8,128)(2,1)S(1)}, bf16[288,128]{1,0:T(8,128)(2,1)S(1)}, u32[]{:S(2)}, u32[]{:S(2)}) collective-permute-start(bf16[288,128]{1,0:T(8,128)(2,1)S(1)} %get-tuple-element.53), channel_id=1, source_target_pairs={{0,10},{2,8},{4,14},{6,12},{8,2},{10,0},{12,6},{14,4},{1,11},{3,9}... | collective-permute-start | bytes 221192 | tf_op jit(solution)/shard_map/ppermute | solution.py:414
  11.4 10.1 %collective-permute-start.5 = (bf16[288,128]{1,0:T(8,128)(2,1)S(1)}, bf16[288,128]{1,0:T(8,128)(2,1)S(1)}, u32[]{:S(2)}, u32[]{:S(2)}) collective-permute-start(bf16[288,128]{1,0:T(8,128)(2,1)S(1)} %get-tuple-element.54), channel_id=1, source_target_pairs={{0,12},{2,14},{4,8},{6,10},{8,4},{10,6},{12,0},{14,2},{1,13},{3,15... | collective-permute-start | bytes 221192 | tf_op jit(solution)/shard_map/ppermute | solution.py:414
  15.0 7.2 %collective-permute-start.6 = (bf16[288,128]{1,0:T(8,128)(2,1)S(1)}, bf16[288,128]{1,0:T(8,128)(2,1)S(1)}, u32[]{:S(2)}, u32[]{:S(2)}) collective-permute-start(bf16[288,128]{1,0:T(8,128)(2,1)S(1)} %get-tuple-element.55), channel_id=1, source_target_pairs={{0,14},{2,12},{4,10},{6,8},{8,6},{10,4},{12,2},{14,0},{1,15},{3,13... | collective-permute-start | bytes 221192 | tf_op jit(solution)/shard_map/ppermute | solution.py:414
  22.7 2.1 %collective-permute-start.7 = (bf16[72,2048]{1,0:T(8,128)(2,1)S(1)}, bf16[72,2048]{1,0:T(8,128)(2,1)S(1)}, u32[]{:S(2)}, u32[]{:S(2)}) collective-permute-start(bf16[72,2048]{1,0:T(8,128)(2,1)S(1)} %get-tuple-element.57.x_own), channel_id=1, source_target_pairs={{0,1},{1,0},{2,3},{3,2},{4,5},{5,4},{6,7},{7,6},{8,9},{9,8},{10,11... | collective-permute-start | bytes 884744 | tf_op jit(solution)/shard_map/ppermute | solution.py:418
  22.7 5.9 %collective-permute-start.9 = (bf16[72,2048]{1,0:T(8,128)(2,1)S(1)}, bf16[72,2048]{1,0:T(8,128)(2,1)S(1)}, u32[]{:S(2)}, u32[]{:S(2)}) collective-permute-start(bf16[72,2048]{1,0:T(8,128)(2,1)S(1)} %get-tuple-element.65.g_own), channel_id=1, source_target_pairs={{0,1},{1,0},{2,3},{3,2},{4,5},{5,4},{6,7},{7,6},{8,9},{9,8},{10,11... | collective-permute-start | bytes 884744 | tf_op jit(solution)/shard_map/ppermute | solution.py:418
  28.5 8.9 %collective-permute-start.8 = (bf16[72,2048]{1,0:T(8,128)(2,1)S(1)}, bf16[72,2048]{1,0:T(8,128)(2,1)S(1)}, u32[]{:S(2)}, u32[]{:S(2)}) collective-permute-start(bf16[72,2048]{1,0:T(8,128)(2,1)S(1)} %get-tuple-element.64), channel_id=1, source_target_pairs={{0,1},{1,0},{2,3},{3,2},{4,5},{5,4},{6,7},{7,6},{8,9},{9,8},{10,11... | collective-permute-start | bytes 884744 | tf_op jit(solution)/shard_map/ppermute | solution.py:418
  34.0 3.5 %collective-permute-start.10 = (bf16[72,2048]{1,0:T(8,128)(2,1)S(1)}, bf16[72,2048]{1,0:T(8,128)(2,1)S(1)}, u32[]{:S(2)}, u32[]{:S(2)}) collective-permute-start(bf16[72,2048]{1,0:T(8,128)(2,1)S(1)} %get-tuple-element.70), channel_id=1, source_target_pairs={{0,1},{1,0},{2,3},{3,2},{4,5},{5,4},{6,7},{7,6},{8,9},{9,8},{10,11... | collective-permute-start | bytes 884744 | tf_op jit(solution)/shard_map/ppermute | solution.py:418
  38.1 7.7 %collective-permute-start.11 = (bf16[288,128]{1,0:T(8,128)(2,1)S(1)}, bf16[288,128]{1,0:T(8,128)(2,1)S(1)}, u32[]{:S(2)}, u32[]{:S(2)}) collective-permute-start(bf16[288,128]{1,0:T(8,128)(2,1)S(1)} %get-tuple-element.72), channel_id=1, source_target_pairs={{0,2},{2,0},{4,6},{6,4},{8,10},{10,8},{12,14},{14,12},{1,3},{3,1},... | collective-permute-start | bytes 221192 | tf_op jit(solution)/shard_map/ppermute | solution.py:414
  39.2 9.5 %collective-permute-start.12 = (bf16[288,128]{1,0:T(8,128)(2,1)S(1)}, bf16[288,128]{1,0:T(8,128)(2,1)S(1)}, u32[]{:S(2)}, u32[]{:S(2)}) collective-permute-start(bf16[288,128]{1,0:T(8,128)(2,1)S(1)} %get-tuple-element.73), channel_id=1, source_target_pairs={{0,4},{2,6},{4,0},{6,2},{8,12},{10,14},{12,8},{14,10},{1,5},{3,7},... | collective-permute-start | bytes 221192 | tf_op jit(solution)/shard_map/ppermute | solution.py:414
  41.9 18.6 %collective-permute-start.13 = (bf16[288,128]{1,0:T(8,128)(2,1)S(1)}, bf16[288,128]{1,0:T(8,128)(2,1)S(1)}, u32[]{:S(2)}, u32[]{:S(2)}) collective-permute-start(bf16[288,128]{1,0:T(8,128)(2,1)S(1)} %get-tuple-element.74), channel_id=1, source_target_pairs={{0,6},{2,4},{4,2},{6,0},{8,14},{10,12},{12,10},{14,8},{1,7},{3,5},... | collective-permute-start | bytes 221192 | tf_op jit(solution)/shard_map/ppermute | solution.py:414
  42.6 17.9 %collective-permute-start.14 = (bf16[288,128]{1,0:T(8,128)(2,1)S(1)}, bf16[288,128]{1,0:T(8,128)(2,1)S(1)}, u32[]{:S(2)}, u32[]{:S(2)}) collective-permute-start(bf16[288,128]{1,0:T(8,128)(2,1)S(1)} %get-tuple-element.75), channel_id=1, source_target_pairs={{0,8},{2,10},{4,12},{6,14},{8,0},{10,2},{12,4},{14,6},{1,9},{3,11}... | collective-permute-start | bytes 221192 | tf_op jit(solution)/shard_map/ppermute | solution.py:414
  45.7 14.8 %collective-permute-start.15 = (bf16[288,128]{1,0:T(8,128)(2,1)S(1)}, bf16[288,128]{1,0:T(8,128)(2,1)S(1)}, u32[]{:S(2)}, u32[]{:S(2)}) collective-permute-start(bf16[288,128]{1,0:T(8,128)(2,1)S(1)} %get-tuple-element.76), channel_id=1, source_target_pairs={{0,10},{2,8},{4,14},{6,12},{8,2},{10,0},{12,6},{14,4},{1,11},{3,9}... | collective-permute-start | bytes 221192 | tf_op jit(solution)/shard_map/ppermute | solution.py:414
  45.8 14.8 %collective-permute-start.16 = (bf16[288,128]{1,0:T(8,128)(2,1)S(1)}, bf16[288,128]{1,0:T(8,128)(2,1)S(1)}, u32[]{:S(2)}, u32[]{:S(2)}) collective-permute-start(bf16[288,128]{1,0:T(8,128)(2,1)S(1)} %get-tuple-element.77), channel_id=1, source_target_pairs={{0,12},{2,14},{4,8},{6,10},{8,4},{10,6},{12,0},{14,2},{1,13},{3,15... | collective-permute-start | bytes 221192 | tf_op jit(solution)/shard_map/ppermute | solution.py:414
  48.6 11.9 %collective-permute-start.17 = (bf16[288,128]{1,0:T(8,128)(2,1)S(1)}, bf16[288,128]{1,0:T(8,128)(2,1)S(1)}, u32[]{:S(2)}, u32[]{:S(2)}) collective-permute-start(bf16[288,128]{1,0:T(8,128)(2,1)S(1)} %get-tuple-element.78), channel_id=1, source_target_pairs={{0,14},{2,12},{4,10},{6,8},{8,6},{10,4},{12,2},{14,0},{1,15},{3,13... | collective-permute-start | bytes 221192 | tf_op jit(solution)/shard_map/ppermute | solution.py:414

commit v4 on v3

--- a/solution.py
+++ b/solution.py
@@ -171,7 +171,9 @@
     top, tok = ids.shape
     rows = devices * capacity
     order = lax.broadcasted_iota(jnp.int32, (devices, tok), 0)
-    expert = order ^ lax.axis_index("expert")
+    half = devices // 2
+    bits = jnp.where(order == 0, 0, jnp.where(order <= half, order + half - 1, order - half))
+    expert = bits ^ lax.axis_index("expert")
     member = jnp.zeros((devices, tok), jnp.float32)
     mixing = jnp.zeros((devices, tok), jnp.float32)
     copies[0].wait()
@@ -211,14 +213,11 @@
     rows_to_blocks(scratch, outs, capacity * subs, g_part, subs)
 
 
-def hold_kernel(count, *refs):
-    held, sems = refs[2 * count :]
+def hold_kernel(source, kept, held, sem):
+    copy = pltpu.make_async_copy(source, kept, sem)
+    copy.start()
     held[...] = jnp.zeros_like(held)
-    copies = [pltpu.make_async_copy(refs[i], refs[count + i], sems.at[i]) for i in range(count)]
-    for copy in copies:
-        copy.start()
-    for copy in copies:
-        copy.wait()
+    copy.wait()
 
 
 def arrive_kernel(devices, capacity, subs, *refs):
@@ -276,55 +275,86 @@
     return jnp.dot(left, right, preferred_element_type=jnp.float32)
 
 
-def project_own_kernel(step, x_own, w_gate, w_up, gate_part, up_part):
-    half_width = x_own.shape[1]
-    own, _ = half_starts(half_width)
-    rows = pl.ds(own, half_width)
-
-    def project(i, carry):
-        cols = chunk(i, step)
-        gate_part[:, cols] = dot(x_own[...], w_gate[0, rows, cols])
-        up_part[:, cols] = dot(x_own[...], w_up[0, rows, cols])
-        return carry
-
-    lax.fori_loop(0, gate_part.shape[1] // step, project, 0)
+def stream(step, start, matrices, held, sems):
+    copies = []
+    for i in range(held[0].shape[0] // step):
+        for which, (matrix, kept) in enumerate(zip(matrices, held)):
+            copies.append(
+                pltpu.make_async_copy(
+                    matrix.at[0, chunk(i, step, start), :], kept.at[i * step : (i + 1) * step, :], sems.at[which, i]
+                )
+            )
+    for copy in copies:
+        copy.start()
+    return copies
+
+
+def project_own_kernel(step, x_own, w_gate, w_up, gate_part, up_part, gate_held, up_held, sems):
+    own, _ = half_starts(x_own.shape[1])
+    copies = stream(step, own, (w_gate, w_up), (gate_held, up_held), sems)
+    parts = ((gate_part, gate_held), (up_part, up_held))
+    for at, copy in enumerate(copies):
+        copy.wait()
+        here = slice(at // 2 * step, (at // 2 + 1) * step)
+        part, held = parts[at % 2]
+        term = dot(x_own[:, here], held[here, :])
+        part[...] = term if at < 2 else part[...] + term
 
 
 def forward_kernel(
-    step, x_own, x_other, gate_part, up_part, w_gate, w_up, w_down, x_full, gate, up, hidden, out_own, out_other
+    step,
+    wide,
+    x_own,
+    x_other,
+    gate_part,
+    up_part,
+    w_gate,
+    w_up,
+    w_down,
+    x_full,
+    gate,
+    up,
+    hidden,
+    out_own,
+    out_other,
+    gate_held,
+    up_held,
+    gate_sum,
+    up_sum,
+    sems,
 ):
     half_width = x_own.shape[1]
     own, other = half_starts(half_width)
+    copies = stream(step, other, (w_gate, w_up), (gate_held, up_held), sems)
     x_full[:, pl.ds(own, half_width)] = x_own[...]
     x_full[:, pl.ds(other, half_width)] = x_other[...]
-    rows = pl.ds(other, half_width)
-
-    def project(i, carry):
-        cols = chunk(i, step)
-        gate_low = (gate_part[:, cols] + dot(x_other[...], w_gate[0, rows, cols])).astype(jnp.bfloat16)
-        up_low = (up_part[:, cols] + dot(x_other[...], w_up[0, rows, cols])).astype(jnp.bfloat16)
-        gate[:, cols] = gate_low
-        up[:, cols] = up_low
-        value = gate_low.astype(jnp.float32)
-        hidden[:, cols] = (value * jax.nn.sigmoid(value) * up_low.astype(jnp.float32)).astype(jnp.bfloat16)
+    parts = ((gate_part, gate_sum, gate_held), (up_part, up_sum, up_held))
+    for at, copy in enumerate(copies):
+        copy.wait()
+        here = slice(at // 2 * step, (at // 2 + 1) * step)
+        part, total, held = parts[at % 2]
+        total[...] = (part if at < 2 else total)[...] + dot(x_other[:, here], held[here, :])
+    gate_low = gate_sum[...].astype(jnp.bfloat16)
+    up_low = up_sum[...].astype(jnp.bfloat16)
+    gate[...] = gate_low
+    up[...] = up_low
+    value = gate_low.astype(jnp.float32)
+    hidden[...] = (value * jax.nn.sigmoid(value) * up_low.astype(jnp.float32)).astype(jnp.bfloat16)
+
+    def spread(i, carry):
+        here = chunk(i, wide)
+        out_other[:, here] = dot(hidden[...], w_down[0, :, chunk(i, wide, other)]).astype(jnp.bfloat16)
+        out_own[:, here] = dot(hidden[...], w_down[0, :, chunk(i, wide, own)])
         return carry
 
-    lax.fori_loop(0, gate.shape[1] // step, project, 0)
-
-    def spread(i, carry):
-        here = chunk(i, step)
-        out_other[:, here] = dot(hidden[...], w_down[0, :, chunk(i, step, other)]).astype(jnp.bfloat16)
-        out_own[:, here] = dot(hidden[...], w_down[0, :, chunk(i, step, own)])
-        return carry
-
-    lax.fori_loop(0, half_width // step, spread, 0)
-
-
-def input_term(pre_gate, pre_up, w_gate, w_up, there):
-    return contract_cols(pre_gate[...], w_gate[0, there, :]) + contract_cols(pre_up[...], w_up[0, there, :])
-
-
-def backward_kernel(step, g_own, g_other, gate, up, w_gate, w_up, w_down, g_full, pre_gate, pre_up, dx_other):
+    lax.fori_loop(0, half_width // wide, spread, 0)
+
+
+def input_term(pre_gate, pre_up, gate_held, up_held, there):
+    return contract_cols(pre_gate[...], gate_held[there, :]) + contract_cols(pre_up[...], up_held[there, :])
+
+
+def backward_kernel(step, g_own, g_other, gate, up, gate_held, up_held, w_down, g_full, pre_gate, pre_up, dx_other):
     half_width = g_own.shape[1]
     own, other = half_starts(half_width)
     g_full[:, pl.ds(own, half_width)] = g_own[...]
@@ -345,23 +375,20 @@
     lax.fori_loop(0, gate.shape[1] // step, pull, 0)
 
     def spread(i, carry):
-        dx_other[:, chunk(i, step)] = input_term(pre_gate, pre_up, w_gate, w_up, chunk(i, step, other)).astype(
-            jnp.bfloat16
-        )
+        here = chunk(i, step)
+        dx_other[:, here] = input_term(pre_gate, pre_up, gate_held, up_held, here).astype(jnp.bfloat16)
         return carry
 
     lax.fori_loop(0, half_width // step, spread, 0)
 
 
-def backward_own_kernel(step, pre_gate, pre_up, w_gate, w_up, dx_own):
-    half_width = dx_own.shape[1]
-    own, _ = half_starts(half_width)
-
+def backward_own_kernel(step, pre_gate, pre_up, gate_held, up_held, dx_own):
     def spread(i, carry):
-        dx_own[:, chunk(i, step)] = input_term(pre_gate, pre_up, w_gate, w_up, chunk(i, step, own))
+        here = chunk(i, step)
+        dx_own[:, here] = input_term(pre_gate, pre_up, gate_held, up_held, here)
         return carry
 
-    lax.fori_loop(0, half_width // step, spread, 0)
+    lax.fori_loop(0, dx_own.shape[1] // step, spread, 0)
 
 
 def gradient_kernel(
@@ -409,9 +436,16 @@
         tall_copy(1, grad_up, i, i % 2).wait()
 
 
+def partner_bits(count):
+    return [0, *range(count // 2, count), *range(1, count // 2)]
+
+
 def exchange(blocks):
-    pairs = [[(i, i ^ k) for i in range(len(blocks))] for k in range(len(blocks))]
-    return [blocks[0]] + [lax.ppermute(blocks[k], "expert", pairs[k]) for k in range(1, len(blocks))]
+    arrived = []
+    for block, bits in zip(blocks, partner_bits(len(blocks))):
+        pairs = [(i, i ^ bits) for i in range(len(blocks))]
+        arrived.append(lax.ppermute(block, "expert", pairs) if bits else block)
+    return arrived
 
 
 def swap(value):
@@ -452,13 +486,14 @@
     arrived = exchange(routed[:devices])
 
     weights = (gate_weight, up_weight, down_weight)
-    w_gate, w_up, w_down, held = call(
-        functools.partial(hold_kernel, 3),
-        [vmem(w.shape, w.dtype) for w in weights] + [vmem((8, LANES), full)],
-        in_hbm(weights),
-        in_spaces=[pl.ANY] * 3,
-        scratch=[pltpu.SemaphoreType.DMA((3,))],
-        traffic=sum(w.size * 2 for w in weights),
+    w_gate, w_up = in_hbm(weights[:2])
+    w_down, held = call(
+        hold_kernel,
+        [vmem(down_weight.shape, low), vmem((8, LANES), full)],
+        in_hbm(weights[2:]),
+        in_spaces=[pl.ANY],
+        scratch=[pltpu.SemaphoreType.DMA],
+        traffic=down_weight.size * 2,
     )
     x_own, g_own = call(
         functools.partial(arrive_kernel, *sizes),
@@ -469,32 +504,41 @@
     )
     x_other = swap(x_own)
     g_other = swap(g_own)
-    gate_part, up_part = call(
-        functools.partial(project_own_kernel, step),
-        [vmem((rows, lanes), full)] * 2,
+    deep = 512 if sub_width % 512 == 0 else sub_width
+    stream_sems = pltpu.SemaphoreType.DMA((2, sub_width // deep))
+    gate_part, up_part, gate_own, up_own = call(
+        functools.partial(project_own_kernel, deep),
+        [vmem((rows, lanes), full)] * 2 + [vmem((sub_width, lanes), low)] * 2,
         (x_own, w_gate, w_up),
+        in_spaces=[pltpu.VMEM, pl.ANY, pl.ANY],
+        scratch=[stream_sems],
         flops=2 * half_flops,
-    )
-    x_full, gate, up, hidden, out_own, out_other = call(
-        functools.partial(forward_kernel, step),
+        traffic=4 * sub_width * lanes,
+    )
+    x_full, gate, up, hidden, out_own, out_other, gate_other, up_other = call(
+        functools.partial(forward_kernel, deep, step),
         [vmem((rows, width), low)]
         + [vmem((rows, lanes), low)] * 3
-        + [vmem((rows, sub_width), full), vmem((rows, sub_width), low)],
+        + [vmem((rows, sub_width), full), vmem((rows, sub_width), low)]
+        + [vmem((sub_width, lanes), low)] * 2,
         (x_own, x_other, gate_part, up_part, w_gate, w_up, w_down),
+        in_spaces=[pltpu.VMEM] * 4 + [pl.ANY, pl.ANY, pltpu.VMEM],
+        scratch=[pltpu.VMEM((rows, lanes), full)] * 2 + [stream_sems],
         flops=4 * half_flops,
+        traffic=4 * sub_width * lanes,
     )
     out_arrived = swap(out_other)
     g_full, pre_gate, pre_up, dx_other = call(
         functools.partial(backward_kernel, step),
         [vmem((rows, width), low)] + [vmem((rows, lanes), low)] * 2 + [vmem((rows, sub_width), low)],
-        (g_own, g_other, gate, up, w_gate, w_up, w_down),
+        (g_own, g_other, gate, up, gate_other, up_other, w_down),
         flops=4 * half_flops,
     )
     dx_arrived = swap(dx_other)
     (dx_own,) = call(
         functools.partial(backward_own_kernel, step),
         [vmem((rows, sub_width), full)],
-        (pre_gate, pre_up, w_gate, w_up),
+        (pre_gate, pre_up, gate_own, up_own),
         flops=2 * half_flops,
     )
     returned = exchange(

time: 62.4 us -> 68.6 us (1.099)
  waiting for transfers between devices: 0.69 us -> 6.94 us
    ppermute x14, waiting for transfers between devices: 0.68 us -> 6.92 us  [exchange(): arrived.append(lax.ppermute(block, 'expert', pairs) if bits else block)]
  transfers between devices with their start and end apart: 18 -> 18, of which waited for: 1 -> 3; matrix products, arithmetic and copies ran while one was open for 0% -> 0% of each run, Pallas kernels for 48% -> 43%
where the time goes in v4:
time: 68.6 us; the launch traced here: 68.4 us
  Pallas kernels  34.4 us (50%)
  starting transfers between devices  26.3 us (38%)
  waiting for transfers between devices  6.94 us (10%)
  between operations  0.8 us (1%)
    pallas_call x10, Pallas kernels, call(): pl.pallas_call(kernel, out_shape=tuple(out_shape), in_specs=[pl.BlockSpec...  34.4 us
    ppermute x14, starting transfers between devices, exchange(): arrived.append(lax.ppermute(block, 'expert', pairs) if bits else block)  25.1 us
    ppermute x14, waiting for transfers between devices, exchange(): arrived.append(lax.ppermute(block, 'expert', pairs) if bits else block)  6.92 us
  transfers between devices with their start and end apart: 18, of which 3 were waited for; matrix products, arithmetic and copies ran while one was open for 0% of the time, Pallas kernels for 43%

profile of v4, /device:TPU:0, one launch (start us, length us, event | category | flops | bytes accessed | tf_op | source)
XLA Modules:
  0.0 68.4 jit_solution(12551592246655354767)
XLA Ops:
  0.6 1.9 %shard_map.110 = (bf16[288,128]{1,0:T(8,128)(2,1)S(1)}, bf16[288,128]{1,0:T(8,128)(2,1)S(1)}, bf16[288,128]{1,0:T(8,128)(2,1)S(1)}, bf16[288,128]{1,0:T(8,128)(2...) custom-call(s32[8,128]{1,0:T(8,128)} %bitcast.2, ...), custom_call_target="tpu_custom_call" | custom-call | bytes 1048576 | tf_op jit(solution)/shard_map/pallas_call | solution.py:132
  2.6 4.1 %collective-permute-start = (bf16[288,128]{1,0:T(8,128)(2,1)S(1)}, bf16[288,128]{1,0:T(8,128)(2,1)S(1)}, u32[]{:S(2)}, u32[]{:S(2)}) collective-permute-start(bf16[288,128]{1,0:T(8,128)(2,1)S(1)} %get-tuple-element.51), channel_id=1, source_target_pairs={{0,8},{2,10},{4,12},{6,14},{8,0},{10,2},{12,4},{14,6},{1,9},{3,11}... | collective-permute-start | bytes 221192 | tf_op jit(solution)/shard_map/ppermute | solution.py:447
  6.7 1.3 %collective-permute-start.1 = (bf16[288,128]{1,0:T(8,128)(2,1)S(1)}, bf16[288,128]{1,0:T(8,128)(2,1)S(1)}, u32[]{:S(2)}, u32[]{:S(2)}) collective-permute-start(bf16[288,128]{1,0:T(8,128)(2,1)S(1)} %get-tuple-element.52), channel_id=1, source_target_pairs={{0,10},{2,8},{4,14},{6,12},{8,2},{10,0},{12,6},{14,4},{1,11},{3,9}... | collective-permute-start | bytes 221192 | tf_op jit(solution)/shard_map/ppermute | solution.py:447
  7.9 3.6 %collective-permute-start.2 = (bf16[288,128]{1,0:T(8,128)(2,1)S(1)}, bf16[288,128]{1,0:T(8,128)(2,1)S(1)}, u32[]{:S(2)}, u32[]{:S(2)}) collective-permute-start(bf16[288,128]{1,0:T(8,128)(2,1)S(1)} %get-tuple-element.53), channel_id=1, source_target_pairs={{0,12},{2,14},{4,8},{6,10},{8,4},{10,6},{12,0},{14,2},{1,13},{3,15... | collective-permute-start | bytes 221192 | tf_op jit(solution)/shard_map/ppermute | solution.py:447
  11.5 1.7 %collective-permute-start.4 = (bf16[288,128]{1,0:T(8,128)(2,1)S(1)}, bf16[288,128]{1,0:T(8,128)(2,1)S(1)}, u32[]{:S(2)}, u32[]{:S(2)}) collective-permute-start(bf16[288,128]{1,0:T(8,128)(2,1)S(1)} %get-tuple-element.55), channel_id=1, source_target_pairs={{0,2},{2,0},{4,6},{6,4},{8,10},{10,8},{12,14},{14,12},{1,3},{3,1},... | collective-permute-start | bytes 221192 | tf_op jit(solution)/shard_map/ppermute | solution.py:447
  13.2 0.0 collective-permute-done.refs_1_
  13.2 1.6 %collective-permute-start.5 = (bf16[288,128]{1,0:T(8,128)(2,1)S(1)}, bf16[288,128]{1,0:T(8,128)(2,1)S(1)}, u32[]{:S(2)}, u32[]{:S(2)}) collective-permute-start(bf16[288,128]{1,0:T(8,128)(2,1)S(1)} %get-tuple-element.56), channel_id=1, source_target_pairs={{0,4},{2,6},{4,0},{6,2},{8,12},{10,14},{12,8},{14,10},{1,5},{3,7},... | collective-permute-start | bytes 221192 | tf_op jit(solution)/shard_map/ppermute | solution.py:447
  14.9 2.8 %collective-permute-done.1.refs_2_ = bf16[288,128]{1,0:T(8,128)(2,1)S(1)} collective-permute-done((bf16[288,128]{1,0:T(8,128)(2,1)S(1)}, bf16[288,128]{1,0:T(8,128)(2,1)S(1)}, u32[]{:S(2)}, u32[]{:S(2)}) %collective-permute-start.1) | collective-permute-done | bytes 73760 | tf_op jit(solution)/shard_map/ppermute | solution.py:447
  17.7 0.9 %collective-permute-start.6 = (bf16[288,128]{1,0:T(8,128)(2,1)S(1)}, bf16[288,128]{1,0:T(8,128)(2,1)S(1)}, u32[]{:S(2)}, u32[]{:S(2)}) collective-permute-start(bf16[288,128]{1,0:T(8,128)(2,1)S(1)} %get-tuple-element.57), channel_id=1, source_target_pairs={{0,6},{2,4},{4,2},{6,0},{8,14},{10,12},{12,10},{14,8},{1,7},{3,5},... | collective-permute-start | bytes 221192 | tf_op jit(solution)/shard_map/ppermute | solution.py:447
  18.6 2.8 %shard_map.111 = (bf16[1,768,4096]{2,1,0:T(8,128)(2,1)S(1)}, f32[8,128]{1,0:T(8,128)S(1)}) custom-call(bf16[1,768,4096]{2,1,0:T(8,128)(2,1)} %source.1), custom_call_target="tpu_custom_call" | custom-call | bytes 6291456 | tf_op jit(solution)/shard_map/pallas_call | solution.py:132
  21.4 0.0 collective-permute-done.3.refs_4_
  21.4 0.0 collective-permute-done.4.refs_5_
  21.4 1.5 %collective-permute-done.6.refs_7_ = bf16[288,128]{1,0:T(8,128)(2,1)S(1)} collective-permute-done((bf16[288,128]{1,0:T(8,128)(2,1)S(1)}, bf16[288,128]{1,0:T(8,128)(2,1)S(1)}, u32[]{:S(2)}, u32[]{:S(2)}) %collective-permute-start.6) | collective-permute-done | bytes 73760 | tf_op jit(solution)/shard_map/ppermute | solution.py:447
  23.0 0.5 shard_map.112
  23.4 0.1 collective-permute-start.7
  23.5 0.5 collective-permute-start.9
  24.0 3.2 %shard_map.113 = (f32[72,768]{1,0:T(8,128)S(1)}, f32[72,768]{1,0:T(8,128)S(1)}, bf16[2048,768]{1,0:T(8,128)(2,1)S(1)}, bf16[2048,768]{1,0:T(8,128)(2,1)S(1)}) custom-call(bf16[72,2048]{1,0:T(8,128)(2,1)S(1)} %get-tuple-element.59.x_own, bf16[1,4096,768]{2,1,0:T(8,128)(2,1)} %w_gate.3, bf16[1,4096,768]{2,1,0:T(8,128)(2,1)} %w_up.3), custom_call_target="tpu_custom_call" | custom-call | flops 452984832 | bytes 6291456 | tf_op jit(solution)/shard_map/pallas_call | solution.py:132
  27.2 5.4 %shard_map.114 = (bf16[72,4096]{1,0:T(8,128)(2,1)S(1)}, bf16[72,768]{1,0:T(8,128)(2,1)S(1)}, bf16[72,768]{1,0:T(8,128)(2,1)S(1)}, bf16[72,768]{1,0:T(8,128)(2,1)...) custom-call(bf16[72,2048]{1,0:T(8,128)(2,1)S(1)} %get-tuple-element., ...), custom_call_target="tpu_custom_call" | custom-call | flops 905969664 | bytes 6291456 | tf_op jit(solution)/shard_map/pallas_call | solution.py:132
  32.6 0.1 collective-permute-start.8
  32.7 5.3 %shard_map.115 = (bf16[72,4096]{1,0:T(8,128)(2,1)S(1)}, bf16[72,768]{1,0:T(8,128)(2,1)S(1)}, bf16[72,768]{1,0:T(8,128)(2,1)S(1)}, bf16[72,2048]{1,0:T(8,128)(2,1)S(1)}) custom-call(bf16[72,2048]{1,0:T(8,128)(2,1)S(1)} %get-tuple-element.65.g_own, bf16[72,2048]{1,0:T(8,128)(2,1)S(1)} %collective-permute-done.9.g_other, ...), custom_call_target="tpu_custom_call" | custom-call | flops 905969664 | tf_op jit(solution)/shard_map/pallas_call | solution.py:132
  38.1 0.5 collective-permute-start.10
  38.6 2.9 %shard_map.116.dx_own = f32[72,2048]{1,0:T(8,128)S(1)} custom-call(bf16[72,768]{1,0:T(8,128)(2,1)S(1)} %get-tuple-element.70.pre_gate, bf16[72,768]{1,0:T(8,128)(2,1)S(1)} %get-tuple-element.71.pre_up, bf16[2048,768]{1,0:T(8,128)(2,1)S(1)} %get-tuple-element.72.gate_held, bf16[2048,768]{1,0:T(8,128)(2,1)S(1)} %get-tuple-element.73.up_held), custom_call_target="tpu_custom_call" | custom-call | flops 452984832 | tf_op jit(solution)/shard_map/pallas_call | solution.py:132
  41.5 0.7 shard_map.117
  42.2 2.3 %collective-permute-start.11 = (bf16[288,128]{1,0:T(8,128)(2,1)S(1)}, bf16[288,128]{1,0:T(8,128)(2,1)S(1)}, u32[]{:S(2)}, u32[]{:S(2)}) collective-permute-start(bf16[288,128]{1,0:T(8,128)(2,1)S(1)} %get-tuple-element.76), channel_id=1, source_target_pairs={{0,8},{2,10},{4,12},{6,14},{8,0},{10,2},{12,4},{14,6},{1,9},{3,11}... | collective-permute-start | bytes 221192 | tf_op jit(solution)/shard_map/ppermute | solution.py:447
  44.5 2.1 %collective-permute-start.12 = (bf16[288,128]{1,0:T(8,128)(2,1)S(1)}, bf16[288,128]{1,0:T(8,128)(2,1)S(1)}, u32[]{:S(2)}, u32[]{:S(2)}) collective-permute-start(bf16[288,128]{1,0:T(8,128)(2,1)S(1)} %get-tuple-element.77), channel_id=1, source_target_pairs={{0,10},{2,8},{4,14},{6,12},{8,2},{10,0},{12,6},{14,4},{1,11},{3,9}... | collective-permute-start | bytes 221192 | tf_op jit(solution)/shard_map/ppermute | solution.py:447
  46.5 2.5 %collective-permute-start.13 = (bf16[288,128]{1,0:T(8,128)(2,1)S(1)}, bf16[288,128]{1,0:T(8,128)(2,1)S(1)}, u32[]{:S(2)}, u32[]{:S(2)}) collective-permute-start(bf16[288,128]{1,0:T(8,128)(2,1)S(1)} %get-tuple-element.78), channel_id=1, source_target_pairs={{0,12},{2,14},{4,8},{6,10},{8,4},{10,6},{12,0},{14,2},{1,13},{3,15... | collective-permute-start | bytes 221192 | tf_op jit(solution)/shard_map/ppermute | solution.py:447
  49.0 0.9 %collective-permute-start.14 = (bf16[288,128]{1,0:T(8,128)(2,1)S(1)}, bf16[288,128]{1,0:T(8,128)(2,1)S(1)}, u32[]{:S(2)}, u32[]{:S(2)}) collective-permute-start(bf16[288,128]{1,0:T(8,128)(2,1)S(1)} %get-tuple-element.79), channel_id=1, source_target_pairs={{0,14},{2,12},{4,10},{6,8},{8,6},{10,4},{12,2},{14,0},{1,15},{3,13... | collective-permute-start | bytes 221192 | tf_op jit(solution)/shard_map/ppermute | solution.py:447
  49.9 1.9 %collective-permute-start.15 = (bf16[288,128]{1,0:T(8,128)(2,1)S(1)}, bf16[288,128]{1,0:T(8,128)(2,1)S(1)}, u32[]{:S(2)}, u32[]{:S(2)}) collective-permute-start(bf16[288,128]{1,0:T(8,128)(2,1)S(1)} %get-tuple-element.80), channel_id=1, source_target_pairs={{0,2},{2,0},{4,6},{6,4},{8,10},{10,8},{12,14},{14,12},{1,3},{3,1},... | collective-permute-start | bytes 221192 | tf_op jit(solution)/shard_map/ppermute | solution.py:447
  51.8 2.3 %collective-permute-start.16 = (bf16[288,128]{1,0:T(8,128)(2,1)S(1)}, bf16[288,128]{1,0:T(8,128)(2,1)S(1)}, u32[]{:S(2)}, u32[]{:S(2)}) collective-permute-start(bf16[288,128]{1,0:T(8,128)(2,1)S(1)} %get-tuple-element.81), channel_id=1, source_target_pairs={{0,4},{2,6},{4,0},{6,2},{8,12},{10,14},{12,8},{14,10},{1,5},{3,7},... | collective-permute-start | bytes 221192 | tf_op jit(solution)/shard_map/ppermute | solution.py:447
  54.1 2.5 %collective-permute-done.12.refs_2_ = bf16[288,128]{1,0:T(8,128)(2,1)S(1)} collective-permute-done((bf16[288,128]{1,0:T(8,128)(2,1)S(1)}, bf16[288,128]{1,0:T(8,128)(2,1)S(1)}, u32[]{:S(2)}, u32[]{:S(2)}) %collective-permute-start.12) | collective-permute-done | bytes 73760 | tf_op jit(solution)/shard_map/ppermute | solution.py:447
  56.6 10.0 %shard_map.119 = (bf16[1,4096,768]{2,1,0:T(8,128)(2,1)}, bf16[1,4096,768]{2,1,0:T(8,128)(2,1)}, bf16[1,768,4096]{2,1,0:T(8,128)(2,1)}) custom-call(bf16[72,4096]{1,0:T(8,128)(2,1)S(1)} %get-tuple-element.85.x, bf16[72,4096]{1,0:T(8,128)(2,1)S(1)} %get-tuple-element.86.g, bf16[72,768]{1,0:T(8,128)(2,1)S(1)} %get-tuple-element.87.hidden, ...), custom_call_target="tpu_custom_call" | custom-call | flops 1358954496 | bytes 18874368 | tf_op jit(solution)/shard_map/pallas_call | solution.py:132
  66.7 1.7 %shard_map.118 = (bf16[128,2048]{1,0:T(8,128)(2,1)}, bf16[128,2048]{1,0:T(8,128)(2,1)}) custom-call(bf16[72,128]{1,0:T(8,128)(2,1)S(1)} %get-tuple-element.48.place, f32[72,128]{1,0:T(8,128)S(1)} %get-tuple-element.49.mix, bf16[288,128]{1,0:T(8,128)(2,1)S(1)} %get-tuple-element.75.refs_0_, bf16[288,128]{1,0:T(8,128)(2,1)S(1)} %collective-permute-done.11.refs_1_, ...), custom_call_target="tpu_custom_call" | custom-call | bytes 2097152 | tf_op jit(solution)/shard_map/pallas_call | solution.py:132
  (14 shorter events, 0.0 us)
Async XLA Ops:
  2.6 10.7 %collective-permute-start = (bf16[288,128]{1,0:T(8,128)(2,1)S(1)}, bf16[288,128]{1,0:T(8,128)(2,1)S(1)}, u32[]{:S(2)}, u32[]{:S(2)}) collective-permute-start(bf16[288,128]{1,0:T(8,128)(2,1)S(1)} %get-tuple-element.51), channel_id=1, source_target_pairs={{0,8},{2,10},{4,12},{6,14},{8,0},{10,2},{12,4},{14,6},{1,9},{3,11}... | collective-permute-start | bytes 221192 | tf_op jit(solution)/shard_map/ppermute | solution.py:447
  6.7 11.0 %collective-permute-start.1 = (bf16[288,128]{1,0:T(8,128)(2,1)S(1)}, bf16[288,128]{1,0:T(8,128)(2,1)S(1)}, u32[]{:S(2)}, u32[]{:S(2)}) collective-permute-start(bf16[288,128]{1,0:T(8,128)(2,1)S(1)} %get-tuple-element.52), channel_id=1, source_target_pairs={{0,10},{2,8},{4,14},{6,12},{8,2},{10,0},{12,6},{14,4},{1,11},{3,9}... | collective-permute-start | bytes 221192 | tf_op jit(solution)/shard_map/ppermute | solution.py:447
  7.9 13.5 %collective-permute-start.2 = (bf16[288,128]{1,0:T(8,128)(2,1)S(1)}, bf16[288,128]{1,0:T(8,128)(2,1)S(1)}, u32[]{:S(2)}, u32[]{:S(2)}) collective-permute-start(bf16[288,128]{1,0:T(8,128)(2,1)S(1)} %get-tuple-element.53), channel_id=1, source_target_pairs={{0,12},{2,14},{4,8},{6,10},{8,4},{10,6},{12,0},{14,2},{1,13},{3,15... | collective-permute-start | bytes 221192 | tf_op jit(solution)/shard_map/ppermute | solution.py:447
  11.5 9.9 %collective-permute-start.3 = (bf16[288,128]{1,0:T(8,128)(2,1)S(1)}, bf16[288,128]{1,0:T(8,128)(2,1)S(1)}, u32[]{:S(2)}, u32[]{:S(2)}) collective-permute-start(bf16[288,128]{1,0:T(8,128)(2,1)S(1)} %get-tuple-element.54), channel_id=1, source_target_pairs={{0,14},{2,12},{4,10},{6,8},{8,6},{10,4},{12,2},{14,0},{1,15},{3,13... | collective-permute-start | bytes 221192 | tf_op jit(solution)/shard_map/ppermute | solution.py:447
  11.5 9.9 %collective-permute-start.4 = (bf16[288,128]{1,0:T(8,128)(2,1)S(1)}, bf16[288,128]{1,0:T(8,128)(2,1)S(1)}, u32[]{:S(2)}, u32[]{:S(2)}) collective-permute-start(bf16[288,128]{1,0:T(8,128)(2,1)S(1)} %get-tuple-element.55), channel_id=1, source_target_pairs={{0,2},{2,0},{4,6},{6,4},{8,10},{10,8},{12,14},{14,12},{1,3},{3,1},... | collective-permute-start | bytes 221192 | tf_op jit(solution)/shard_map/ppermute | solution.py:447
  13.2 8.2 %collective-permute-start.5 = (bf16[288,128]{1,0:T(8,128)(2,1)S(1)}, bf16[288,128]{1,0:T(8,128)(2,1)S(1)}, u32[]{:S(2)}, u32[]{:S(2)}) collective-permute-start(bf16[288,128]{1,0:T(8,128)(2,1)S(1)} %get-tuple-element.56), channel_id=1, source_target_pairs={{0,4},{2,6},{4,0},{6,2},{8,12},{10,14},{12,8},{14,10},{1,5},{3,7},... | collective-permute-start | bytes 221192 | tf_op jit(solution)/shard_map/ppermute | solution.py:447
  17.7 5.3 %collective-permute-start.6 = (bf16[288,128]{1,0:T(8,128)(2,1)S(1)}, bf16[288,128]{1,0:T(8,128)(2,1)S(1)}, u32[]{:S(2)}, u32[]{:S(2)}) collective-permute-start(bf16[288,128]{1,0:T(8,128)(2,1)S(1)} %get-tuple-element.57), channel_id=1, source_target_pairs={{0,6},{2,4},{4,2},{6,0},{8,14},{10,12},{12,10},{14,8},{1,7},{3,5},... | collective-permute-start | bytes 221192 | tf_op jit(solution)/shard_map/ppermute | solution.py:447
  23.4 3.8 %collective-permute-start.7 = (bf16[72,2048]{1,0:T(8,128)(2,1)S(1)}, bf16[72,2048]{1,0:T(8,128)(2,1)S(1)}, u32[]{:S(2)}, u32[]{:S(2)}) collective-permute-start(bf16[72,2048]{1,0:T(8,128)(2,1)S(1)} %get-tuple-element.59.x_own), channel_id=1, source_target_pairs={{0,1},{1,0},{2,3},{3,2},{4,5},{5,4},{6,7},{7,6},{8,9},{9,8},{10,11... | collective-permute-start | bytes 884744 | tf_op jit(solution)/shard_map/ppermute | solution.py:452
  23.5 9.2 %collective-permute-start.9 = (bf16[72,2048]{1,0:T(8,128)(2,1)S(1)}, bf16[72,2048]{1,0:T(8,128)(2,1)S(1)}, u32[]{:S(2)}, u32[]{:S(2)}) collective-permute-start(bf16[72,2048]{1,0:T(8,128)(2,1)S(1)} %get-tuple-element.65.g_own), channel_id=1, source_target_pairs={{0,1},{1,0},{2,3},{3,2},{4,5},{5,4},{6,7},{7,6},{8,9},{9,8},{10,11... | collective-permute-start | bytes 884744 | tf_op jit(solution)/shard_map/ppermute | solution.py:452
  32.6 8.9 %collective-permute-start.8 = (bf16[72,2048]{1,0:T(8,128)(2,1)S(1)}, bf16[72,2048]{1,0:T(8,128)(2,1)S(1)}, u32[]{:S(2)}, u32[]{:S(2)}) collective-permute-start(bf16[72,2048]{1,0:T(8,128)(2,1)S(1)} %get-tuple-element.64), channel_id=1, source_target_pairs={{0,1},{1,0},{2,3},{3,2},{4,5},{5,4},{6,7},{7,6},{8,9},{9,8},{10,11... | collective-permute-start | bytes 884744 | tf_op jit(solution)/shard_map/ppermute | solution.py:452
  38.1 3.4 %collective-permute-start.10 = (bf16[72,2048]{1,0:T(8,128)(2,1)S(1)}, bf16[72,2048]{1,0:T(8,128)(2,1)S(1)}, u32[]{:S(2)}, u32[]{:S(2)}) collective-permute-start(bf16[72,2048]{1,0:T(8,128)(2,1)S(1)} %get-tuple-element.74), channel_id=1, source_target_pairs={{0,1},{1,0},{2,3},{3,2},{4,5},{5,4},{6,7},{7,6},{8,9},{9,8},{10,11... | collective-permute-start | bytes 884744 | tf_op jit(solution)/shard_map/ppermute | solution.py:452
  42.2 9.6 %collective-permute-start.11 = (bf16[288,128]{1,0:T(8,128)(2,1)S(1)}, bf16[288,128]{1,0:T(8,128)(2,1)S(1)}, u32[]{:S(2)}, u32[]{:S(2)}) collective-permute-start(bf16[288,128]{1,0:T(8,128)(2,1)S(1)} %get-tuple-element.76), channel_id=1, source_target_pairs={{0,8},{2,10},{4,12},{6,14},{8,0},{10,2},{12,4},{14,6},{1,9},{3,11}... | collective-permute-start | bytes 221192 | tf_op jit(solution)/shard_map/ppermute | solution.py:447
  44.5 12.2 %collective-permute-start.12 = (bf16[288,128]{1,0:T(8,128)(2,1)S(1)}, bf16[288,128]{1,0:T(8,128)(2,1)S(1)}, u32[]{:S(2)}, u32[]{:S(2)}) collective-permute-start(bf16[288,128]{1,0:T(8,128)(2,1)S(1)} %get-tuple-element.77), channel_id=1, source_target_pairs={{0,10},{2,8},{4,14},{6,12},{8,2},{10,0},{12,6},{14,4},{1,11},{3,9}... | collective-permute-start | bytes 221192 | tf_op jit(solution)/shard_map/ppermute | solution.py:447
  46.5 20.2 %collective-permute-start.13 = (bf16[288,128]{1,0:T(8,128)(2,1)S(1)}, bf16[288,128]{1,0:T(8,128)(2,1)S(1)}, u32[]{:S(2)}, u32[]{:S(2)}) collective-permute-start(bf16[288,128]{1,0:T(8,128)(2,1)S(1)} %get-tuple-element.78), channel_id=1, source_target_pairs={{0,12},{2,14},{4,8},{6,10},{8,4},{10,6},{12,0},{14,2},{1,13},{3,15... | collective-permute-start | bytes 221192 | tf_op jit(solution)/shard_map/ppermute | solution.py:447
  49.0 17.7 %collective-permute-start.14 = (bf16[288,128]{1,0:T(8,128)(2,1)S(1)}, bf16[288,128]{1,0:T(8,128)(2,1)S(1)}, u32[]{:S(2)}, u32[]{:S(2)}) collective-permute-start(bf16[288,128]{1,0:T(8,128)(2,1)S(1)} %get-tuple-element.79), channel_id=1, source_target_pairs={{0,14},{2,12},{4,10},{6,8},{8,6},{10,4},{12,2},{14,0},{1,15},{3,13... | collective-permute-start | bytes 221192 | tf_op jit(solution)/shard_map/ppermute | solution.py:447
  49.9 16.8 %collective-permute-start.15 = (bf16[288,128]{1,0:T(8,128)(2,1)S(1)}, bf16[288,128]{1,0:T(8,128)(2,1)S(1)}, u32[]{:S(2)}, u32[]{:S(2)}) collective-permute-start(bf16[288,128]{1,0:T(8,128)(2,1)S(1)} %get-tuple-element.80), channel_id=1, source_target_pairs={{0,2},{2,0},{4,6},{6,4},{8,10},{10,8},{12,14},{14,12},{1,3},{3,1},... | collective-permute-start | bytes 221192 | tf_op jit(solution)/shard_map/ppermute | solution.py:447
  51.8 14.9 %collective-permute-start.16 = (bf16[288,128]{1,0:T(8,128)(2,1)S(1)}, bf16[288,128]{1,0:T(8,128)(2,1)S(1)}, u32[]{:S(2)}, u32[]{:S(2)}) collective-permute-start(bf16[288,128]{1,0:T(8,128)(2,1)S(1)} %get-tuple-element.81), channel_id=1, source_target_pairs={{0,4},{2,6},{4,0},{6,2},{8,12},{10,14},{12,8},{14,10},{1,5},{3,7},... | collective-permute-start | bytes 221192 | tf_op jit(solution)/shard_map/ppermute | solution.py:447
  56.6 10.1 %collective-permute-start.17 = (bf16[288,128]{1,0:T(8,128)(2,1)S(1)}, bf16[288,128]{1,0:T(8,128)(2,1)S(1)}, u32[]{:S(2)}, u32[]{:S(2)}) collective-permute-start(bf16[288,128]{1,0:T(8,128)(2,1)S(1)} %get-tuple-element.82), channel_id=1, source_target_pairs={{0,6},{2,4},{4,2},{6,0},{8,14},{10,12},{12,10},{14,8},{1,7},{3,5},... | collective-permute-start | bytes 221192 | tf_op jit(solution)/shard_map/ppermute | solution.py:447

commit v5 on v3

--- a/solution.py
+++ b/solution.py
@@ -320,8 +320,12 @@
     lax.fori_loop(0, half_width // step, spread, 0)
 
 
+def flip(value):
+    return value.astype(jnp.float32).T
+
+
 def input_term(pre_gate, pre_up, w_gate, w_up, there):
-    return contract_cols(pre_gate[...], w_gate[0, there, :]) + contract_cols(pre_up[...], w_up[0, there, :])
+    return flip(contract_cols(w_gate[0, there, :], pre_gate[...]) + contract_cols(w_up[0, there, :], pre_up[...]))
 
 
 def backward_kernel(step, g_own, g_other, gate, up, w_gate, w_up, w_down, g_full, pre_gate, pre_up, dx_other):
@@ -332,7 +336,7 @@
 
     def pull(i, carry):
         cols = chunk(i, step)
-        part = contract_cols(g_full[...], w_down[0, cols, :]).astype(jnp.bfloat16)
+        part = flip(contract_cols(w_down[0, cols, :], g_full[...])).astype(jnp.bfloat16)
         grad_hidden = part.astype(jnp.float32)
         value = gate[:, cols].astype(jnp.float32)
         sig = jax.nn.sigmoid(value)
@@ -364,12 +368,16 @@
     lax.fori_loop(0, half_width // step, spread, 0)
 
 
+def pieces_of(total, size):
+    return [slice(at, min(at + size, total)) for at in range(0, total, size)]
+
+
 def gradient_kernel(
-    step, x, g, hidden, pre_gate, pre_up, grad_gate, grad_up, grad_down, flipped, tall, wide, tall_sems, wide_sems
+    step, x, g, hidden, pre_gate, pre_up, grad_gate, grad_up, grad_down, flipped, turned, tall, wide, tall_sems, wide_sems
 ):
     width, lanes = x.shape[1], hidden.shape[1]
     count = width // step
-    flipped[...] = hidden[...].astype(jnp.float32).T.astype(flipped.dtype)
+    flipped[...] = flip(hidden[...]).astype(flipped.dtype)
 
     def wide_copy(i, slot):
         return pltpu.make_async_copy(wide.at[slot], grad_down.at[0, :, chunk(i, step)], wide_sems.at[slot])
@@ -384,7 +392,10 @@
         def _():
             wide_copy(i - 2, slot).wait()
 
-        wide[slot] = dot(flipped[...], g[:, chunk(i, step)]).astype(wide.dtype)
+        for cut in pieces_of(step, 256):
+            right = g[:, chunk(i, step)][:, cut]
+            for high in pieces_of(lanes, 256):
+                wide[slot, high, cut] = dot(flipped[high, :], right).astype(wide.dtype)
         wide_copy(i, slot).start()
         return carry
 
@@ -392,13 +403,16 @@
 
     def inputs(i, carry):
         slot = i % 2
+        turned[...] = flip(x[:, chunk(i, step)]).astype(turned.dtype)
         for which, (right, out) in enumerate(((pre_gate, grad_gate), (pre_up, grad_up))):
 
             @pl.when(i >= 2)
             def _():
                 tall_copy(which, out, i - 2, slot).wait()
 
-            tall[which, slot] = contract_rows(x[:, chunk(i, step)], right[...]).astype(tall.dtype)
+            for cut in pieces_of(lanes, 256):
+                for high in pieces_of(step, 256):
+                    tall[which, slot, high, cut] = dot(turned[high, :], right[:, cut]).astype(tall.dtype)
             tall_copy(which, out, i, slot).start()
         return carry
 
@@ -514,6 +528,7 @@
         out_spaces=[pl.ANY] * 3,
         scratch=[
             pltpu.VMEM((lanes, rows), low),
+            pltpu.VMEM((cut, rows), low),
             pltpu.VMEM((2, 2, cut, lanes), low),
             pltpu.VMEM((2, lanes, cut), low),
             pltpu.SemaphoreType.DMA((2, 2)),

time: 62.4 us -> 62.1 us (level)
  no operation moved by 1% of the time
where the time goes in v5:
time: 62.1 us; the launch traced here: 61.9 us
  Pallas kernels  34.3 us (55%)
  starting transfers between devices  26.1 us (42%)
  between operations  0.8 us (1%)
  waiting for transfers between devices  0.69 us (1%)
    pallas_call x10, Pallas kernels, call(): pl.pallas_call(kernel, out_shape=tuple(out_shape), in_specs=[pl.BlockSpec...  34.3 us
    ppermute x14, starting transfers between devices, exchange(): lax.ppermute(blocks[k], 'expert', pairs[k])  24.8 us
  transfers between devices with their start and end apart: 18, of which 1 were waited for; matrix products, arithmetic and copies ran while one was open for 0% of the time, Pallas kernels for 48%

profile of v5, /device:TPU:0, one launch (start us, length us, event | category | flops | bytes accessed | tf_op | source)
XLA Modules:
  0.0 61.9 jit_solution(2754265633045653017)
XLA Ops:
  0.6 1.9 %shard_map.110 = (bf16[288,128]{1,0:T(8,128)(2,1)S(1)}, bf16[288,128]{1,0:T(8,128)(2,1)S(1)}, bf16[288,128]{1,0:T(8,128)(2,1)S(1)}, bf16[288,128]{1,0:T(8,128)(2...) custom-call(s32[8,128]{1,0:T(8,128)} %bitcast.2, ...), custom_call_target="tpu_custom_call" | custom-call | bytes 1048576 | tf_op jit(solution)/shard_map/pallas_call | solution.py:132
  2.6 3.0 %collective-permute-start = (bf16[288,128]{1,0:T(8,128)(2,1)S(1)}, bf16[288,128]{1,0:T(8,128)(2,1)S(1)}, u32[]{:S(2)}, u32[]{:S(2)}) collective-permute-start(bf16[288,128]{1,0:T(8,128)(2,1)S(1)} %get-tuple-element.49), channel_id=1, source_target_pairs={{0,2},{2,0},{4,6},{6,4},{8,10},{10,8},{12,14},{14,12},{1,3},{3,1},... | collective-permute-start | bytes 221192 | tf_op jit(solution)/shard_map/ppermute | solution.py:428
  5.6 1.6 %collective-permute-start.1 = (bf16[288,128]{1,0:T(8,128)(2,1)S(1)}, bf16[288,128]{1,0:T(8,128)(2,1)S(1)}, u32[]{:S(2)}, u32[]{:S(2)}) collective-permute-start(bf16[288,128]{1,0:T(8,128)(2,1)S(1)} %get-tuple-element.50), channel_id=1, source_target_pairs={{0,4},{2,6},{4,0},{6,2},{8,12},{10,14},{12,8},{14,10},{1,5},{3,7},... | collective-permute-start | bytes 221192 | tf_op jit(solution)/shard_map/ppermute | solution.py:428
  7.1 0.0 collective-permute-start.2
  7.2 3.0 %collective-permute-start.3 = (bf16[288,128]{1,0:T(8,128)(2,1)S(1)}, bf16[288,128]{1,0:T(8,128)(2,1)S(1)}, u32[]{:S(2)}, u32[]{:S(2)}) collective-permute-start(bf16[288,128]{1,0:T(8,128)(2,1)S(1)} %get-tuple-element.52), channel_id=1, source_target_pairs={{0,8},{2,10},{4,12},{6,14},{8,0},{10,2},{12,4},{14,6},{1,9},{3,11}... | collective-permute-start | bytes 221192 | tf_op jit(solution)/shard_map/ppermute | solution.py:428
  10.2 1.3 %collective-permute-start.4 = (bf16[288,128]{1,0:T(8,128)(2,1)S(1)}, bf16[288,128]{1,0:T(8,128)(2,1)S(1)}, u32[]{:S(2)}, u32[]{:S(2)}) collective-permute-start(bf16[288,128]{1,0:T(8,128)(2,1)S(1)} %get-tuple-element.53), channel_id=1, source_target_pairs={{0,10},{2,8},{4,14},{6,12},{8,2},{10,0},{12,6},{14,4},{1,11},{3,9}... | collective-permute-start | bytes 221192 | tf_op jit(solution)/shard_map/ppermute | solution.py:428
  11.4 0.0 collective-permute-done.refs_1_
  11.4 3.6 %collective-permute-start.5 = (bf16[288,128]{1,0:T(8,128)(2,1)S(1)}, bf16[288,128]{1,0:T(8,128)(2,1)S(1)}, u32[]{:S(2)}, u32[]{:S(2)}) collective-permute-start(bf16[288,128]{1,0:T(8,128)(2,1)S(1)} %get-tuple-element.54), channel_id=1, source_target_pairs={{0,12},{2,14},{4,8},{6,10},{8,4},{10,6},{12,0},{14,2},{1,13},{3,15... | collective-permute-start | bytes 221192 | tf_op jit(solution)/shard_map/ppermute | solution.py:428
  15.0 0.0 collective-permute-start.6
  15.1 6.4 %shard_map.111 = (bf16[1,4096,768]{2,1,0:T(8,128)(2,1)S(1)}, bf16[1,4096,768]{2,1,0:T(8,128)(2,1)S(1)}, bf16[1,768,4096]{2,1,0:T(8,128)(2,1)S(1)}, f32[8,128]{1,0:T(8,128)S(1)}) custom-call(bf16[1,4096,768]{2,1,0:T(8,128)(2,1)} %refs_0_.1, bf16[1,4096,768]{2,1,0:T(8,128)(2,1)} %refs_1_.1, bf16[1,768,4096]{2,1,0:T(8,128)(2,1)} %refs_2_.1), custom_call_target="tpu_custom_call" | custom-call | bytes 18874368 | tf_op jit(solution)/shard_map/pallas_call | solution.py:132
  21.5 0.0 collective-permute-done.2.refs_3_
  21.5 0.0 collective-permute-done.4.refs_5_
  21.6 0.6 %collective-permute-done.6.refs_7_ = bf16[288,128]{1,0:T(8,128)(2,1)S(1)} collective-permute-done((bf16[288,128]{1,0:T(8,128)(2,1)S(1)}, bf16[288,128]{1,0:T(8,128)(2,1)S(1)}, u32[]{:S(2)}, u32[]{:S(2)}) %collective-permute-start.6) | collective-permute-done | bytes 73760 | tf_op jit(solution)/shard_map/ppermute | solution.py:428
  22.2 0.5 shard_map.112
  22.7 0.1 collective-permute-start.7
  22.7 0.5 collective-permute-start.9
  23.2 1.5 %shard_map.113 = (f32[72,768]{1,0:T(8,128)S(1)}, f32[72,768]{1,0:T(8,128)S(1)}) custom-call(bf16[72,2048]{1,0:T(8,128)(2,1)S(1)} %get-tuple-element.57.x_own, bf16[1,4096,768]{2,1,0:T(8,128)(2,1)S(1)} %get-tuple-element.58.w_gate, bf16[1,4096,768]{2,1,0:T(8,128)(2,1)S(1)} %get-tuple-element.59.w_up), custom_call_target="tpu_custom_call" | custom-call | flops 452984832 | tf_op jit(solution)/shard_map/pallas_call | solution.py:132
  24.7 3.7 %shard_map.114 = (bf16[72,4096]{1,0:T(8,128)(2,1)S(1)}, bf16[72,768]{1,0:T(8,128)(2,1)S(1)}, bf16[72,768]{1,0:T(8,128)(2,1)S(1)}, bf16[72,768]{1,0:T(8,128)(2,1)...) custom-call(bf16[72,2048]{1,0:T(8,128)(2,1)S(1)} %get-tuple-element.57.x_own, ...), custom_call_target="tpu_custom_call" | custom-call | flops 905969664 | tf_op jit(solution)/shard_map/pallas_call | solution.py:132
  28.5 0.1 collective-permute-start.8
  28.6 5.7 %shard_map.115 = (bf16[72,4096]{1,0:T(8,128)(2,1)S(1)}, bf16[72,768]{1,0:T(8,128)(2,1)S(1)}, bf16[72,768]{1,0:T(8,128)(2,1)S(1)}, bf16[72,2048]{1,0:T(8,128)(2,1)S(1)}) custom-call(bf16[72,2048]{1,0:T(8,128)(2,1)S(1)} %get-tuple-element.65.g_own, bf16[72,2048]{1,0:T(8,128)(2,1)S(1)} %collective-permute-done.9.g_other, ...), custom_call_target="tpu_custom_call" | custom-call | flops 905969664 | tf_op jit(solution)/shard_map/pallas_call | solution.py:132
  34.3 0.5 collective-permute-start.10
  34.8 3.3 %shard_map.116.dx_own = f32[72,2048]{1,0:T(8,128)S(1)} custom-call(bf16[72,768]{1,0:T(8,128)(2,1)S(1)} %get-tuple-element.68.pre_gate, bf16[72,768]{1,0:T(8,128)(2,1)S(1)} %get-tuple-element.69.pre_up, bf16[1,4096,768]{2,1,0:T(8,128)(2,1)S(1)} %get-tuple-element.58.w_gate, bf16[1,4096,768]{2,1,0:T(8,128)(2,1)S(1)} %get-tuple-element.59.w_up), custom_call_target="tpu_custom_call" | custom-call | flops 452984832 | tf_op jit(solution)/shard_map/pallas_call | solution.py:132
  38.1 0.7 %shard_map.117 = (bf16[288,128]{1,0:T(8,128)(2,1)S(1)}, bf16[288,128]{1,0:T(8,128)(2,1)S(1)}, bf16[288,128]{1,0:T(8,128)(2,1)S(1)}, bf16[288,128]{1,0:T(8,128)(2...) custom-call(f32[72,2048]{1,0:T(8,128)S(1)} %get-tuple-element.63.out, ...), custom_call_target="tpu_custom_call" | custom-call | bytes 2359296 | tf_op jit(solution)/shard_map/pallas_call | solution.py:132
  38.8 1.1 %collective-permute-start.11 = (bf16[288,128]{1,0:T(8,128)(2,1)S(1)}, bf16[288,128]{1,0:T(8,128)(2,1)S(1)}, u32[]{:S(2)}, u32[]{:S(2)}) collective-permute-start(bf16[288,128]{1,0:T(8,128)(2,1)S(1)} %get-tuple-element.72), channel_id=1, source_target_pairs={{0,2},{2,0},{4,6},{6,4},{8,10},{10,8},{12,14},{14,12},{1,3},{3,1},... | collective-permute-start | bytes 221192 | tf_op jit(solution)/shard_map/ppermute | solution.py:428
  39.8 2.8 %collective-permute-start.12 = (bf16[288,128]{1,0:T(8,128)(2,1)S(1)}, bf16[288,128]{1,0:T(8,128)(2,1)S(1)}, u32[]{:S(2)}, u32[]{:S(2)}) collective-permute-start(bf16[288,128]{1,0:T(8,128)(2,1)S(1)} %get-tuple-element.73), channel_id=1, source_target_pairs={{0,4},{2,6},{4,0},{6,2},{8,12},{10,14},{12,8},{14,10},{1,5},{3,7},... | collective-permute-start | bytes 221192 | tf_op jit(solution)/shard_map/ppermute | solution.py:428
  42.6 0.7 %collective-permute-start.13 = (bf16[288,128]{1,0:T(8,128)(2,1)S(1)}, bf16[288,128]{1,0:T(8,128)(2,1)S(1)}, u32[]{:S(2)}, u32[]{:S(2)}) collective-permute-start(bf16[288,128]{1,0:T(8,128)(2,1)S(1)} %get-tuple-element.74), channel_id=1, source_target_pairs={{0,6},{2,4},{4,2},{6,0},{8,14},{10,12},{12,10},{14,8},{1,7},{3,5},... | collective-permute-start | bytes 221192 | tf_op jit(solution)/shard_map/ppermute | solution.py:428
  43.2 3.1 %collective-permute-start.14 = (bf16[288,128]{1,0:T(8,128)(2,1)S(1)}, bf16[288,128]{1,0:T(8,128)(2,1)S(1)}, u32[]{:S(2)}, u32[]{:S(2)}) collective-permute-start(bf16[288,128]{1,0:T(8,128)(2,1)S(1)} %get-tuple-element.75), channel_id=1, source_target_pairs={{0,8},{2,10},{4,12},{6,14},{8,0},{10,2},{12,4},{14,6},{1,9},{3,11}... | collective-permute-start | bytes 221192 | tf_op jit(solution)/shard_map/ppermute | solution.py:428
  46.4 0.0 collective-permute-start.15
  46.4 2.9 %collective-permute-start.16 = (bf16[288,128]{1,0:T(8,128)(2,1)S(1)}, bf16[288,128]{1,0:T(8,128)(2,1)S(1)}, u32[]{:S(2)}, u32[]{:S(2)}) collective-permute-start(bf16[288,128]{1,0:T(8,128)(2,1)S(1)} %get-tuple-element.77), channel_id=1, source_target_pairs={{0,12},{2,14},{4,8},{6,10},{8,4},{10,6},{12,0},{14,2},{1,13},{3,15... | collective-permute-start | bytes 221192 | tf_op jit(solution)/shard_map/ppermute | solution.py:428
  49.3 1.8 %collective-permute-start.17 = (bf16[288,128]{1,0:T(8,128)(2,1)S(1)}, bf16[288,128]{1,0:T(8,128)(2,1)S(1)}, u32[]{:S(2)}, u32[]{:S(2)}) collective-permute-start(bf16[288,128]{1,0:T(8,128)(2,1)S(1)} %get-tuple-element.78), channel_id=1, source_target_pairs={{0,14},{2,12},{4,10},{6,8},{8,6},{10,4},{12,2},{14,0},{1,15},{3,13... | collective-permute-start | bytes 221192 | tf_op jit(solution)/shard_map/ppermute | solution.py:428
  51.1 9.1 %shard_map.119 = (bf16[1,4096,768]{2,1,0:T(8,128)(2,1)}, bf16[1,4096,768]{2,1,0:T(8,128)(2,1)}, bf16[1,768,4096]{2,1,0:T(8,128)(2,1)}) custom-call(bf16[72,4096]{1,0:T(8,128)(2,1)S(1)} %get-tuple-element.81.x, bf16[72,4096]{1,0:T(8,128)(2,1)S(1)} %get-tuple-element.82.g, bf16[72,768]{1,0:T(8,128)(2,1)S(1)} %get-tuple-element.83.hidden, ...), custom_call_target="tpu_custom_call" | custom-call | flops 1358954496 | bytes 18874368 | tf_op jit(solution)/shard_map/pallas_call | solution.py:132
  60.2 1.6 %shard_map.118 = (bf16[128,2048]{1,0:T(8,128)(2,1)}, bf16[128,2048]{1,0:T(8,128)(2,1)}) custom-call(bf16[72,128]{1,0:T(8,128)(2,1)S(1)} %get-tuple-element.46.place, f32[72,128]{1,0:T(8,128)S(1)} %get-tuple-element.47.mix, bf16[288,128]{1,0:T(8,128)(2,1)S(1)} %get-tuple-element.71.refs_0_, bf16[288,128]{1,0:T(8,128)(2,1)S(1)} %collective-permute-done.11.refs_1_, ...), custom_call_target="tpu_custom_call" | custom-call | bytes 2097152 | tf_op jit(solution)/shard_map/pallas_call | solution.py:132
  (14 shorter events, 0.0 us)
Async XLA Ops:
  2.6 8.9 %collective-permute-start = (bf16[288,128]{1,0:T(8,128)(2,1)S(1)}, bf16[288,128]{1,0:T(8,128)(2,1)S(1)}, u32[]{:S(2)}, u32[]{:S(2)}) collective-permute-start(bf16[288,128]{1,0:T(8,128)(2,1)S(1)} %get-tuple-element.49), channel_id=1, source_target_pairs={{0,2},{2,0},{4,6},{6,4},{8,10},{10,8},{12,14},{14,12},{1,3},{3,1},... | collective-permute-start | bytes 221192 | tf_op jit(solution)/shard_map/ppermute | solution.py:428
  5.6 9.5 %collective-permute-start.1 = (bf16[288,128]{1,0:T(8,128)(2,1)S(1)}, bf16[288,128]{1,0:T(8,128)(2,1)S(1)}, u32[]{:S(2)}, u32[]{:S(2)}) collective-permute-start(bf16[288,128]{1,0:T(8,128)(2,1)S(1)} %get-tuple-element.50), channel_id=1, source_target_pairs={{0,4},{2,6},{4,0},{6,2},{8,12},{10,14},{12,8},{14,10},{1,5},{3,7},... | collective-permute-start | bytes 221192 | tf_op jit(solution)/shard_map/ppermute | solution.py:428
  7.1 14.4 %collective-permute-start.2 = (bf16[288,128]{1,0:T(8,128)(2,1)S(1)}, bf16[288,128]{1,0:T(8,128)(2,1)S(1)}, u32[]{:S(2)}, u32[]{:S(2)}) collective-permute-start(bf16[288,128]{1,0:T(8,128)(2,1)S(1)} %get-tuple-element.51), channel_id=1, source_target_pairs={{0,6},{2,4},{4,2},{6,0},{8,14},{10,12},{12,10},{14,8},{1,7},{3,5},... | collective-permute-start | bytes 221192 | tf_op jit(solution)/shard_map/ppermute | solution.py:428
  7.2 14.4 %collective-permute-start.3 = (bf16[288,128]{1,0:T(8,128)(2,1)S(1)}, bf16[288,128]{1,0:T(8,128)(2,1)S(1)}, u32[]{:S(2)}, u32[]{:S(2)}) collective-permute-start(bf16[288,128]{1,0:T(8,128)(2,1)S(1)} %get-tuple-element.52), channel_id=1, source_target_pairs={{0,8},{2,10},{4,12},{6,14},{8,0},{10,2},{12,4},{14,6},{1,9},{3,11}... | collective-permute-start | bytes 221192 | tf_op jit(solution)/shard_map/ppermute | solution.py:428
  10.2 11.4 %collective-permute-start.4 = (bf16[288,128]{1,0:T(8,128)(2,1)S(1)}, bf16[288,128]{1,0:T(8,128)(2,1)S(1)}, u32[]{:S(2)}, u32[]{:S(2)}) collective-permute-start(bf16[288,128]{1,0:T(8,128)(2,1)S(1)} %get-tuple-element.53), channel_id=1, source_target_pairs={{0,10},{2,8},{4,14},{6,12},{8,2},{10,0},{12,6},{14,4},{1,11},{3,9}... | collective-permute-start | bytes 221192 | tf_op jit(solution)/shard_map/ppermute | solution.py:428
  11.4 10.1 %collective-permute-start.5 = (bf16[288,128]{1,0:T(8,128)(2,1)S(1)}, bf16[288,128]{1,0:T(8,128)(2,1)S(1)}, u32[]{:S(2)}, u32[]{:S(2)}) collective-permute-start(bf16[288,128]{1,0:T(8,128)(2,1)S(1)} %get-tuple-element.54), channel_id=1, source_target_pairs={{0,12},{2,14},{4,8},{6,10},{8,4},{10,6},{12,0},{14,2},{1,13},{3,15... | collective-permute-start | bytes 221192 | tf_op jit(solution)/shard_map/ppermute | solution.py:428
  15.0 7.2 %collective-permute-start.6 = (bf16[288,128]{1,0:T(8,128)(2,1)S(1)}, bf16[288,128]{1,0:T(8,128)(2,1)S(1)}, u32[]{:S(2)}, u32[]{:S(2)}) collective-permute-start(bf16[288,128]{1,0:T(8,128)(2,1)S(1)} %get-tuple-element.55), channel_id=1, source_target_pairs={{0,14},{2,12},{4,10},{6,8},{8,6},{10,4},{12,2},{14,0},{1,15},{3,13... | collective-permute-start | bytes 221192 | tf_op jit(solution)/shard_map/ppermute | solution.py:428
  22.7 2.1 %collective-permute-start.7 = (bf16[72,2048]{1,0:T(8,128)(2,1)S(1)}, bf16[72,2048]{1,0:T(8,128)(2,1)S(1)}, u32[]{:S(2)}, u32[]{:S(2)}) collective-permute-start(bf16[72,2048]{1,0:T(8,128)(2,1)S(1)} %get-tuple-element.57.x_own), channel_id=1, source_target_pairs={{0,1},{1,0},{2,3},{3,2},{4,5},{5,4},{6,7},{7,6},{8,9},{9,8},{10,11... | collective-permute-start | bytes 884744 | tf_op jit(solution)/shard_map/ppermute | solution.py:432
  22.7 5.9 %collective-permute-start.9 = (bf16[72,2048]{1,0:T(8,128)(2,1)S(1)}, bf16[72,2048]{1,0:T(8,128)(2,1)S(1)}, u32[]{:S(2)}, u32[]{:S(2)}) collective-permute-start(bf16[72,2048]{1,0:T(8,128)(2,1)S(1)} %get-tuple-element.65.g_own), channel_id=1, source_target_pairs={{0,1},{1,0},{2,3},{3,2},{4,5},{5,4},{6,7},{7,6},{8,9},{9,8},{10,11... | collective-permute-start | bytes 884744 | tf_op jit(solution)/shard_map/ppermute | solution.py:432
  28.5 9.6 %collective-permute-start.8 = (bf16[72,2048]{1,0:T(8,128)(2,1)S(1)}, bf16[72,2048]{1,0:T(8,128)(2,1)S(1)}, u32[]{:S(2)}, u32[]{:S(2)}) collective-permute-start(bf16[72,2048]{1,0:T(8,128)(2,1)S(1)} %get-tuple-element.64), channel_id=1, source_target_pairs={{0,1},{1,0},{2,3},{3,2},{4,5},{5,4},{6,7},{7,6},{8,9},{9,8},{10,11... | collective-permute-start | bytes 884744 | tf_op jit(solution)/shard_map/ppermute | solution.py:432
  34.3 3.8 %collective-permute-start.10 = (bf16[72,2048]{1,0:T(8,128)(2,1)S(1)}, bf16[72,2048]{1,0:T(8,128)(2,1)S(1)}, u32[]{:S(2)}, u32[]{:S(2)}) collective-permute-start(bf16[72,2048]{1,0:T(8,128)(2,1)S(1)} %get-tuple-element.70), channel_id=1, source_target_pairs={{0,1},{1,0},{2,3},{3,2},{4,5},{5,4},{6,7},{7,6},{8,9},{9,8},{10,11... | collective-permute-start | bytes 884744 | tf_op jit(solution)/shard_map/ppermute | solution.py:432
  38.8 7.7 %collective-permute-start.11 = (bf16[288,128]{1,0:T(8,128)(2,1)S(1)}, bf16[288,128]{1,0:T(8,128)(2,1)S(1)}, u32[]{:S(2)}, u32[]{:S(2)}) collective-permute-start(bf16[288,128]{1,0:T(8,128)(2,1)S(1)} %get-tuple-element.72), channel_id=1, source_target_pairs={{0,2},{2,0},{4,6},{6,4},{8,10},{10,8},{12,14},{14,12},{1,3},{3,1},... | collective-permute-start | bytes 221192 | tf_op jit(solution)/shard_map/ppermute | solution.py:428
  39.8 9.5 %collective-permute-start.12 = (bf16[288,128]{1,0:T(8,128)(2,1)S(1)}, bf16[288,128]{1,0:T(8,128)(2,1)S(1)}, u32[]{:S(2)}, u32[]{:S(2)}) collective-permute-start(bf16[288,128]{1,0:T(8,128)(2,1)S(1)} %get-tuple-element.73), channel_id=1, source_target_pairs={{0,4},{2,6},{4,0},{6,2},{8,12},{10,14},{12,8},{14,10},{1,5},{3,7},... | collective-permute-start | bytes 221192 | tf_op jit(solution)/shard_map/ppermute | solution.py:428
  42.6 17.6 %collective-permute-start.13 = (bf16[288,128]{1,0:T(8,128)(2,1)S(1)}, bf16[288,128]{1,0:T(8,128)(2,1)S(1)}, u32[]{:S(2)}, u32[]{:S(2)}) collective-permute-start(bf16[288,128]{1,0:T(8,128)(2,1)S(1)} %get-tuple-element.74), channel_id=1, source_target_pairs={{0,6},{2,4},{4,2},{6,0},{8,14},{10,12},{12,10},{14,8},{1,7},{3,5},... | collective-permute-start | bytes 221192 | tf_op jit(solution)/shard_map/ppermute | solution.py:428
  43.2 17.0 %collective-permute-start.14 = (bf16[288,128]{1,0:T(8,128)(2,1)S(1)}, bf16[288,128]{1,0:T(8,128)(2,1)S(1)}, u32[]{:S(2)}, u32[]{:S(2)}) collective-permute-start(bf16[288,128]{1,0:T(8,128)(2,1)S(1)} %get-tuple-element.75), channel_id=1, source_target_pairs={{0,8},{2,10},{4,12},{6,14},{8,0},{10,2},{12,4},{14,6},{1,9},{3,11}... | collective-permute-start | bytes 221192 | tf_op jit(solution)/shard_map/ppermute | solution.py:428
  46.4 13.9 %collective-permute-start.15 = (bf16[288,128]{1,0:T(8,128)(2,1)S(1)}, bf16[288,128]{1,0:T(8,128)(2,1)S(1)}, u32[]{:S(2)}, u32[]{:S(2)}) collective-permute-start(bf16[288,128]{1,0:T(8,128)(2,1)S(1)} %get-tuple-element.76), channel_id=1, source_target_pairs={{0,10},{2,8},{4,14},{6,12},{8,2},{10,0},{12,6},{14,4},{1,11},{3,9}... | collective-permute-start | bytes 221192 | tf_op jit(solution)/shard_map/ppermute | solution.py:428
  46.4 13.8 %collective-permute-start.16 = (bf16[288,128]{1,0:T(8,128)(2,1)S(1)}, bf16[288,128]{1,0:T(8,128)(2,1)S(1)}, u32[]{:S(2)}, u32[]{:S(2)}) collective-permute-start(bf16[288,128]{1,0:T(8,128)(2,1)S(1)} %get-tuple-element.77), channel_id=1, source_target_pairs={{0,12},{2,14},{4,8},{6,10},{8,4},{10,6},{12,0},{14,2},{1,13},{3,15... | collective-permute-start | bytes 221192 | tf_op jit(solution)/shard_map/ppermute | solution.py:428
  49.3 10.9 %collective-permute-start.17 = (bf16[288,128]{1,0:T(8,128)(2,1)S(1)}, bf16[288,128]{1,0:T(8,128)(2,1)S(1)}, u32[]{:S(2)}, u32[]{:S(2)}) collective-permute-start(bf16[288,128]{1,0:T(8,128)(2,1)S(1)} %get-tuple-element.78), channel_id=1, source_target_pairs={{0,14},{2,12},{4,10},{6,8},{8,6},{10,4},{12,2},{14,0},{1,15},{3,13... | collective-permute-start | bytes 221192 | tf_op jit(solution)/shard_map/ppermute | solution.py:428

commit v6 on v5

--- a/solution.py
+++ b/solution.py
@@ -140,38 +140,46 @@
     )(*args)
 
 
-def rows_to_blocks(scratch, outs, at, take, subs):
-    total = scratch.shape[0]
-    size = total // len(outs)
+def blocks_to_rows(scratch, blocks, put, subs):
+    size = blocks[0].shape[0]
+    for p, block in enumerate(blocks):
+        scratch[p * size : (p + 1) * size, :] = block[...].astype(jnp.float32)
     for sub in range(subs):
-        scratch[pl.ds(sub, total // subs, stride=subs), :] = take(sub)
-    for k, out in enumerate(outs):
-        out[at : at + size, :] = scratch[k * size : (k + 1) * size, :].astype(out.dtype)
-
-
-def blocks_to_rows(scratch, blocks, at, put, subs):
-    total = scratch.shape[0]
-    size = total // len(blocks)
-    for k, block in enumerate(blocks):
-        scratch[k * size : (k + 1) * size, :] = block[at : at + size, :].astype(jnp.float32)
-    for sub in range(subs):
-        put(sub, scratch[pl.ds(sub, total // subs, stride=subs), :])
+        put(sub, scratch[pl.ds(sub, len(blocks) * size // subs, stride=subs), :])
+
+
+def spread_lanes(scratch, sub, subs, value):
+    scratch[pl.ds(sub, value.shape[0], stride=subs), :] = value
+
+
+def part(ref, start, count):
+    return ref.at[start : start + count, :]
 
 
 def lanes_of(sub):
     return slice(sub * LANES, (sub + 1) * LANES)
 
 
+def even_masks(count):
+    return [*range(count // 2, count, 2), *range(2, count // 2, 2)]
+
+
 def route_kernel(devices, capacity, subs, ids_in, weight_in, x_in, g_in, *refs):
-    outs, (place_out, mix_out, scratch, ids, weight, x, g, sems) = refs[:devices], refs[devices:]
+    mine, theirs, near, here, place_out, mix_out, scratch, ids, weight, x, g, sems = refs
     pairs = ((ids_in, ids), (weight_in, weight), (x_in, x), (g_in, g))
     copies = [pltpu.make_async_copy(src, dst, sems.at[i]) for i, (src, dst) in enumerate(pairs)]
     for copy in copies:
         copy.start()
     top, tok = ids.shape
     rows = devices * capacity
+    core = lax.axis_index("ffn")
+    masks = even_masks(devices)
+    masks = [mask + core for mask in masks] + [mask + 1 - core for mask in masks] + [1, 0]
     order = lax.broadcasted_iota(jnp.int32, (devices, tok), 0)
-    expert = order ^ lax.axis_index("expert")
+    bits = jnp.zeros((devices, tok), jnp.int32)
+    for p, mask in enumerate(masks):
+        bits = jnp.where(order == p, mask, bits)
+    expert = bits ^ lax.axis_index("expert")
     member = jnp.zeros((devices, tok), jnp.float32)
     mixing = jnp.zeros((devices, tok), jnp.float32)
     copies[0].wait()
@@ -181,34 +189,83 @@
         member = jnp.where(hit, 1.0, member)
         mixing = jnp.where(hit, weight[route : route + 1, :], mixing)
     before = lax.broadcasted_iota(jnp.int32, (tok, tok), 0) < lax.broadcasted_iota(jnp.int32, (tok, tok), 1)
-    slots = jnp.dot(
-        member.astype(jnp.bfloat16),
-        jnp.where(before, 1.0, 0.0).astype(jnp.bfloat16),
-        preferred_element_type=jnp.float32,
-    )
+    slots = dot(member.astype(jnp.bfloat16), jnp.where(before, 1.0, 0.0).astype(jnp.bfloat16))
     target = jnp.where(member > 0, slots + capacity * order.astype(jnp.float32), -1.0)
     row = lax.broadcasted_iota(jnp.int32, (rows, tok), 0).astype(jnp.float32)
     place = jnp.zeros((rows, tok), jnp.float32)
     mix = jnp.zeros((rows, tok), jnp.float32)
-    for k in range(devices):
-        equal = target[k : k + 1, :] == row
+    for p in range(devices):
+        equal = target[p : p + 1, :] == row
         place = jnp.where(equal, 1.0, place)
-        mix = jnp.where(equal, mixing[k : k + 1, :], mix)
+        mix = jnp.where(equal, mixing[p : p + 1, :], mix)
     row_weight = jnp.broadcast_to(jnp.sum(mix, axis=1, keepdims=True), (rows, LANES))
     low = place.astype(jnp.bfloat16)
     place_out[...] = low
     mix_out[...] = row_weight
-
-    def x_part(sub):
-        return jnp.dot(low, x[:, lanes_of(sub)], preferred_element_type=jnp.float32)
-
-    def g_part(sub):
-        return jnp.dot(low, g[:, lanes_of(sub)], preferred_element_type=jnp.float32) * row_weight
+    size = capacity * subs
+    count = devices // 2 - 1
+
+    def write(at):
+        def block(p):
+            return scratch[p * size : (p + 1) * size, :].astype(mine.dtype)
+
+        for j in range(count):
+            part(mine, 2 * j * size + at, size)[...] = block(j)
+            part(theirs, 2 * j * size + at, size)[...] = block(count + j)
+        part(near, at, size)[...] = block(2 * count)
+        part(here, at, size)[...] = block(2 * count + 1)
 
     copies[2].wait()
-    rows_to_blocks(scratch, outs, 0, x_part, subs)
+    for sub in range(subs):
+        spread_lanes(scratch, sub, subs, dot(low, x[:, lanes_of(sub)]))
+    write(0)
     copies[3].wait()
-    rows_to_blocks(scratch, outs, capacity * subs, g_part, subs)
+    for sub in range(subs):
+        spread_lanes(scratch, sub, subs, dot(low, g[:, lanes_of(sub)]) * row_weight)
+    write(size)
+
+
+def pack_kernel(size, mine, swapped, *outs):
+    for j, out in enumerate(outs):
+        part(out, 0, 2 * size)[...] = part(mine, 2 * j * size, 2 * size)[...]
+        part(out, 2 * size, 2 * size)[...] = part(swapped, 2 * j * size, 2 * size)[...]
+
+
+def gather_kernel(size, *refs):
+    blocks, (near, here, _, x_out, g_out) = refs[:-5], refs[-5:]
+    for at, out in ((0, x_out), (size, g_out)):
+        for j, block in enumerate(blocks):
+            part(out, 2 * j * size, size)[...] = part(block, at, size)[...]
+            part(out, (2 * j + 1) * size, size)[...] = part(block, 2 * size + at, size)[...]
+        part(out, 2 * len(blocks) * size, size)[...] = part(near, at, size)[...]
+        part(out, (2 * len(blocks) + 1) * size, size)[...] = part(here, at, size)[...]
+
+
+def full_rows(devices, subs, scratch, own_sent, other_sent, out):
+    size = own_sent.shape[0] // devices
+    count = devices // 2 - 1
+    own, other = half_starts(out.shape[1] // 2)
+    first, second, last = range(0, 2 * count, 2), range(1, 2 * count, 2), range(2 * count, devices)
+    layouts = (
+        (own, [(own_sent, i) for i in first] + [(other_sent, i) for i in second] + [(own_sent, i) for i in last]),
+        (other, [(own_sent, i) for i in second] + [(other_sent, i) for i in first] + [(other_sent, i) for i in last]),
+    )
+    for start, layout in layouts:
+
+        def put(sub, value):
+            out[:, pl.ds(start + sub * LANES, LANES)] = value.astype(out.dtype)
+
+        blocks_to_rows(scratch, [part(ref, i * size, size) for ref, i in layout], put, subs)
+
+
+def split_terms(count, size, scratch, own_half, keep, send):
+    keep[0 : count * size, :] = scratch[0 : count * size, :]
+    send[0 : count * size, :] = scratch[count * size : 2 * count * size, :].astype(send.dtype)
+    rest = scratch[2 * count * size :, :]
+    if own_half:
+        keep[count * size :, :] = rest
+    else:
+        send[count * size :, :] = rest.astype(send.dtype)
 
 
 def hold_kernel(count, *refs):
@@ -221,34 +278,37 @@
         copy.wait()
 
 
-def arrive_kernel(devices, capacity, subs, *refs):
-    blocks, (_, x_own, g_own, scratch) = refs[:devices], refs[devices:]
-
-    def put_into(out):
-        def put(sub, value):
-            out[:, lanes_of(sub)] = value.astype(out.dtype)
-
-        return put
-
-    blocks_to_rows(scratch, blocks, 0, put_into(x_own), subs)
-    blocks_to_rows(scratch, blocks, capacity * subs, put_into(g_own), subs)
-
-
-def leave_kernel(capacity, subs, out_own, out_other, dx_own, dx_other, *refs):
-    outs, scratch = refs[:-1], refs[-1]
-
-    def sum_of(own, other):
-        def take(sub):
-            return own[:, lanes_of(sub)] + other[:, lanes_of(sub)].astype(jnp.float32)
-
-        return take
-
-    rows_to_blocks(scratch, outs, 0, sum_of(out_own, out_other), subs)
-    rows_to_blocks(scratch, outs, capacity * subs, sum_of(dx_own, dx_other), subs)
-
-
-def join_kernel(devices, capacity, subs, place, mix, *refs):
-    blocks, (out_tokens, grad_tokens, scratch) = refs[:devices], refs[devices:]
+def leave_kernel(size, *refs):
+    terms, outs = (refs[:4], refs[4:8]), refs[8:]
+    count = len(outs) - 2
+    for at, (keep_own, keep_other, came_own, came_other) in zip((0, size), terms):
+
+        def own(p):
+            total = part(keep_own, p * size, size)[...] + part(came_own, p * size, size)[...].astype(jnp.float32)
+            return total.astype(outs[0].dtype)
+
+        for j, out in enumerate(outs[:count]):
+            part(out, at, size)[...] = own(j)
+            total = part(keep_other, j * size, size)[...] + part(came_other, j * size, size)[...].astype(jnp.float32)
+            part(out, 2 * size + at, size)[...] = total.astype(out.dtype)
+        part(outs[count], at, size)[...] = own(count)
+        part(outs[count + 1], at, size)[...] = own(count + 1)
+
+
+def share_kernel(size, *refs):
+    blocks, (_, _, out) = refs[:-3], refs[-3:]
+    for j, block in enumerate(blocks):
+        part(out, 2 * j * size, 2 * size)[...] = part(block, 2 * size, 2 * size)[...]
+
+
+def join_kernel(count, subs, place, mix, *refs):
+    blocks, (near, here, shared, out_tokens, grad_tokens, scratch) = refs[:count], refs[count:]
+    size = near.shape[0] // 2
+
+    def layout(at):
+        first = [part(block, at, size) for block in blocks]
+        second = [part(shared, 2 * j * size + at, size) for j in range(count)]
+        return first + second + [part(near, at, size), part(here, at, size)]
 
     def put_out(sub, value):
         low = (value * mix[...]).astype(jnp.bfloat16)
@@ -257,8 +317,8 @@
     def put_grad(sub, value):
         grad_tokens[:, lanes_of(sub)] = contract_rows(place[...], value.astype(jnp.bfloat16)).astype(grad_tokens.dtype)
 
-    blocks_to_rows(scratch, blocks, 0, put_out, subs)
-    blocks_to_rows(scratch, blocks, capacity * subs, put_grad, subs)
+    blocks_to_rows(scratch, layout(0), put_out, subs)
+    blocks_to_rows(scratch, layout(size), put_grad, subs)
 
 
 def half_starts(half_width):
@@ -276,33 +336,41 @@
     return jnp.dot(left, right, preferred_element_type=jnp.float32)
 
 
-def project_own_kernel(step, x_own, w_gate, w_up, gate_part, up_part):
-    half_width = x_own.shape[1]
-    own, _ = half_starts(half_width)
-    rows = pl.ds(own, half_width)
+def halves_of_output(devices, subs, step, scratch, own_half, term, keep, send):
+    size = scratch.shape[0] // devices
+    for at in range(0, subs * LANES, step):
+        value = term(at)
+        for i in range(step // LANES):
+            spread_lanes(scratch, at // LANES + i, subs, value[:, lanes_of(i)])
+    split_terms(devices // 2 - 1, size, scratch, own_half, keep, send)
+
+
+def forward_kernel(
+    devices,
+    subs,
+    step,
+    x_sent,
+    x_swapped,
+    w_gate,
+    w_up,
+    w_down,
+    x_full,
+    gate,
+    up,
+    hidden,
+    keep_own,
+    keep_other,
+    send_own,
+    send_other,
+    scratch,
+):
+    own, other = half_starts(subs * LANES)
+    full_rows(devices, subs, scratch, x_sent, x_swapped, x_full)
 
     def project(i, carry):
         cols = chunk(i, step)
-        gate_part[:, cols] = dot(x_own[...], w_gate[0, rows, cols])
-        up_part[:, cols] = dot(x_own[...], w_up[0, rows, cols])
-        return carry
-
-    lax.fori_loop(0, gate_part.shape[1] // step, project, 0)
-
-
-def forward_kernel(
-    step, x_own, x_other, gate_part, up_part, w_gate, w_up, w_down, x_full, gate, up, hidden, out_own, out_other
-):
-    half_width = x_own.shape[1]
-    own, other = half_starts(half_width)
-    x_full[:, pl.ds(own, half_width)] = x_own[...]
-    x_full[:, pl.ds(other, half_width)] = x_other[...]
-    rows = pl.ds(other, half_width)
-
-    def project(i, carry):
-        cols = chunk(i, step)
-        gate_low = (gate_part[:, cols] + dot(x_other[...], w_gate[0, rows, cols])).astype(jnp.bfloat16)
-        up_low = (up_part[:, cols] + dot(x_other[...], w_up[0, rows, cols])).astype(jnp.bfloat16)
+        gate_low = dot(x_full[...], w_gate[0, :, cols]).astype(jnp.bfloat16)
+        up_low = dot(x_full[...], w_up[0, :, cols]).astype(jnp.bfloat16)
         gate[:, cols] = gate_low
         up[:, cols] = up_low
         value = gate_low.astype(jnp.float32)
@@ -311,33 +379,46 @@
 
     lax.fori_loop(0, gate.shape[1] // step, project, 0)
 
-    def spread(i, carry):
-        here = chunk(i, step)
-        out_other[:, here] = dot(hidden[...], w_down[0, :, chunk(i, step, other)]).astype(jnp.bfloat16)
-        out_own[:, here] = dot(hidden[...], w_down[0, :, chunk(i, step, own)])
-        return carry
-
-    lax.fori_loop(0, half_width // step, spread, 0)
-
-
-def flip(value):
-    return value.astype(jnp.float32).T
-
-
-def input_term(pre_gate, pre_up, w_gate, w_up, there):
-    return flip(contract_cols(w_gate[0, there, :], pre_gate[...]) + contract_cols(w_up[0, there, :], pre_up[...]))
-
-
-def backward_kernel(step, g_own, g_other, gate, up, w_gate, w_up, w_down, g_full, pre_gate, pre_up, dx_other):
-    half_width = g_own.shape[1]
-    own, other = half_starts(half_width)
-    g_full[:, pl.ds(own, half_width)] = g_own[...]
-    g_full[:, pl.ds(other, half_width)] = g_other[...]
+    def term(start):
+        return lambda at: dot(hidden[...], w_down[0, :, pl.ds(start + at, step)])
+
+    halves_of_output(devices, subs, step, scratch, False, term(other), keep_other, send_other)
+    halves_of_output(devices, subs, step, scratch, True, term(own), keep_own, send_own)
+
+
+def input_term(step, pre_gate, pre_up, w_gate, w_up, start):
+    def term(at):
+        there = pl.ds(start + at, step)
+        return contract_cols(pre_gate[...], w_gate[0, there, :]) + contract_cols(pre_up[...], w_up[0, there, :])
+
+    return term
+
+
+def backward_kernel(
+    devices,
+    subs,
+    step,
+    g_sent,
+    g_swapped,
+    gate,
+    up,
+    w_gate,
+    w_up,
+    w_down,
+    g_full,
+    pre_gate,
+    pre_up,
+    keep_other,
+    send_other,
+    scratch,
+):
+    _, other = half_starts(subs * LANES)
+    full_rows(devices, subs, scratch, g_sent, g_swapped, g_full)
 
     def pull(i, carry):
         cols = chunk(i, step)
-        part = flip(contract_cols(w_down[0, cols, :], g_full[...])).astype(jnp.bfloat16)
-        grad_hidden = part.astype(jnp.float32)
+        low = contract_cols(g_full[...], w_down[0, cols, :]).astype(jnp.bfloat16)
+        grad_hidden = low.astype(jnp.float32)
         value = gate[:, cols].astype(jnp.float32)
         sig = jax.nn.sigmoid(value)
         pre_gate[:, cols] = (
@@ -347,25 +428,18 @@
         return carry
 
     lax.fori_loop(0, gate.shape[1] // step, pull, 0)
-
-    def spread(i, carry):
-        dx_other[:, chunk(i, step)] = input_term(pre_gate, pre_up, w_gate, w_up, chunk(i, step, other)).astype(
-            jnp.bfloat16
-        )
-        return carry
-
-    lax.fori_loop(0, half_width // step, spread, 0)
-
-
-def backward_own_kernel(step, pre_gate, pre_up, w_gate, w_up, dx_own):
-    half_width = dx_own.shape[1]
-    own, _ = half_starts(half_width)
-
-    def spread(i, carry):
-        dx_own[:, chunk(i, step)] = input_term(pre_gate, pre_up, w_gate, w_up, chunk(i, step, own))
-        return carry
-
-    lax.fori_loop(0, half_width // step, spread, 0)
+    term = input_term(step, pre_gate, pre_up, w_gate, w_up, other)
+    halves_of_output(devices, subs, step, scratch, False, term, keep_other, send_other)
+
+
+def backward_own_kernel(devices, subs, step, pre_gate, pre_up, w_gate, w_up, keep_own, send_own, scratch):
+    own, _ = half_starts(subs * LANES)
+    term = input_term(step, pre_gate, pre_up, w_gate, w_up, own)
+    halves_of_output(devices, subs, step, scratch, True, term, keep_own, send_own)
+
+
+def flip(value):
+    return value.astype(jnp.float32).T
 
 
 def pieces_of(total, size):
@@ -373,8 +447,24 @@
 
 
 def gradient_kernel(
-    step, x, g, hidden, pre_gate, pre_up, grad_gate, grad_up, grad_down, flipped, turned, tall, wide, tall_sems, wide_sems
+    step,
+    x,
+    g,
+    hidden,
+    pre_gate,
+    pre_up,
+    grad_gate,
+    grad_up,
+    grad_down,
+    written,
+    flipped,
+    turned,
+    tall,
+    wide,
+    tall_sems,
+    wide_sems,
 ):
+    written[...] = jnp.zeros_like(written)
     width, lanes = x.shape[1], hidden.shape[1]
     count = width // step
     flipped[...] = flip(hidden[...]).astype(flipped.dtype)
@@ -423,9 +513,12 @@
         tall_copy(1, grad_up, i, i % 2).wait()
 
 
-def exchange(blocks):
-    pairs = [[(i, i ^ k) for i in range(len(blocks))] for k in range(len(blocks))]
-    return [blocks[0]] + [lax.ppermute(blocks[k], "expert", pairs[k]) for k in range(1, len(blocks))]
+def exchange(blocks, near, devices):
+    arrived = []
+    for block, mask in zip(blocks, even_masks(devices)):
+        pairs = [(2 * i + core, 2 * (i ^ (mask + core)) + core) for i in range(devices) for core in range(2)]
+        arrived.append(lax.ppermute(block, ("expert", "ffn"), pairs))
+    return arrived, lax.ppermute(near, "expert", [(i, i ^ 1) for i in range(devices)])
 
 
 def swap(value):
@@ -445,16 +538,23 @@
     rows = devices * capacity
     subs = sub_width // LANES
     low, full = jnp.bfloat16, jnp.float32
-    blocks = [jax.ShapeDtypeStruct((2 * capacity * subs, LANES), low)] * devices
-    spread_scratch = [pltpu.VMEM((rows * subs, LANES), full)]
-    sizes = (devices, capacity, subs)
+    size = capacity * subs
+    count = devices // 2 - 1
+    spread_scratch = [pltpu.VMEM((devices * size, LANES), full)]
     step = 256
     half_flops = 2 * rows * width * lanes // 2
 
+    def lines(number, dtype=low):
+        return jax.ShapeDtypeStruct((number * size, LANES), dtype)
+
+    def lines_in_vmem(number, dtype=low):
+        return vmem((number * size, LANES), dtype)
+
     sources = (route_ids.T, route_weight.T, tokens, grad_out)
-    routed = call(
-        functools.partial(route_kernel, *sizes),
-        blocks + [jax.ShapeDtypeStruct((rows, tok_dev), low), jax.ShapeDtypeStruct((rows, LANES), full)],
+    mine, theirs, near, here, place, mix = call(
+        functools.partial(route_kernel, devices, capacity, subs),
+        [lines(2 * count), lines(2 * count), lines(2), lines(2)]
+        + [jax.ShapeDtypeStruct((rows, tok_dev), low), jax.ShapeDtypeStruct((rows, LANES), full)],
         in_hbm(sources),
         in_spaces=[pl.ANY] * 4,
         scratch=spread_scratch
@@ -462,8 +562,8 @@
         + [pltpu.SemaphoreType.DMA((4,))],
         traffic=4 * tok_dev * sub_width,
     )
-    place, mix = routed[devices:]
-    arrived = exchange(routed[:devices])
+    packed = call(functools.partial(pack_kernel, size), [lines(4)] * count, (mine, swap(theirs)))
+    arrived, near = exchange(packed, near, devices)
 
     weights = (gate_weight, up_weight, down_weight)
     w_gate, w_up, w_down, held = call(
@@ -474,58 +574,53 @@
         scratch=[pltpu.SemaphoreType.DMA((3,))],
         traffic=sum(w.size * 2 for w in weights),
     )
-    x_own, g_own = call(
-        functools.partial(arrive_kernel, *sizes),
-        [vmem((rows, sub_width), low)] * 2,
-        (*arrived, held),
+    x_sent, g_sent = call(
+        functools.partial(gather_kernel, size), [lines(devices)] * 2, (*arrived, near, here, held)
+    )
+    x_swapped = swap(x_sent)
+    g_swapped = swap(g_sent)
+    terms = [
+        lines_in_vmem(count + 2, full),
+        lines_in_vmem(count, full),
+        lines_in_vmem(count),
+        lines_in_vmem(count + 2),
+    ]
+    x_full, gate, up, hidden, out_own, out_other, send_own, send_other = call(
+        functools.partial(forward_kernel, devices, subs, step),
+        [vmem((rows, width), low)] + [vmem((rows, lanes), low)] * 3 + terms,
+        (x_sent, x_swapped, w_gate, w_up, w_down),
         scratch=spread_scratch,
-        traffic=8 * rows * sub_width,
-    )
-    x_other = swap(x_own)
-    g_other = swap(g_own)
-    gate_part, up_part = call(
-        functools.partial(project_own_kernel, step),
-        [vmem((rows, lanes), full)] * 2,
-        (x_own, w_gate, w_up),
+        flops=6 * half_flops,
+    )
+    out_terms = (out_own, out_other, swap(send_other), swap(send_own))
+    g_full, pre_gate, pre_up, dx_other, send_other = call(
+        functools.partial(backward_kernel, devices, subs, step),
+        [vmem((rows, width), low)] + [vmem((rows, lanes), low)] * 2 + [terms[1], terms[3]],
+        (g_sent, g_swapped, gate, up, w_gate, w_up, w_down),
+        scratch=spread_scratch,
+        flops=4 * half_flops,
+    )
+    came_own = swap(send_other)
+    dx_own, send_own = call(
+        functools.partial(backward_own_kernel, devices, subs, step),
+        [terms[0], terms[2]],
+        (pre_gate, pre_up, w_gate, w_up),
+        scratch=spread_scratch,
         flops=2 * half_flops,
     )
-    x_full, gate, up, hidden, out_own, out_other = call(
-        functools.partial(forward_kernel, step),
-        [vmem((rows, width), low)]
-        + [vmem((rows, lanes), low)] * 3
-        + [vmem((rows, sub_width), full), vmem((rows, sub_width), low)],
-        (x_own, x_other, gate_part, up_part, w_gate, w_up, w_down),
-        flops=4 * half_flops,
-    )
-    out_arrived = swap(out_other)
-    g_full, pre_gate, pre_up, dx_other = call(
-        functools.partial(backward_kernel, step),
-        [vmem((rows, width), low)] + [vmem((rows, lanes), low)] * 2 + [vmem((rows, sub_width), low)],
-        (g_own, g_other, gate, up, w_gate, w_up, w_down),
-        flops=4 * half_flops,
-    )
-    dx_arrived = swap(dx_other)
-    (dx_own,) = call(
-        functools.partial(backward_own_kernel, step),
-        [vmem((rows, sub_width), full)],
-        (pre_gate, pre_up, w_gate, w_up),
-        flops=2 * half_flops,
-    )
-    returned = exchange(
-        call(
-            functools.partial(leave_kernel, capacity, subs),
-            blocks,
-            (out_own, out_arrived, dx_own, dx_arrived),
-            scratch=spread_scratch,
-            traffic=16 * rows * sub_width,
-        )
-    )
+    dx_terms = (dx_own, dx_other, came_own, swap(send_own))
+    *leaving, near, here = call(
+        functools.partial(leave_kernel, size),
+        [lines(4)] * count + [lines(2)] * 2,
+        (*out_terms, *dx_terms),
+    )
+    returned, near = exchange(leaving, near, devices)
     cut = 1024 if width % 1024 == 0 else width
-    grad_gate, grad_up, grad_down = call(
+    grad_gate, grad_up, grad_down, written = call(
         functools.partial(gradient_kernel, cut),
-        [jax.ShapeDtypeStruct(w.shape, low) for w in weights],
+        [jax.ShapeDtypeStruct(w.shape, low) for w in weights] + [vmem((8, LANES), full)],
         (x_full, g_full, hidden, pre_gate, pre_up),
-        out_spaces=[pl.ANY] * 3,
+        out_spaces=[pl.ANY] * 3 + [pltpu.VMEM],
         scratch=[
             pltpu.VMEM((lanes, rows), low),
             pltpu.VMEM((cut, rows), low),
@@ -538,10 +633,11 @@
         traffic=sum(w.size * 2 for w in weights),
         limit=32,
     )
+    (sharing,) = call(functools.partial(share_kernel, size), [lines(2 * count)], (*returned, near, written))
     out_tokens, grad_tokens = call(
-        functools.partial(join_kernel, *sizes),
+        functools.partial(join_kernel, count, subs),
         [jax.ShapeDtypeStruct((tok_dev, sub_width), low)] * 2,
-        (place, mix, *returned),
+        (place, mix, *returned, near, here, swap(sharing)),
         scratch=spread_scratch,
         traffic=8 * tok_dev * sub_width,
     )
@@ -552,7 +648,7 @@
     tokens, gate_weight = args[0], args[4]
     halves = lax.axis_size("ffn")
     devices = lax.axis_size("expert")
-    if halves == 2 and devices & (devices - 1) == 0 and tokens.shape[1] * halves == gate_weight.shape[1]:
+    if halves == 2 and devices >= 4 and devices & (devices - 1) == 0 and tokens.shape[1] * halves == gate_weight.shape[1]:
         return one_piece_shards(*args)
     return general_shards(*args)
 

time: 62.1 us -> 57.3 us (0.923)
  starting transfers between devices: 26.1 us -> 15.6 us
  waiting for transfers between devices: 0.69 us -> 10 us
  Pallas kernels: 34.3 us -> 30.8 us
    ppermute x14 -> x8, starting transfers between devices: 24.8 us -> 13.1 us  [the longest x6 10.5 us: exchange(): arrived.append(lax.ppermute(block, ('expert', 'ffn'), pairs))]
    ppermute x4 -> x8, waiting for transfers between devices: 0.01 us -> 4.89 us  [swap(): return lax.ppermute(value, 'ffn', [(0, 1), (1, 0)])]
    ppermute x14 -> x8, waiting for transfers between devices: 0.68 us -> 5.15 us  [the longest x6 5.15 us: exchange(): arrived.append(lax.ppermute(block, ('expert', 'ffn'), pairs))]
    pallas_call x10 -> x11, Pallas kernels: 34.3 us -> 30.8 us  [call(): pl.pallas_call(kernel, out_shape=tuple(out_shape), in_specs=[pl.BlockSpec...]
    ppermute x4 -> x8, starting transfers between devices: 1.21 us -> 2.48 us  [swap(): return lax.ppermute(value, 'ffn', [(0, 1), (1, 0)])]
  transfers between devices with their start and end apart: 18 -> 16, of which waited for: 1 -> 8; matrix products, arithmetic and copies ran while one was open for 0% -> 0% of each run, Pallas kernels for 48% -> 47%
where the time goes in v6:
time: 57.3 us; the launch traced here: 57.1 us
  Pallas kernels  30.8 us (54%)
  starting transfers between devices  15.6 us (27%)
  waiting for transfers between devices  10 us (17%)
  between operations  0.73 us (1%)
    pallas_call x11, Pallas kernels, call(): pl.pallas_call(kernel, out_shape=tuple(out_shape), in_specs=[pl.BlockSpec...  30.8 us
    ppermute x6, starting transfers between devices, exchange(): arrived.append(lax.ppermute(block, ('expert', 'ffn'), pairs))  10.5 us
    ppermute x6, waiting for transfers between devices, exchange(): arrived.append(lax.ppermute(block, ('expert', 'ffn'), pairs))  5.15 us
    ppermute x8, waiting for transfers between devices, swap(): return lax.ppermute(value, 'ffn', [(0, 1), (1, 0)])  4.89 us
    ppermute x2, starting transfers between devices, exchange(): lax.ppermute(near, 'expert', [(i, i ^ 1) for i in range(devices)])  2.63 us
    ppermute x8, starting transfers between devices, swap(): return lax.ppermute(value, 'ffn', [(0, 1), (1, 0)])  2.48 us
  transfers between devices with their start and end apart: 16, of which 8 were waited for; matrix products, arithmetic and copies ran while one was open for 0% of the time, Pallas kernels for 47%

profile of v6, /device:TPU:0, one launch (start us, length us, event | category | flops | bytes accessed | tf_op | source)
XLA Modules:
  0.0 57.1 jit_solution(6954937987678761535)
XLA Ops:
  0.6 1.9 %shard_map.110 = (bf16[864,128]{1,0:T(8,128)(2,1)S(1)}, bf16[864,128]{1,0:T(8,128)(2,1)S(1)}, bf16[288,128]{1,0:T(8,128)(2,1)S(1)}, bf16[288,128]{1,0:T(8,128)(2...) custom-call(s32[8,128]{1,0:T(8,128)} %bitcast.2, f32[8,128]{1,0:T(8,128)} %bitcast.3, ...), custom_call_target="tpu_custom_call" | custom-call | bytes 1048576 | tf_op jit(solution)/shard_map/pallas_call | solution.py:132
  2.6 0.5 collective-permute-start
  3.1 1.1 %collective-permute-done.swapped = bf16[864,128]{1,0:T(8,128)(2,1)S(1)} collective-permute-done((bf16[864,128]{1,0:T(8,128)(2,1)S(1)}, bf16[864,128]{1,0:T(8,128)(2,1)S(1)}, u32[]{:S(2)}, u32[]{:S(2)}) %collective-permute-start) | collective-permute-done | bytes 221216 | tf_op jit(solution)/shard_map/ppermute | solution.py:525
  4.2 4.0 %collective-permute-start.1 = (bf16[576,128]{1,0:T(8,128)(2,1)S(1)}, bf16[576,128]{1,0:T(8,128)(2,1)S(1)}, u32[]{:S(2)}, u32[]{:S(2)}) collective-permute-start(bf16[576,128]{1,0:T(8,128)(2,1)S(1)} %get-tuple-element.50), channel_id=1, source_target_pairs={{0,8},{1,11},{2,10},{3,9},{4,12},{5,15},{6,14},{7,13},{8,0},{9,3},... | collective-permute-start | bytes 442376 | tf_op jit(solution)/shard_map/ppermute | solution.py:520
  8.3 1.3 %collective-permute-start.2 = (bf16[576,128]{1,0:T(8,128)(2,1)S(1)}, bf16[576,128]{1,0:T(8,128)(2,1)S(1)}, u32[]{:S(2)}, u32[]{:S(2)}) collective-permute-start(bf16[576,128]{1,0:T(8,128)(2,1)S(1)} %get-tuple-element.51), channel_id=1, source_target_pairs={{0,12},{1,15},{2,14},{3,13},{4,8},{5,11},{6,10},{7,9},{8,4},{9,7},... | collective-permute-start | bytes 442376 | tf_op jit(solution)/shard_map/ppermute | solution.py:520
  9.6 0.2 collective-permute-start.3
  9.8 1.5 %collective-permute-start.4 = (bf16[288,128]{1,0:T(8,128)(2,1)S(1)}, bf16[288,128]{1,0:T(8,128)(2,1)S(1)}, u32[]{:S(2)}, u32[]{:S(2)}) collective-permute-start(bf16[288,128]{1,0:T(8,128)(2,1)S(1)} %get-tuple-element.53), channel_id=1, source_target_pairs={{0,2},{2,0},{4,6},{6,4},{8,10},{10,8},{12,14},{14,12},{1,3},{3,1},... | collective-permute-start | bytes 221192 | tf_op jit(solution)/shard_map/ppermute | solution.py:521
  11.3 6.4 %shard_map.112 = (bf16[1,4096,768]{2,1,0:T(8,128)(2,1)S(1)}, bf16[1,4096,768]{2,1,0:T(8,128)(2,1)S(1)}, bf16[1,768,4096]{2,1,0:T(8,128)(2,1)S(1)}, f32[8,128]{1,0:T(8,128)S(1)}) custom-call(bf16[1,4096,768]{2,1,0:T(8,128)(2,1)} %refs_0_.1, bf16[1,4096,768]{2,1,0:T(8,128)(2,1)} %refs_1_.1, bf16[1,768,4096]{2,1,0:T(8,128)(2,1)} %refs_2_.1), custom_call_target="tpu_custom_call" | custom-call | bytes 18874368 | tf_op jit(solution)/shard_map/pallas_call | solution.py:132
  17.8 1.3 %collective-permute-done.1.refs_0_ = bf16[576,128]{1,0:T(8,128)(2,1)S(1)} collective-permute-done((bf16[576,128]{1,0:T(8,128)(2,1)S(1)}, bf16[576,128]{1,0:T(8,128)(2,1)S(1)}, u32[]{:S(2)}, u32[]{:S(2)}) %collective-permute-start.1) | collective-permute-done | bytes 147488 | tf_op jit(solution)/shard_map/ppermute | solution.py:520
  19.0 1.8 %collective-permute-done.3.refs_2_ = bf16[576,128]{1,0:T(8,128)(2,1)S(1)} collective-permute-done((bf16[576,128]{1,0:T(8,128)(2,1)S(1)}, bf16[576,128]{1,0:T(8,128)(2,1)S(1)}, u32[]{:S(2)}, u32[]{:S(2)}) %collective-permute-start.3) | collective-permute-done | bytes 147488 | tf_op jit(solution)/shard_map/ppermute | solution.py:520
  20.9 0.6 %collective-permute-start.5 = (bf16[1152,128]{1,0:T(8,128)(2,1)S(1)}, bf16[1152,128]{1,0:T(8,128)(2,1)S(1)}, u32[]{:S(2)}, u32[]{:S(2)}) collective-permute-start(bf16[1152,128]{1,0:T(8,128)(2,1)S(1)} %get-tuple-element.56.x_sent), channel_id=1, source_target_pairs={{0,1},{1,0},{2,3},{3,2},{4,5},{5,4},{6,7},{7,6},{8,9},{9,8},{10,11... | collective-permute-start | bytes 884744 | tf_op jit(solution)/shard_map/ppermute | solution.py:525
  21.5 0.1 collective-permute-start.8
  21.6 1.1 %collective-permute-done.5.x_swapped = bf16[1152,128]{1,0:T(8,128)(2,1)S(1)} collective-permute-done((bf16[1152,128]{1,0:T(8,128)(2,1)S(1)}, bf16[1152,128]{1,0:T(8,128)(2,1)S(1)}, u32[]{:S(2)}, u32[]{:S(2)}) %collective-permute-start.5) | collective-permute-done | bytes 294944 | tf_op jit(solution)/shard_map/ppermute | solution.py:525
  22.7 4.5 %shard_map.114 = (bf16[72,4096]{1,0:T(8,128)(2,1)S(1)}, bf16[72,768]{1,0:T(8,128)(2,1)S(1)}, bf16[72,768]{1,0:T(8,128)(2,1)S(1)}, bf16[72,768]{1,0:T(8,128)(2,1)...) custom-call(bf16[1152,128]{1,0:T(8,128)(2,1)S(1)} %get-tuple-element, ...), custom_call_target="tpu_custom_call" | custom-call | flops 1358954496 | tf_op jit(solution)/shard_map/pallas_call | solution.py:132
  27.2 0.4 collective-permute-start.6
  27.7 4.9 %shard_map.115 = (bf16[72,4096]{1,0:T(8,128)(2,1)S(1)}, bf16[72,768]{1,0:T(8,128)(2,1)S(1)}, bf16[72,768]{1,0:T(8,128)(2,1)S(1)}, f32[432,128]{1,0:T(8,128)S(1)}, bf16[720,128]{1,0:T(8,128)(2,1)S(1)}) custom-call(bf16[1152,128]{1,0:T(8,128)(2,1)S(1)} %get-tuple-element.64.g_sent, bf16[1152,128]{1,0:T(8,128)(2,1)S(1)} %collective-permute-done.8.g_swapped, ...), custom_call_target="tpu_custom_call" | custom-call | flops 905969664 | tf_op jit(solution)/shard_map/pallas_call | solution.py:132
  32.6 0.2 collective-permute-start.9
  32.8 0.4 collective-permute-start.7
  33.1 2.1 %shard_map.116 = (f32[720,128]{1,0:T(8,128)S(1)}, bf16[432,128]{1,0:T(8,128)(2,1)S(1)}) custom-call(bf16[72,768]{1,0:T(8,128)(2,1)S(1)} %get-tuple-element.67.pre_gate, bf16[72,768]{1,0:T(8,128)(2,1)S(1)} %get-tuple-element.68.pre_up, bf16[1,4096,768]{2,1,0:T(8,128)(2,1)S(1)} %get-tuple-element.57.w_gate, bf16[1,4096,768]{2,1,0:T(8,128)(2,1)S(1)} %get-tuple-element.58.w_up), custom_call_target="tpu_custom_call" | custom-call | flops 452984832 | tf_op jit(solution)/shard_map/pallas_call | solution.py:132
  35.2 0.2 collective-permute-start.10
  35.4 1.2 %collective-permute-done.10.refs_7_ = bf16[432,128]{1,0:T(8,128)(2,1)S(1)} collective-permute-done((bf16[432,128]{1,0:T(8,128)(2,1)S(1)}, bf16[432,128]{1,0:T(8,128)(2,1)S(1)}, u32[]{:S(2)}, u32[]{:S(2)}) %collective-permute-start.10) | collective-permute-done | bytes 110624 | tf_op jit(solution)/shard_map/ppermute | solution.py:525
  36.6 0.1 shard_map.117
  36.8 4.2 %collective-permute-start.11 = (bf16[576,128]{1,0:T(8,128)(2,1)S(1)}, bf16[576,128]{1,0:T(8,128)(2,1)S(1)}, u32[]{:S(2)}, u32[]{:S(2)}) collective-permute-start(bf16[576,128]{1,0:T(8,128)(2,1)S(1)} %get-tuple-element.73), channel_id=1, source_target_pairs={{0,8},{1,11},{2,10},{3,9},{4,12},{5,15},{6,14},{7,13},{8,0},{9,3},... | collective-permute-start | bytes 442376 | tf_op jit(solution)/shard_map/ppermute | solution.py:520
  41.0 0.4 collective-permute-start.12
  41.4 0.2 collective-permute-start.13
  41.6 1.1 %collective-permute-start.14 = (bf16[288,128]{1,0:T(8,128)(2,1)S(1)}, bf16[288,128]{1,0:T(8,128)(2,1)S(1)}, u32[]{:S(2)}, u32[]{:S(2)}) collective-permute-start(bf16[288,128]{1,0:T(8,128)(2,1)S(1)} %get-tuple-element.76), channel_id=1, source_target_pairs={{0,2},{2,0},{4,6},{6,4},{8,10},{10,8},{12,14},{14,12},{1,3},{3,1},... | collective-permute-start | bytes 221192 | tf_op jit(solution)/shard_map/ppermute | solution.py:521
  42.8 9.1 %shard_map.118 = (bf16[1,4096,768]{2,1,0:T(8,128)(2,1)}, bf16[1,4096,768]{2,1,0:T(8,128)(2,1)}, bf16[1,768,4096]{2,1,0:T(8,128)(2,1)}, f32[8,128]{1,0:T(8,128)S(1)}) custom-call(bf16[72,4096]{1,0:T(8,128)(2,1)S(1)} %get-tuple-element.78.x, bf16[72,4096]{1,0:T(8,128)(2,1)S(1)} %get-tuple-element.79.g, bf16[72,768]{1,0:T(8,128)(2,1)S(1)} %get-tuple-element.80.hidden, ...), custom_call_target="tpu_custom_call" | custom-call | flops 1358954496 | bytes 18874368 | tf_op jit(solution)/shard_map/pallas_call | solution.py:132
  51.9 0.2 collective-permute-done.11.refs_0_
  52.0 1.9 %collective-permute-done.13.refs_2_ = bf16[576,128]{1,0:T(8,128)(2,1)S(1)} collective-permute-done((bf16[576,128]{1,0:T(8,128)(2,1)S(1)}, bf16[576,128]{1,0:T(8,128)(2,1)S(1)}, u32[]{:S(2)}, u32[]{:S(2)}) %collective-permute-start.13) | collective-permute-done | bytes 147488 | tf_op jit(solution)/shard_map/ppermute | solution.py:520
  54.0 0.1 collective-permute-start.15
  54.0 1.5 %collective-permute-done.15.refs_5_ = bf16[864,128]{1,0:T(8,128)(2,1)S(1)} collective-permute-done((bf16[864,128]{1,0:T(8,128)(2,1)S(1)}, bf16[864,128]{1,0:T(8,128)(2,1)S(1)}, u32[]{:S(2)}, u32[]{:S(2)}) %collective-permute-start.15) | collective-permute-done | bytes 221216 | tf_op jit(solution)/shard_map/ppermute | solution.py:525
  55.5 1.6 %shard_map.120 = (bf16[128,2048]{1,0:T(8,128)(2,1)}, bf16[128,2048]{1,0:T(8,128)(2,1)}) custom-call(bf16[72,128]{1,0:T(8,128)(2,1)S(1)} %get-tuple-element.46.place, f32[72,128]{1,0:T(8,128)S(1)} %get-tuple-element.47.mix, bf16[576,128]{1,0:T(8,128)(2,1)S(1)} %collective-permute-done.11.refs_0_, bf16[576,128]{1,0:T(8,128)(2,1)S(1)} %collective-permute-done.12.refs_1_, ...), custom_call_target="tpu_custom_call" | custom-call | bytes 2097152 | tf_op jit(solution)/shard_map/pallas_call | solution.py:132
  (11 shorter events, 0.1 us)
Async XLA Ops:
  2.6 1.6 %collective-permute-start = (bf16[864,128]{1,0:T(8,128)(2,1)S(1)}, bf16[864,128]{1,0:T(8,128)(2,1)S(1)}, u32[]{:S(2)}, u32[]{:S(2)}) collective-permute-start(bf16[864,128]{1,0:T(8,128)(2,1)S(1)} %get-tuple-element.49), channel_id=1, source_target_pairs={{0,1},{1,0},{2,3},{3,2},{4,5},{5,4},{6,7},{7,6},{8,9},{9,8},{10,11... | collective-permute-start | bytes 663560 | tf_op jit(solution)/shard_map/ppermute | solution.py:525
  4.2 14.8 %collective-permute-start.1 = (bf16[576,128]{1,0:T(8,128)(2,1)S(1)}, bf16[576,128]{1,0:T(8,128)(2,1)S(1)}, u32[]{:S(2)}, u32[]{:S(2)}) collective-permute-start(bf16[576,128]{1,0:T(8,128)(2,1)S(1)} %get-tuple-element.50), channel_id=1, source_target_pairs={{0,8},{1,11},{2,10},{3,9},{4,12},{5,15},{6,14},{7,13},{8,0},{9,3},... | collective-permute-start | bytes 442376 | tf_op jit(solution)/shard_map/ppermute | solution.py:520
  8.3 10.8 %collective-permute-start.2 = (bf16[576,128]{1,0:T(8,128)(2,1)S(1)}, bf16[576,128]{1,0:T(8,128)(2,1)S(1)}, u32[]{:S(2)}, u32[]{:S(2)}) collective-permute-start(bf16[576,128]{1,0:T(8,128)(2,1)S(1)} %get-tuple-element.51), channel_id=1, source_target_pairs={{0,12},{1,15},{2,14},{3,13},{4,8},{5,11},{6,10},{7,9},{8,4},{9,7},... | collective-permute-start | bytes 442376 | tf_op jit(solution)/shard_map/ppermute | solution.py:520
  9.6 11.2 %collective-permute-start.3 = (bf16[576,128]{1,0:T(8,128)(2,1)S(1)}, bf16[576,128]{1,0:T(8,128)(2,1)S(1)}, u32[]{:S(2)}, u32[]{:S(2)}) collective-permute-start(bf16[576,128]{1,0:T(8,128)(2,1)S(1)} %get-tuple-element.52), channel_id=1, source_target_pairs={{0,4},{1,7},{2,6},{3,5},{4,0},{5,3},{6,2},{7,1},{8,12},{9,15},{10,... | collective-permute-start | bytes 442376 | tf_op jit(solution)/shard_map/ppermute | solution.py:520
  9.8 7.9 %collective-permute-start.4 = (bf16[288,128]{1,0:T(8,128)(2,1)S(1)}, bf16[288,128]{1,0:T(8,128)(2,1)S(1)}, u32[]{:S(2)}, u32[]{:S(2)}) collective-permute-start(bf16[288,128]{1,0:T(8,128)(2,1)S(1)} %get-tuple-element.53), channel_id=1, source_target_pairs={{0,2},{2,0},{4,6},{6,4},{8,10},{10,8},{12,14},{14,12},{1,3},{3,1},... | collective-permute-start | bytes 221192 | tf_op jit(solution)/shard_map/ppermute | solution.py:521
  20.9 1.8 %collective-permute-start.5 = (bf16[1152,128]{1,0:T(8,128)(2,1)S(1)}, bf16[1152,128]{1,0:T(8,128)(2,1)S(1)}, u32[]{:S(2)}, u32[]{:S(2)}) collective-permute-start(bf16[1152,128]{1,0:T(8,128)(2,1)S(1)} %get-tuple-element.56.x_sent), channel_id=1, source_target_pairs={{0,1},{1,0},{2,3},{3,2},{4,5},{5,4},{6,7},{7,6},{8,9},{9,8},{10,11... | collective-permute-start | bytes 884744 | tf_op jit(solution)/shard_map/ppermute | solution.py:525
  21.5 6.2 %collective-permute-start.8 = (bf16[1152,128]{1,0:T(8,128)(2,1)S(1)}, bf16[1152,128]{1,0:T(8,128)(2,1)S(1)}, u32[]{:S(2)}, u32[]{:S(2)}) collective-permute-start(bf16[1152,128]{1,0:T(8,128)(2,1)S(1)} %get-tuple-element.64.g_sent), channel_id=1, source_target_pairs={{0,1},{1,0},{2,3},{3,2},{4,5},{5,4},{6,7},{7,6},{8,9},{9,8},{10,11... | collective-permute-start | bytes 884744 | tf_op jit(solution)/shard_map/ppermute | solution.py:525
  27.2 9.4 %collective-permute-start.6 = (bf16[720,128]{1,0:T(8,128)(2,1)S(1)}, bf16[720,128]{1,0:T(8,128)(2,1)S(1)}, u32[]{:S(2)}, u32[]{:S(2)}) collective-permute-start(bf16[720,128]{1,0:T(8,128)(2,1)S(1)} %get-tuple-element.62), channel_id=1, source_target_pairs={{0,1},{1,0},{2,3},{3,2},{4,5},{5,4},{6,7},{7,6},{8,9},{9,8},{10,11... | collective-permute-start | bytes 552968 | tf_op jit(solution)/shard_map/ppermute | solution.py:525
  32.6 4.1 %collective-permute-start.9 = (bf16[720,128]{1,0:T(8,128)(2,1)S(1)}, bf16[720,128]{1,0:T(8,128)(2,1)S(1)}, u32[]{:S(2)}, u32[]{:S(2)}) collective-permute-start(bf16[720,128]{1,0:T(8,128)(2,1)S(1)} %get-tuple-element.71), channel_id=1, source_target_pairs={{0,1},{1,0},{2,3},{3,2},{4,5},{5,4},{6,7},{7,6},{8,9},{9,8},{10,11... | collective-permute-start | bytes 552968 | tf_op jit(solution)/shard_map/ppermute | solution.py:525
  32.8 2.7 %collective-permute-start.7 = (bf16[432,128]{1,0:T(8,128)(2,1)S(1)}, bf16[432,128]{1,0:T(8,128)(2,1)S(1)}, u32[]{:S(2)}, u32[]{:S(2)}) collective-permute-start(bf16[432,128]{1,0:T(8,128)(2,1)S(1)} %get-tuple-element.63), channel_id=1, source_target_pairs={{0,1},{1,0},{2,3},{3,2},{4,5},{5,4},{6,7},{7,6},{8,9},{9,8},{10,11... | collective-permute-start | bytes 331784 | tf_op jit(solution)/shard_map/ppermute | solution.py:525
  35.2 1.4 %collective-permute-start.10 = (bf16[432,128]{1,0:T(8,128)(2,1)S(1)}, bf16[432,128]{1,0:T(8,128)(2,1)S(1)}, u32[]{:S(2)}, u32[]{:S(2)}) collective-permute-start(bf16[432,128]{1,0:T(8,128)(2,1)S(1)} %get-tuple-element.72), channel_id=1, source_target_pairs={{0,1},{1,0},{2,3},{3,2},{4,5},{5,4},{6,7},{7,6},{8,9},{9,8},{10,11... | collective-permute-start | bytes 331784 | tf_op jit(solution)/shard_map/ppermute | solution.py:525
  36.8 15.3 %collective-permute-start.11 = (bf16[576,128]{1,0:T(8,128)(2,1)S(1)}, bf16[576,128]{1,0:T(8,128)(2,1)S(1)}, u32[]{:S(2)}, u32[]{:S(2)}) collective-permute-start(bf16[576,128]{1,0:T(8,128)(2,1)S(1)} %get-tuple-element.73), channel_id=1, source_target_pairs={{0,8},{1,11},{2,10},{3,9},{4,12},{5,15},{6,14},{7,13},{8,0},{9,3},... | collective-permute-start | bytes 442376 | tf_op jit(solution)/shard_map/ppermute | solution.py:520
  41.0 11.1 %collective-permute-start.12 = (bf16[576,128]{1,0:T(8,128)(2,1)S(1)}, bf16[576,128]{1,0:T(8,128)(2,1)S(1)}, u32[]{:S(2)}, u32[]{:S(2)}) collective-permute-start(bf16[576,128]{1,0:T(8,128)(2,1)S(1)} %get-tuple-element.74), channel_id=1, source_target_pairs={{0,12},{1,15},{2,14},{3,13},{4,8},{5,11},{6,10},{7,9},{8,4},{9,7},... | collective-permute-start | bytes 442376 | tf_op jit(solution)/shard_map/ppermute | solution.py:520
  41.4 12.5 %collective-permute-start.13 = (bf16[576,128]{1,0:T(8,128)(2,1)S(1)}, bf16[576,128]{1,0:T(8,128)(2,1)S(1)}, u32[]{:S(2)}, u32[]{:S(2)}) collective-permute-start(bf16[576,128]{1,0:T(8,128)(2,1)S(1)} %get-tuple-element.75), channel_id=1, source_target_pairs={{0,4},{1,7},{2,6},{3,5},{4,0},{5,3},{6,2},{7,1},{8,12},{9,15},{10,... | collective-permute-start | bytes 442376 | tf_op jit(solution)/shard_map/ppermute | solution.py:520
  41.6 10.2 %collective-permute-start.14 = (bf16[288,128]{1,0:T(8,128)(2,1)S(1)}, bf16[288,128]{1,0:T(8,128)(2,1)S(1)}, u32[]{:S(2)}, u32[]{:S(2)}) collective-permute-start(bf16[288,128]{1,0:T(8,128)(2,1)S(1)} %get-tuple-element.76), channel_id=1, source_target_pairs={{0,2},{2,0},{4,6},{6,4},{8,10},{10,8},{12,14},{14,12},{1,3},{3,1},... | collective-permute-start | bytes 221192 | tf_op jit(solution)/shard_map/ppermute | solution.py:521
  54.0 1.5 %collective-permute-start.15 = (bf16[864,128]{1,0:T(8,128)(2,1)S(1)}, bf16[864,128]{1,0:T(8,128)(2,1)S(1)}, u32[]{:S(2)}, u32[]{:S(2)}) collective-permute-start(bf16[864,128]{1,0:T(8,128)(2,1)S(1)} %shard_map.119), channel_id=1, source_target_pairs={{0,1},{1,0},{2,3},{3,2},{4,5},{5,4},{6,7},{7,6},{8,9},{9,8},{10,11... | collective-permute-start | bytes 663560 | tf_op jit(solution)/shard_map/ppermute | solution.py:525

commit v7 on v6

--- a/solution.py
+++ b/solution.py
@@ -165,7 +165,7 @@
 
 
 def route_kernel(devices, capacity, subs, ids_in, weight_in, x_in, g_in, *refs):
-    mine, theirs, near, here, place_out, mix_out, scratch, ids, weight, x, g, sems = refs
+    (*outs, theirs, place_out, mix_out, scratch, ids, weight, x, g, sems) = refs
     pairs = ((ids_in, ids), (weight_in, weight), (x_in, x), (g_in, g))
     copies = [pltpu.make_async_copy(src, dst, sems.at[i]) for i, (src, dst) in enumerate(pairs)]
     for copy in copies:
@@ -205,40 +205,40 @@
     size = capacity * subs
     count = devices // 2 - 1
 
-    def write(at):
+    def write(mine, near, here, at):
         def block(p):
             return scratch[p * size : (p + 1) * size, :].astype(mine.dtype)
 
         for j in range(count):
-            part(mine, 2 * j * size + at, size)[...] = block(j)
-            part(theirs, 2 * j * size + at, size)[...] = block(count + j)
-        part(near, at, size)[...] = block(2 * count)
-        part(here, at, size)[...] = block(2 * count + 1)
+            part(mine, j * size, size)[...] = block(j)
+            part(theirs, (at + j) * size, size)[...] = block(count + j)
+        near[...] = block(2 * count)
+        here[...] = block(2 * count + 1)
 
     copies[2].wait()
     for sub in range(subs):
         spread_lanes(scratch, sub, subs, dot(low, x[:, lanes_of(sub)]))
-    write(0)
+    write(*outs[:3], 0)
     copies[3].wait()
     for sub in range(subs):
         spread_lanes(scratch, sub, subs, dot(low, g[:, lanes_of(sub)]) * row_weight)
-    write(size)
-
-
-def pack_kernel(size, mine, swapped, *outs):
-    for j, out in enumerate(outs):
-        part(out, 0, 2 * size)[...] = part(mine, 2 * j * size, 2 * size)[...]
-        part(out, 2 * size, 2 * size)[...] = part(swapped, 2 * j * size, 2 * size)[...]
+    write(*outs[3:], count)
+
+
+def pack_kernel(size, x_mine, g_mine, swapped, *outs):
+    count = len(outs) // 2
+    for i, out in enumerate(outs):
+        mine = x_mine if i < count else g_mine
+        part(out, 0, size)[...] = part(mine, i % count * size, size)[...]
+        part(out, size, size)[...] = part(swapped, i * size, size)[...]
 
 
 def gather_kernel(size, *refs):
-    blocks, (near, here, _, x_out, g_out) = refs[:-5], refs[-5:]
-    for at, out in ((0, x_out), (size, g_out)):
-        for j, block in enumerate(blocks):
-            part(out, 2 * j * size, size)[...] = part(block, at, size)[...]
-            part(out, (2 * j + 1) * size, size)[...] = part(block, 2 * size + at, size)[...]
-        part(out, 2 * len(blocks) * size, size)[...] = part(near, at, size)[...]
-        part(out, (2 * len(blocks) + 1) * size, size)[...] = part(here, at, size)[...]
+    blocks, (near, here, _, out) = refs[:-4], refs[-4:]
+    for j, block in enumerate(blocks):
+        part(out, 2 * j * size, 2 * size)[...] = block[...]
+    part(out, 2 * len(blocks) * size, size)[...] = near[...]
+    part(out, (2 * len(blocks) + 1) * size, size)[...] = here[...]
 
 
 def full_rows(devices, subs, scratch, own_sent, other_sent, out):
@@ -268,16 +268,6 @@
         send[count * size :, :] = rest.astype(send.dtype)
 
 
-def hold_kernel(count, *refs):
-    held, sems = refs[2 * count :]
-    held[...] = jnp.zeros_like(held)
-    copies = [pltpu.make_async_copy(refs[i], refs[count + i], sems.at[i]) for i in range(count)]
-    for copy in copies:
-        copy.start()
-    for copy in copies:
-        copy.wait()
-
-
 def leave_kernel(size, *refs):
     terms, outs = (refs[:4], refs[4:8]), refs[8:]
     count = len(outs) - 2
@@ -345,39 +335,19 @@
     split_terms(devices // 2 - 1, size, scratch, own_half, keep, send)
 
 
-def forward_kernel(
-    devices,
-    subs,
-    step,
-    x_sent,
-    x_swapped,
-    w_gate,
-    w_up,
-    w_down,
-    x_full,
-    gate,
-    up,
-    hidden,
-    keep_own,
-    keep_other,
-    send_own,
-    send_other,
-    scratch,
-):
-    own, other = half_starts(subs * LANES)
+def forward_kernel(devices, subs, step, x_sent, x_swapped, w_gate, w_up, x_full, gate, up, hidden, scratch):
     full_rows(devices, subs, scratch, x_sent, x_swapped, x_full)
-
-    def project(i, carry):
-        cols = chunk(i, step)
+    for cols in pieces_of(gate.shape[1], step):
         gate_low = dot(x_full[...], w_gate[0, :, cols]).astype(jnp.bfloat16)
         up_low = dot(x_full[...], w_up[0, :, cols]).astype(jnp.bfloat16)
         gate[:, cols] = gate_low
         up[:, cols] = up_low
         value = gate_low.astype(jnp.float32)
         hidden[:, cols] = (value * jax.nn.sigmoid(value) * up_low.astype(jnp.float32)).astype(jnp.bfloat16)
-        return carry
-
-    lax.fori_loop(0, gate.shape[1] // step, project, 0)
+
+
+def output_kernel(devices, subs, step, hidden, w_down, keep_own, keep_other, send_own, send_other, scratch):
+    own, other = half_starts(subs * LANES)
 
     def term(start):
         return lambda at: dot(hidden[...], w_down[0, :, pl.ds(start + at, step)])
@@ -551,10 +521,10 @@
         return vmem((number * size, LANES), dtype)
 
     sources = (route_ids.T, route_weight.T, tokens, grad_out)
-    mine, theirs, near, here, place, mix = call(
+    x_mine, x_near, x_here, g_mine, g_near, g_here, theirs, place, mix = call(
         functools.partial(route_kernel, devices, capacity, subs),
-        [lines(2 * count), lines(2 * count), lines(2), lines(2)]
-        + [jax.ShapeDtypeStruct((rows, tok_dev), low), jax.ShapeDtypeStruct((rows, LANES), full)],
+        [lines(count), lines(1), lines(1)] * 2
+        + [lines(2 * count), jax.ShapeDtypeStruct((rows, tok_dev), low), jax.ShapeDtypeStruct((rows, LANES), full)],
         in_hbm(sources),
         in_spaces=[pl.ANY] * 4,
         scratch=spread_scratch
@@ -562,35 +532,44 @@
         + [pltpu.SemaphoreType.DMA((4,))],
         traffic=4 * tok_dev * sub_width,
     )
-    packed = call(functools.partial(pack_kernel, size), [lines(4)] * count, (mine, swap(theirs)))
-    arrived, near = exchange(packed, near, devices)
+    packed = call(
+        functools.partial(pack_kernel, size),
+        [lines(2)] * (2 * count),
+        (x_mine, g_mine, swap(theirs)),
+        flops=24 * half_flops,
+    )
+    x_arrived, x_near = exchange(packed[:count], x_near, devices)
+    g_arrived, g_near = exchange(packed[count:], g_near, devices)
 
     weights = (gate_weight, up_weight, down_weight)
-    w_gate, w_up, w_down, held = call(
-        functools.partial(hold_kernel, 3),
-        [vmem(w.shape, w.dtype) for w in weights] + [vmem((8, LANES), full)],
-        in_hbm(weights),
-        in_spaces=[pl.ANY] * 3,
-        scratch=[pltpu.SemaphoreType.DMA((3,))],
-        traffic=sum(w.size * 2 for w in weights),
-    )
-    x_sent, g_sent = call(
-        functools.partial(gather_kernel, size), [lines(devices)] * 2, (*arrived, near, here, held)
-    )
+    w_gate, w_up, w_down = [pltpu.with_memory_space_constraint(w, pltpu.VMEM) for w in weights]
+
+    def gather(arrived, near, here, after):
+        return call(functools.partial(gather_kernel, size), [lines(devices)], (*arrived, near, here, after))[0]
+
+    x_sent = gather(x_arrived, x_near, x_here, mix)
     x_swapped = swap(x_sent)
-    g_swapped = swap(g_sent)
     terms = [
         lines_in_vmem(count + 2, full),
         lines_in_vmem(count, full),
         lines_in_vmem(count),
         lines_in_vmem(count + 2),
     ]
-    x_full, gate, up, hidden, out_own, out_other, send_own, send_other = call(
+    x_full, gate, up, hidden = call(
         functools.partial(forward_kernel, devices, subs, step),
-        [vmem((rows, width), low)] + [vmem((rows, lanes), low)] * 3 + terms,
-        (x_sent, x_swapped, w_gate, w_up, w_down),
+        [vmem((rows, width), low)] + [vmem((rows, lanes), low)] * 3,
+        (x_sent, x_swapped, w_gate, w_up),
         scratch=spread_scratch,
-        flops=6 * half_flops,
+        flops=4 * half_flops,
+    )
+    g_sent = gather(g_arrived, g_near, g_here, hidden)
+    g_swapped = swap(g_sent)
+    out_own, out_other, send_own, send_other = call(
+        functools.partial(output_kernel, devices, subs, step),
+        terms,
+        (hidden, w_down),
+        scratch=spread_scratch,
+        flops=2 * half_flops,
     )
     out_terms = (out_own, out_other, swap(send_other), swap(send_own))
     g_full, pre_gate, pre_up, dx_other, send_other = call(

time: 57.3 us -> 58.7 us (1.024)
  Pallas kernels: 30.8 us -> 24.2 us
  starting transfers between devices: 15.6 us -> 21 us
  waiting for transfers between devices: 10 us -> 12.5 us
    pallas_call x11 -> x12, Pallas kernels: 30.8 us -> 24.2 us  [call(): pl.pallas_call(kernel, out_shape=tuple(out_shape), in_specs=[pl.BlockSpec...]
    ppermute x6 -> x9, starting transfers between devices: 10.5 us -> 14.1 us  [exchange(): arrived.append(lax.ppermute(block, ('expert', 'ffn'), pairs))]
    ppermute x2 -> x3, waiting for transfers between devices: 0.01 us -> 3.04 us  [exchange(): lax.ppermute(near, 'expert', [(i, i ^ 1) for i in range(devices)])]
    ppermute x8, waiting for transfers between devices: 4.89 us -> 3.2 us  [swap(): return lax.ppermute(value, 'ffn', [(0, 1), (1, 0)])]
    ppermute x2 -> x3, starting transfers between devices: 2.63 us -> 3.8 us  [exchange(): lax.ppermute(near, 'expert', [(i, i ^ 1) for i in range(devices)])]
    ppermute x6 -> x9, waiting for transfers between devices: 5.15 us -> 6.26 us  [exchange(): arrived.append(lax.ppermute(block, ('expert', 'ffn'), pairs))]
    ppermute x8, starting transfers between devices: 2.48 us -> 3.07 us  [swap(): return lax.ppermute(value, 'ffn', [(0, 1), (1, 0)])]
  transfers between devices with their start and end apart: 16 -> 20, of which waited for: 8 -> 9; matrix products, arithmetic and copies ran while one was open for 0% -> 0% of each run, Pallas kernels for 47% -> 35%
where the time goes in v7:
time: 58.7 us; the launch traced here: 58.5 us
  Pallas kernels  24.2 us (41%)
  starting transfers between devices  21 us (36%)
  waiting for transfers between devices  12.5 us (21%)
  between operations  0.8 us (1%)
    pallas_call x12, Pallas kernels, call(): pl.pallas_call(kernel, out_shape=tuple(out_shape), in_specs=[pl.BlockSpec...  24.2 us
    ppermute x9, starting transfers between devices, exchange(): arrived.append(lax.ppermute(block, ('expert', 'ffn'), pairs))  14.1 us
    ppermute x9, waiting for transfers between devices, exchange(): arrived.append(lax.ppermute(block, ('expert', 'ffn'), pairs))  6.26 us
    ppermute x3, starting transfers between devices, exchange(): lax.ppermute(near, 'expert', [(i, i ^ 1) for i in range(devices)])  3.8 us
    ppermute x8, waiting for transfers between devices, swap(): return lax.ppermute(value, 'ffn', [(0, 1), (1, 0)])  3.2 us
    ppermute x8, starting transfers between devices, swap(): return lax.ppermute(value, 'ffn', [(0, 1), (1, 0)])  3.07 us
    ppermute x3, waiting for transfers between devices, exchange(): lax.ppermute(near, 'expert', [(i, i ^ 1) for i in range(devices)])  3.04 us
  transfers between devices with their start and end apart: 20, of which 9 were waited for; matrix products, arithmetic and copies ran while one was open for 0% of the time, Pallas kernels for 35%

profile of v7, /device:TPU:0, one launch (start us, length us, event | category | flops | bytes accessed | tf_op | source)
XLA Modules:
  0.0 58.5 jit_solution(6156047206549827192)
XLA Ops:
  0.7 2.1 %shard_map.110 = (bf16[432,128]{1,0:T(8,128)(2,1)S(1)}, bf16[144,128]{1,0:T(8,128)(2,1)S(1)}, bf16[144,128]{1,0:T(8,128)(2,1)S(1)}, bf16[432,128]{1,0:T(8,128)(2...) custom-call(s32[8,128]{1,0:T(8,128)} %bitcast.8, ...), custom_call_target="tpu_custom_call" | custom-call | bytes 1048576 | tf_op jit(solution)/shard_map/pallas_call | solution.py:132
  2.7 0.5 collective-permute-start
  3.3 1.1 %collective-permute-done.swapped = bf16[864,128]{1,0:T(8,128)(2,1)S(1)} collective-permute-done((bf16[864,128]{1,0:T(8,128)(2,1)S(1)}, bf16[864,128]{1,0:T(8,128)(2,1)S(1)}, u32[]{:S(2)}, u32[]{:S(2)}) %collective-permute-start) | collective-permute-done | bytes 221216 | tf_op jit(solution)/shard_map/ppermute | solution.py:495
  4.4 4.0 %collective-permute-start.1 = (bf16[288,128]{1,0:T(8,128)(2,1)S(1)}, bf16[288,128]{1,0:T(8,128)(2,1)S(1)}, u32[]{:S(2)}, u32[]{:S(2)}) collective-permute-start(bf16[288,128]{1,0:T(8,128)(2,1)S(1)} %get-tuple-element.51), channel_id=1, source_target_pairs={{0,8},{1,11},{2,10},{3,9},{4,12},{5,15},{6,14},{7,13},{8,0},{9,3},... | collective-permute-start | bytes 221192 | tf_op jit(solution)/shard_map/ppermute | solution.py:490
  8.4 1.3 %collective-permute-start.2 = (bf16[288,128]{1,0:T(8,128)(2,1)S(1)}, bf16[288,128]{1,0:T(8,128)(2,1)S(1)}, u32[]{:S(2)}, u32[]{:S(2)}) collective-permute-start(bf16[288,128]{1,0:T(8,128)(2,1)S(1)} %get-tuple-element.52), channel_id=1, source_target_pairs={{0,12},{1,15},{2,14},{3,13},{4,8},{5,11},{6,10},{7,9},{8,4},{9,7},... | collective-permute-start | bytes 221192 | tf_op jit(solution)/shard_map/ppermute | solution.py:490
  10.0 1.5 %collective-permute-start.4 = (bf16[144,128]{1,0:T(8,128)(2,1)S(1)}, bf16[144,128]{1,0:T(8,128)(2,1)S(1)}, u32[]{:S(2)}, u32[]{:S(2)}) collective-permute-start(bf16[144,128]{1,0:T(8,128)(2,1)S(1)} %get-tuple-element.54), channel_id=1, source_target_pairs={{0,2},{2,0},{4,6},{6,4},{8,10},{10,8},{12,14},{14,12},{1,3},{3,1},... | collective-permute-start | bytes 110600 | tf_op jit(solution)/shard_map/ppermute | solution.py:491
  11.5 3.0 %collective-permute-done.4.refs_3_ = bf16[144,128]{1,0:T(8,128)(2,1)S(1)} collective-permute-done((bf16[144,128]{1,0:T(8,128)(2,1)S(1)}, bf16[144,128]{1,0:T(8,128)(2,1)S(1)}, u32[]{:S(2)}, u32[]{:S(2)}) %collective-permute-start.4) | collective-permute-done | bytes 36896 | tf_op jit(solution)/shard_map/ppermute | solution.py:491
  14.5 0.9 %collective-permute-done.2.refs_1_ = bf16[288,128]{1,0:T(8,128)(2,1)S(1)} collective-permute-done((bf16[288,128]{1,0:T(8,128)(2,1)S(1)}, bf16[288,128]{1,0:T(8,128)(2,1)S(1)}, u32[]{:S(2)}, u32[]{:S(2)}) %collective-permute-start.2) | collective-permute-done | bytes 73760 | tf_op jit(solution)/shard_map/ppermute | solution.py:490
  15.4 0.7 %collective-permute-done.3.refs_2_ = bf16[288,128]{1,0:T(8,128)(2,1)S(1)} collective-permute-done((bf16[288,128]{1,0:T(8,128)(2,1)S(1)}, bf16[288,128]{1,0:T(8,128)(2,1)S(1)}, u32[]{:S(2)}, u32[]{:S(2)}) %collective-permute-start.3) | collective-permute-done | bytes 73760 | tf_op jit(solution)/shard_map/ppermute | solution.py:490
  16.2 0.3 collective-permute-start.5
  16.5 1.4 %collective-permute-start.11 = (bf16[144,128]{1,0:T(8,128)(2,1)S(1)}, bf16[144,128]{1,0:T(8,128)(2,1)S(1)}, u32[]{:S(2)}, u32[]{:S(2)}) collective-permute-start(bf16[144,128]{1,0:T(8,128)(2,1)S(1)} %get-tuple-element.64), channel_id=1, source_target_pairs={{0,2},{2,0},{4,6},{6,4},{8,10},{10,8},{12,14},{14,12},{1,3},{3,1},... | collective-permute-start | bytes 110600 | tf_op jit(solution)/shard_map/ppermute | solution.py:491
  17.9 2.8 %collective-permute-start.8 = (bf16[288,128]{1,0:T(8,128)(2,1)S(1)}, bf16[288,128]{1,0:T(8,128)(2,1)S(1)}, u32[]{:S(2)}, u32[]{:S(2)}) collective-permute-start(bf16[288,128]{1,0:T(8,128)(2,1)S(1)} %get-tuple-element.61), channel_id=1, source_target_pairs={{0,8},{1,11},{2,10},{3,9},{4,12},{5,15},{6,14},{7,13},{8,0},{9,3},... | collective-permute-start | bytes 221192 | tf_op jit(solution)/shard_map/ppermute | solution.py:490
  20.6 0.9 %collective-permute-start.9 = (bf16[288,128]{1,0:T(8,128)(2,1)S(1)}, bf16[288,128]{1,0:T(8,128)(2,1)S(1)}, u32[]{:S(2)}, u32[]{:S(2)}) collective-permute-start(bf16[288,128]{1,0:T(8,128)(2,1)S(1)} %get-tuple-element.62), channel_id=1, source_target_pairs={{0,12},{1,15},{2,14},{3,13},{4,8},{5,11},{6,10},{7,9},{8,4},{9,7},... | collective-permute-start | bytes 221192 | tf_op jit(solution)/shard_map/ppermute | solution.py:490
  21.5 0.6 collective-permute-start.10
  22.1 2.7 %shard_map.113 = (bf16[72,4096]{1,0:T(8,128)(2,1)S(1)}, bf16[72,768]{1,0:T(8,128)(2,1)S(1)}, bf16[72,768]{1,0:T(8,128)(2,1)S(1)}, bf16[72,768]{1,0:T(8,128)(2,1)S(1)}) custom-call(bf16[1152,128]{1,0:T(8,128)(2,1)S(1)} %shard_map.112.x_sent, bf16[1152,128]{1,0:T(8,128)(2,1)S(1)} %collective-permute-done.5.x_swapped, bf16[1,4096,768]{2,1,0:T(8,128)(2,1)S(1)} %bitcast.3, ...), custom_call_target="tpu_custom_call" | custom-call | flops 905969664 | tf_op jit(solution)/shard_map/pallas_call | solution.py:132
  24.8 2.7 %collective-permute-done.9.refs_1_ = bf16[288,128]{1,0:T(8,128)(2,1)S(1)} collective-permute-done((bf16[288,128]{1,0:T(8,128)(2,1)S(1)}, bf16[288,128]{1,0:T(8,128)(2,1)S(1)}, u32[]{:S(2)}, u32[]{:S(2)}) %collective-permute-start.9) | collective-permute-done | bytes 73760 | tf_op jit(solution)/shard_map/ppermute | solution.py:490
  27.8 0.6 %collective-permute-start.12 = (bf16[1152,128]{1,0:T(8,128)(2,1)S(1)}, bf16[1152,128]{1,0:T(8,128)(2,1)S(1)}, u32[]{:S(2)}, u32[]{:S(2)}) collective-permute-start(bf16[1152,128]{1,0:T(8,128)(2,1)S(1)} %shard_map.115.g_sent), channel_id=1, source_target_pairs={{0,1},{1,0},{2,3},{3,2},{4,5},{5,4},{6,7},{7,6},{8,9},{9,8},{10,11... | collective-permute-start | bytes 884744 | tf_op jit(solution)/shard_map/ppermute | solution.py:495
  28.4 1.5 %shard_map.114 = (f32[720,128]{1,0:T(8,128)S(1)}, f32[432,128]{1,0:T(8,128)S(1)}, bf16[432,128]{1,0:T(8,128)(2,1)S(1)}, bf16[720,128]{1,0:T(8,128)(2,1)S(1)}) custom-call(bf16[72,768]{1,0:T(8,128)(2,1)S(1)} %get-tuple-element.56.hidden.refs_5_, bf16[1,768,4096]{2,1,0:T(8,128)(2,1)S(1)} %bitcast.7), custom_call_target="tpu_custom_call" | custom-call | flops 452984832 | tf_op jit(solution)/shard_map/pallas_call | solution.py:132
  30.0 4.9 %shard_map.116 = (bf16[72,4096]{1,0:T(8,128)(2,1)S(1)}, bf16[72,768]{1,0:T(8,128)(2,1)S(1)}, bf16[72,768]{1,0:T(8,128)(2,1)S(1)}, f32[432,128]{1,0:T(8,128)S(1)}, bf16[720,128]{1,0:T(8,128)(2,1)S(1)}) custom-call(bf16[1152,128]{1,0:T(8,128)(2,1)S(1)} %shard_map.115.g_sent, bf16[1152,128]{1,0:T(8,128)(2,1)S(1)} %collective-permute-done.12.g_swapped, ...), custom_call_target="tpu_custom_call" | custom-call | flops 905969664 | tf_op jit(solution)/shard_map/pallas_call | solution.py:132
  34.9 0.5 collective-permute-start.13
  35.5 2.1 %shard_map.117 = (f32[720,128]{1,0:T(8,128)S(1)}, bf16[432,128]{1,0:T(8,128)(2,1)S(1)}) custom-call(bf16[72,768]{1,0:T(8,128)(2,1)S(1)} %get-tuple-element.68.pre_gate, bf16[72,768]{1,0:T(8,128)(2,1)S(1)} %get-tuple-element.69.pre_up, bf16[1,4096,768]{2,1,0:T(8,128)(2,1)S(1)} %bitcast.3, bf16[1,4096,768]{2,1,0:T(8,128)(2,1)S(1)} %bitcast.5), custom_call_target="tpu_custom_call" | custom-call | flops 452984832 | tf_op jit(solution)/shard_map/pallas_call | solution.py:132
  37.6 0.5 collective-permute-start.14
  38.1 1.0 %collective-permute-done.14.refs_7_ = bf16[432,128]{1,0:T(8,128)(2,1)S(1)} collective-permute-done((bf16[432,128]{1,0:T(8,128)(2,1)S(1)}, bf16[432,128]{1,0:T(8,128)(2,1)S(1)}, u32[]{:S(2)}, u32[]{:S(2)}) %collective-permute-start.14) | collective-permute-done | bytes 110624 | tf_op jit(solution)/shard_map/ppermute | solution.py:495
  39.2 2.9 %collective-permute-start.15 = (bf16[576,128]{1,0:T(8,128)(2,1)S(1)}, bf16[576,128]{1,0:T(8,128)(2,1)S(1)}, u32[]{:S(2)}, u32[]{:S(2)}) collective-permute-start(bf16[576,128]{1,0:T(8,128)(2,1)S(1)} %get-tuple-element.74), channel_id=1, source_target_pairs={{0,8},{1,11},{2,10},{3,9},{4,12},{5,15},{6,14},{7,13},{8,0},{9,3},... | collective-permute-start | bytes 442376 | tf_op jit(solution)/shard_map/ppermute | solution.py:490
  42.1 0.9 %collective-permute-start.16 = (bf16[576,128]{1,0:T(8,128)(2,1)S(1)}, bf16[576,128]{1,0:T(8,128)(2,1)S(1)}, u32[]{:S(2)}, u32[]{:S(2)}) collective-permute-start(bf16[576,128]{1,0:T(8,128)(2,1)S(1)} %get-tuple-element.75), channel_id=1, source_target_pairs={{0,12},{1,15},{2,14},{3,13},{4,8},{5,11},{6,10},{7,9},{8,4},{9,7},... | collective-permute-start | bytes 442376 | tf_op jit(solution)/shard_map/ppermute | solution.py:490
  43.1 0.5 collective-permute-start.17
  43.6 0.9 %collective-permute-start.18 = (bf16[288,128]{1,0:T(8,128)(2,1)S(1)}, bf16[288,128]{1,0:T(8,128)(2,1)S(1)}, u32[]{:S(2)}, u32[]{:S(2)}) collective-permute-start(bf16[288,128]{1,0:T(8,128)(2,1)S(1)} %get-tuple-element.77), channel_id=1, source_target_pairs={{0,2},{2,0},{4,6},{6,4},{8,10},{10,8},{12,14},{14,12},{1,3},{3,1},... | collective-permute-start | bytes 221192 | tf_op jit(solution)/shard_map/ppermute | solution.py:491
  44.5 9.1 %shard_map.119 = (bf16[1,4096,768]{2,1,0:T(8,128)(2,1)}, bf16[1,4096,768]{2,1,0:T(8,128)(2,1)}, bf16[1,768,4096]{2,1,0:T(8,128)(2,1)}, f32[8,128]{1,0:T(8,128)S(1)}) custom-call(bf16[72,4096]{1,0:T(8,128)(2,1)S(1)} %get-tuple-element.79.x, bf16[72,4096]{1,0:T(8,128)(2,1)S(1)} %get-tuple-element.80.g, bf16[72,768]{1,0:T(8,128)(2,1)S(1)} %get-tuple-element.56.hidden.refs_5_, ...), custom_call_target="tpu_custom_call" | custom-call | flops 1358954496 | bytes 18874368 | tf_op jit(solution)/shard_map/pallas_call | solution.py:132
  53.6 1.7 %collective-permute-done.17.refs_2_ = bf16[576,128]{1,0:T(8,128)(2,1)S(1)} collective-permute-done((bf16[576,128]{1,0:T(8,128)(2,1)S(1)}, bf16[576,128]{1,0:T(8,128)(2,1)S(1)}, u32[]{:S(2)}, u32[]{:S(2)}) %collective-permute-start.17) | collective-permute-done | bytes 147488 | tf_op jit(solution)/shard_map/ppermute | solution.py:490
  55.3 0.4 collective-permute-start.19
  55.7 1.1 %collective-permute-done.19.refs_5_ = bf16[864,128]{1,0:T(8,128)(2,1)S(1)} collective-permute-done((bf16[864,128]{1,0:T(8,128)(2,1)S(1)}, bf16[864,128]{1,0:T(8,128)(2,1)S(1)}, u32[]{:S(2)}, u32[]{:S(2)}) %collective-permute-start.19) | collective-permute-done | bytes 221216 | tf_op jit(solution)/shard_map/ppermute | solution.py:495
  56.9 1.6 %shard_map.121 = (bf16[128,2048]{1,0:T(8,128)(2,1)}, bf16[128,2048]{1,0:T(8,128)(2,1)}) custom-call(bf16[72,128]{1,0:T(8,128)(2,1)S(1)} %get-tuple-element.46.place, f32[72,128]{1,0:T(8,128)S(1)} %get-tuple-element.47.refs_5_.mix, bf16[576,128]{1,0:T(8,128)(2,1)S(1)} %collective-permute-done.15.refs_0_, ...), custom_call_target="tpu_custom_call" | custom-call | bytes 2097152 | tf_op jit(solution)/shard_map/pallas_call | solution.py:132
  (35 shorter events, 0.9 us)
Async XLA Ops:
  0.6 21.4 %slice-start = ((s8[6291456]{0:T(1024)(128)(4,1)}), s8[4194304]{0:T(1024)(128)(4,1)S(1)}, s32[]{:S(2)}) async-start(s8[6291456]{0:T(1024)(128)(4,1)} %bitcast.2), calls=%async_computation | async-start | bytes 8388608
  0.6 21.4 %slice-start.2 = ((s8[6291456]{0:T(1024)(128)(4,1)}), s8[4194304]{0:T(1024)(128)(4,1)S(1)}, s32[]{:S(2)}) async-start(s8[6291456]{0:T(1024)(128)(4,1)} %bitcast.4), calls=%async_computation.2 | async-start | bytes 8388608
  2.7 1.6 %collective-permute-start = (bf16[864,128]{1,0:T(8,128)(2,1)S(1)}, bf16[864,128]{1,0:T(8,128)(2,1)S(1)}, u32[]{:S(2)}, u32[]{:S(2)}) collective-permute-start(bf16[864,128]{1,0:T(8,128)(2,1)S(1)} %get-tuple-element.50), channel_id=1, source_target_pairs={{0,1},{1,0},{2,3},{3,2},{4,5},{5,4},{6,7},{7,6},{8,9},{9,8},{10,11... | collective-permute-start | bytes 663560 | tf_op jit(solution)/shard_map/ppermute | solution.py:495
  4.4 17.7 %slice-start.1 = ((s8[6291456]{0:T(1024)(128)(4,1)}), s8[2097152]{0:T(1024)(128)(4,1)S(1)}, s32[]{:S(2)}) async-start(s8[6291456]{0:T(1024)(128)(4,1)} %bitcast.2), calls=%async_computation.1 | async-start | bytes 4194304
  4.4 17.7 %slice-start.3 = ((s8[6291456]{0:T(1024)(128)(4,1)}), s8[2097152]{0:T(1024)(128)(4,1)S(1)}, s32[]{:S(2)}) async-start(s8[6291456]{0:T(1024)(128)(4,1)} %bitcast.4), calls=%async_computation.3 | async-start | bytes 4194304
  4.4 10.1 %collective-permute-start.1 = (bf16[288,128]{1,0:T(8,128)(2,1)S(1)}, bf16[288,128]{1,0:T(8,128)(2,1)S(1)}, u32[]{:S(2)}, u32[]{:S(2)}) collective-permute-start(bf16[288,128]{1,0:T(8,128)(2,1)S(1)} %get-tuple-element.51), channel_id=1, source_target_pairs={{0,8},{1,11},{2,10},{3,9},{4,12},{5,15},{6,14},{7,13},{8,0},{9,3},... | collective-permute-start | bytes 221192 | tf_op jit(solution)/shard_map/ppermute | solution.py:490
  8.4 7.0 %collective-permute-start.2 = (bf16[288,128]{1,0:T(8,128)(2,1)S(1)}, bf16[288,128]{1,0:T(8,128)(2,1)S(1)}, u32[]{:S(2)}, u32[]{:S(2)}) collective-permute-start(bf16[288,128]{1,0:T(8,128)(2,1)S(1)} %get-tuple-element.52), channel_id=1, source_target_pairs={{0,12},{1,15},{2,14},{3,13},{4,8},{5,11},{6,10},{7,9},{8,4},{9,7},... | collective-permute-start | bytes 221192 | tf_op jit(solution)/shard_map/ppermute | solution.py:490
  9.8 6.4 %collective-permute-start.3 = (bf16[288,128]{1,0:T(8,128)(2,1)S(1)}, bf16[288,128]{1,0:T(8,128)(2,1)S(1)}, u32[]{:S(2)}, u32[]{:S(2)}) collective-permute-start(bf16[288,128]{1,0:T(8,128)(2,1)S(1)} %get-tuple-element.53), channel_id=1, source_target_pairs={{0,4},{1,7},{2,6},{3,5},{4,0},{5,3},{6,2},{7,1},{8,12},{9,15},{10,... | collective-permute-start | bytes 221192 | tf_op jit(solution)/shard_map/ppermute | solution.py:490
  10.0 4.5 %collective-permute-start.4 = (bf16[144,128]{1,0:T(8,128)(2,1)S(1)}, bf16[144,128]{1,0:T(8,128)(2,1)S(1)}, u32[]{:S(2)}, u32[]{:S(2)}) collective-permute-start(bf16[144,128]{1,0:T(8,128)(2,1)S(1)} %get-tuple-element.54), channel_id=1, source_target_pairs={{0,2},{2,0},{4,6},{6,4},{8,10},{10,8},{12,14},{14,12},{1,3},{3,1},... | collective-permute-start | bytes 110600 | tf_op jit(solution)/shard_map/ppermute | solution.py:491
  16.2 5.9 %collective-permute-start.5 = (bf16[1152,128]{1,0:T(8,128)(2,1)S(1)}, bf16[1152,128]{1,0:T(8,128)(2,1)S(1)}, u32[]{:S(2)}, u32[]{:S(2)}) collective-permute-start(bf16[1152,128]{1,0:T(8,128)(2,1)S(1)} %shard_map.112.x_sent), channel_id=1, source_target_pairs={{0,1},{1,0},{2,3},{3,2},{4,5},{5,4},{6,7},{7,6},{8,9},{9,8},{10,11... | collective-permute-start | bytes 884744 | tf_op jit(solution)/shard_map/ppermute | solution.py:495
  16.5 8.3 %collective-permute-start.11 = (bf16[144,128]{1,0:T(8,128)(2,1)S(1)}, bf16[144,128]{1,0:T(8,128)(2,1)S(1)}, u32[]{:S(2)}, u32[]{:S(2)}) collective-permute-start(bf16[144,128]{1,0:T(8,128)(2,1)S(1)} %get-tuple-element.64), channel_id=1, source_target_pairs={{0,2},{2,0},{4,6},{6,4},{8,10},{10,8},{12,14},{14,12},{1,3},{3,1},... | collective-permute-start | bytes 110600 | tf_op jit(solution)/shard_map/ppermute | solution.py:491
  17.9 6.9 %collective-permute-start.8 = (bf16[288,128]{1,0:T(8,128)(2,1)S(1)}, bf16[288,128]{1,0:T(8,128)(2,1)S(1)}, u32[]{:S(2)}, u32[]{:S(2)}) collective-permute-start(bf16[288,128]{1,0:T(8,128)(2,1)S(1)} %get-tuple-element.61), channel_id=1, source_target_pairs={{0,8},{1,11},{2,10},{3,9},{4,12},{5,15},{6,14},{7,13},{8,0},{9,3},... | collective-permute-start | bytes 221192 | tf_op jit(solution)/shard_map/ppermute | solution.py:490
  20.6 6.9 %collective-permute-start.9 = (bf16[288,128]{1,0:T(8,128)(2,1)S(1)}, bf16[288,128]{1,0:T(8,128)(2,1)S(1)}, u32[]{:S(2)}, u32[]{:S(2)}) collective-permute-start(bf16[288,128]{1,0:T(8,128)(2,1)S(1)} %get-tuple-element.62), channel_id=1, source_target_pairs={{0,12},{1,15},{2,14},{3,13},{4,8},{5,11},{6,10},{7,9},{8,4},{9,7},... | collective-permute-start | bytes 221192 | tf_op jit(solution)/shard_map/ppermute | solution.py:490
  21.5 6.9 %slice-start.4 = ((s8[6291456]{0:T(1024)(128)(4,1)}), s8[4194304]{0:T(1024)(128)(4,1)S(1)}, s32[]{:S(2)}) async-start(s8[6291456]{0:T(1024)(128)(4,1)} %bitcast.6), calls=%async_computation.4 | async-start | bytes 8388608
  21.5 6.9 %slice-start.5 = ((s8[6291456]{0:T(1024)(128)(4,1)}), s8[2097152]{0:T(1024)(128)(4,1)S(1)}, s32[]{:S(2)}) async-start(s8[6291456]{0:T(1024)(128)(4,1)} %bitcast.6), calls=%async_computation.5 | async-start | bytes 4194304
  21.5 6.3 %collective-permute-start.10 = (bf16[288,128]{1,0:T(8,128)(2,1)S(1)}, bf16[288,128]{1,0:T(8,128)(2,1)S(1)}, u32[]{:S(2)}, u32[]{:S(2)}) collective-permute-start(bf16[288,128]{1,0:T(8,128)(2,1)S(1)} %get-tuple-element.63), channel_id=1, source_target_pairs={{0,4},{1,7},{2,6},{3,5},{4,0},{5,3},{6,2},{7,1},{8,12},{9,15},{10,... | collective-permute-start | bytes 221192 | tf_op jit(solution)/shard_map/ppermute | solution.py:490
  27.8 2.3 %collective-permute-start.12 = (bf16[1152,128]{1,0:T(8,128)(2,1)S(1)}, bf16[1152,128]{1,0:T(8,128)(2,1)S(1)}, u32[]{:S(2)}, u32[]{:S(2)}) collective-permute-start(bf16[1152,128]{1,0:T(8,128)(2,1)S(1)} %shard_map.115.g_sent), channel_id=1, source_target_pairs={{0,1},{1,0},{2,3},{3,2},{4,5},{5,4},{6,7},{7,6},{8,9},{9,8},{10,11... | collective-permute-start | bytes 884744 | tf_op jit(solution)/shard_map/ppermute | solution.py:495
  29.9 8.2 %collective-permute-start.6 = (bf16[720,128]{1,0:T(8,128)(2,1)S(1)}, bf16[720,128]{1,0:T(8,128)(2,1)S(1)}, u32[]{:S(2)}, u32[]{:S(2)}) collective-permute-start(bf16[720,128]{1,0:T(8,128)(2,1)S(1)} %get-tuple-element.59), channel_id=1, source_target_pairs={{0,1},{1,0},{2,3},{3,2},{4,5},{5,4},{6,7},{7,6},{8,9},{9,8},{10,11... | collective-permute-start | bytes 552968 | tf_op jit(solution)/shard_map/ppermute | solution.py:495
  34.9 4.2 %collective-permute-start.13 = (bf16[720,128]{1,0:T(8,128)(2,1)S(1)}, bf16[720,128]{1,0:T(8,128)(2,1)S(1)}, u32[]{:S(2)}, u32[]{:S(2)}) collective-permute-start(bf16[720,128]{1,0:T(8,128)(2,1)S(1)} %get-tuple-element.72), channel_id=1, source_target_pairs={{0,1},{1,0},{2,3},{3,2},{4,5},{5,4},{6,7},{7,6},{8,9},{9,8},{10,11... | collective-permute-start | bytes 552968 | tf_op jit(solution)/shard_map/ppermute | solution.py:495
  35.5 2.7 %collective-permute-start.7 = (bf16[432,128]{1,0:T(8,128)(2,1)S(1)}, bf16[432,128]{1,0:T(8,128)(2,1)S(1)}, u32[]{:S(2)}, u32[]{:S(2)}) collective-permute-start(bf16[432,128]{1,0:T(8,128)(2,1)S(1)} %get-tuple-element.60), channel_id=1, source_target_pairs={{0,1},{1,0},{2,3},{3,2},{4,5},{5,4},{6,7},{7,6},{8,9},{9,8},{10,11... | collective-permute-start | bytes 331784 | tf_op jit(solution)/shard_map/ppermute | solution.py:495
  37.6 1.5 %collective-permute-start.14 = (bf16[432,128]{1,0:T(8,128)(2,1)S(1)}, bf16[432,128]{1,0:T(8,128)(2,1)S(1)}, u32[]{:S(2)}, u32[]{:S(2)}) collective-permute-start(bf16[432,128]{1,0:T(8,128)(2,1)S(1)} %get-tuple-element.73), channel_id=1, source_target_pairs={{0,1},{1,0},{2,3},{3,2},{4,5},{5,4},{6,7},{7,6},{8,9},{9,8},{10,11... | collective-permute-start | bytes 331784 | tf_op jit(solution)/shard_map/ppermute | solution.py:495
  39.2 14.4 %collective-permute-start.15 = (bf16[576,128]{1,0:T(8,128)(2,1)S(1)}, bf16[576,128]{1,0:T(8,128)(2,1)S(1)}, u32[]{:S(2)}, u32[]{:S(2)}) collective-permute-start(bf16[576,128]{1,0:T(8,128)(2,1)S(1)} %get-tuple-element.74), channel_id=1, source_target_pairs={{0,8},{1,11},{2,10},{3,9},{4,12},{5,15},{6,14},{7,13},{8,0},{9,3},... | collective-permute-start | bytes 442376 | tf_op jit(solution)/shard_map/ppermute | solution.py:490
  42.1 11.5 %collective-permute-start.16 = (bf16[576,128]{1,0:T(8,128)(2,1)S(1)}, bf16[576,128]{1,0:T(8,128)(2,1)S(1)}, u32[]{:S(2)}, u32[]{:S(2)}) collective-permute-start(bf16[576,128]{1,0:T(8,128)(2,1)S(1)} %get-tuple-element.75), channel_id=1, source_target_pairs={{0,12},{1,15},{2,14},{3,13},{4,8},{5,11},{6,10},{7,9},{8,4},{9,7},... | collective-permute-start | bytes 442376 | tf_op jit(solution)/shard_map/ppermute | solution.py:490
  43.1 12.2 %collective-permute-start.17 = (bf16[576,128]{1,0:T(8,128)(2,1)S(1)}, bf16[576,128]{1,0:T(8,128)(2,1)S(1)}, u32[]{:S(2)}, u32[]{:S(2)}) collective-permute-start(bf16[576,128]{1,0:T(8,128)(2,1)S(1)} %get-tuple-element.76), channel_id=1, source_target_pairs={{0,4},{1,7},{2,6},{3,5},{4,0},{5,3},{6,2},{7,1},{8,12},{9,15},{10,... | collective-permute-start | bytes 442376 | tf_op jit(solution)/shard_map/ppermute | solution.py:490
  43.6 10.0 %collective-permute-start.18 = (bf16[288,128]{1,0:T(8,128)(2,1)S(1)}, bf16[288,128]{1,0:T(8,128)(2,1)S(1)}, u32[]{:S(2)}, u32[]{:S(2)}) collective-permute-start(bf16[288,128]{1,0:T(8,128)(2,1)S(1)} %get-tuple-element.77), channel_id=1, source_target_pairs={{0,2},{2,0},{4,6},{6,4},{8,10},{10,8},{12,14},{14,12},{1,3},{3,1},... | collective-permute-start | bytes 221192 | tf_op jit(solution)/shard_map/ppermute | solution.py:491
  55.3 1.5 %collective-permute-start.19 = (bf16[864,128]{1,0:T(8,128)(2,1)S(1)}, bf16[864,128]{1,0:T(8,128)(2,1)S(1)}, u32[]{:S(2)}, u32[]{:S(2)}) collective-permute-start(bf16[864,128]{1,0:T(8,128)(2,1)S(1)} %shard_map.120), channel_id=1, source_target_pairs={{0,1},{1,0},{2,3},{3,2},{4,5},{5,4},{6,7},{7,6},{8,9},{9,8},{10,11... | collective-permute-start | bytes 663560 | tf_op jit(solution)/shard_map/ppermute | solution.py:495

commit v8 on v7

--- a/solution.py
+++ b/solution.py
@@ -165,7 +165,7 @@
 
 
 def route_kernel(devices, capacity, subs, ids_in, weight_in, x_in, g_in, *refs):
-    (*outs, theirs, place_out, mix_out, scratch, ids, weight, x, g, sems) = refs
+    x_mine, g_mine, near, here, theirs, place_out, mix_out, scratch, ids, weight, x, g, sems = refs
     pairs = ((ids_in, ids), (weight_in, weight), (x_in, x), (g_in, g))
     copies = [pltpu.make_async_copy(src, dst, sems.at[i]) for i, (src, dst) in enumerate(pairs)]
     for copy in copies:
@@ -205,40 +205,49 @@
     size = capacity * subs
     count = devices // 2 - 1
 
-    def write(mine, near, here, at):
+    def write(mine, at):
         def block(p):
-            return scratch[p * size : (p + 1) * size, :].astype(mine.dtype)
+            return scratch[p * size : (p + 1) * size, :].astype(theirs.dtype)
 
         for j in range(count):
             part(mine, j * size, size)[...] = block(j)
             part(theirs, (at + j) * size, size)[...] = block(count + j)
-        near[...] = block(2 * count)
-        here[...] = block(2 * count + 1)
+        start = size if at else 0
+        part(near, start, size)[...] = block(2 * count)
+        part(here, start, size)[...] = block(2 * count + 1)
 
     copies[2].wait()
     for sub in range(subs):
         spread_lanes(scratch, sub, subs, dot(low, x[:, lanes_of(sub)]))
-    write(*outs[:3], 0)
+    write(x_mine, 0)
     copies[3].wait()
     for sub in range(subs):
         spread_lanes(scratch, sub, subs, dot(low, g[:, lanes_of(sub)]) * row_weight)
-    write(*outs[3:], count)
-
-
-def pack_kernel(size, x_mine, g_mine, swapped, *outs):
-    count = len(outs) // 2
-    for i, out in enumerate(outs):
-        mine = x_mine if i < count else g_mine
-        part(out, 0, size)[...] = part(mine, i % count * size, size)[...]
-        part(out, size, size)[...] = part(swapped, i * size, size)[...]
-
-
-def gather_kernel(size, *refs):
+    write(g_mine, count)
+
+
+def pack_kernel(size, late, x_mine, g_mine, swapped, *outs):
+    count = len(outs) - len(late)
+
+    def put(out, at, mine, j, i):
+        part(out, at, size)[...] = part(mine, j * size, size)[...]
+        part(out, at + size, size)[...] = part(swapped, i * size, size)[...]
+
+    for j, out in enumerate(outs[:count]):
+        put(out, 0, x_mine, j, j)
+        if j not in late:
+            put(out, 2 * size, g_mine, j, count + j)
+    for j, out in zip(late, outs[count:]):
+        put(out, 0, g_mine, j, count + j)
+
+
+def gather_kernel(size, at, *refs):
     blocks, (near, here, _, out) = refs[:-4], refs[-4:]
     for j, block in enumerate(blocks):
-        part(out, 2 * j * size, 2 * size)[...] = block[...]
-    part(out, 2 * len(blocks) * size, size)[...] = near[...]
-    part(out, (2 * len(blocks) + 1) * size, size)[...] = here[...]
+        start = block.shape[0] - 2 * size if at else 0
+        part(out, 2 * j * size, 2 * size)[...] = part(block, start, 2 * size)[...]
+    part(out, 2 * len(blocks) * size, size)[...] = part(near, at, size)[...]
+    part(out, (2 * len(blocks) + 1) * size, size)[...] = part(here, at, size)[...]
 
 
 def full_rows(devices, subs, scratch, own_sent, other_sent, out):
@@ -483,12 +492,16 @@
         tall_copy(1, grad_up, i, i % 2).wait()
 
 
-def exchange(blocks, near, devices):
+def exchange(blocks, masks, devices):
     arrived = []
-    for block, mask in zip(blocks, even_masks(devices)):
+    for block, mask in zip(blocks, masks):
         pairs = [(2 * i + core, 2 * (i ^ (mask + core)) + core) for i in range(devices) for core in range(2)]
         arrived.append(lax.ppermute(block, ("expert", "ffn"), pairs))
-    return arrived, lax.ppermute(near, "expert", [(i, i ^ 1) for i in range(devices)])
+    return arrived
+
+
+def exchange_near(block, devices):
+    return lax.ppermute(block, "expert", [(i, i ^ 1) for i in range(devices)])
 
 
 def swap(value):
@@ -521,9 +534,9 @@
         return vmem((number * size, LANES), dtype)
 
     sources = (route_ids.T, route_weight.T, tokens, grad_out)
-    x_mine, x_near, x_here, g_mine, g_near, g_here, theirs, place, mix = call(
+    x_mine, g_mine, near, here, theirs, place, mix = call(
         functools.partial(route_kernel, devices, capacity, subs),
-        [lines(count), lines(1), lines(1)] * 2
+        [lines(count), lines(count), lines(2), lines(2)]
         + [lines(2 * count), jax.ShapeDtypeStruct((rows, tok_dev), low), jax.ShapeDtypeStruct((rows, LANES), full)],
         in_hbm(sources),
         in_spaces=[pl.ANY] * 4,
@@ -532,22 +545,27 @@
         + [pltpu.SemaphoreType.DMA((4,))],
         traffic=4 * tok_dev * sub_width,
     )
+    masks = even_masks(devices)
+    late = list(range(devices // 8, devices // 4))
     packed = call(
-        functools.partial(pack_kernel, size),
-        [lines(2)] * (2 * count),
+        functools.partial(pack_kernel, size, late),
+        [lines(2 if j in late else 4) for j in range(count)] + [lines(2)] * len(late),
         (x_mine, g_mine, swap(theirs)),
         flops=24 * half_flops,
     )
-    x_arrived, x_near = exchange(packed[:count], x_near, devices)
-    g_arrived, g_near = exchange(packed[count:], g_near, devices)
+    x_arrived = exchange(packed[:count], masks, devices)
+    near = exchange_near(near, devices)
+    g_arrived = list(x_arrived)
+    g_arrived[late[0] : late[-1] + 1] = exchange(packed[count:], [masks[j] for j in late], devices)
 
     weights = (gate_weight, up_weight, down_weight)
     w_gate, w_up, w_down = [pltpu.with_memory_space_constraint(w, pltpu.VMEM) for w in weights]
 
-    def gather(arrived, near, here, after):
-        return call(functools.partial(gather_kernel, size), [lines(devices)], (*arrived, near, here, after))[0]
-
-    x_sent = gather(x_arrived, x_near, x_here, mix)
+    def gather(arrived, at, after):
+        kernel = functools.partial(gather_kernel, size, at)
+        return call(kernel, [lines(devices)], (*arrived, near, here, after))[0]
+
+    x_sent = gather(x_arrived, 0, mix)
     x_swapped = swap(x_sent)
     terms = [
         lines_in_vmem(count + 2, full),
@@ -562,7 +580,7 @@
         scratch=spread_scratch,
         flops=4 * half_flops,
     )
-    g_sent = gather(g_arrived, g_near, g_here, hidden)
+    g_sent = gather(g_arrived, size, hidden)
     g_swapped = swap(g_sent)
     out_own, out_other, send_own, send_other = call(
         functools.partial(output_kernel, devices, subs, step),
@@ -588,12 +606,13 @@
         flops=2 * half_flops,
     )
     dx_terms = (dx_own, dx_other, came_own, swap(send_own))
-    *leaving, near, here = call(
+    *leaving, back, kept = call(
         functools.partial(leave_kernel, size),
         [lines(4)] * count + [lines(2)] * 2,
         (*out_terms, *dx_terms),
     )
-    returned, near = exchange(leaving, near, devices)
+    returned = exchange(leaving, masks, devices)
+    back = exchange_near(back, devices)
     cut = 1024 if width % 1024 == 0 else width
     grad_gate, grad_up, grad_down, written = call(
         functools.partial(gradient_kernel, cut),
@@ -612,11 +631,11 @@
         traffic=sum(w.size * 2 for w in weights),
         limit=32,
     )
-    (sharing,) = call(functools.partial(share_kernel, size), [lines(2 * count)], (*returned, near, written))
+    (sharing,) = call(functools.partial(share_kernel, size), [lines(2 * count)], (*returned, back, written))
     out_tokens, grad_tokens = call(
         functools.partial(join_kernel, count, subs),
         [jax.ShapeDtypeStruct((tok_dev, sub_width), low)] * 2,
-        (place, mix, *returned, near, here, swap(sharing)),
+        (place, mix, *returned, back, kept, swap(sharing)),
         scratch=spread_scratch,
         traffic=8 * tok_dev * sub_width,
     )

time: 58.7 us -> 56.9 us (0.969)
  starting transfers between devices: 21 us -> 16.6 us
  waiting for transfers between devices: 12.5 us -> 15.2 us
    ppermute x9 -> x7, starting transfers between devices: 14.1 us -> 12 us  [exchange(): arrived.append(lax.ppermute(block, ('expert', 'ffn'), pairs))]
    ppermute x3 -> x2, waiting for transfers between devices: 3.04 us -> 4.38 us  [exchange_near(): return lax.ppermute(block, 'expert', [(i, i ^ 1) for i in range(devices)])]
    ppermute x3 -> x2, starting transfers between devices: 3.8 us -> 2.48 us  [exchange_near(): return lax.ppermute(block, 'expert', [(i, i ^ 1) for i in range(devices)])]
    ppermute x8, starting transfers between devices: 3.07 us -> 2.09 us  [swap(): return lax.ppermute(value, 'ffn', [(0, 1), (1, 0)])]
    ppermute x9 -> x7, waiting for transfers between devices: 6.26 us -> 7.08 us  [exchange(): arrived.append(lax.ppermute(block, ('expert', 'ffn'), pairs))]
  transfers between devices with their start and end apart: 20 -> 17, of which waited for: 9 -> 8; matrix products, arithmetic and copies ran while one was open for 0% -> 0% of each run, Pallas kernels for 35% -> 36%
where the time goes in v8:
time: 56.9 us; the launch traced here: 56.7 us
  Pallas kernels  24.2 us (43%)
  starting transfers between devices  16.6 us (29%)
  waiting for transfers between devices  15.2 us (27%)
  between operations  0.81 us (1%)
    pallas_call x12, Pallas kernels, call(): pl.pallas_call(kernel, out_shape=tuple(out_shape), in_specs=[pl.BlockSpec...  24.2 us
    ppermute x7, starting transfers between devices, exchange(): arrived.append(lax.ppermute(block, ('expert', 'ffn'), pairs))  12 us
    ppermute x7, waiting for transfers between devices, exchange(): arrived.append(lax.ppermute(block, ('expert', 'ffn'), pairs))  7.08 us
    ppermute x2, waiting for transfers between devices, exchange_near(): return lax.ppermute(block, 'expert', [(i, i ^ 1) for i in range(devices)])  4.38 us
    ppermute x8, waiting for transfers between devices, swap(): return lax.ppermute(value, 'ffn', [(0, 1), (1, 0)])  3.73 us
    ppermute x2, starting transfers between devices, exchange_near(): return lax.ppermute(block, 'expert', [(i, i ^ 1) for i in range(devices)])  2.48 us
    ppermute x8, starting transfers between devices, swap(): return lax.ppermute(value, 'ffn', [(0, 1), (1, 0)])  2.09 us
  transfers between devices with their start and end apart: 17, of which 8 were waited for; matrix products, arithmetic and copies ran while one was open for 0% of the time, Pallas kernels for 36%

profile of v8, /device:TPU:0, one launch (start us, length us, event | category | flops | bytes accessed | tf_op | source)
XLA Modules:
  0.0 56.7 jit_solution(18370345473187020714)
XLA Ops:
  0.7 2.1 %shard_map.110 = (bf16[432,128]{1,0:T(8,128)(2,1)S(1)}, bf16[432,128]{1,0:T(8,128)(2,1)S(1)}, bf16[288,128]{1,0:T(8,128)(2,1)S(1)}, bf16[288,128]{1,0:T(8,128)(2...) custom-call(s32[8,128]{1,0:T(8,128)} %bitcast.8, f32[8,128]{1,0:T(8,128)} %bitcast.9, ...), custom_call_target="tpu_custom_call" | custom-call | bytes 1048576 | tf_op jit(solution)/shard_map/pallas_call | solution.py:132
  2.7 0.5 collective-permute-start
  3.3 1.1 %collective-permute-done.swapped = bf16[864,128]{1,0:T(8,128)(2,1)S(1)} collective-permute-done((bf16[864,128]{1,0:T(8,128)(2,1)S(1)}, bf16[864,128]{1,0:T(8,128)(2,1)S(1)}, u32[]{:S(2)}, u32[]{:S(2)}) %collective-permute-start) | collective-permute-done | bytes 221216 | tf_op jit(solution)/shard_map/ppermute | solution.py:508
  4.4 4.0 %collective-permute-start.1 = (bf16[576,128]{1,0:T(8,128)(2,1)S(1)}, bf16[576,128]{1,0:T(8,128)(2,1)S(1)}, u32[]{:S(2)}, u32[]{:S(2)}) collective-permute-start(bf16[576,128]{1,0:T(8,128)(2,1)S(1)} %get-tuple-element.47), channel_id=1, source_target_pairs={{0,8},{1,11},{2,10},{3,9},{4,12},{5,15},{6,14},{7,13},{8,0},{9,3},... | collective-permute-start | bytes 442376 | tf_op jit(solution)/shard_map/ppermute | solution.py:499
  8.4 1.6 %collective-permute-start.3 = (bf16[576,128]{1,0:T(8,128)(2,1)S(1)}, bf16[576,128]{1,0:T(8,128)(2,1)S(1)}, u32[]{:S(2)}, u32[]{:S(2)}) collective-permute-start(bf16[576,128]{1,0:T(8,128)(2,1)S(1)} %get-tuple-element.49), channel_id=1, source_target_pairs={{0,4},{1,7},{2,6},{3,5},{4,0},{5,3},{6,2},{7,1},{8,12},{9,15},{10,... | collective-permute-start | bytes 442376 | tf_op jit(solution)/shard_map/ppermute | solution.py:499
  10.0 1.5 %collective-permute-start.4 = (bf16[288,128]{1,0:T(8,128)(2,1)S(1)}, bf16[288,128]{1,0:T(8,128)(2,1)S(1)}, u32[]{:S(2)}, u32[]{:S(2)}) collective-permute-start(bf16[288,128]{1,0:T(8,128)(2,1)S(1)} %get-tuple-element.50), channel_id=1, source_target_pairs={{0,2},{2,0},{4,6},{6,4},{8,10},{10,8},{12,14},{14,12},{1,3},{3,1},... | collective-permute-start | bytes 221192 | tf_op jit(solution)/shard_map/ppermute | solution.py:504
  11.5 0.2 collective-permute-start.2
  11.7 4.4 %collective-permute-done.4.refs_3_ = bf16[288,128]{1,0:T(8,128)(2,1)S(1)} collective-permute-done((bf16[288,128]{1,0:T(8,128)(2,1)S(1)}, bf16[288,128]{1,0:T(8,128)(2,1)S(1)}, u32[]{:S(2)}, u32[]{:S(2)}) %collective-permute-start.4) | collective-permute-done | bytes 73760 | tf_op jit(solution)/shard_map/ppermute | solution.py:504
  16.1 3.2 %collective-permute-done.2.refs_1_ = bf16[288,128]{1,0:T(8,128)(2,1)S(1)} collective-permute-done((bf16[288,128]{1,0:T(8,128)(2,1)S(1)}, bf16[288,128]{1,0:T(8,128)(2,1)S(1)}, u32[]{:S(2)}, u32[]{:S(2)}) %collective-permute-start.2) | collective-permute-done | bytes 73760 | tf_op jit(solution)/shard_map/ppermute | solution.py:499
  19.3 0.1 collective-permute-start.5
  19.4 2.5 %collective-permute-start.8 = (bf16[288,128]{1,0:T(8,128)(2,1)S(1)}, bf16[288,128]{1,0:T(8,128)(2,1)S(1)}, u32[]{:S(2)}, u32[]{:S(2)}) collective-permute-start(bf16[288,128]{1,0:T(8,128)(2,1)S(1)} %get-tuple-element.57), channel_id=1, source_target_pairs={{0,12},{1,15},{2,14},{3,13},{4,8},{5,11},{6,10},{7,9},{8,4},{9,7},... | collective-permute-start | bytes 221192 | tf_op jit(solution)/shard_map/ppermute | solution.py:499
  22.0 2.7 %shard_map.113 = (bf16[72,4096]{1,0:T(8,128)(2,1)S(1)}, bf16[72,768]{1,0:T(8,128)(2,1)S(1)}, bf16[72,768]{1,0:T(8,128)(2,1)S(1)}, bf16[72,768]{1,0:T(8,128)(2,1)S(1)}) custom-call(bf16[1152,128]{1,0:T(8,128)(2,1)S(1)} %shard_map.112.x_sent, bf16[1152,128]{1,0:T(8,128)(2,1)S(1)} %collective-permute-done.5.x_swapped, bf16[1,4096,768]{2,1,0:T(8,128)(2,1)S(1)} %bitcast.3, ...), custom_call_target="tpu_custom_call" | custom-call | flops 905969664 | tf_op jit(solution)/shard_map/pallas_call | solution.py:132
  24.7 1.7 %collective-permute-done.8.refs_1_ = bf16[288,128]{1,0:T(8,128)(2,1)S(1)} collective-permute-done((bf16[288,128]{1,0:T(8,128)(2,1)S(1)}, bf16[288,128]{1,0:T(8,128)(2,1)S(1)}, u32[]{:S(2)}, u32[]{:S(2)}) %collective-permute-start.8) | collective-permute-done | bytes 73760 | tf_op jit(solution)/shard_map/ppermute | solution.py:499
  26.4 0.1 collective-permute-start.9
  26.5 1.5 %shard_map.114 = (f32[720,128]{1,0:T(8,128)S(1)}, f32[432,128]{1,0:T(8,128)S(1)}, bf16[432,128]{1,0:T(8,128)(2,1)S(1)}, bf16[720,128]{1,0:T(8,128)(2,1)S(1)}) custom-call(bf16[72,768]{1,0:T(8,128)(2,1)S(1)} %get-tuple-element.52.hidden.refs_5_, bf16[1,768,4096]{2,1,0:T(8,128)(2,1)S(1)} %bitcast.7), custom_call_target="tpu_custom_call" | custom-call | flops 452984832 | tf_op jit(solution)/shard_map/pallas_call | solution.py:132
  28.0 0.5 collective-permute-start.6
  28.5 4.9 %shard_map.116 = (bf16[72,4096]{1,0:T(8,128)(2,1)S(1)}, bf16[72,768]{1,0:T(8,128)(2,1)S(1)}, bf16[72,768]{1,0:T(8,128)(2,1)S(1)}, f32[432,128]{1,0:T(8,128)S(1)}, bf16[720,128]{1,0:T(8,128)(2,1)S(1)}) custom-call(bf16[1152,128]{1,0:T(8,128)(2,1)S(1)} %shard_map.115.g_sent, bf16[1152,128]{1,0:T(8,128)(2,1)S(1)} %collective-permute-done.9.g_swapped, ...), custom_call_target="tpu_custom_call" | custom-call | flops 905969664 | tf_op jit(solution)/shard_map/pallas_call | solution.py:132
  33.4 0.1 collective-permute-start.10
  33.5 0.5 collective-permute-start.7
  34.0 2.1 %shard_map.117 = (f32[720,128]{1,0:T(8,128)S(1)}, bf16[432,128]{1,0:T(8,128)(2,1)S(1)}) custom-call(bf16[72,768]{1,0:T(8,128)(2,1)S(1)} %get-tuple-element.60.pre_gate, bf16[72,768]{1,0:T(8,128)(2,1)S(1)} %get-tuple-element.61.pre_up, bf16[1,4096,768]{2,1,0:T(8,128)(2,1)S(1)} %bitcast.3, bf16[1,4096,768]{2,1,0:T(8,128)(2,1)S(1)} %bitcast.5), custom_call_target="tpu_custom_call" | custom-call | flops 452984832 | tf_op jit(solution)/shard_map/pallas_call | solution.py:132
  36.1 0.1 collective-permute-start.11
  36.2 1.2 %collective-permute-done.11.refs_7_ = bf16[432,128]{1,0:T(8,128)(2,1)S(1)} collective-permute-done((bf16[432,128]{1,0:T(8,128)(2,1)S(1)}, bf16[432,128]{1,0:T(8,128)(2,1)S(1)}, u32[]{:S(2)}, u32[]{:S(2)}) %collective-permute-start.11) | collective-permute-done | bytes 110624 | tf_op jit(solution)/shard_map/ppermute | solution.py:508
  37.5 0.1 shard_map.118
  37.6 2.8 %collective-permute-start.12 = (bf16[576,128]{1,0:T(8,128)(2,1)S(1)}, bf16[576,128]{1,0:T(8,128)(2,1)S(1)}, u32[]{:S(2)}, u32[]{:S(2)}) collective-permute-start(bf16[576,128]{1,0:T(8,128)(2,1)S(1)} %get-tuple-element.66), channel_id=1, source_target_pairs={{0,8},{1,11},{2,10},{3,9},{4,12},{5,15},{6,14},{7,13},{8,0},{9,3},... | collective-permute-start | bytes 442376 | tf_op jit(solution)/shard_map/ppermute | solution.py:499
  40.4 0.9 %collective-permute-start.13 = (bf16[576,128]{1,0:T(8,128)(2,1)S(1)}, bf16[576,128]{1,0:T(8,128)(2,1)S(1)}, u32[]{:S(2)}, u32[]{:S(2)}) collective-permute-start(bf16[576,128]{1,0:T(8,128)(2,1)S(1)} %get-tuple-element.67), channel_id=1, source_target_pairs={{0,12},{1,15},{2,14},{3,13},{4,8},{5,11},{6,10},{7,9},{8,4},{9,7},... | collective-permute-start | bytes 442376 | tf_op jit(solution)/shard_map/ppermute | solution.py:499
  41.2 1.0 %collective-permute-start.15 = (bf16[288,128]{1,0:T(8,128)(2,1)S(1)}, bf16[288,128]{1,0:T(8,128)(2,1)S(1)}, u32[]{:S(2)}, u32[]{:S(2)}) collective-permute-start(bf16[288,128]{1,0:T(8,128)(2,1)S(1)} %get-tuple-element.69), channel_id=1, source_target_pairs={{0,2},{2,0},{4,6},{6,4},{8,10},{10,8},{12,14},{14,12},{1,3},{3,1},... | collective-permute-start | bytes 221192 | tf_op jit(solution)/shard_map/ppermute | solution.py:504
  42.2 9.1 %shard_map.119 = (bf16[1,4096,768]{2,1,0:T(8,128)(2,1)}, bf16[1,4096,768]{2,1,0:T(8,128)(2,1)}, bf16[1,768,4096]{2,1,0:T(8,128)(2,1)}, f32[8,128]{1,0:T(8,128)S(1)}) custom-call(bf16[72,4096]{1,0:T(8,128)(2,1)S(1)} %get-tuple-element.71.x, bf16[72,4096]{1,0:T(8,128)(2,1)S(1)} %get-tuple-element.72.g, bf16[72,768]{1,0:T(8,128)(2,1)S(1)} %get-tuple-element.52.hidden.refs_5_, ...), custom_call_target="tpu_custom_call" | custom-call | flops 1358954496 | bytes 18874368 | tf_op jit(solution)/shard_map/pallas_call | solution.py:132
  51.3 0.3 collective-permute-done.12.refs_0_
  51.6 1.9 %collective-permute-done.14.refs_2_ = bf16[576,128]{1,0:T(8,128)(2,1)S(1)} collective-permute-done((bf16[576,128]{1,0:T(8,128)(2,1)S(1)}, bf16[576,128]{1,0:T(8,128)(2,1)S(1)}, u32[]{:S(2)}, u32[]{:S(2)}) %collective-permute-start.14) | collective-permute-done | bytes 147488 | tf_op jit(solution)/shard_map/ppermute | solution.py:499
  53.6 0.2 collective-permute-start.16
  53.7 1.4 %collective-permute-done.16.refs_5_ = bf16[864,128]{1,0:T(8,128)(2,1)S(1)} collective-permute-done((bf16[864,128]{1,0:T(8,128)(2,1)S(1)}, bf16[864,128]{1,0:T(8,128)(2,1)S(1)}, u32[]{:S(2)}, u32[]{:S(2)}) %collective-permute-start.16) | collective-permute-done | bytes 221216 | tf_op jit(solution)/shard_map/ppermute | solution.py:508
  55.1 1.6 %shard_map.121 = (bf16[128,2048]{1,0:T(8,128)(2,1)}, bf16[128,2048]{1,0:T(8,128)(2,1)}) custom-call(bf16[72,128]{1,0:T(8,128)(2,1)S(1)} %get-tuple-element.42.place, f32[72,128]{1,0:T(8,128)S(1)} %get-tuple-element.43.refs_5_.mix, bf16[576,128]{1,0:T(8,128)(2,1)S(1)} %collective-permute-done.12.refs_0_, ...), custom_call_target="tpu_custom_call" | custom-call | bytes 2097152 | tf_op jit(solution)/shard_map/pallas_call | solution.py:132
  (29 shorter events, 0.1 us)
Async XLA Ops:
  0.6 21.3 %slice-start = ((s8[6291456]{0:T(1024)(128)(4,1)}), s8[4194304]{0:T(1024)(128)(4,1)S(1)}, s32[]{:S(2)}) async-start(s8[6291456]{0:T(1024)(128)(4,1)} %bitcast.2), calls=%async_computation | async-start | bytes 8388608
  0.6 21.3 %slice-start.2 = ((s8[6291456]{0:T(1024)(128)(4,1)}), s8[4194304]{0:T(1024)(128)(4,1)S(1)}, s32[]{:S(2)}) async-start(s8[6291456]{0:T(1024)(128)(4,1)} %bitcast.4), calls=%async_computation.2 | async-start | bytes 8388608
  2.7 1.6 %collective-permute-start = (bf16[864,128]{1,0:T(8,128)(2,1)S(1)}, bf16[864,128]{1,0:T(8,128)(2,1)S(1)}, u32[]{:S(2)}, u32[]{:S(2)}) collective-permute-start(bf16[864,128]{1,0:T(8,128)(2,1)S(1)} %get-tuple-element.46), channel_id=1, source_target_pairs={{0,1},{1,0},{2,3},{3,2},{4,5},{5,4},{6,7},{7,6},{8,9},{9,8},{10,11... | collective-permute-start | bytes 663560 | tf_op jit(solution)/shard_map/ppermute | solution.py:508
  4.4 17.6 %slice-start.1 = ((s8[6291456]{0:T(1024)(128)(4,1)}), s8[2097152]{0:T(1024)(128)(4,1)S(1)}, s32[]{:S(2)}) async-start(s8[6291456]{0:T(1024)(128)(4,1)} %bitcast.2), calls=%async_computation.1 | async-start | bytes 4194304
  4.4 17.6 %slice-start.3 = ((s8[6291456]{0:T(1024)(128)(4,1)}), s8[2097152]{0:T(1024)(128)(4,1)S(1)}, s32[]{:S(2)}) async-start(s8[6291456]{0:T(1024)(128)(4,1)} %bitcast.4), calls=%async_computation.3 | async-start | bytes 4194304
  4.4 14.9 %collective-permute-start.1 = (bf16[576,128]{1,0:T(8,128)(2,1)S(1)}, bf16[576,128]{1,0:T(8,128)(2,1)S(1)}, u32[]{:S(2)}, u32[]{:S(2)}) collective-permute-start(bf16[576,128]{1,0:T(8,128)(2,1)S(1)} %get-tuple-element.47), channel_id=1, source_target_pairs={{0,8},{1,11},{2,10},{3,9},{4,12},{5,15},{6,14},{7,13},{8,0},{9,3},... | collective-permute-start | bytes 442376 | tf_op jit(solution)/shard_map/ppermute | solution.py:499
  8.4 10.8 %collective-permute-start.3 = (bf16[576,128]{1,0:T(8,128)(2,1)S(1)}, bf16[576,128]{1,0:T(8,128)(2,1)S(1)}, u32[]{:S(2)}, u32[]{:S(2)}) collective-permute-start(bf16[576,128]{1,0:T(8,128)(2,1)S(1)} %get-tuple-element.49), channel_id=1, source_target_pairs={{0,4},{1,7},{2,6},{3,5},{4,0},{5,3},{6,2},{7,1},{8,12},{9,15},{10,... | collective-permute-start | bytes 442376 | tf_op jit(solution)/shard_map/ppermute | solution.py:499
  10.0 6.1 %collective-permute-start.4 = (bf16[288,128]{1,0:T(8,128)(2,1)S(1)}, bf16[288,128]{1,0:T(8,128)(2,1)S(1)}, u32[]{:S(2)}, u32[]{:S(2)}) collective-permute-start(bf16[288,128]{1,0:T(8,128)(2,1)S(1)} %get-tuple-element.50), channel_id=1, source_target_pairs={{0,2},{2,0},{4,6},{6,4},{8,10},{10,8},{12,14},{14,12},{1,3},{3,1},... | collective-permute-start | bytes 221192 | tf_op jit(solution)/shard_map/ppermute | solution.py:504
  11.5 7.8 %collective-permute-start.2 = (bf16[288,128]{1,0:T(8,128)(2,1)S(1)}, bf16[288,128]{1,0:T(8,128)(2,1)S(1)}, u32[]{:S(2)}, u32[]{:S(2)}) collective-permute-start(bf16[288,128]{1,0:T(8,128)(2,1)S(1)} %get-tuple-element.48), channel_id=1, source_target_pairs={{0,12},{1,15},{2,14},{3,13},{4,8},{5,11},{6,10},{7,9},{8,4},{9,7},... | collective-permute-start | bytes 221192 | tf_op jit(solution)/shard_map/ppermute | solution.py:499
  19.3 2.6 %collective-permute-start.5 = (bf16[1152,128]{1,0:T(8,128)(2,1)S(1)}, bf16[1152,128]{1,0:T(8,128)(2,1)S(1)}, u32[]{:S(2)}, u32[]{:S(2)}) collective-permute-start(bf16[1152,128]{1,0:T(8,128)(2,1)S(1)} %shard_map.112.x_sent), channel_id=1, source_target_pairs={{0,1},{1,0},{2,3},{3,2},{4,5},{5,4},{6,7},{7,6},{8,9},{9,8},{10,11... | collective-permute-start | bytes 884744 | tf_op jit(solution)/shard_map/ppermute | solution.py:508
  19.4 7.1 %slice-start.4 = ((s8[6291456]{0:T(1024)(128)(4,1)}), s8[4194304]{0:T(1024)(128)(4,1)S(1)}, s32[]{:S(2)}) async-start(s8[6291456]{0:T(1024)(128)(4,1)} %bitcast.6), calls=%async_computation.4 | async-start | bytes 8388608
  19.4 7.1 %slice-start.5 = ((s8[6291456]{0:T(1024)(128)(4,1)}), s8[2097152]{0:T(1024)(128)(4,1)S(1)}, s32[]{:S(2)}) async-start(s8[6291456]{0:T(1024)(128)(4,1)} %bitcast.6), calls=%async_computation.5 | async-start | bytes 4194304
  19.4 7.0 %collective-permute-start.8 = (bf16[288,128]{1,0:T(8,128)(2,1)S(1)}, bf16[288,128]{1,0:T(8,128)(2,1)S(1)}, u32[]{:S(2)}, u32[]{:S(2)}) collective-permute-start(bf16[288,128]{1,0:T(8,128)(2,1)S(1)} %get-tuple-element.57), channel_id=1, source_target_pairs={{0,12},{1,15},{2,14},{3,13},{4,8},{5,11},{6,10},{7,9},{8,4},{9,7},... | collective-permute-start | bytes 221192 | tf_op jit(solution)/shard_map/ppermute | solution.py:499
  26.4 2.1 %collective-permute-start.9 = (bf16[1152,128]{1,0:T(8,128)(2,1)S(1)}, bf16[1152,128]{1,0:T(8,128)(2,1)S(1)}, u32[]{:S(2)}, u32[]{:S(2)}) collective-permute-start(bf16[1152,128]{1,0:T(8,128)(2,1)S(1)} %shard_map.115.g_sent), channel_id=1, source_target_pairs={{0,1},{1,0},{2,3},{3,2},{4,5},{5,4},{6,7},{7,6},{8,9},{9,8},{10,11... | collective-permute-start | bytes 884744 | tf_op jit(solution)/shard_map/ppermute | solution.py:508
  28.0 8.2 %collective-permute-start.6 = (bf16[720,128]{1,0:T(8,128)(2,1)S(1)}, bf16[720,128]{1,0:T(8,128)(2,1)S(1)}, u32[]{:S(2)}, u32[]{:S(2)}) collective-permute-start(bf16[720,128]{1,0:T(8,128)(2,1)S(1)} %get-tuple-element.55), channel_id=1, source_target_pairs={{0,1},{1,0},{2,3},{3,2},{4,5},{5,4},{6,7},{7,6},{8,9},{9,8},{10,11... | collective-permute-start | bytes 552968 | tf_op jit(solution)/shard_map/ppermute | solution.py:508
  33.4 4.0 %collective-permute-start.10 = (bf16[720,128]{1,0:T(8,128)(2,1)S(1)}, bf16[720,128]{1,0:T(8,128)(2,1)S(1)}, u32[]{:S(2)}, u32[]{:S(2)}) collective-permute-start(bf16[720,128]{1,0:T(8,128)(2,1)S(1)} %get-tuple-element.64), channel_id=1, source_target_pairs={{0,1},{1,0},{2,3},{3,2},{4,5},{5,4},{6,7},{7,6},{8,9},{9,8},{10,11... | collective-permute-start | bytes 552968 | tf_op jit(solution)/shard_map/ppermute | solution.py:508
  33.5 2.7 %collective-permute-start.7 = (bf16[432,128]{1,0:T(8,128)(2,1)S(1)}, bf16[432,128]{1,0:T(8,128)(2,1)S(1)}, u32[]{:S(2)}, u32[]{:S(2)}) collective-permute-start(bf16[432,128]{1,0:T(8,128)(2,1)S(1)} %get-tuple-element.56), channel_id=1, source_target_pairs={{0,1},{1,0},{2,3},{3,2},{4,5},{5,4},{6,7},{7,6},{8,9},{9,8},{10,11... | collective-permute-start | bytes 331784 | tf_op jit(solution)/shard_map/ppermute | solution.py:508
  36.1 1.4 %collective-permute-start.11 = (bf16[432,128]{1,0:T(8,128)(2,1)S(1)}, bf16[432,128]{1,0:T(8,128)(2,1)S(1)}, u32[]{:S(2)}, u32[]{:S(2)}) collective-permute-start(bf16[432,128]{1,0:T(8,128)(2,1)S(1)} %get-tuple-element.65), channel_id=1, source_target_pairs={{0,1},{1,0},{2,3},{3,2},{4,5},{5,4},{6,7},{7,6},{8,9},{9,8},{10,11... | collective-permute-start | bytes 331784 | tf_op jit(solution)/shard_map/ppermute | solution.py:508
  37.6 14.0 %collective-permute-start.12 = (bf16[576,128]{1,0:T(8,128)(2,1)S(1)}, bf16[576,128]{1,0:T(8,128)(2,1)S(1)}, u32[]{:S(2)}, u32[]{:S(2)}) collective-permute-start(bf16[576,128]{1,0:T(8,128)(2,1)S(1)} %get-tuple-element.66), channel_id=1, source_target_pairs={{0,8},{1,11},{2,10},{3,9},{4,12},{5,15},{6,14},{7,13},{8,0},{9,3},... | collective-permute-start | bytes 442376 | tf_op jit(solution)/shard_map/ppermute | solution.py:499
  40.4 11.3 %collective-permute-start.13 = (bf16[576,128]{1,0:T(8,128)(2,1)S(1)}, bf16[576,128]{1,0:T(8,128)(2,1)S(1)}, u32[]{:S(2)}, u32[]{:S(2)}) collective-permute-start(bf16[576,128]{1,0:T(8,128)(2,1)S(1)} %get-tuple-element.67), channel_id=1, source_target_pairs={{0,12},{1,15},{2,14},{3,13},{4,8},{5,11},{6,10},{7,9},{8,4},{9,7},... | collective-permute-start | bytes 442376 | tf_op jit(solution)/shard_map/ppermute | solution.py:499
  41.2 12.3 %collective-permute-start.14 = (bf16[576,128]{1,0:T(8,128)(2,1)S(1)}, bf16[576,128]{1,0:T(8,128)(2,1)S(1)}, u32[]{:S(2)}, u32[]{:S(2)}) collective-permute-start(bf16[576,128]{1,0:T(8,128)(2,1)S(1)} %get-tuple-element.68), channel_id=1, source_target_pairs={{0,4},{1,7},{2,6},{3,5},{4,0},{5,3},{6,2},{7,1},{8,12},{9,15},{10,... | collective-permute-start | bytes 442376 | tf_op jit(solution)/shard_map/ppermute | solution.py:499
  41.2 10.1 %collective-permute-start.15 = (bf16[288,128]{1,0:T(8,128)(2,1)S(1)}, bf16[288,128]{1,0:T(8,128)(2,1)S(1)}, u32[]{:S(2)}, u32[]{:S(2)}) collective-permute-start(bf16[288,128]{1,0:T(8,128)(2,1)S(1)} %get-tuple-element.69), channel_id=1, source_target_pairs={{0,2},{2,0},{4,6},{6,4},{8,10},{10,8},{12,14},{14,12},{1,3},{3,1},... | collective-permute-start | bytes 221192 | tf_op jit(solution)/shard_map/ppermute | solution.py:504
  53.6 1.5 %collective-permute-start.16 = (bf16[864,128]{1,0:T(8,128)(2,1)S(1)}, bf16[864,128]{1,0:T(8,128)(2,1)S(1)}, u32[]{:S(2)}, u32[]{:S(2)}) collective-permute-start(bf16[864,128]{1,0:T(8,128)(2,1)S(1)} %shard_map.120), channel_id=1, source_target_pairs={{0,1},{1,0},{2,3},{3,2},{4,5},{5,4},{6,7},{7,6},{8,9},{9,8},{10,11... | collective-permute-start | bytes 663560 | tf_op jit(solution)/shard_map/ppermute | solution.py:508

commit v9 on v8

--- a/solution.py
+++ b/solution.py
@@ -346,7 +346,7 @@
 
 def forward_kernel(devices, subs, step, x_sent, x_swapped, w_gate, w_up, x_full, gate, up, hidden, scratch):
     full_rows(devices, subs, scratch, x_sent, x_swapped, x_full)
-    for cols in pieces_of(gate.shape[1], step):
+    for cols in pieces_of(gate.shape[1], 768):
         gate_low = dot(x_full[...], w_gate[0, :, cols]).astype(jnp.bfloat16)
         up_low = dot(x_full[...], w_up[0, :, cols]).astype(jnp.bfloat16)
         gate[:, cols] = gate_low
@@ -394,8 +394,7 @@
     _, other = half_starts(subs * LANES)
     full_rows(devices, subs, scratch, g_sent, g_swapped, g_full)
 
-    def pull(i, carry):
-        cols = chunk(i, step)
+    for cols in pieces_of(gate.shape[1], 768):
         low = contract_cols(g_full[...], w_down[0, cols, :]).astype(jnp.bfloat16)
         grad_hidden = low.astype(jnp.float32)
         value = gate[:, cols].astype(jnp.float32)
@@ -404,9 +403,6 @@
             grad_hidden * up[:, cols].astype(jnp.float32) * sig * (1.0 + value * (1.0 - sig))
         ).astype(jnp.bfloat16)
         pre_up[:, cols] = (grad_hidden * value * sig).astype(jnp.bfloat16)
-        return carry
-
-    lax.fori_loop(0, gate.shape[1] // step, pull, 0)
     term = input_term(step, pre_gate, pre_up, w_gate, w_up, other)
     halves_of_output(devices, subs, step, scratch, False, term, keep_other, send_other)
 
@@ -438,58 +434,54 @@
     written,
     flipped,
     turned,
+    both,
     tall,
     wide,
     tall_sems,
     wide_sems,
 ):
-    written[...] = jnp.zeros_like(written)
     width, lanes = x.shape[1], hidden.shape[1]
     count = width // step
+    written[...] = jnp.zeros_like(written)
     flipped[...] = flip(hidden[...]).astype(flipped.dtype)
-
-    def wide_copy(i, slot):
-        return pltpu.make_async_copy(wide.at[slot], grad_down.at[0, :, chunk(i, step)], wide_sems.at[slot])
-
-    def tall_copy(which, out, i, slot):
-        return pltpu.make_async_copy(tall.at[which, slot], out.at[0, chunk(i, step), :], tall_sems.at[which, slot])
+    both[:, :lanes] = pre_gate[...]
+    both[:, lanes:] = pre_up[...]
+
+    def wide_copy(i):
+        return pltpu.make_async_copy(wide.at[i], grad_down.at[0, :, chunk(i, step)], wide_sems.at[i])
+
+    def tall_copy(which, i):
+        out = (grad_gate, grad_up)[which]
+        return pltpu.make_async_copy(tall.at[which, i], out.at[0, chunk(i, step), :], tall_sems.at[which, i])
 
     def down(i, carry):
-        slot = i % 2
-
-        @pl.when(i >= 2)
-        def _():
-            wide_copy(i - 2, slot).wait()
-
-        for cut in pieces_of(step, 256):
-            right = g[:, chunk(i, step)][:, cut]
-            for high in pieces_of(lanes, 256):
-                wide[slot, high, cut] = dot(flipped[high, :], right).astype(wide.dtype)
-        wide_copy(i, slot).start()
+        right = g[:, chunk(i, step)]
+        for high in pieces_of(lanes, 128):
+            wide[i, high, :] = dot(flipped[high, :], right).astype(wide.dtype)
+        wide_copy(i).start()
         return carry
 
     lax.fori_loop(0, count, down, 0)
 
     def inputs(i, carry):
-        slot = i % 2
         turned[...] = flip(x[:, chunk(i, step)]).astype(turned.dtype)
-        for which, (right, out) in enumerate(((pre_gate, grad_gate), (pre_up, grad_up))):
-
-            @pl.when(i >= 2)
-            def _():
-                tall_copy(which, out, i - 2, slot).wait()
-
-            for cut in pieces_of(lanes, 256):
-                for high in pieces_of(step, 256):
-                    tall[which, slot, high, cut] = dot(turned[high, :], right[:, cut]).astype(tall.dtype)
-            tall_copy(which, out, i, slot).start()
+        for cut in pieces_of(2 * lanes, 512):
+            for high in pieces_of(step, 128):
+                value = dot(turned[high, :], both[:, cut]).astype(tall.dtype)
+                split = max(0, min(lanes, cut.stop) - cut.start)
+                if split:
+                    tall[0, i, high, cut.start : cut.start + split] = value[:, :split]
+                if split < cut.stop - cut.start:
+                    tall[1, i, high, cut.start + split - lanes : cut.stop - lanes] = value[:, split:]
+        tall_copy(0, i).start()
+        tall_copy(1, i).start()
         return carry
 
     lax.fori_loop(0, count, inputs, 0)
-    for i in range(max(0, count - 2), count):
-        wide_copy(i, i % 2).wait()
-        tall_copy(0, grad_gate, i, i % 2).wait()
-        tall_copy(1, grad_up, i, i % 2).wait()
+    for i in range(count):
+        wide_copy(i).wait()
+        tall_copy(0, i).wait()
+        tall_copy(1, i).wait()
 
 
 def exchange(blocks, masks, devices):
@@ -524,7 +516,7 @@
     size = capacity * subs
     count = devices // 2 - 1
     spread_scratch = [pltpu.VMEM((devices * size, LANES), full)]
-    step = 256
+    step = 512 if sub_width % 512 == 0 else LANES
     half_flops = 2 * rows * width * lanes // 2
 
     def lines(number, dtype=low):
@@ -613,7 +605,7 @@
     )
     returned = exchange(leaving, masks, devices)
     back = exchange_near(back, devices)
-    cut = 1024 if width % 1024 == 0 else width
+    cut = 512 if width % 512 == 0 else width
     grad_gate, grad_up, grad_down, written = call(
         functools.partial(gradient_kernel, cut),
         [jax.ShapeDtypeStruct(w.shape, low) for w in weights] + [vmem((8, LANES), full)],
@@ -622,14 +614,15 @@
         scratch=[
             pltpu.VMEM((lanes, rows), low),
             pltpu.VMEM((cut, rows), low),
-            pltpu.VMEM((2, 2, cut, lanes), low),
-            pltpu.VMEM((2, lanes, cut), low),
-            pltpu.SemaphoreType.DMA((2, 2)),
-            pltpu.SemaphoreType.DMA((2,)),
+            pltpu.VMEM((rows, 2 * lanes), low),
+            pltpu.VMEM((2, width // cut, cut, lanes), low),
+            pltpu.VMEM((width // cut, lanes, cut), low),
+            pltpu.SemaphoreType.DMA((2, width // cut)),
+            pltpu.SemaphoreType.DMA((width // cut,)),
         ],
         flops=6 * half_flops,
         traffic=sum(w.size * 2 for w in weights),
-        limit=32,
+        limit=40,
     )
     (sharing,) = call(functools.partial(share_kernel, size), [lines(2 * count)], (*returned, back, written))
     out_tokens, grad_tokens = call(

time: 56.9 us -> 57.3 us (level)
  Pallas kernels: 24.2 us -> 24.9 us
    pallas_call x12, Pallas kernels: 24.2 us -> 24.9 us  [call(): pl.pallas_call(kernel, out_shape=tuple(out_shape), in_specs=[pl.BlockSpec...]
  transfers between devices with their start and end apart: 17 -> 17, of which waited for: 8 -> 7; matrix products, arithmetic and copies ran while one was open for 0% -> 0% of each run, Pallas kernels for 36% -> 37%
where the time goes in v9:
time: 57.3 us; the launch traced here: 57.2 us
  Pallas kernels  24.9 us (43%)
  starting transfers between devices  16.6 us (29%)
  waiting for transfers between devices  14.9 us (26%)
  between operations  0.8 us (1%)
    pallas_call x12, Pallas kernels, call(): pl.pallas_call(kernel, out_shape=tuple(out_shape), in_specs=[pl.BlockSpec...  24.9 us
    ppermute x7, starting transfers between devices, exchange(): arrived.append(lax.ppermute(block, ('expert', 'ffn'), pairs))  12 us
    ppermute x7, waiting for transfers between devices, exchange(): arrived.append(lax.ppermute(block, ('expert', 'ffn'), pairs))  6.8 us
    ppermute x2, waiting for transfers between devices, exchange_near(): return lax.ppermute(block, 'expert', [(i, i ^ 1) for i in range(devices)])  4.38 us
    ppermute x8, waiting for transfers between devices, swap(): return lax.ppermute(value, 'ffn', [(0, 1), (1, 0)])  3.73 us
    ppermute x2, starting transfers between devices, exchange_near(): return lax.ppermute(block, 'expert', [(i, i ^ 1) for i in range(devices)])  2.48 us
    ppermute x8, starting transfers between devices, swap(): return lax.ppermute(value, 'ffn', [(0, 1), (1, 0)])  2.09 us
  transfers between devices with their start and end apart: 17, of which 7 were waited for; matrix products, arithmetic and copies ran while one was open for 0% of the time, Pallas kernels for 37%

profile of v9, /device:TPU:0, one launch (start us, length us, event | category | flops | bytes accessed | tf_op | source)
XLA Modules:
  0.0 57.2 jit_solution(11722213417932756062)
XLA Ops:
  0.7 2.1 %shard_map.110 = (bf16[432,128]{1,0:T(8,128)(2,1)S(1)}, bf16[432,128]{1,0:T(8,128)(2,1)S(1)}, bf16[288,128]{1,0:T(8,128)(2,1)S(1)}, bf16[288,128]{1,0:T(8,128)(2...) custom-call(s32[8,128]{1,0:T(8,128)} %bitcast.8, f32[8,128]{1,0:T(8,128)} %bitcast.9, ...), custom_call_target="tpu_custom_call" | custom-call | bytes 1048576 | tf_op jit(solution)/shard_map/pallas_call | solution.py:132
  2.7 0.5 collective-permute-start
  3.3 1.1 %collective-permute-done.swapped = bf16[864,128]{1,0:T(8,128)(2,1)S(1)} collective-permute-done((bf16[864,128]{1,0:T(8,128)(2,1)S(1)}, bf16[864,128]{1,0:T(8,128)(2,1)S(1)}, u32[]{:S(2)}, u32[]{:S(2)}) %collective-permute-start) | collective-permute-done | bytes 221216 | tf_op jit(solution)/shard_map/ppermute | solution.py:500
  4.4 4.0 %collective-permute-start.1 = (bf16[576,128]{1,0:T(8,128)(2,1)S(1)}, bf16[576,128]{1,0:T(8,128)(2,1)S(1)}, u32[]{:S(2)}, u32[]{:S(2)}) collective-permute-start(bf16[576,128]{1,0:T(8,128)(2,1)S(1)} %get-tuple-element.47), channel_id=1, source_target_pairs={{0,8},{1,11},{2,10},{3,9},{4,12},{5,15},{6,14},{7,13},{8,0},{9,3},... | collective-permute-start | bytes 442376 | tf_op jit(solution)/shard_map/ppermute | solution.py:491
  8.4 1.6 %collective-permute-start.3 = (bf16[576,128]{1,0:T(8,128)(2,1)S(1)}, bf16[576,128]{1,0:T(8,128)(2,1)S(1)}, u32[]{:S(2)}, u32[]{:S(2)}) collective-permute-start(bf16[576,128]{1,0:T(8,128)(2,1)S(1)} %get-tuple-element.49), channel_id=1, source_target_pairs={{0,4},{1,7},{2,6},{3,5},{4,0},{5,3},{6,2},{7,1},{8,12},{9,15},{10,... | collective-permute-start | bytes 442376 | tf_op jit(solution)/shard_map/ppermute | solution.py:491
  10.0 1.5 %collective-permute-start.4 = (bf16[288,128]{1,0:T(8,128)(2,1)S(1)}, bf16[288,128]{1,0:T(8,128)(2,1)S(1)}, u32[]{:S(2)}, u32[]{:S(2)}) collective-permute-start(bf16[288,128]{1,0:T(8,128)(2,1)S(1)} %get-tuple-element.50), channel_id=1, source_target_pairs={{0,2},{2,0},{4,6},{6,4},{8,10},{10,8},{12,14},{14,12},{1,3},{3,1},... | collective-permute-start | bytes 221192 | tf_op jit(solution)/shard_map/ppermute | solution.py:496
  11.5 0.2 collective-permute-start.2
  11.7 4.4 %collective-permute-done.4.refs_3_ = bf16[288,128]{1,0:T(8,128)(2,1)S(1)} collective-permute-done((bf16[288,128]{1,0:T(8,128)(2,1)S(1)}, bf16[288,128]{1,0:T(8,128)(2,1)S(1)}, u32[]{:S(2)}, u32[]{:S(2)}) %collective-permute-start.4) | collective-permute-done | bytes 73760 | tf_op jit(solution)/shard_map/ppermute | solution.py:496
  16.1 3.2 %collective-permute-done.2.refs_1_ = bf16[288,128]{1,0:T(8,128)(2,1)S(1)} collective-permute-done((bf16[288,128]{1,0:T(8,128)(2,1)S(1)}, bf16[288,128]{1,0:T(8,128)(2,1)S(1)}, u32[]{:S(2)}, u32[]{:S(2)}) %collective-permute-start.2) | collective-permute-done | bytes 73760 | tf_op jit(solution)/shard_map/ppermute | solution.py:491
  19.3 0.1 collective-permute-start.5
  19.4 2.5 %collective-permute-start.8 = (bf16[288,128]{1,0:T(8,128)(2,1)S(1)}, bf16[288,128]{1,0:T(8,128)(2,1)S(1)}, u32[]{:S(2)}, u32[]{:S(2)}) collective-permute-start(bf16[288,128]{1,0:T(8,128)(2,1)S(1)} %get-tuple-element.57), channel_id=1, source_target_pairs={{0,12},{1,15},{2,14},{3,13},{4,8},{5,11},{6,10},{7,9},{8,4},{9,7},... | collective-permute-start | bytes 221192 | tf_op jit(solution)/shard_map/ppermute | solution.py:491
  22.0 2.7 %shard_map.113 = (bf16[72,4096]{1,0:T(8,128)(2,1)S(1)}, bf16[72,768]{1,0:T(8,128)(2,1)S(1)}, bf16[72,768]{1,0:T(8,128)(2,1)S(1)}, bf16[72,768]{1,0:T(8,128)(2,1)S(1)}) custom-call(bf16[1152,128]{1,0:T(8,128)(2,1)S(1)} %shard_map.112.x_sent, bf16[1152,128]{1,0:T(8,128)(2,1)S(1)} %collective-permute-done.5.x_swapped, bf16[1,4096,768]{2,1,0:T(8,128)(2,1)S(1)} %bitcast.3, ...), custom_call_target="tpu_custom_call" | custom-call | flops 905969664 | tf_op jit(solution)/shard_map/pallas_call | solution.py:132
  24.7 1.7 %collective-permute-done.8.refs_1_ = bf16[288,128]{1,0:T(8,128)(2,1)S(1)} collective-permute-done((bf16[288,128]{1,0:T(8,128)(2,1)S(1)}, bf16[288,128]{1,0:T(8,128)(2,1)S(1)}, u32[]{:S(2)}, u32[]{:S(2)}) %collective-permute-start.8) | collective-permute-done | bytes 73760 | tf_op jit(solution)/shard_map/ppermute | solution.py:491
  26.4 0.1 collective-permute-start.9
  26.5 1.4 %shard_map.114 = (f32[720,128]{1,0:T(8,128)S(1)}, f32[432,128]{1,0:T(8,128)S(1)}, bf16[432,128]{1,0:T(8,128)(2,1)S(1)}, bf16[720,128]{1,0:T(8,128)(2,1)S(1)}) custom-call(bf16[72,768]{1,0:T(8,128)(2,1)S(1)} %get-tuple-element.52.hidden.refs_5_, bf16[1,768,4096]{2,1,0:T(8,128)(2,1)S(1)} %bitcast.7), custom_call_target="tpu_custom_call" | custom-call | flops 452984832 | tf_op jit(solution)/shard_map/pallas_call | solution.py:132
  27.9 0.5 collective-permute-start.6
  28.4 5.4 %shard_map.116 = (bf16[72,4096]{1,0:T(8,128)(2,1)S(1)}, bf16[72,768]{1,0:T(8,128)(2,1)S(1)}, bf16[72,768]{1,0:T(8,128)(2,1)S(1)}, f32[432,128]{1,0:T(8,128)S(1)}, bf16[720,128]{1,0:T(8,128)(2,1)S(1)}) custom-call(bf16[1152,128]{1,0:T(8,128)(2,1)S(1)} %shard_map.115.g_sent, bf16[1152,128]{1,0:T(8,128)(2,1)S(1)} %collective-permute-done.9.g_swapped, ...), custom_call_target="tpu_custom_call" | custom-call | flops 905969664 | tf_op jit(solution)/shard_map/pallas_call | solution.py:132
  33.8 0.1 collective-permute-start.10
  33.9 0.4 collective-permute-start.7
  34.4 2.1 %shard_map.117 = (f32[720,128]{1,0:T(8,128)S(1)}, bf16[432,128]{1,0:T(8,128)(2,1)S(1)}) custom-call(bf16[72,768]{1,0:T(8,128)(2,1)S(1)} %get-tuple-element.60.pre_gate, bf16[72,768]{1,0:T(8,128)(2,1)S(1)} %get-tuple-element.61.pre_up, bf16[1,4096,768]{2,1,0:T(8,128)(2,1)S(1)} %bitcast.3, bf16[1,4096,768]{2,1,0:T(8,128)(2,1)S(1)} %bitcast.5), custom_call_target="tpu_custom_call" | custom-call | flops 452984832 | tf_op jit(solution)/shard_map/pallas_call | solution.py:132
  36.5 0.1 collective-permute-start.11
  36.6 1.2 %collective-permute-done.11.refs_7_ = bf16[432,128]{1,0:T(8,128)(2,1)S(1)} collective-permute-done((bf16[432,128]{1,0:T(8,128)(2,1)S(1)}, bf16[432,128]{1,0:T(8,128)(2,1)S(1)}, u32[]{:S(2)}, u32[]{:S(2)}) %collective-permute-start.11) | collective-permute-done | bytes 110624 | tf_op jit(solution)/shard_map/ppermute | solution.py:500
  37.9 0.1 shard_map.118
  38.0 2.8 %collective-permute-start.12 = (bf16[576,128]{1,0:T(8,128)(2,1)S(1)}, bf16[576,128]{1,0:T(8,128)(2,1)S(1)}, u32[]{:S(2)}, u32[]{:S(2)}) collective-permute-start(bf16[576,128]{1,0:T(8,128)(2,1)S(1)} %get-tuple-element.66), channel_id=1, source_target_pairs={{0,8},{1,11},{2,10},{3,9},{4,12},{5,15},{6,14},{7,13},{8,0},{9,3},... | collective-permute-start | bytes 442376 | tf_op jit(solution)/shard_map/ppermute | solution.py:491
  40.8 0.9 %collective-permute-start.13 = (bf16[576,128]{1,0:T(8,128)(2,1)S(1)}, bf16[576,128]{1,0:T(8,128)(2,1)S(1)}, u32[]{:S(2)}, u32[]{:S(2)}) collective-permute-start(bf16[576,128]{1,0:T(8,128)(2,1)S(1)} %get-tuple-element.67), channel_id=1, source_target_pairs={{0,12},{1,15},{2,14},{3,13},{4,8},{5,11},{6,10},{7,9},{8,4},{9,7},... | collective-permute-start | bytes 442376 | tf_op jit(solution)/shard_map/ppermute | solution.py:491
  41.6 1.0 %collective-permute-start.15 = (bf16[288,128]{1,0:T(8,128)(2,1)S(1)}, bf16[288,128]{1,0:T(8,128)(2,1)S(1)}, u32[]{:S(2)}, u32[]{:S(2)}) collective-permute-start(bf16[288,128]{1,0:T(8,128)(2,1)S(1)} %get-tuple-element.69), channel_id=1, source_target_pairs={{0,2},{2,0},{4,6},{6,4},{8,10},{10,8},{12,14},{14,12},{1,3},{3,1},... | collective-permute-start | bytes 221192 | tf_op jit(solution)/shard_map/ppermute | solution.py:496
  42.6 9.4 %shard_map.119 = (bf16[1,4096,768]{2,1,0:T(8,128)(2,1)}, bf16[1,4096,768]{2,1,0:T(8,128)(2,1)}, bf16[1,768,4096]{2,1,0:T(8,128)(2,1)}, f32[8,128]{1,0:T(8,128)S(1)}) custom-call(bf16[72,4096]{1,0:T(8,128)(2,1)S(1)} %get-tuple-element.71.x, bf16[72,4096]{1,0:T(8,128)(2,1)S(1)} %get-tuple-element.72.g, bf16[72,768]{1,0:T(8,128)(2,1)S(1)} %get-tuple-element.52.hidden.refs_5_, ...), custom_call_target="tpu_custom_call" | custom-call | flops 1358954496 | bytes 18874368 | tf_op jit(solution)/shard_map/pallas_call | solution.py:132
  52.0 0.0 collective-permute-done.12.refs_0_
  52.1 1.9 %collective-permute-done.14.refs_2_ = bf16[576,128]{1,0:T(8,128)(2,1)S(1)} collective-permute-done((bf16[576,128]{1,0:T(8,128)(2,1)S(1)}, bf16[576,128]{1,0:T(8,128)(2,1)S(1)}, u32[]{:S(2)}, u32[]{:S(2)}) %collective-permute-start.14) | collective-permute-done | bytes 147488 | tf_op jit(solution)/shard_map/ppermute | solution.py:491
  54.0 0.2 collective-permute-start.16
  54.2 1.4 %collective-permute-done.16.refs_5_ = bf16[864,128]{1,0:T(8,128)(2,1)S(1)} collective-permute-done((bf16[864,128]{1,0:T(8,128)(2,1)S(1)}, bf16[864,128]{1,0:T(8,128)(2,1)S(1)}, u32[]{:S(2)}, u32[]{:S(2)}) %collective-permute-start.16) | collective-permute-done | bytes 221216 | tf_op jit(solution)/shard_map/ppermute | solution.py:500
  55.5 1.6 %shard_map.121 = (bf16[128,2048]{1,0:T(8,128)(2,1)}, bf16[128,2048]{1,0:T(8,128)(2,1)}) custom-call(bf16[72,128]{1,0:T(8,128)(2,1)S(1)} %get-tuple-element.42.place, f32[72,128]{1,0:T(8,128)S(1)} %get-tuple-element.43.refs_5_.mix, bf16[576,128]{1,0:T(8,128)(2,1)S(1)} %collective-permute-done.12.refs_0_, ...), custom_call_target="tpu_custom_call" | custom-call | bytes 2097152 | tf_op jit(solution)/shard_map/pallas_call | solution.py:132
  (29 shorter events, 0.1 us)
Async XLA Ops:
  0.6 21.3 %slice-start = ((s8[6291456]{0:T(1024)(128)(4,1)}), s8[4194304]{0:T(1024)(128)(4,1)S(1)}, s32[]{:S(2)}) async-start(s8[6291456]{0:T(1024)(128)(4,1)} %bitcast.2), calls=%async_computation | async-start | bytes 8388608
  0.6 21.3 %slice-start.2 = ((s8[6291456]{0:T(1024)(128)(4,1)}), s8[4194304]{0:T(1024)(128)(4,1)S(1)}, s32[]{:S(2)}) async-start(s8[6291456]{0:T(1024)(128)(4,1)} %bitcast.4), calls=%async_computation.2 | async-start | bytes 8388608
  2.7 1.6 %collective-permute-start = (bf16[864,128]{1,0:T(8,128)(2,1)S(1)}, bf16[864,128]{1,0:T(8,128)(2,1)S(1)}, u32[]{:S(2)}, u32[]{:S(2)}) collective-permute-start(bf16[864,128]{1,0:T(8,128)(2,1)S(1)} %get-tuple-element.46), channel_id=1, source_target_pairs={{0,1},{1,0},{2,3},{3,2},{4,5},{5,4},{6,7},{7,6},{8,9},{9,8},{10,11... | collective-permute-start | bytes 663560 | tf_op jit(solution)/shard_map/ppermute | solution.py:500
  4.4 17.6 %slice-start.1 = ((s8[6291456]{0:T(1024)(128)(4,1)}), s8[2097152]{0:T(1024)(128)(4,1)S(1)}, s32[]{:S(2)}) async-start(s8[6291456]{0:T(1024)(128)(4,1)} %bitcast.2), calls=%async_computation.1 | async-start | bytes 4194304
  4.4 17.6 %slice-start.3 = ((s8[6291456]{0:T(1024)(128)(4,1)}), s8[2097152]{0:T(1024)(128)(4,1)S(1)}, s32[]{:S(2)}) async-start(s8[6291456]{0:T(1024)(128)(4,1)} %bitcast.4), calls=%async_computation.3 | async-start | bytes 4194304
  4.4 14.9 %collective-permute-start.1 = (bf16[576,128]{1,0:T(8,128)(2,1)S(1)}, bf16[576,128]{1,0:T(8,128)(2,1)S(1)}, u32[]{:S(2)}, u32[]{:S(2)}) collective-permute-start(bf16[576,128]{1,0:T(8,128)(2,1)S(1)} %get-tuple-element.47), channel_id=1, source_target_pairs={{0,8},{1,11},{2,10},{3,9},{4,12},{5,15},{6,14},{7,13},{8,0},{9,3},... | collective-permute-start | bytes 442376 | tf_op jit(solution)/shard_map/ppermute | solution.py:491
  8.4 10.8 %collective-permute-start.3 = (bf16[576,128]{1,0:T(8,128)(2,1)S(1)}, bf16[576,128]{1,0:T(8,128)(2,1)S(1)}, u32[]{:S(2)}, u32[]{:S(2)}) collective-permute-start(bf16[576,128]{1,0:T(8,128)(2,1)S(1)} %get-tuple-element.49), channel_id=1, source_target_pairs={{0,4},{1,7},{2,6},{3,5},{4,0},{5,3},{6,2},{7,1},{8,12},{9,15},{10,... | collective-permute-start | bytes 442376 | tf_op jit(solution)/shard_map/ppermute | solution.py:491
  10.0 6.1 %collective-permute-start.4 = (bf16[288,128]{1,0:T(8,128)(2,1)S(1)}, bf16[288,128]{1,0:T(8,128)(2,1)S(1)}, u32[]{:S(2)}, u32[]{:S(2)}) collective-permute-start(bf16[288,128]{1,0:T(8,128)(2,1)S(1)} %get-tuple-element.50), channel_id=1, source_target_pairs={{0,2},{2,0},{4,6},{6,4},{8,10},{10,8},{12,14},{14,12},{1,3},{3,1},... | collective-permute-start | bytes 221192 | tf_op jit(solution)/shard_map/ppermute | solution.py:496
  11.5 7.8 %collective-permute-start.2 = (bf16[288,128]{1,0:T(8,128)(2,1)S(1)}, bf16[288,128]{1,0:T(8,128)(2,1)S(1)}, u32[]{:S(2)}, u32[]{:S(2)}) collective-permute-start(bf16[288,128]{1,0:T(8,128)(2,1)S(1)} %get-tuple-element.48), channel_id=1, source_target_pairs={{0,12},{1,15},{2,14},{3,13},{4,8},{5,11},{6,10},{7,9},{8,4},{9,7},... | collective-permute-start | bytes 221192 | tf_op jit(solution)/shard_map/ppermute | solution.py:491
  19.3 2.6 %collective-permute-start.5 = (bf16[1152,128]{1,0:T(8,128)(2,1)S(1)}, bf16[1152,128]{1,0:T(8,128)(2,1)S(1)}, u32[]{:S(2)}, u32[]{:S(2)}) collective-permute-start(bf16[1152,128]{1,0:T(8,128)(2,1)S(1)} %shard_map.112.x_sent), channel_id=1, source_target_pairs={{0,1},{1,0},{2,3},{3,2},{4,5},{5,4},{6,7},{7,6},{8,9},{9,8},{10,11... | collective-permute-start | bytes 884744 | tf_op jit(solution)/shard_map/ppermute | solution.py:500
  19.4 7.1 %slice-start.4 = ((s8[6291456]{0:T(1024)(128)(4,1)}), s8[4194304]{0:T(1024)(128)(4,1)S(1)}, s32[]{:S(2)}) async-start(s8[6291456]{0:T(1024)(128)(4,1)} %bitcast.6), calls=%async_computation.4 | async-start | bytes 8388608
  19.4 7.1 %slice-start.5 = ((s8[6291456]{0:T(1024)(128)(4,1)}), s8[2097152]{0:T(1024)(128)(4,1)S(1)}, s32[]{:S(2)}) async-start(s8[6291456]{0:T(1024)(128)(4,1)} %bitcast.6), calls=%async_computation.5 | async-start | bytes 4194304
  19.4 7.0 %collective-permute-start.8 = (bf16[288,128]{1,0:T(8,128)(2,1)S(1)}, bf16[288,128]{1,0:T(8,128)(2,1)S(1)}, u32[]{:S(2)}, u32[]{:S(2)}) collective-permute-start(bf16[288,128]{1,0:T(8,128)(2,1)S(1)} %get-tuple-element.57), channel_id=1, source_target_pairs={{0,12},{1,15},{2,14},{3,13},{4,8},{5,11},{6,10},{7,9},{8,4},{9,7},... | collective-permute-start | bytes 221192 | tf_op jit(solution)/shard_map/ppermute | solution.py:491
  26.4 2.0 %collective-permute-start.9 = (bf16[1152,128]{1,0:T(8,128)(2,1)S(1)}, bf16[1152,128]{1,0:T(8,128)(2,1)S(1)}, u32[]{:S(2)}, u32[]{:S(2)}) collective-permute-start(bf16[1152,128]{1,0:T(8,128)(2,1)S(1)} %shard_map.115.g_sent), channel_id=1, source_target_pairs={{0,1},{1,0},{2,3},{3,2},{4,5},{5,4},{6,7},{7,6},{8,9},{9,8},{10,11... | collective-permute-start | bytes 884744 | tf_op jit(solution)/shard_map/ppermute | solution.py:500
  27.9 8.8 %collective-permute-start.6 = (bf16[720,128]{1,0:T(8,128)(2,1)S(1)}, bf16[720,128]{1,0:T(8,128)(2,1)S(1)}, u32[]{:S(2)}, u32[]{:S(2)}) collective-permute-start(bf16[720,128]{1,0:T(8,128)(2,1)S(1)} %get-tuple-element.55), channel_id=1, source_target_pairs={{0,1},{1,0},{2,3},{3,2},{4,5},{5,4},{6,7},{7,6},{8,9},{9,8},{10,11... | collective-permute-start | bytes 552968 | tf_op jit(solution)/shard_map/ppermute | solution.py:500
  33.8 4.1 %collective-permute-start.10 = (bf16[720,128]{1,0:T(8,128)(2,1)S(1)}, bf16[720,128]{1,0:T(8,128)(2,1)S(1)}, u32[]{:S(2)}, u32[]{:S(2)}) collective-permute-start(bf16[720,128]{1,0:T(8,128)(2,1)S(1)} %get-tuple-element.64), channel_id=1, source_target_pairs={{0,1},{1,0},{2,3},{3,2},{4,5},{5,4},{6,7},{7,6},{8,9},{9,8},{10,11... | collective-permute-start | bytes 552968 | tf_op jit(solution)/shard_map/ppermute | solution.py:500
  33.9 2.7 %collective-permute-start.7 = (bf16[432,128]{1,0:T(8,128)(2,1)S(1)}, bf16[432,128]{1,0:T(8,128)(2,1)S(1)}, u32[]{:S(2)}, u32[]{:S(2)}) collective-permute-start(bf16[432,128]{1,0:T(8,128)(2,1)S(1)} %get-tuple-element.56), channel_id=1, source_target_pairs={{0,1},{1,0},{2,3},{3,2},{4,5},{5,4},{6,7},{7,6},{8,9},{9,8},{10,11... | collective-permute-start | bytes 331784 | tf_op jit(solution)/shard_map/ppermute | solution.py:500
  36.5 1.4 %collective-permute-start.11 = (bf16[432,128]{1,0:T(8,128)(2,1)S(1)}, bf16[432,128]{1,0:T(8,128)(2,1)S(1)}, u32[]{:S(2)}, u32[]{:S(2)}) collective-permute-start(bf16[432,128]{1,0:T(8,128)(2,1)S(1)} %get-tuple-element.65), channel_id=1, source_target_pairs={{0,1},{1,0},{2,3},{3,2},{4,5},{5,4},{6,7},{7,6},{8,9},{9,8},{10,11... | collective-permute-start | bytes 331784 | tf_op jit(solution)/shard_map/ppermute | solution.py:500
  38.0 14.0 %collective-permute-start.12 = (bf16[576,128]{1,0:T(8,128)(2,1)S(1)}, bf16[576,128]{1,0:T(8,128)(2,1)S(1)}, u32[]{:S(2)}, u32[]{:S(2)}) collective-permute-start(bf16[576,128]{1,0:T(8,128)(2,1)S(1)} %get-tuple-element.66), channel_id=1, source_target_pairs={{0,8},{1,11},{2,10},{3,9},{4,12},{5,15},{6,14},{7,13},{8,0},{9,3},... | collective-permute-start | bytes 442376 | tf_op jit(solution)/shard_map/ppermute | solution.py:491
  40.8 11.3 %collective-permute-start.13 = (bf16[576,128]{1,0:T(8,128)(2,1)S(1)}, bf16[576,128]{1,0:T(8,128)(2,1)S(1)}, u32[]{:S(2)}, u32[]{:S(2)}) collective-permute-start(bf16[576,128]{1,0:T(8,128)(2,1)S(1)} %get-tuple-element.67), channel_id=1, source_target_pairs={{0,12},{1,15},{2,14},{3,13},{4,8},{5,11},{6,10},{7,9},{8,4},{9,7},... | collective-permute-start | bytes 442376 | tf_op jit(solution)/shard_map/ppermute | solution.py:491
  41.6 12.3 %collective-permute-start.14 = (bf16[576,128]{1,0:T(8,128)(2,1)S(1)}, bf16[576,128]{1,0:T(8,128)(2,1)S(1)}, u32[]{:S(2)}, u32[]{:S(2)}) collective-permute-start(bf16[576,128]{1,0:T(8,128)(2,1)S(1)} %get-tuple-element.68), channel_id=1, source_target_pairs={{0,4},{1,7},{2,6},{3,5},{4,0},{5,3},{6,2},{7,1},{8,12},{9,15},{10,... | collective-permute-start | bytes 442376 | tf_op jit(solution)/shard_map/ppermute | solution.py:491
  41.6 10.4 %collective-permute-start.15 = (bf16[288,128]{1,0:T(8,128)(2,1)S(1)}, bf16[288,128]{1,0:T(8,128)(2,1)S(1)}, u32[]{:S(2)}, u32[]{:S(2)}) collective-permute-start(bf16[288,128]{1,0:T(8,128)(2,1)S(1)} %get-tuple-element.69), channel_id=1, source_target_pairs={{0,2},{2,0},{4,6},{6,4},{8,10},{10,8},{12,14},{14,12},{1,3},{3,1},... | collective-permute-start | bytes 221192 | tf_op jit(solution)/shard_map/ppermute | solution.py:496
  54.0 1.5 %collective-permute-start.16 = (bf16[864,128]{1,0:T(8,128)(2,1)S(1)}, bf16[864,128]{1,0:T(8,128)(2,1)S(1)}, u32[]{:S(2)}, u32[]{:S(2)}) collective-permute-start(bf16[864,128]{1,0:T(8,128)(2,1)S(1)} %shard_map.120), channel_id=1, source_target_pairs={{0,1},{1,0},{2,3},{3,2},{4,5},{5,4},{6,7},{7,6},{8,9},{9,8},{10,11... | collective-permute-start | bytes 663560 | tf_op jit(solution)/shard_map/ppermute | solution.py:500

commit v10 on v7

--- a/solution.py
+++ b/solution.py
@@ -161,11 +161,15 @@
 
 
 def even_masks(count):
-    return [*range(count // 2, count, 2), *range(2, count // 2, 2)]
+    return [*range(count // 2 + 2, count, 2), *range(2, count // 2, 2)]
+
+
+def both_masks(count):
+    return [count // 2, count // 2 + 1, 1, 0]
 
 
 def route_kernel(devices, capacity, subs, ids_in, weight_in, x_in, g_in, *refs):
-    (*outs, theirs, place_out, mix_out, scratch, ids, weight, x, g, sems) = refs
+    mine, theirs, *both, place_out, mix_out, scratch, ids, weight, x, g, sems = refs
     pairs = ((ids_in, ids), (weight_in, weight), (x_in, x), (g_in, g))
     copies = [pltpu.make_async_copy(src, dst, sems.at[i]) for i, (src, dst) in enumerate(pairs)]
     for copy in copies:
@@ -174,7 +178,8 @@
     rows = devices * capacity
     core = lax.axis_index("ffn")
     masks = even_masks(devices)
-    masks = [mask + core for mask in masks] + [mask + 1 - core for mask in masks] + [1, 0]
+    count = len(masks)
+    masks = [mask + core for mask in masks] + [mask + 1 - core for mask in masks] + both_masks(devices)
     order = lax.broadcasted_iota(jnp.int32, (devices, tok), 0)
     bits = jnp.zeros((devices, tok), jnp.int32)
     for p, mask in enumerate(masks):
@@ -203,47 +208,46 @@
     place_out[...] = low
     mix_out[...] = row_weight
     size = capacity * subs
-    count = devices // 2 - 1
-
-    def write(mine, near, here, at):
+
+    def write(at):
         def block(p):
-            return scratch[p * size : (p + 1) * size, :].astype(mine.dtype)
+            return scratch[p * size : (p + 1) * size, :].astype(theirs.dtype)
 
         for j in range(count):
-            part(mine, j * size, size)[...] = block(j)
-            part(theirs, (at + j) * size, size)[...] = block(count + j)
-        near[...] = block(2 * count)
-        here[...] = block(2 * count + 1)
+            part(mine, 2 * j * size + at, size)[...] = block(j)
+            part(theirs, 2 * j * size + at, size)[...] = block(count + j)
+        for i, out in enumerate(both):
+            part(out, at, size)[...] = block(2 * count + i)
 
     copies[2].wait()
     for sub in range(subs):
         spread_lanes(scratch, sub, subs, dot(low, x[:, lanes_of(sub)]))
-    write(*outs[:3], 0)
+    write(0)
     copies[3].wait()
     for sub in range(subs):
         spread_lanes(scratch, sub, subs, dot(low, g[:, lanes_of(sub)]) * row_weight)
-    write(*outs[3:], count)
-
-
-def pack_kernel(size, x_mine, g_mine, swapped, *outs):
-    count = len(outs) // 2
-    for i, out in enumerate(outs):
-        mine = x_mine if i < count else g_mine
-        part(out, 0, size)[...] = part(mine, i % count * size, size)[...]
-        part(out, size, size)[...] = part(swapped, i * size, size)[...]
-
-
-def gather_kernel(size, *refs):
-    blocks, (near, here, _, out) = refs[:-4], refs[-4:]
-    for j, block in enumerate(blocks):
-        part(out, 2 * j * size, 2 * size)[...] = block[...]
-    part(out, 2 * len(blocks) * size, size)[...] = near[...]
-    part(out, (2 * len(blocks) + 1) * size, size)[...] = here[...]
+    write(size)
+
+
+def pack_kernel(size, mine, swapped, *outs):
+    for j, out in enumerate(outs):
+        part(out, 0, 2 * size)[...] = part(mine, 2 * j * size, 2 * size)[...]
+        part(out, 2 * size, 2 * size)[...] = part(swapped, 2 * j * size, 2 * size)[...]
+
+
+def gather_kernel(size, count, *refs):
+    blocks, both, (x_out, g_out) = refs[:count], refs[count:-2], refs[-2:]
+    for at, out in ((0, x_out), (size, g_out)):
+        for j, block in enumerate(blocks):
+            part(out, 2 * j * size, size)[...] = part(block, at, size)[...]
+            part(out, (2 * j + 1) * size, size)[...] = part(block, 2 * size + at, size)[...]
+        for i, block in enumerate(both):
+            part(out, (2 * count + i) * size, size)[...] = part(block, at, size)[...]
 
 
 def full_rows(devices, subs, scratch, own_sent, other_sent, out):
     size = own_sent.shape[0] // devices
-    count = devices // 2 - 1
+    count = len(even_masks(devices))
     own, other = half_starts(out.shape[1] // 2)
     first, second, last = range(0, 2 * count, 2), range(1, 2 * count, 2), range(2 * count, devices)
     layouts = (
@@ -268,47 +272,58 @@
         send[count * size :, :] = rest.astype(send.dtype)
 
 
-def leave_kernel(size, *refs):
+def leave_kernel(size, count, *refs):
     terms, outs = (refs[:4], refs[4:8]), refs[8:]
-    count = len(outs) - 2
     for at, (keep_own, keep_other, came_own, came_other) in zip((0, size), terms):
 
         def own(p):
             total = part(keep_own, p * size, size)[...] + part(came_own, p * size, size)[...].astype(jnp.float32)
             return total.astype(outs[0].dtype)
 
+        for p, out in enumerate(outs):
+            part(out, at, size)[...] = own(p)
         for j, out in enumerate(outs[:count]):
-            part(out, at, size)[...] = own(j)
             total = part(keep_other, j * size, size)[...] + part(came_other, j * size, size)[...].astype(jnp.float32)
             part(out, 2 * size + at, size)[...] = total.astype(out.dtype)
-        part(outs[count], at, size)[...] = own(count)
-        part(outs[count + 1], at, size)[...] = own(count + 1)
-
-
-def share_kernel(size, *refs):
-    blocks, (_, _, out) = refs[:-3], refs[-3:]
-    for j, block in enumerate(blocks):
-        part(out, 2 * j * size, 2 * size)[...] = part(block, 2 * size, 2 * size)[...]
+
+
+def share_kernel(size, count, *refs):
+    for j, block in enumerate(refs[:count]):
+        part(refs[-1], 2 * j * size, 2 * size)[...] = part(block, 2 * size, 2 * size)[...]
+
+
+def token_sums(subs, place, mix, scratch, rows, blocks, out, before):
+    size = scratch.shape[0] // len(blocks)
+    for p, block in enumerate(blocks):
+        here = slice(p * size, (p + 1) * size)
+        scratch[here, :] = jnp.zeros((size, LANES), jnp.float32) if block is None else block[...].astype(jnp.float32)
+    for sub in range(subs):
+        value = scratch[pl.ds(sub, rows.shape[0], stride=subs), :]
+        if mix is not None:
+            value = value * mix[...]
+        rows[:, lanes_of(sub)] = value.astype(rows.dtype)
+    for cut in pieces_of(subs * LANES, 512):
+        total = contract_rows(place[...], rows[:, cut])
+        if before is not None:
+            total = total + before[:, cut]
+        out[:, cut] = total.astype(out.dtype)
 
 
 def join_kernel(count, subs, place, mix, *refs):
-    blocks, (near, here, shared, out_tokens, grad_tokens, scratch) = refs[:count], refs[count:]
-    size = near.shape[0] // 2
-
-    def layout(at):
+    blocks, both, (out_sum, grad_sum, scratch, rows) = refs[:count], refs[count:-4], refs[-4:]
+    size = both[0].shape[0] // 2
+    for at, scale, out in ((0, mix, out_sum), (size, None, grad_sum)):
         first = [part(block, at, size) for block in blocks]
-        second = [part(shared, 2 * j * size + at, size) for j in range(count)]
-        return first + second + [part(near, at, size), part(here, at, size)]
-
-    def put_out(sub, value):
-        low = (value * mix[...]).astype(jnp.bfloat16)
-        out_tokens[:, lanes_of(sub)] = contract_rows(place[...], low).astype(out_tokens.dtype)
-
-    def put_grad(sub, value):
-        grad_tokens[:, lanes_of(sub)] = contract_rows(place[...], value.astype(jnp.bfloat16)).astype(grad_tokens.dtype)
-
-    blocks_to_rows(scratch, layout(0), put_out, subs)
-    blocks_to_rows(scratch, layout(size), put_grad, subs)
+        last = [part(block, at, size) for block in both]
+        token_sums(subs, place, scale, scratch, rows, first + [None] * count + last, out, None)
+
+
+def finish_kernel(count, subs, place, mix, shared, out_sum, grad_sum, out_tokens, grad_tokens, scratch, rows):
+    size = shared.shape[0] // (2 * count)
+    rest = scratch.shape[0] // size - 2 * count
+    for at, scale, before, out in ((0, mix, out_sum, out_tokens), (size, None, grad_sum, grad_tokens)):
+        blocks = [part(shared, 2 * j * size + at, size) for j in range(count)]
+        token_sums(subs, place, scale, scratch, rows, [None] * count + blocks + [None] * rest, out, before)
 
 
 def half_starts(half_width):
@@ -332,7 +347,7 @@
         value = term(at)
         for i in range(step // LANES):
             spread_lanes(scratch, at // LANES + i, subs, value[:, lanes_of(i)])
-    split_terms(devices // 2 - 1, size, scratch, own_half, keep, send)
+    split_terms(len(even_masks(devices)), size, scratch, own_half, keep, send)
 
 
 def forward_kernel(devices, subs, step, x_sent, x_swapped, w_gate, w_up, x_full, gate, up, hidden, scratch):
@@ -483,12 +498,19 @@
         tall_copy(1, grad_up, i, i % 2).wait()
 
 
-def exchange(blocks, near, devices):
+def exchange(blocks, masks, devices):
     arrived = []
-    for block, mask in zip(blocks, even_masks(devices)):
+    for block, mask in zip(blocks, masks):
         pairs = [(2 * i + core, 2 * (i ^ (mask + core)) + core) for i in range(devices) for core in range(2)]
         arrived.append(lax.ppermute(block, ("expert", "ffn"), pairs))
-    return arrived, lax.ppermute(near, "expert", [(i, i ^ 1) for i in range(devices)])
+    return arrived
+
+
+def exchange_both(blocks, devices):
+    arrived = []
+    for block, mask in zip(blocks, both_masks(devices)):
+        arrived.append(lax.ppermute(block, "expert", [(i, i ^ mask) for i in range(devices)]) if mask else block)
+    return arrived
 
 
 def swap(value):
@@ -509,7 +531,8 @@
     subs = sub_width // LANES
     low, full = jnp.bfloat16, jnp.float32
     size = capacity * subs
-    count = devices // 2 - 1
+    masks = even_masks(devices)
+    count, shared_count = len(masks), len(both_masks(devices))
     spread_scratch = [pltpu.VMEM((devices * size, LANES), full)]
     step = 256
     half_flops = 2 * rows * width * lanes // 2
@@ -521,10 +544,11 @@
         return vmem((number * size, LANES), dtype)
 
     sources = (route_ids.T, route_weight.T, tokens, grad_out)
-    x_mine, x_near, x_here, g_mine, g_near, g_here, theirs, place, mix = call(
+    mine, theirs, *both, place, mix = call(
         functools.partial(route_kernel, devices, capacity, subs),
-        [lines(count), lines(1), lines(1)] * 2
-        + [lines(2 * count), jax.ShapeDtypeStruct((rows, tok_dev), low), jax.ShapeDtypeStruct((rows, LANES), full)],
+        [lines(2 * count)] * 2
+        + [lines(2)] * shared_count
+        + [jax.ShapeDtypeStruct((rows, tok_dev), low), jax.ShapeDtypeStruct((rows, LANES), full)],
         in_hbm(sources),
         in_spaces=[pl.ANY] * 4,
         scratch=spread_scratch
@@ -532,28 +556,25 @@
         + [pltpu.SemaphoreType.DMA((4,))],
         traffic=4 * tok_dev * sub_width,
     )
+    both = exchange_both(both, devices)
     packed = call(
-        functools.partial(pack_kernel, size),
-        [lines(2)] * (2 * count),
-        (x_mine, g_mine, swap(theirs)),
-        flops=24 * half_flops,
-    )
-    x_arrived, x_near = exchange(packed[:count], x_near, devices)
-    g_arrived, g_near = exchange(packed[count:], g_near, devices)
+        functools.partial(pack_kernel, size), [lines(4)] * count, (mine, swap(theirs)), flops=24 * half_flops
+    )
+    arrived = exchange(packed, masks, devices)
 
     weights = (gate_weight, up_weight, down_weight)
     w_gate, w_up, w_down = [pltpu.with_memory_space_constraint(w, pltpu.VMEM) for w in weights]
 
-    def gather(arrived, near, here, after):
-        return call(functools.partial(gather_kernel, size), [lines(devices)], (*arrived, near, here, after))[0]
-
-    x_sent = gather(x_arrived, x_near, x_here, mix)
+    x_sent, g_sent = call(
+        functools.partial(gather_kernel, size, count), [lines(devices)] * 2, (*arrived, *both)
+    )
     x_swapped = swap(x_sent)
+    g_swapped = swap(g_sent)
     terms = [
-        lines_in_vmem(count + 2, full),
+        lines_in_vmem(count + shared_count, full),
         lines_in_vmem(count, full),
         lines_in_vmem(count),
-        lines_in_vmem(count + 2),
+        lines_in_vmem(count + shared_count),
     ]
     x_full, gate, up, hidden = call(
         functools.partial(forward_kernel, devices, subs, step),
@@ -562,10 +583,8 @@
         scratch=spread_scratch,
         flops=4 * half_flops,
     )
-    g_sent = gather(g_arrived, g_near, g_here, hidden)
-    g_swapped = swap(g_sent)
     out_own, out_other, send_own, send_other = call(
-        functools.partial(output_kernel, devices, subs, step),
+        functools.partial(output_kernel, devices, subs, 2 * step),
         terms,
         (hidden, w_down),
         scratch=spread_scratch,
@@ -588,12 +607,13 @@
         flops=2 * half_flops,
     )
     dx_terms = (dx_own, dx_other, came_own, swap(send_own))
-    *leaving, near, here = call(
-        functools.partial(leave_kernel, size),
-        [lines(4)] * count + [lines(2)] * 2,
+    leaving = call(
+        functools.partial(leave_kernel, size, count),
+        [lines(4)] * count + [lines(2)] * shared_count,
         (*out_terms, *dx_terms),
     )
-    returned, near = exchange(leaving, near, devices)
+    returned = exchange(leaving[:count], masks, devices)
+    both = exchange_both(leaving[count:], devices)
     cut = 1024 if width % 1024 == 0 else width
     grad_gate, grad_up, grad_down, written = call(
         functools.partial(gradient_kernel, cut),
@@ -612,12 +632,23 @@
         traffic=sum(w.size * 2 for w in weights),
         limit=32,
     )
-    (sharing,) = call(functools.partial(share_kernel, size), [lines(2 * count)], (*returned, near, written))
+    (sharing,) = call(
+        functools.partial(share_kernel, size, count), [lines(2 * count)], (*returned, *both, written)
+    )
+    shared = swap(sharing)
+    rows_scratch = [pltpu.VMEM((rows, sub_width), low)]
+    sums = call(
+        functools.partial(join_kernel, count, subs),
+        [vmem((tok_dev, sub_width), full)] * 2,
+        (place, mix, *returned, *both),
+        scratch=spread_scratch + rows_scratch,
+        flops=4 * rows * tok_dev * sub_width,
+    )
     out_tokens, grad_tokens = call(
-        functools.partial(join_kernel, count, subs),
+        functools.partial(finish_kernel, count, subs),
         [jax.ShapeDtypeStruct((tok_dev, sub_width), low)] * 2,
-        (place, mix, *returned, near, here, swap(sharing)),
-        scratch=spread_scratch,
+        (place, mix, shared, *sums),
+        scratch=spread_scratch + rows_scratch,
         traffic=8 * tok_dev * sub_width,
     )
     return out_tokens, grad_tokens, grad_gate, grad_up, grad_down
@@ -627,7 +658,7 @@
     tokens, gate_weight = args[0], args[4]
     halves = lax.axis_size("ffn")
     devices = lax.axis_size("expert")
-    if halves == 2 and devices >= 4 and devices & (devices - 1) == 0 and tokens.shape[1] * halves == gate_weight.shape[1]:
+    if halves == 2 and devices >= 8 and devices & (devices - 1) == 0 and tokens.shape[1] * halves == gate_weight.shape[1]:
         return one_piece_shards(*args)
     return general_shards(*args)
 

time: 58.7 us -> 57.5 us (0.980)
  starting transfers between devices: 21 us -> 18.7 us
  Pallas kernels: 24.2 us -> 25 us
    ppermute x9 -> x4, starting transfers between devices: 14.1 us -> 7.57 us  [exchange(): arrived.append(lax.ppermute(block, ('expert', 'ffn'), pairs))]
    ppermute x3 -> x6, waiting for transfers between devices: 3.04 us -> 9.31 us  [exchange_both(): lax.ppermute(block, 'expert', [(i, i ^ mask) for i in range(devices)])]
    ppermute x9 -> x4, waiting for transfers between devices: 6.26 us -> 0.01 us  [exchange(): arrived.append(lax.ppermute(block, ('expert', 'ffn'), pairs))]
    ppermute x3 -> x6, starting transfers between devices: 3.8 us -> 8.77 us  [exchange_both(): lax.ppermute(block, 'expert', [(i, i ^ mask) for i in range(devices)])]
    pallas_call x12, Pallas kernels: 24.2 us -> 25 us  [call(): pl.pallas_call(kernel, out_shape=tuple(out_shape), in_specs=[pl.BlockSpec...]
    ppermute x8, starting transfers between devices: 3.07 us -> 2.36 us  [swap(): return lax.ppermute(value, 'ffn', [(0, 1), (1, 0)])]
  transfers between devices with their start and end apart: 20 -> 18, of which waited for: 9 -> 6; matrix products, arithmetic and copies ran while one was open for 0% -> 0% of each run, Pallas kernels for 35% -> 37%
where the time goes in v10:
time: 57.5 us; the launch traced here: 57.4 us
  Pallas kernels  25 us (43%)
  starting transfers between devices  18.7 us (33%)
  waiting for transfers between devices  12.8 us (22%)
  between operations  0.85 us (1%)
    pallas_call x12, Pallas kernels, call(): pl.pallas_call(kernel, out_shape=tuple(out_shape), in_specs=[pl.BlockSpec...  25 us
    ppermute x6, waiting for transfers between devices, exchange_both(): lax.ppermute(block, 'expert', [(i, i ^ mask) for i in range(devices)])  9.31 us
    ppermute x6, starting transfers between devices, exchange_both(): lax.ppermute(block, 'expert', [(i, i ^ mask) for i in range(devices)])  8.77 us
    ppermute x4, starting transfers between devices, exchange(): arrived.append(lax.ppermute(block, ('expert', 'ffn'), pairs))  7.57 us
    ppermute x8, waiting for transfers between devices, swap(): return lax.ppermute(value, 'ffn', [(0, 1), (1, 0)])  3.44 us
    ppermute x8, starting transfers between devices, swap(): return lax.ppermute(value, 'ffn', [(0, 1), (1, 0)])  2.36 us
  transfers between devices with their start and end apart: 18, of which 6 were waited for; matrix products, arithmetic and copies ran while one was open for 0% of the time, Pallas kernels for 37%

profile of v10, /device:TPU:0, one launch (start us, length us, event | category | flops | bytes accessed | tf_op | source)
XLA Modules:
  0.0 57.4 jit_solution(9665299940695075433)
XLA Ops:
  0.6 0.0 slice-start
  0.7 2.1 %shard_map.110 = (bf16[576,128]{1,0:T(8,128)(2,1)S(1)}, bf16[576,128]{1,0:T(8,128)(2,1)S(1)}, bf16[288,128]{1,0:T(8,128)(2,1)S(1)}, bf16[288,128]{1,0:T(8,128)(2...) custom-call(s32[8,128]{1,0:T(8,128)} %bitcast.8, ...), custom_call_target="tpu_custom_call" | custom-call | bytes 1048576 | tf_op jit(solution)/shard_map/pallas_call | solution.py:132
  2.7 0.5 collective-permute-start
  3.3 1.0 %collective-permute-done.swapped = bf16[576,128]{1,0:T(8,128)(2,1)S(1)} collective-permute-done((bf16[576,128]{1,0:T(8,128)(2,1)S(1)}, bf16[576,128]{1,0:T(8,128)(2,1)S(1)}, u32[]{:S(2)}, u32[]{:S(2)}) %collective-permute-start) | collective-permute-done | bytes 147488 | tf_op jit(solution)/shard_map/ppermute | solution.py:517
  4.3 5.0 %collective-permute-start.1 = (bf16[576,128]{1,0:T(8,128)(2,1)S(1)}, bf16[576,128]{1,0:T(8,128)(2,1)S(1)}, u32[]{:S(2)}, u32[]{:S(2)}) collective-permute-start(bf16[576,128]{1,0:T(8,128)(2,1)S(1)} %get-tuple-element.50), channel_id=1, source_target_pairs={{0,12},{1,15},{2,14},{3,13},{4,8},{5,11},{6,10},{7,9},{8,4},{9,7},... | collective-permute-start | bytes 442376 | tf_op jit(solution)/shard_map/ppermute | solution.py:505
  9.3 0.6 %collective-permute-start.3 = (bf16[288,128]{1,0:T(8,128)(2,1)S(1)}, bf16[288,128]{1,0:T(8,128)(2,1)S(1)}, u32[]{:S(2)}, u32[]{:S(2)}) collective-permute-start(bf16[288,128]{1,0:T(8,128)(2,1)S(1)} %get-tuple-element.52), channel_id=1, source_target_pairs={{0,8},{2,10},{4,12},{6,14},{8,0},{10,2},{12,4},{14,6},{1,9},{3,11}... | collective-permute-start | bytes 221192 | tf_op jit(solution)/shard_map/ppermute | solution.py:512
  10.0 3.2 %collective-permute-start.4 = (bf16[288,128]{1,0:T(8,128)(2,1)S(1)}, bf16[288,128]{1,0:T(8,128)(2,1)S(1)}, u32[]{:S(2)}, u32[]{:S(2)}) collective-permute-start(bf16[288,128]{1,0:T(8,128)(2,1)S(1)} %get-tuple-element.53), channel_id=1, source_target_pairs={{0,10},{2,8},{4,14},{6,12},{8,2},{10,0},{12,6},{14,4},{1,11},{3,9}... | collective-permute-start | bytes 221192 | tf_op jit(solution)/shard_map/ppermute | solution.py:512
  13.2 0.5 collective-permute-start.5
  13.7 7.5 %collective-permute-done.3.refs_2_ = bf16[288,128]{1,0:T(8,128)(2,1)S(1)} collective-permute-done((bf16[288,128]{1,0:T(8,128)(2,1)S(1)}, bf16[288,128]{1,0:T(8,128)(2,1)S(1)}, u32[]{:S(2)}, u32[]{:S(2)}) %collective-permute-start.3) | collective-permute-done | bytes 73760 | tf_op jit(solution)/shard_map/ppermute | solution.py:512
  21.3 1.8 %collective-permute-done.4.refs_3_ = bf16[288,128]{1,0:T(8,128)(2,1)S(1)} collective-permute-done((bf16[288,128]{1,0:T(8,128)(2,1)S(1)}, bf16[288,128]{1,0:T(8,128)(2,1)S(1)}, u32[]{:S(2)}, u32[]{:S(2)}) %collective-permute-start.4) | collective-permute-done | bytes 73760 | tf_op jit(solution)/shard_map/ppermute | solution.py:512
  23.1 0.1 collective-permute-start.6
  23.2 0.5 collective-permute-start.9
  23.7 1.1 %collective-permute-done.6.x_swapped = bf16[1152,128]{1,0:T(8,128)(2,1)S(1)} collective-permute-done((bf16[1152,128]{1,0:T(8,128)(2,1)S(1)}, bf16[1152,128]{1,0:T(8,128)(2,1)S(1)}, u32[]{:S(2)}, u32[]{:S(2)}) %collective-permute-start.6) | collective-permute-done | bytes 294944 | tf_op jit(solution)/shard_map/ppermute | solution.py:517
  24.8 2.7 %shard_map.113 = (bf16[72,4096]{1,0:T(8,128)(2,1)S(1)}, bf16[72,768]{1,0:T(8,128)(2,1)S(1)}, bf16[72,768]{1,0:T(8,128)(2,1)S(1)}, bf16[72,768]{1,0:T(8,128)(2,1)S(1)}) custom-call(bf16[1152,128]{1,0:T(8,128)(2,1)S(1)} %get-tuple-element.56.x_sent, bf16[1152,128]{1,0:T(8,128)(2,1)S(1)} %collective-permute-done.6.x_swapped, bf16[1,4096,768]{2,1,0:T(8,128)(2,1)S(1)} %bitcast.3, ...), custom_call_target="tpu_custom_call" | custom-call | flops 905969664 | tf_op jit(solution)/shard_map/pallas_call | solution.py:132
  27.5 1.4 %shard_map.114 = (f32[864,128]{1,0:T(8,128)S(1)}, f32[288,128]{1,0:T(8,128)S(1)}, bf16[288,128]{1,0:T(8,128)(2,1)S(1)}, bf16[864,128]{1,0:T(8,128)(2,1)S(1)}) custom-call(bf16[72,768]{1,0:T(8,128)(2,1)S(1)} %get-tuple-element.57.hidden, bf16[1,768,4096]{2,1,0:T(8,128)(2,1)S(1)} %bitcast.7), custom_call_target="tpu_custom_call" | custom-call | flops 452984832 | tf_op jit(solution)/shard_map/pallas_call | solution.py:132
  28.9 0.2 collective-permute-start.7
  29.1 4.9 %shard_map.115 = (bf16[72,4096]{1,0:T(8,128)(2,1)S(1)}, bf16[72,768]{1,0:T(8,128)(2,1)S(1)}, bf16[72,768]{1,0:T(8,128)(2,1)S(1)}, f32[288,128]{1,0:T(8,128)S(1)}, bf16[864,128]{1,0:T(8,128)(2,1)S(1)}) custom-call(bf16[1152,128]{1,0:T(8,128)(2,1)S(1)} %get-tuple-element.62.g_sent, bf16[1152,128]{1,0:T(8,128)(2,1)S(1)} %collective-permute-done.9.g_swapped, ...), custom_call_target="tpu_custom_call" | custom-call | flops 905969664 | tf_op jit(solution)/shard_map/pallas_call | solution.py:132
  34.0 0.4 collective-permute-start.10
  34.4 0.1 collective-permute-start.8
  34.6 2.1 %shard_map.116 = (f32[864,128]{1,0:T(8,128)S(1)}, bf16[288,128]{1,0:T(8,128)(2,1)S(1)}) custom-call(bf16[72,768]{1,0:T(8,128)(2,1)S(1)} %get-tuple-element.65.pre_gate, bf16[72,768]{1,0:T(8,128)(2,1)S(1)} %get-tuple-element.66.pre_up, bf16[1,4096,768]{2,1,0:T(8,128)(2,1)S(1)} %bitcast.3, bf16[1,4096,768]{2,1,0:T(8,128)(2,1)S(1)} %bitcast.5), custom_call_target="tpu_custom_call" | custom-call | flops 452984832 | tf_op jit(solution)/shard_map/pallas_call | solution.py:132
  36.7 0.4 collective-permute-start.11
  37.1 0.9 %collective-permute-done.11.refs_7_ = bf16[288,128]{1,0:T(8,128)(2,1)S(1)} collective-permute-done((bf16[288,128]{1,0:T(8,128)(2,1)S(1)}, bf16[288,128]{1,0:T(8,128)(2,1)S(1)}, u32[]{:S(2)}, u32[]{:S(2)}) %collective-permute-start.11) | collective-permute-done | bytes 73760 | tf_op jit(solution)/shard_map/ppermute | solution.py:517
  38.0 0.1 shard_map.117
  38.1 2.5 %collective-permute-start.12 = (bf16[576,128]{1,0:T(8,128)(2,1)S(1)}, bf16[576,128]{1,0:T(8,128)(2,1)S(1)}, u32[]{:S(2)}, u32[]{:S(2)}) collective-permute-start(bf16[576,128]{1,0:T(8,128)(2,1)S(1)} %get-tuple-element.71), channel_id=1, source_target_pairs={{0,12},{1,15},{2,14},{3,13},{4,8},{5,11},{6,10},{7,9},{8,4},{9,7},... | collective-permute-start | bytes 442376 | tf_op jit(solution)/shard_map/ppermute | solution.py:505
  40.7 1.9 %collective-permute-start.14 = (bf16[288,128]{1,0:T(8,128)(2,1)S(1)}, bf16[288,128]{1,0:T(8,128)(2,1)S(1)}, u32[]{:S(2)}, u32[]{:S(2)}) collective-permute-start(bf16[288,128]{1,0:T(8,128)(2,1)S(1)} %get-tuple-element.73), channel_id=1, source_target_pairs={{0,8},{2,10},{4,12},{6,14},{8,0},{10,2},{12,4},{14,6},{1,9},{3,11}... | collective-permute-start | bytes 221192 | tf_op jit(solution)/shard_map/ppermute | solution.py:512
  42.6 1.8 %collective-permute-start.15 = (bf16[288,128]{1,0:T(8,128)(2,1)S(1)}, bf16[288,128]{1,0:T(8,128)(2,1)S(1)}, u32[]{:S(2)}, u32[]{:S(2)}) collective-permute-start(bf16[288,128]{1,0:T(8,128)(2,1)S(1)} %get-tuple-element.74), channel_id=1, source_target_pairs={{0,10},{2,8},{4,14},{6,12},{8,2},{10,0},{12,6},{14,4},{1,11},{3,9}... | collective-permute-start | bytes 221192 | tf_op jit(solution)/shard_map/ppermute | solution.py:512
  44.4 0.7 %collective-permute-start.16 = (bf16[288,128]{1,0:T(8,128)(2,1)S(1)}, bf16[288,128]{1,0:T(8,128)(2,1)S(1)}, u32[]{:S(2)}, u32[]{:S(2)}) collective-permute-start(bf16[288,128]{1,0:T(8,128)(2,1)S(1)} %get-tuple-element.75), channel_id=1, source_target_pairs={{0,2},{2,0},{4,6},{6,4},{8,10},{10,8},{12,14},{14,12},{1,3},{3,1},... | collective-permute-start | bytes 221192 | tf_op jit(solution)/shard_map/ppermute | solution.py:512
  45.1 9.1 %shard_map.118 = (bf16[1,4096,768]{2,1,0:T(8,128)(2,1)}, bf16[1,4096,768]{2,1,0:T(8,128)(2,1)}, bf16[1,768,4096]{2,1,0:T(8,128)(2,1)}, f32[8,128]{1,0:T(8,128)S(1)}) custom-call(bf16[72,4096]{1,0:T(8,128)(2,1)S(1)} %get-tuple-element.77.x, bf16[72,4096]{1,0:T(8,128)(2,1)S(1)} %get-tuple-element.78.g, bf16[72,768]{1,0:T(8,128)(2,1)S(1)} %get-tuple-element.57.hidden, ...), custom_call_target="tpu_custom_call" | custom-call | flops 1358954496 | bytes 18874368 | tf_op jit(solution)/shard_map/pallas_call | solution.py:132
  54.2 0.1 collective-permute-start.17
  54.3 0.9 %shard_map.120 = (f32[128,2048]{1,0:T(8,128)S(1)}, f32[128,2048]{1,0:T(8,128)S(1)}) custom-call(bf16[72,128]{1,0:T(8,128)(2,1)S(1)} %get-tuple-element.46.place, f32[72,128]{1,0:T(8,128)S(1)} %get-tuple-element.47.mix, bf16[576,128]{1,0:T(8,128)(2,1)S(1)} %collective-permute-done.12.refs_0_, bf16[576,128]{1,0:T(8,128)(2,1)S(1)} %collective-permute-done.13.refs_1_, ...), custom_call_target="tpu_custom_call" | custom-call | flops 75497472 | tf_op jit(solution)/shard_map/pallas_call | solution.py:132
  55.2 0.4 collective-permute-done.17.shared
  55.7 1.7 %shard_map.121 = (bf16[128,2048]{1,0:T(8,128)(2,1)}, bf16[128,2048]{1,0:T(8,128)(2,1)}) custom-call(bf16[72,128]{1,0:T(8,128)(2,1)S(1)} %get-tuple-element.46.place, f32[72,128]{1,0:T(8,128)S(1)} %get-tuple-element.47.mix, bf16[576,128]{1,0:T(8,128)(2,1)S(1)} %collective-permute-done.17.shared, f32[128,2048]{1,0:T(8,128)S(1)} %get-tuple-element.80.out_sum, ...), custom_call_target="tpu_custom_call" | custom-call | bytes 2097152 | tf_op jit(solution)/shard_map/pallas_call | solution.py:132
  (31 shorter events, 0.1 us)
Async XLA Ops:
  0.6 24.1 %slice-start = ((s8[6291456]{0:T(1024)(128)(4,1)}), s8[4194304]{0:T(1024)(128)(4,1)S(1)}, s32[]{:S(2)}) async-start(s8[6291456]{0:T(1024)(128)(4,1)} %bitcast.2), calls=%async_computation | async-start | bytes 8388608
  0.6 24.1 %slice-start.2 = ((s8[6291456]{0:T(1024)(128)(4,1)}), s8[4194304]{0:T(1024)(128)(4,1)S(1)}, s32[]{:S(2)}) async-start(s8[6291456]{0:T(1024)(128)(4,1)} %bitcast.4), calls=%async_computation.2 | async-start | bytes 8388608
  2.7 1.5 %collective-permute-start = (bf16[576,128]{1,0:T(8,128)(2,1)S(1)}, bf16[576,128]{1,0:T(8,128)(2,1)S(1)}, u32[]{:S(2)}, u32[]{:S(2)}) collective-permute-start(bf16[576,128]{1,0:T(8,128)(2,1)S(1)} %get-tuple-element.49), channel_id=1, source_target_pairs={{0,1},{1,0},{2,3},{3,2},{4,5},{5,4},{6,7},{7,6},{8,9},{9,8},{10,11... | collective-permute-start | bytes 442376 | tf_op jit(solution)/shard_map/ppermute | solution.py:517
  4.3 20.5 %slice-start.1 = ((s8[6291456]{0:T(1024)(128)(4,1)}), s8[2097152]{0:T(1024)(128)(4,1)S(1)}, s32[]{:S(2)}) async-start(s8[6291456]{0:T(1024)(128)(4,1)} %bitcast.2), calls=%async_computation.1 | async-start | bytes 4194304
  4.3 20.5 %slice-start.3 = ((s8[6291456]{0:T(1024)(128)(4,1)}), s8[2097152]{0:T(1024)(128)(4,1)S(1)}, s32[]{:S(2)}) async-start(s8[6291456]{0:T(1024)(128)(4,1)} %bitcast.4), calls=%async_computation.3 | async-start | bytes 4194304
  4.3 18.7 %collective-permute-start.1 = (bf16[576,128]{1,0:T(8,128)(2,1)S(1)}, bf16[576,128]{1,0:T(8,128)(2,1)S(1)}, u32[]{:S(2)}, u32[]{:S(2)}) collective-permute-start(bf16[576,128]{1,0:T(8,128)(2,1)S(1)} %get-tuple-element.50), channel_id=1, source_target_pairs={{0,12},{1,15},{2,14},{3,13},{4,8},{5,11},{6,10},{7,9},{8,4},{9,7},... | collective-permute-start | bytes 442376 | tf_op jit(solution)/shard_map/ppermute | solution.py:505
  9.3 13.7 %collective-permute-start.2 = (bf16[576,128]{1,0:T(8,128)(2,1)S(1)}, bf16[576,128]{1,0:T(8,128)(2,1)S(1)}, u32[]{:S(2)}, u32[]{:S(2)}) collective-permute-start(bf16[576,128]{1,0:T(8,128)(2,1)S(1)} %get-tuple-element.51), channel_id=1, source_target_pairs={{0,4},{1,7},{2,6},{3,5},{4,0},{5,3},{6,2},{7,1},{8,12},{9,15},{10,... | collective-permute-start | bytes 442376 | tf_op jit(solution)/shard_map/ppermute | solution.py:505
  9.3 11.9 %collective-permute-start.3 = (bf16[288,128]{1,0:T(8,128)(2,1)S(1)}, bf16[288,128]{1,0:T(8,128)(2,1)S(1)}, u32[]{:S(2)}, u32[]{:S(2)}) collective-permute-start(bf16[288,128]{1,0:T(8,128)(2,1)S(1)} %get-tuple-element.52), channel_id=1, source_target_pairs={{0,8},{2,10},{4,12},{6,14},{8,0},{10,2},{12,4},{14,6},{1,9},{3,11}... | collective-permute-start | bytes 221192 | tf_op jit(solution)/shard_map/ppermute | solution.py:512
  10.0 13.1 %collective-permute-start.4 = (bf16[288,128]{1,0:T(8,128)(2,1)S(1)}, bf16[288,128]{1,0:T(8,128)(2,1)S(1)}, u32[]{:S(2)}, u32[]{:S(2)}) collective-permute-start(bf16[288,128]{1,0:T(8,128)(2,1)S(1)} %get-tuple-element.53), channel_id=1, source_target_pairs={{0,10},{2,8},{4,14},{6,12},{8,2},{10,0},{12,6},{14,4},{1,11},{3,9}... | collective-permute-start | bytes 221192 | tf_op jit(solution)/shard_map/ppermute | solution.py:512
  13.2 9.8 %collective-permute-start.5 = (bf16[288,128]{1,0:T(8,128)(2,1)S(1)}, bf16[288,128]{1,0:T(8,128)(2,1)S(1)}, u32[]{:S(2)}, u32[]{:S(2)}) collective-permute-start(bf16[288,128]{1,0:T(8,128)(2,1)S(1)} %get-tuple-element.54), channel_id=1, source_target_pairs={{0,2},{2,0},{4,6},{6,4},{8,10},{10,8},{12,14},{14,12},{1,3},{3,1},... | collective-permute-start | bytes 221192 | tf_op jit(solution)/shard_map/ppermute | solution.py:512
  23.1 1.6 %collective-permute-start.6 = (bf16[1152,128]{1,0:T(8,128)(2,1)S(1)}, bf16[1152,128]{1,0:T(8,128)(2,1)S(1)}, u32[]{:S(2)}, u32[]{:S(2)}) collective-permute-start(bf16[1152,128]{1,0:T(8,128)(2,1)S(1)} %get-tuple-element.56.x_sent), channel_id=1, source_target_pairs={{0,1},{1,0},{2,3},{3,2},{4,5},{5,4},{6,7},{7,6},{8,9},{9,8},{10,11... | collective-permute-start | bytes 884744 | tf_op jit(solution)/shard_map/ppermute | solution.py:517
  23.2 4.3 %slice-start.4 = ((s8[6291456]{0:T(1024)(128)(4,1)}), s8[4194304]{0:T(1024)(128)(4,1)S(1)}, s32[]{:S(2)}) async-start(s8[6291456]{0:T(1024)(128)(4,1)} %bitcast.6), calls=%async_computation.4 | async-start | bytes 8388608
  23.2 4.3 %slice-start.5 = ((s8[6291456]{0:T(1024)(128)(4,1)}), s8[2097152]{0:T(1024)(128)(4,1)S(1)}, s32[]{:S(2)}) async-start(s8[6291456]{0:T(1024)(128)(4,1)} %bitcast.6), calls=%async_computation.5 | async-start | bytes 4194304
  23.2 5.9 %collective-permute-start.9 = (bf16[1152,128]{1,0:T(8,128)(2,1)S(1)}, bf16[1152,128]{1,0:T(8,128)(2,1)S(1)}, u32[]{:S(2)}, u32[]{:S(2)}) collective-permute-start(bf16[1152,128]{1,0:T(8,128)(2,1)S(1)} %get-tuple-element.62.g_sent), channel_id=1, source_target_pairs={{0,1},{1,0},{2,3},{3,2},{4,5},{5,4},{6,7},{7,6},{8,9},{9,8},{10,11... | collective-permute-start | bytes 884744 | tf_op jit(solution)/shard_map/ppermute | solution.py:517
  28.9 9.1 %collective-permute-start.7 = (bf16[864,128]{1,0:T(8,128)(2,1)S(1)}, bf16[864,128]{1,0:T(8,128)(2,1)S(1)}, u32[]{:S(2)}, u32[]{:S(2)}) collective-permute-start(bf16[864,128]{1,0:T(8,128)(2,1)S(1)} %get-tuple-element.60), channel_id=1, source_target_pairs={{0,1},{1,0},{2,3},{3,2},{4,5},{5,4},{6,7},{7,6},{8,9},{9,8},{10,11... | collective-permute-start | bytes 663560 | tf_op jit(solution)/shard_map/ppermute | solution.py:517
  34.0 4.0 %collective-permute-start.10 = (bf16[864,128]{1,0:T(8,128)(2,1)S(1)}, bf16[864,128]{1,0:T(8,128)(2,1)S(1)}, u32[]{:S(2)}, u32[]{:S(2)}) collective-permute-start(bf16[864,128]{1,0:T(8,128)(2,1)S(1)} %get-tuple-element.69), channel_id=1, source_target_pairs={{0,1},{1,0},{2,3},{3,2},{4,5},{5,4},{6,7},{7,6},{8,9},{9,8},{10,11... | collective-permute-start | bytes 663560 | tf_op jit(solution)/shard_map/ppermute | solution.py:517
  34.4 2.7 %collective-permute-start.8 = (bf16[288,128]{1,0:T(8,128)(2,1)S(1)}, bf16[288,128]{1,0:T(8,128)(2,1)S(1)}, u32[]{:S(2)}, u32[]{:S(2)}) collective-permute-start(bf16[288,128]{1,0:T(8,128)(2,1)S(1)} %get-tuple-element.61), channel_id=1, source_target_pairs={{0,1},{1,0},{2,3},{3,2},{4,5},{5,4},{6,7},{7,6},{8,9},{9,8},{10,11... | collective-permute-start | bytes 221192 | tf_op jit(solution)/shard_map/ppermute | solution.py:517
  36.7 1.4 %collective-permute-start.11 = (bf16[288,128]{1,0:T(8,128)(2,1)S(1)}, bf16[288,128]{1,0:T(8,128)(2,1)S(1)}, u32[]{:S(2)}, u32[]{:S(2)}) collective-permute-start(bf16[288,128]{1,0:T(8,128)(2,1)S(1)} %get-tuple-element.70), channel_id=1, source_target_pairs={{0,1},{1,0},{2,3},{3,2},{4,5},{5,4},{6,7},{7,6},{8,9},{9,8},{10,11... | collective-permute-start | bytes 221192 | tf_op jit(solution)/shard_map/ppermute | solution.py:517
  38.1 16.1 %collective-permute-start.12 = (bf16[576,128]{1,0:T(8,128)(2,1)S(1)}, bf16[576,128]{1,0:T(8,128)(2,1)S(1)}, u32[]{:S(2)}, u32[]{:S(2)}) collective-permute-start(bf16[576,128]{1,0:T(8,128)(2,1)S(1)} %get-tuple-element.71), channel_id=1, source_target_pairs={{0,12},{1,15},{2,14},{3,13},{4,8},{5,11},{6,10},{7,9},{8,4},{9,7},... | collective-permute-start | bytes 442376 | tf_op jit(solution)/shard_map/ppermute | solution.py:505
  40.7 13.5 %collective-permute-start.13 = (bf16[576,128]{1,0:T(8,128)(2,1)S(1)}, bf16[576,128]{1,0:T(8,128)(2,1)S(1)}, u32[]{:S(2)}, u32[]{:S(2)}) collective-permute-start(bf16[576,128]{1,0:T(8,128)(2,1)S(1)} %get-tuple-element.72), channel_id=1, source_target_pairs={{0,4},{1,7},{2,6},{3,5},{4,0},{5,3},{6,2},{7,1},{8,12},{9,15},{10,... | collective-permute-start | bytes 442376 | tf_op jit(solution)/shard_map/ppermute | solution.py:505
  40.7 13.5 %collective-permute-start.14 = (bf16[288,128]{1,0:T(8,128)(2,1)S(1)}, bf16[288,128]{1,0:T(8,128)(2,1)S(1)}, u32[]{:S(2)}, u32[]{:S(2)}) collective-permute-start(bf16[288,128]{1,0:T(8,128)(2,1)S(1)} %get-tuple-element.73), channel_id=1, source_target_pairs={{0,8},{2,10},{4,12},{6,14},{8,0},{10,2},{12,4},{14,6},{1,9},{3,11}... | collective-permute-start | bytes 221192 | tf_op jit(solution)/shard_map/ppermute | solution.py:512
  42.6 11.6 %collective-permute-start.15 = (bf16[288,128]{1,0:T(8,128)(2,1)S(1)}, bf16[288,128]{1,0:T(8,128)(2,1)S(1)}, u32[]{:S(2)}, u32[]{:S(2)}) collective-permute-start(bf16[288,128]{1,0:T(8,128)(2,1)S(1)} %get-tuple-element.74), channel_id=1, source_target_pairs={{0,10},{2,8},{4,14},{6,12},{8,2},{10,0},{12,6},{14,4},{1,11},{3,9}... | collective-permute-start | bytes 221192 | tf_op jit(solution)/shard_map/ppermute | solution.py:512
  44.4 9.8 %collective-permute-start.16 = (bf16[288,128]{1,0:T(8,128)(2,1)S(1)}, bf16[288,128]{1,0:T(8,128)(2,1)S(1)}, u32[]{:S(2)}, u32[]{:S(2)}) collective-permute-start(bf16[288,128]{1,0:T(8,128)(2,1)S(1)} %get-tuple-element.75), channel_id=1, source_target_pairs={{0,2},{2,0},{4,6},{6,4},{8,10},{10,8},{12,14},{14,12},{1,3},{3,1},... | collective-permute-start | bytes 221192 | tf_op jit(solution)/shard_map/ppermute | solution.py:512
  54.2 1.4 %collective-permute-start.17 = (bf16[576,128]{1,0:T(8,128)(2,1)S(1)}, bf16[576,128]{1,0:T(8,128)(2,1)S(1)}, u32[]{:S(2)}, u32[]{:S(2)}) collective-permute-start(bf16[576,128]{1,0:T(8,128)(2,1)S(1)} %shard_map.119), channel_id=1, source_target_pairs={{0,1},{1,0},{2,3},{3,2},{4,5},{5,4},{6,7},{7,6},{8,9},{9,8},{10,11... | collective-permute-start | bytes 442376 | tf_op jit(solution)/shard_map/ppermute | solution.py:517

commit v11 on v8

--- a/solution.py
+++ b/solution.py
@@ -165,7 +165,7 @@
 
 
 def route_kernel(devices, capacity, subs, ids_in, weight_in, x_in, g_in, *refs):
-    x_mine, g_mine, near, here, theirs, place_out, mix_out, scratch, ids, weight, x, g, sems = refs
+    x_mine, g_mine, near, here, theirs, place_out, mix_out, place_other, mix_other, scratch, ids, weight, x, g, sems = refs
     pairs = ((ids_in, ids), (weight_in, weight), (x_in, x), (g_in, g))
     copies = [pltpu.make_async_copy(src, dst, sems.at[i]) for i, (src, dst) in enumerate(pairs)]
     for copy in copies:
@@ -191,19 +191,24 @@
     before = lax.broadcasted_iota(jnp.int32, (tok, tok), 0) < lax.broadcasted_iota(jnp.int32, (tok, tok), 1)
     slots = dot(member.astype(jnp.bfloat16), jnp.where(before, 1.0, 0.0).astype(jnp.bfloat16))
     target = jnp.where(member > 0, slots + capacity * order.astype(jnp.float32), -1.0)
-    row = lax.broadcasted_iota(jnp.int32, (rows, tok), 0).astype(jnp.float32)
-    place = jnp.zeros((rows, tok), jnp.float32)
-    mix = jnp.zeros((rows, tok), jnp.float32)
-    for p in range(devices):
-        equal = target[p : p + 1, :] == row
-        place = jnp.where(equal, 1.0, place)
-        mix = jnp.where(equal, mixing[p : p + 1, :], mix)
-    row_weight = jnp.broadcast_to(jnp.sum(mix, axis=1, keepdims=True), (rows, LANES))
-    low = place.astype(jnp.bfloat16)
+    count = devices // 2 - 1
+
+    def placed(first, number):
+        row = lax.broadcasted_iota(jnp.int32, (number, tok), 0).astype(jnp.float32) + first
+        place = jnp.zeros((number, tok), jnp.float32)
+        mix = jnp.zeros((number, tok), jnp.float32)
+        for p in range(devices):
+            equal = target[p : p + 1, :] == row
+            place = jnp.where(equal, 1.0, place)
+            mix = jnp.where(equal, mixing[p : p + 1, :], mix)
+        row_weight = jnp.broadcast_to(jnp.sum(mix, axis=1, keepdims=True), (number, LANES))
+        return place.astype(jnp.bfloat16), row_weight
+
+    low, row_weight = placed(0, rows)
     place_out[...] = low
     mix_out[...] = row_weight
+    place_other[...], mix_other[...] = placed(count * capacity, count * capacity)
     size = capacity * subs
-    count = devices // 2 - 1
 
     def write(mine, at):
         def block(p):
@@ -226,26 +231,18 @@
     write(g_mine, count)
 
 
-def pack_kernel(size, late, x_mine, g_mine, swapped, *outs):
-    count = len(outs) - len(late)
-
-    def put(out, at, mine, j, i):
-        part(out, at, size)[...] = part(mine, j * size, size)[...]
-        part(out, at + size, size)[...] = part(swapped, i * size, size)[...]
-
-    for j, out in enumerate(outs[:count]):
-        put(out, 0, x_mine, j, j)
-        if j not in late:
-            put(out, 2 * size, g_mine, j, count + j)
-    for j, out in zip(late, outs[count:]):
-        put(out, 0, g_mine, j, count + j)
+def pack_kernel(size, x_mine, g_mine, swapped, *outs):
+    count = len(outs)
+    for j, out in enumerate(outs):
+        for i, mine in enumerate((x_mine, g_mine)):
+            part(out, 2 * i * size, size)[...] = part(mine, j * size, size)[...]
+            part(out, (2 * i + 1) * size, size)[...] = part(swapped, (i * count + j) * size, size)[...]
 
 
 def gather_kernel(size, at, *refs):
-    blocks, (near, here, _, out) = refs[:-4], refs[-4:]
+    blocks, (near, here, out) = refs[:-3], refs[-3:]
     for j, block in enumerate(blocks):
-        start = block.shape[0] - 2 * size if at else 0
-        part(out, 2 * j * size, 2 * size)[...] = part(block, start, 2 * size)[...]
+        part(out, 2 * j * size, 2 * size)[...] = part(block, 2 * at, 2 * size)[...]
     part(out, 2 * len(blocks) * size, size)[...] = part(near, at, size)[...]
     part(out, (2 * len(blocks) + 1) * size, size)[...] = part(here, at, size)[...]
 
@@ -300,24 +297,50 @@
         part(out, 2 * j * size, 2 * size)[...] = part(block, 2 * size, 2 * size)[...]
 
 
+def token_sums(subs, place, mix, scratch, rows, blocks, put):
+    size = scratch.shape[0] // len(blocks)
+    for p, block in enumerate(blocks):
+        here = slice(p * size, (p + 1) * size)
+        scratch[here, :] = jnp.zeros((size, LANES), jnp.float32) if block is None else block[...].astype(jnp.float32)
+    for sub in range(subs):
+        value = scratch[pl.ds(sub, rows.shape[0], stride=subs), :]
+        if mix is not None:
+            value = value * mix[...]
+        rows[:, lanes_of(sub)] = value.astype(rows.dtype)
+    for cut in pieces_of(subs * LANES, 512):
+        put(cut, contract_rows(place[...], rows[:, cut]))
+
+
 def join_kernel(count, subs, place, mix, *refs):
-    blocks, (near, here, shared, out_tokens, grad_tokens, scratch) = refs[:count], refs[count:]
+    blocks, (near, here, out_sum, grad_sum, scratch, rows) = refs[:count], refs[count:]
     size = near.shape[0] // 2
-
-    def layout(at):
+    for at, scale, out in ((0, mix, out_sum), (size, None, grad_sum)):
+
+        def put(cut, total):
+            out[:, cut] = total
+
         first = [part(block, at, size) for block in blocks]
-        second = [part(shared, 2 * j * size + at, size) for j in range(count)]
-        return first + second + [part(near, at, size), part(here, at, size)]
-
-    def put_out(sub, value):
-        low = (value * mix[...]).astype(jnp.bfloat16)
-        out_tokens[:, lanes_of(sub)] = contract_rows(place[...], low).astype(out_tokens.dtype)
-
-    def put_grad(sub, value):
-        grad_tokens[:, lanes_of(sub)] = contract_rows(place[...], value.astype(jnp.bfloat16)).astype(grad_tokens.dtype)
-
-    blocks_to_rows(scratch, layout(0), put_out, subs)
-    blocks_to_rows(scratch, layout(size), put_grad, subs)
+        last = [part(near, at, size), part(here, at, size)]
+        token_sums(subs, place, scale, scratch, rows, first + [None] * count + last, put)
+
+
+def finish_kernel(
+    count, subs, place, mix, shared, out_sum, grad_sum, out_tokens, grad_tokens, scratch, rows, low, sems
+):
+    size = shared.shape[0] // (2 * count)
+    copies = []
+    work = ((0, mix, out_sum, out_tokens), (size, None, grad_sum, grad_tokens))
+    for i, (at, scale, before, out) in enumerate(work):
+
+        def put(cut, total):
+            low[i, :, cut] = (before[:, cut] + total).astype(low.dtype)
+
+        blocks = [part(shared, 2 * j * size + at, size) for j in range(count)]
+        token_sums(subs, place, scale, scratch, rows, blocks, put)
+        copies.append(pltpu.make_async_copy(low.at[i], out, sems.at[i]))
+        copies[-1].start()
+    for copy in copies:
+        copy.wait()
 
 
 def half_starts(half_width):
@@ -534,10 +557,13 @@
         return vmem((number * size, LANES), dtype)
 
     sources = (route_ids.T, route_weight.T, tokens, grad_out)
-    x_mine, g_mine, near, here, theirs, place, mix = call(
+    other_rows = count * capacity
+    x_mine, g_mine, near, here, theirs, place, mix, place_other, mix_other = call(
         functools.partial(route_kernel, devices, capacity, subs),
         [lines(count), lines(count), lines(2), lines(2)]
-        + [lines(2 * count), jax.ShapeDtypeStruct((rows, tok_dev), low), jax.ShapeDtypeStruct((rows, LANES), full)],
+        + [lines(2 * count)]
+        + [jax.ShapeDtypeStruct((rows, tok_dev), low), jax.ShapeDtypeStruct((rows, LANES), full)]
+        + [jax.ShapeDtypeStruct((other_rows, tok_dev), low), jax.ShapeDtypeStruct((other_rows, LANES), full)],
         in_hbm(sources),
         in_spaces=[pl.ANY] * 4,
         scratch=spread_scratch
@@ -546,27 +572,25 @@
         traffic=4 * tok_dev * sub_width,
     )
     masks = even_masks(devices)
-    late = list(range(devices // 8, devices // 4))
     packed = call(
-        functools.partial(pack_kernel, size, late),
-        [lines(2 if j in late else 4) for j in range(count)] + [lines(2)] * len(late),
+        functools.partial(pack_kernel, size),
+        [lines(4)] * count,
         (x_mine, g_mine, swap(theirs)),
         flops=24 * half_flops,
     )
-    x_arrived = exchange(packed[:count], masks, devices)
+    arrived = exchange(packed, masks, devices)
     near = exchange_near(near, devices)
-    g_arrived = list(x_arrived)
-    g_arrived[late[0] : late[-1] + 1] = exchange(packed[count:], [masks[j] for j in late], devices)
 
     weights = (gate_weight, up_weight, down_weight)
     w_gate, w_up, w_down = [pltpu.with_memory_space_constraint(w, pltpu.VMEM) for w in weights]
 
-    def gather(arrived, at, after):
-        kernel = functools.partial(gather_kernel, size, at)
-        return call(kernel, [lines(devices)], (*arrived, near, here, after))[0]
-
-    x_sent = gather(x_arrived, 0, mix)
+    def gather(at):
+        return call(functools.partial(gather_kernel, size, at), [lines(devices)], (*arrived, near, here))[0]
+
+    x_sent = gather(0)
     x_swapped = swap(x_sent)
+    g_sent = gather(size)
+    g_swapped = swap(g_sent)
     terms = [
         lines_in_vmem(count + 2, full),
         lines_in_vmem(count, full),
@@ -580,10 +604,8 @@
         scratch=spread_scratch,
         flops=4 * half_flops,
     )
-    g_sent = gather(g_arrived, size, hidden)
-    g_swapped = swap(g_sent)
     out_own, out_other, send_own, send_other = call(
-        functools.partial(output_kernel, devices, subs, step),
+        functools.partial(output_kernel, devices, subs, 2 * step),
         terms,
         (hidden, w_down),
         scratch=spread_scratch,
@@ -632,11 +654,25 @@
         limit=32,
     )
     (sharing,) = call(functools.partial(share_kernel, size), [lines(2 * count)], (*returned, back, written))
+    shared = swap(sharing)
+    sums = call(
+        functools.partial(join_kernel, count, subs),
+        [vmem((tok_dev, sub_width), full)] * 2,
+        (place, mix, *returned, back, kept),
+        scratch=spread_scratch + [pltpu.VMEM((rows, sub_width), low)],
+        flops=4 * rows * tok_dev * sub_width,
+    )
     out_tokens, grad_tokens = call(
-        functools.partial(join_kernel, count, subs),
+        functools.partial(finish_kernel, count, subs),
         [jax.ShapeDtypeStruct((tok_dev, sub_width), low)] * 2,
-        (place, mix, *returned, back, kept, swap(sharing)),
-        scratch=spread_scratch,
+        (place_other, mix_other, shared, *sums),
+        out_spaces=[pl.ANY] * 2,
+        scratch=[
+            pltpu.VMEM((count * size, LANES), full),
+            pltpu.VMEM((other_rows, sub_width), low),
+            pltpu.VMEM((2, tok_dev, sub_width), low),
+            pltpu.SemaphoreType.DMA((2,)),
+        ],
         traffic=8 * tok_dev * sub_width,
     )
     return out_tokens, grad_tokens, grad_gate, grad_up, grad_down

time: 56.9 us -> 56.8 us (level)
  starting transfers between devices: 16.6 us -> 15.6 us
    ppermute x7 -> x6, starting transfers between devices: 12 us -> 10.5 us  [exchange(): arrived.append(lax.ppermute(block, ('expert', 'ffn'), pairs))]
    pallas_call x12 -> x13, Pallas kernels: 24.2 us -> 24.7 us  [call(): pl.pallas_call(kernel, out_shape=tuple(out_shape), in_specs=[pl.BlockSpec...]
    ppermute x7 -> x6, waiting for transfers between devices: 7.08 us -> 7.05 us  [exchange(): arrived.append(lax.ppermute(block, ('expert', 'ffn'), pairs))]
  transfers between devices with their start and end apart: 17 -> 16, of which waited for: 8 -> 9; matrix products, arithmetic and copies ran while one was open for 0% -> 0% of each run, Pallas kernels for 36% -> 37%
where the time goes in v11:
time: 56.8 us; the launch traced here: 56.7 us
  Pallas kernels  24.7 us (43%)
  starting transfers between devices  15.6 us (27%)
  waiting for transfers between devices  15.6 us (27%)
  between operations  0.8 us (1%)
    pallas_call x13, Pallas kernels, call(): pl.pallas_call(kernel, out_shape=tuple(out_shape), in_specs=[pl.BlockSpec...  24.7 us
    ppermute x6, starting transfers between devices, exchange(): arrived.append(lax.ppermute(block, ('expert', 'ffn'), pairs))  10.5 us
    ppermute x6, waiting for transfers between devices, exchange(): arrived.append(lax.ppermute(block, ('expert', 'ffn'), pairs))  7.05 us
    ppermute x2, waiting for transfers between devices, exchange_near(): return lax.ppermute(block, 'expert', [(i, i ^ 1) for i in range(devices)])  4.55 us
    ppermute x8, waiting for transfers between devices, swap(): return lax.ppermute(value, 'ffn', [(0, 1), (1, 0)])  3.96 us
    ppermute x2, starting transfers between devices, exchange_near(): return lax.ppermute(block, 'expert', [(i, i ^ 1) for i in range(devices)])  2.64 us
    ppermute x8, starting transfers between devices, swap(): return lax.ppermute(value, 'ffn', [(0, 1), (1, 0)])  2.5 us
  transfers between devices with their start and end apart: 16, of which 9 were waited for; matrix products, arithmetic and copies ran while one was open for 0% of the time, Pallas kernels for 37%

profile of v11, /device:TPU:0, one launch (start us, length us, event | category | flops | bytes accessed | tf_op | source)
XLA Modules:
  0.0 56.7 jit_solution(2316827669913535365)
XLA Ops:
  0.7 2.1 %shard_map.110 = (bf16[432,128]{1,0:T(8,128)(2,1)S(1)}, bf16[432,128]{1,0:T(8,128)(2,1)S(1)}, bf16[288,128]{1,0:T(8,128)(2,1)S(1)}, bf16[288,128]{1,0:T(8,128)(2...) custom-call(s32[8,128]{1,0:T(8,128)} %bitcast.8, ...), custom_call_target="tpu_custom_call" | custom-call | bytes 1048576 | tf_op jit(solution)/shard_map/pallas_call | solution.py:132
  2.7 0.5 collective-permute-start
  3.3 1.1 %collective-permute-done.swapped = bf16[864,128]{1,0:T(8,128)(2,1)S(1)} collective-permute-done((bf16[864,128]{1,0:T(8,128)(2,1)S(1)}, bf16[864,128]{1,0:T(8,128)(2,1)S(1)}, u32[]{:S(2)}, u32[]{:S(2)}) %collective-permute-start) | collective-permute-done | bytes 221216 | tf_op jit(solution)/shard_map/ppermute | solution.py:531
  4.4 4.0 %collective-permute-start.1 = (bf16[576,128]{1,0:T(8,128)(2,1)S(1)}, bf16[576,128]{1,0:T(8,128)(2,1)S(1)}, u32[]{:S(2)}, u32[]{:S(2)}) collective-permute-start(bf16[576,128]{1,0:T(8,128)(2,1)S(1)} %get-tuple-element.50), channel_id=1, source_target_pairs={{0,8},{1,11},{2,10},{3,9},{4,12},{5,15},{6,14},{7,13},{8,0},{9,3},... | collective-permute-start | bytes 442376 | tf_op jit(solution)/shard_map/ppermute | solution.py:522
  8.4 1.3 %collective-permute-start.2 = (bf16[576,128]{1,0:T(8,128)(2,1)S(1)}, bf16[576,128]{1,0:T(8,128)(2,1)S(1)}, u32[]{:S(2)}, u32[]{:S(2)}) collective-permute-start(bf16[576,128]{1,0:T(8,128)(2,1)S(1)} %get-tuple-element.51), channel_id=1, source_target_pairs={{0,12},{1,15},{2,14},{3,13},{4,8},{5,11},{6,10},{7,9},{8,4},{9,7},... | collective-permute-start | bytes 442376 | tf_op jit(solution)/shard_map/ppermute | solution.py:522
  9.8 0.2 collective-permute-start.3
  10.0 1.5 %collective-permute-start.4 = (bf16[288,128]{1,0:T(8,128)(2,1)S(1)}, bf16[288,128]{1,0:T(8,128)(2,1)S(1)}, u32[]{:S(2)}, u32[]{:S(2)}) collective-permute-start(bf16[288,128]{1,0:T(8,128)(2,1)S(1)} %get-tuple-element.53), channel_id=1, source_target_pairs={{0,2},{2,0},{4,6},{6,4},{8,10},{10,8},{12,14},{14,12},{1,3},{3,1},... | collective-permute-start | bytes 221192 | tf_op jit(solution)/shard_map/ppermute | solution.py:527
  11.5 4.5 %collective-permute-done.4.refs_3_ = bf16[288,128]{1,0:T(8,128)(2,1)S(1)} collective-permute-done((bf16[288,128]{1,0:T(8,128)(2,1)S(1)}, bf16[288,128]{1,0:T(8,128)(2,1)S(1)}, u32[]{:S(2)}, u32[]{:S(2)}) %collective-permute-start.4) | collective-permute-done | bytes 73760 | tf_op jit(solution)/shard_map/ppermute | solution.py:527
  16.1 3.2 %collective-permute-done.1.refs_0_ = bf16[576,128]{1,0:T(8,128)(2,1)S(1)} collective-permute-done((bf16[576,128]{1,0:T(8,128)(2,1)S(1)}, bf16[576,128]{1,0:T(8,128)(2,1)S(1)}, u32[]{:S(2)}, u32[]{:S(2)}) %collective-permute-start.1) | collective-permute-done | bytes 147488 | tf_op jit(solution)/shard_map/ppermute | solution.py:522
  19.2 1.8 %collective-permute-done.3.refs_2_ = bf16[576,128]{1,0:T(8,128)(2,1)S(1)} collective-permute-done((bf16[576,128]{1,0:T(8,128)(2,1)S(1)}, bf16[576,128]{1,0:T(8,128)(2,1)S(1)}, u32[]{:S(2)}, u32[]{:S(2)}) %collective-permute-start.3) | collective-permute-done | bytes 147488 | tf_op jit(solution)/shard_map/ppermute | solution.py:522
  21.1 0.6 %collective-permute-start.5 = (bf16[1152,128]{1,0:T(8,128)(2,1)S(1)}, bf16[1152,128]{1,0:T(8,128)(2,1)S(1)}, u32[]{:S(2)}, u32[]{:S(2)}) collective-permute-start(bf16[1152,128]{1,0:T(8,128)(2,1)S(1)} %shard_map.112.x_sent), channel_id=1, source_target_pairs={{0,1},{1,0},{2,3},{3,2},{4,5},{5,4},{6,7},{7,6},{8,9},{9,8},{10,11... | collective-permute-start | bytes 884744 | tf_op jit(solution)/shard_map/ppermute | solution.py:531
  21.8 1.1 %collective-permute-done.5.x_swapped = bf16[1152,128]{1,0:T(8,128)(2,1)S(1)} collective-permute-done((bf16[1152,128]{1,0:T(8,128)(2,1)S(1)}, bf16[1152,128]{1,0:T(8,128)(2,1)S(1)}, u32[]{:S(2)}, u32[]{:S(2)}) %collective-permute-start.5) | collective-permute-done | bytes 294944 | tf_op jit(solution)/shard_map/ppermute | solution.py:531
  22.9 2.7 %shard_map.113 = (bf16[72,4096]{1,0:T(8,128)(2,1)S(1)}, bf16[72,768]{1,0:T(8,128)(2,1)S(1)}, bf16[72,768]{1,0:T(8,128)(2,1)S(1)}, bf16[72,768]{1,0:T(8,128)(2,1)S(1)}) custom-call(bf16[1152,128]{1,0:T(8,128)(2,1)S(1)} %shard_map.112.x_sent, bf16[1152,128]{1,0:T(8,128)(2,1)S(1)} %collective-permute-done.5.x_swapped, bf16[1,4096,768]{2,1,0:T(8,128)(2,1)S(1)} %bitcast.3, ...), custom_call_target="tpu_custom_call" | custom-call | flops 905969664 | tf_op jit(solution)/shard_map/pallas_call | solution.py:132
  25.6 1.4 %shard_map.114 = (f32[720,128]{1,0:T(8,128)S(1)}, f32[432,128]{1,0:T(8,128)S(1)}, bf16[432,128]{1,0:T(8,128)(2,1)S(1)}, bf16[720,128]{1,0:T(8,128)(2,1)S(1)}) custom-call(bf16[72,768]{1,0:T(8,128)(2,1)S(1)} %get-tuple-element.55.hidden, bf16[1,768,4096]{2,1,0:T(8,128)(2,1)S(1)} %bitcast.7), custom_call_target="tpu_custom_call" | custom-call | flops 452984832 | tf_op jit(solution)/shard_map/pallas_call | solution.py:132
  27.0 0.5 collective-permute-start.6
  27.5 4.9 %shard_map.116 = (bf16[72,4096]{1,0:T(8,128)(2,1)S(1)}, bf16[72,768]{1,0:T(8,128)(2,1)S(1)}, bf16[72,768]{1,0:T(8,128)(2,1)S(1)}, f32[432,128]{1,0:T(8,128)S(1)}, bf16[720,128]{1,0:T(8,128)(2,1)S(1)}) custom-call(bf16[1152,128]{1,0:T(8,128)(2,1)S(1)} %shard_map.115.g_sent, bf16[1152,128]{1,0:T(8,128)(2,1)S(1)} %collective-permute-done.8.g_swapped, ...), custom_call_target="tpu_custom_call" | custom-call | flops 905969664 | tf_op jit(solution)/shard_map/pallas_call | solution.py:132
  32.4 0.2 collective-permute-start.9
  32.6 0.4 collective-permute-start.7
  33.0 2.1 %shard_map.117 = (f32[720,128]{1,0:T(8,128)S(1)}, bf16[432,128]{1,0:T(8,128)(2,1)S(1)}) custom-call(bf16[72,768]{1,0:T(8,128)(2,1)S(1)} %get-tuple-element.62.pre_gate, bf16[72,768]{1,0:T(8,128)(2,1)S(1)} %get-tuple-element.63.pre_up, bf16[1,4096,768]{2,1,0:T(8,128)(2,1)S(1)} %bitcast.3, bf16[1,4096,768]{2,1,0:T(8,128)(2,1)S(1)} %bitcast.5), custom_call_target="tpu_custom_call" | custom-call | flops 452984832 | tf_op jit(solution)/shard_map/pallas_call | solution.py:132
  35.0 0.2 collective-permute-start.10
  35.2 1.2 %collective-permute-done.10.refs_7_ = bf16[432,128]{1,0:T(8,128)(2,1)S(1)} collective-permute-done((bf16[432,128]{1,0:T(8,128)(2,1)S(1)}, bf16[432,128]{1,0:T(8,128)(2,1)S(1)}, u32[]{:S(2)}, u32[]{:S(2)}) %collective-permute-start.10) | collective-permute-done | bytes 110624 | tf_op jit(solution)/shard_map/ppermute | solution.py:531
  36.4 0.1 shard_map.118
  36.6 4.2 %collective-permute-start.11 = (bf16[576,128]{1,0:T(8,128)(2,1)S(1)}, bf16[576,128]{1,0:T(8,128)(2,1)S(1)}, u32[]{:S(2)}, u32[]{:S(2)}) collective-permute-start(bf16[576,128]{1,0:T(8,128)(2,1)S(1)} %get-tuple-element.68), channel_id=1, source_target_pairs={{0,8},{1,11},{2,10},{3,9},{4,12},{5,15},{6,14},{7,13},{8,0},{9,3},... | collective-permute-start | bytes 442376 | tf_op jit(solution)/shard_map/ppermute | solution.py:522
  40.8 0.4 collective-permute-start.12
  41.2 0.2 collective-permute-start.13
  41.4 1.1 %collective-permute-start.14 = (bf16[288,128]{1,0:T(8,128)(2,1)S(1)}, bf16[288,128]{1,0:T(8,128)(2,1)S(1)}, u32[]{:S(2)}, u32[]{:S(2)}) collective-permute-start(bf16[288,128]{1,0:T(8,128)(2,1)S(1)} %get-tuple-element.71), channel_id=1, source_target_pairs={{0,2},{2,0},{4,6},{6,4},{8,10},{10,8},{12,14},{14,12},{1,3},{3,1},... | collective-permute-start | bytes 221192 | tf_op jit(solution)/shard_map/ppermute | solution.py:527
  42.6 9.1 %shard_map.119 = (bf16[1,4096,768]{2,1,0:T(8,128)(2,1)}, bf16[1,4096,768]{2,1,0:T(8,128)(2,1)}, bf16[1,768,4096]{2,1,0:T(8,128)(2,1)}, f32[8,128]{1,0:T(8,128)S(1)}) custom-call(bf16[72,4096]{1,0:T(8,128)(2,1)S(1)} %get-tuple-element.72.x, bf16[72,4096]{1,0:T(8,128)(2,1)S(1)} %get-tuple-element.73.g, bf16[72,768]{1,0:T(8,128)(2,1)S(1)} %get-tuple-element.55.hidden, ...), custom_call_target="tpu_custom_call" | custom-call | flops 1358954496 | bytes 18874368 | tf_op jit(solution)/shard_map/pallas_call | solution.py:132
  51.7 0.2 collective-permute-done.11.refs_0_
  51.8 1.9 %collective-permute-done.13.refs_2_ = bf16[576,128]{1,0:T(8,128)(2,1)S(1)} collective-permute-done((bf16[576,128]{1,0:T(8,128)(2,1)S(1)}, bf16[576,128]{1,0:T(8,128)(2,1)S(1)}, u32[]{:S(2)}, u32[]{:S(2)}) %collective-permute-start.13) | collective-permute-done | bytes 147488 | tf_op jit(solution)/shard_map/ppermute | solution.py:522
  53.8 0.9 %shard_map.121 = (f32[128,2048]{1,0:T(8,128)S(1)}, f32[128,2048]{1,0:T(8,128)S(1)}) custom-call(bf16[72,128]{1,0:T(8,128)(2,1)S(1)} %get-tuple-element.75.place, f32[72,128]{1,0:T(8,128)S(1)} %get-tuple-element.76.mix, bf16[576,128]{1,0:T(8,128)(2,1)S(1)} %collective-permute-done.11.refs_0_, bf16[576,128]{1,0:T(8,128)(2,1)S(1)} %collective-permute-done.12.refs_1_, ...), custom_call_target="tpu_custom_call" | custom-call | flops 75497472 | tf_op jit(solution)/shard_map/pallas_call | solution.py:132
  54.7 0.6 %collective-permute-done.15.shared = bf16[864,128]{1,0:T(8,128)(2,1)S(1)} collective-permute-done((bf16[864,128]{1,0:T(8,128)(2,1)S(1)}, bf16[864,128]{1,0:T(8,128)(2,1)S(1)}, u32[]{:S(2)}, u32[]{:S(2)}) %collective-permute-start.15) | collective-permute-done | bytes 221216 | tf_op jit(solution)/shard_map/ppermute | solution.py:531
  55.3 1.4 %shard_map.122 = (bf16[128,2048]{1,0:T(8,128)(2,1)}, bf16[128,2048]{1,0:T(8,128)(2,1)}) custom-call(bf16[27,128]{1,0:T(8,128)(2,1)S(1)} %get-tuple-element.45.place, f32[27,128]{1,0:T(8,128)S(1)} %get-tuple-element.46.mix, bf16[864,128]{1,0:T(8,128)(2,1)S(1)} %collective-permute-done.15.shared, f32[128,2048]{1,0:T(8,128)S(1)} %get-tuple-element.78.out_sum, ...), custom_call_target="tpu_custom_call" | custom-call | bytes 2097152 | tf_op jit(solution)/shard_map/pallas_call | solution.py:132
  (28 shorter events, 0.3 us)
Async XLA Ops:
  0.6 22.2 %slice-start = ((s8[6291456]{0:T(1024)(128)(4,1)}), s8[4194304]{0:T(1024)(128)(4,1)S(1)}, s32[]{:S(2)}) async-start(s8[6291456]{0:T(1024)(128)(4,1)} %bitcast.2), calls=%async_computation | async-start | bytes 8388608
  0.6 22.2 %slice-start.2 = ((s8[6291456]{0:T(1024)(128)(4,1)}), s8[4194304]{0:T(1024)(128)(4,1)S(1)}, s32[]{:S(2)}) async-start(s8[6291456]{0:T(1024)(128)(4,1)} %bitcast.4), calls=%async_computation.2 | async-start | bytes 8388608
  2.7 1.6 %collective-permute-start = (bf16[864,128]{1,0:T(8,128)(2,1)S(1)}, bf16[864,128]{1,0:T(8,128)(2,1)S(1)}, u32[]{:S(2)}, u32[]{:S(2)}) collective-permute-start(bf16[864,128]{1,0:T(8,128)(2,1)S(1)} %get-tuple-element.49), channel_id=1, source_target_pairs={{0,1},{1,0},{2,3},{3,2},{4,5},{5,4},{6,7},{7,6},{8,9},{9,8},{10,11... | collective-permute-start | bytes 663560 | tf_op jit(solution)/shard_map/ppermute | solution.py:531
  4.4 18.5 %slice-start.1 = ((s8[6291456]{0:T(1024)(128)(4,1)}), s8[2097152]{0:T(1024)(128)(4,1)S(1)}, s32[]{:S(2)}) async-start(s8[6291456]{0:T(1024)(128)(4,1)} %bitcast.2), calls=%async_computation.1 | async-start | bytes 4194304
  4.4 18.5 %slice-start.3 = ((s8[6291456]{0:T(1024)(128)(4,1)}), s8[2097152]{0:T(1024)(128)(4,1)S(1)}, s32[]{:S(2)}) async-start(s8[6291456]{0:T(1024)(128)(4,1)} %bitcast.4), calls=%async_computation.3 | async-start | bytes 4194304
  4.4 14.8 %collective-permute-start.1 = (bf16[576,128]{1,0:T(8,128)(2,1)S(1)}, bf16[576,128]{1,0:T(8,128)(2,1)S(1)}, u32[]{:S(2)}, u32[]{:S(2)}) collective-permute-start(bf16[576,128]{1,0:T(8,128)(2,1)S(1)} %get-tuple-element.50), channel_id=1, source_target_pairs={{0,8},{1,11},{2,10},{3,9},{4,12},{5,15},{6,14},{7,13},{8,0},{9,3},... | collective-permute-start | bytes 442376 | tf_op jit(solution)/shard_map/ppermute | solution.py:522
  8.4 10.8 %collective-permute-start.2 = (bf16[576,128]{1,0:T(8,128)(2,1)S(1)}, bf16[576,128]{1,0:T(8,128)(2,1)S(1)}, u32[]{:S(2)}, u32[]{:S(2)}) collective-permute-start(bf16[576,128]{1,0:T(8,128)(2,1)S(1)} %get-tuple-element.51), channel_id=1, source_target_pairs={{0,12},{1,15},{2,14},{3,13},{4,8},{5,11},{6,10},{7,9},{8,4},{9,7},... | collective-permute-start | bytes 442376 | tf_op jit(solution)/shard_map/ppermute | solution.py:522
  9.8 11.3 %collective-permute-start.3 = (bf16[576,128]{1,0:T(8,128)(2,1)S(1)}, bf16[576,128]{1,0:T(8,128)(2,1)S(1)}, u32[]{:S(2)}, u32[]{:S(2)}) collective-permute-start(bf16[576,128]{1,0:T(8,128)(2,1)S(1)} %get-tuple-element.52), channel_id=1, source_target_pairs={{0,4},{1,7},{2,6},{3,5},{4,0},{5,3},{6,2},{7,1},{8,12},{9,15},{10,... | collective-permute-start | bytes 442376 | tf_op jit(solution)/shard_map/ppermute | solution.py:522
  10.0 6.0 %collective-permute-start.4 = (bf16[288,128]{1,0:T(8,128)(2,1)S(1)}, bf16[288,128]{1,0:T(8,128)(2,1)S(1)}, u32[]{:S(2)}, u32[]{:S(2)}) collective-permute-start(bf16[288,128]{1,0:T(8,128)(2,1)S(1)} %get-tuple-element.53), channel_id=1, source_target_pairs={{0,2},{2,0},{4,6},{6,4},{8,10},{10,8},{12,14},{14,12},{1,3},{3,1},... | collective-permute-start | bytes 221192 | tf_op jit(solution)/shard_map/ppermute | solution.py:527
  21.1 1.8 %collective-permute-start.5 = (bf16[1152,128]{1,0:T(8,128)(2,1)S(1)}, bf16[1152,128]{1,0:T(8,128)(2,1)S(1)}, u32[]{:S(2)}, u32[]{:S(2)}) collective-permute-start(bf16[1152,128]{1,0:T(8,128)(2,1)S(1)} %shard_map.112.x_sent), channel_id=1, source_target_pairs={{0,1},{1,0},{2,3},{3,2},{4,5},{5,4},{6,7},{7,6},{8,9},{9,8},{10,11... | collective-permute-start | bytes 884744 | tf_op jit(solution)/shard_map/ppermute | solution.py:531
  21.7 4.0 %slice-start.4 = ((s8[6291456]{0:T(1024)(128)(4,1)}), s8[4194304]{0:T(1024)(128)(4,1)S(1)}, s32[]{:S(2)}) async-start(s8[6291456]{0:T(1024)(128)(4,1)} %bitcast.6), calls=%async_computation.4 | async-start | bytes 8388608
  21.7 4.0 %slice-start.5 = ((s8[6291456]{0:T(1024)(128)(4,1)}), s8[2097152]{0:T(1024)(128)(4,1)S(1)}, s32[]{:S(2)}) async-start(s8[6291456]{0:T(1024)(128)(4,1)} %bitcast.6), calls=%async_computation.5 | async-start | bytes 4194304
  21.7 5.8 %collective-permute-start.8 = (bf16[1152,128]{1,0:T(8,128)(2,1)S(1)}, bf16[1152,128]{1,0:T(8,128)(2,1)S(1)}, u32[]{:S(2)}, u32[]{:S(2)}) collective-permute-start(bf16[1152,128]{1,0:T(8,128)(2,1)S(1)} %shard_map.115.g_sent), channel_id=1, source_target_pairs={{0,1},{1,0},{2,3},{3,2},{4,5},{5,4},{6,7},{7,6},{8,9},{9,8},{10,11... | collective-permute-start | bytes 884744 | tf_op jit(solution)/shard_map/ppermute | solution.py:531
  27.0 9.4 %collective-permute-start.6 = (bf16[720,128]{1,0:T(8,128)(2,1)S(1)}, bf16[720,128]{1,0:T(8,128)(2,1)S(1)}, u32[]{:S(2)}, u32[]{:S(2)}) collective-permute-start(bf16[720,128]{1,0:T(8,128)(2,1)S(1)} %get-tuple-element.58), channel_id=1, source_target_pairs={{0,1},{1,0},{2,3},{3,2},{4,5},{5,4},{6,7},{7,6},{8,9},{9,8},{10,11... | collective-permute-start | bytes 552968 | tf_op jit(solution)/shard_map/ppermute | solution.py:531
  32.4 4.1 %collective-permute-start.9 = (bf16[720,128]{1,0:T(8,128)(2,1)S(1)}, bf16[720,128]{1,0:T(8,128)(2,1)S(1)}, u32[]{:S(2)}, u32[]{:S(2)}) collective-permute-start(bf16[720,128]{1,0:T(8,128)(2,1)S(1)} %get-tuple-element.66), channel_id=1, source_target_pairs={{0,1},{1,0},{2,3},{3,2},{4,5},{5,4},{6,7},{7,6},{8,9},{9,8},{10,11... | collective-permute-start | bytes 552968 | tf_op jit(solution)/shard_map/ppermute | solution.py:531
  32.6 2.7 %collective-permute-start.7 = (bf16[432,128]{1,0:T(8,128)(2,1)S(1)}, bf16[432,128]{1,0:T(8,128)(2,1)S(1)}, u32[]{:S(2)}, u32[]{:S(2)}) collective-permute-start(bf16[432,128]{1,0:T(8,128)(2,1)S(1)} %get-tuple-element.59), channel_id=1, source_target_pairs={{0,1},{1,0},{2,3},{3,2},{4,5},{5,4},{6,7},{7,6},{8,9},{9,8},{10,11... | collective-permute-start | bytes 331784 | tf_op jit(solution)/shard_map/ppermute | solution.py:531
  35.0 1.4 %collective-permute-start.10 = (bf16[432,128]{1,0:T(8,128)(2,1)S(1)}, bf16[432,128]{1,0:T(8,128)(2,1)S(1)}, u32[]{:S(2)}, u32[]{:S(2)}) collective-permute-start(bf16[432,128]{1,0:T(8,128)(2,1)S(1)} %get-tuple-element.67), channel_id=1, source_target_pairs={{0,1},{1,0},{2,3},{3,2},{4,5},{5,4},{6,7},{7,6},{8,9},{9,8},{10,11... | collective-permute-start | bytes 331784 | tf_op jit(solution)/shard_map/ppermute | solution.py:531
  36.6 15.3 %collective-permute-start.11 = (bf16[576,128]{1,0:T(8,128)(2,1)S(1)}, bf16[576,128]{1,0:T(8,128)(2,1)S(1)}, u32[]{:S(2)}, u32[]{:S(2)}) collective-permute-start(bf16[576,128]{1,0:T(8,128)(2,1)S(1)} %get-tuple-element.68), channel_id=1, source_target_pairs={{0,8},{1,11},{2,10},{3,9},{4,12},{5,15},{6,14},{7,13},{8,0},{9,3},... | collective-permute-start | bytes 442376 | tf_op jit(solution)/shard_map/ppermute | solution.py:522
  40.8 11.1 %collective-permute-start.12 = (bf16[576,128]{1,0:T(8,128)(2,1)S(1)}, bf16[576,128]{1,0:T(8,128)(2,1)S(1)}, u32[]{:S(2)}, u32[]{:S(2)}) collective-permute-start(bf16[576,128]{1,0:T(8,128)(2,1)S(1)} %get-tuple-element.69), channel_id=1, source_target_pairs={{0,12},{1,15},{2,14},{3,13},{4,8},{5,11},{6,10},{7,9},{8,4},{9,7},... | collective-permute-start | bytes 442376 | tf_op jit(solution)/shard_map/ppermute | solution.py:522
  41.2 12.5 %collective-permute-start.13 = (bf16[576,128]{1,0:T(8,128)(2,1)S(1)}, bf16[576,128]{1,0:T(8,128)(2,1)S(1)}, u32[]{:S(2)}, u32[]{:S(2)}) collective-permute-start(bf16[576,128]{1,0:T(8,128)(2,1)S(1)} %get-tuple-element.70), channel_id=1, source_target_pairs={{0,4},{1,7},{2,6},{3,5},{4,0},{5,3},{6,2},{7,1},{8,12},{9,15},{10,... | collective-permute-start | bytes 442376 | tf_op jit(solution)/shard_map/ppermute | solution.py:522
  41.4 10.2 %collective-permute-start.14 = (bf16[288,128]{1,0:T(8,128)(2,1)S(1)}, bf16[288,128]{1,0:T(8,128)(2,1)S(1)}, u32[]{:S(2)}, u32[]{:S(2)}) collective-permute-start(bf16[288,128]{1,0:T(8,128)(2,1)S(1)} %get-tuple-element.71), channel_id=1, source_target_pairs={{0,2},{2,0},{4,6},{6,4},{8,10},{10,8},{12,14},{14,12},{1,3},{3,1},... | collective-permute-start | bytes 221192 | tf_op jit(solution)/shard_map/ppermute | solution.py:527
  53.8 1.5 %collective-permute-start.15 = (bf16[864,128]{1,0:T(8,128)(2,1)S(1)}, bf16[864,128]{1,0:T(8,128)(2,1)S(1)}, u32[]{:S(2)}, u32[]{:S(2)}) collective-permute-start(bf16[864,128]{1,0:T(8,128)(2,1)S(1)} %shard_map.120), channel_id=1, source_target_pairs={{0,1},{1,0},{2,3},{3,2},{4,5},{5,4},{6,7},{7,6},{8,9},{9,8},{10,11... | collective-permute-start | bytes 663560 | tf_op jit(solution)/shard_map/ppermute | solution.py:531

commit v12 on v11

--- a/solution.py
+++ b/solution.py
@@ -266,7 +266,12 @@
 
 def split_terms(count, size, scratch, own_half, keep, send):
     keep[0 : count * size, :] = scratch[0 : count * size, :]
-    send[0 : count * size, :] = scratch[count * size : 2 * count * size, :].astype(send.dtype)
+    for j in range(count):
+        value = scratch[(count + j) * size : (count + j + 1) * size, :].astype(jnp.bfloat16)
+        if isinstance(send, list):
+            send[j][...] = value
+        else:
+            part(send, j * size, size)[...] = value
     rest = scratch[2 * count * size :, :]
     if own_half:
         keep[count * size :, :] = rest
@@ -274,27 +279,44 @@
         send[count * size :, :] = rest.astype(send.dtype)
 
 
-def leave_kernel(size, *refs):
-    terms, outs = (refs[:4], refs[4:8]), refs[8:]
-    count = len(outs) - 2
-    for at, (keep_own, keep_other, came_own, came_other) in zip((0, size), terms):
+def early_kernel(size, keep_own, keep_other, came_own, came_other, out):
+    for at, keep, came in ((0, keep_own, came_own), (size, keep_other, came_other)):
+        total = part(keep, 0, size)[...] + part(came, 0, size)[...].astype(jnp.float32)
+        part(out, at, size)[...] = total.astype(out.dtype)
+
+
+def leave_kernel(size, count, *refs):
+    terms, outs = (refs[:4], refs[4 : 7 + count]), refs[8 + count :]
+    for which, (keep_own, keep_other, came_own, *came_other) in enumerate(terms):
+
+        def total(keep, came, p):
+            return (keep[p * size : (p + 1) * size, :] + came.astype(jnp.float32)).astype(jnp.bfloat16)
 
         def own(p):
-            total = part(keep_own, p * size, size)[...] + part(came_own, p * size, size)[...].astype(jnp.float32)
-            return total.astype(outs[0].dtype)
+            return total(keep_own, part(came_own, p * size, size)[...], p)
 
         for j, out in enumerate(outs[:count]):
+            if j == 0 and which == 0:
+                continue
+            at = 2 * size if j and which else 0
             part(out, at, size)[...] = own(j)
-            total = part(keep_other, j * size, size)[...] + part(came_other, j * size, size)[...].astype(jnp.float32)
-            part(out, 2 * size + at, size)[...] = total.astype(out.dtype)
-        part(outs[count], at, size)[...] = own(count)
-        part(outs[count + 1], at, size)[...] = own(count + 1)
-
-
-def share_kernel(size, *refs):
-    blocks, (_, _, out) = refs[:-3], refs[-3:]
-    for j, block in enumerate(blocks):
-        part(out, 2 * j * size, 2 * size)[...] = part(block, 2 * size, 2 * size)[...]
+            came = came_other[j][...] if which else part(came_other[0], j * size, size)[...]
+            part(out, at + size, size)[...] = total(keep_other, came, j)
+        part(outs[count], which * size, size)[...] = own(count)
+        part(outs[count + 1], which * size, size)[...] = own(count + 1)
+
+
+def returned_parts(size, early, blocks, which):
+    if which:
+        return [part(block, 2 * size if j else 0, 2 * size) for j, block in enumerate(blocks)]
+    return [part(block, 0, 2 * size) for block in (early, *blocks[1:])]
+
+
+def share_kernel(size, count, early, *refs):
+    blocks, out = refs[:count], refs[-1]
+    for which in range(2):
+        for j, both in enumerate(returned_parts(size, early, blocks, which)):
+            part(out, (2 * j + which) * size, size)[...] = part(both, size, size)[...]
 
 
 def token_sums(subs, place, mix, scratch, rows, blocks, put):
@@ -311,16 +333,16 @@
         put(cut, contract_rows(place[...], rows[:, cut]))
 
 
-def join_kernel(count, subs, place, mix, *refs):
+def join_kernel(count, subs, place, mix, early, *refs):
     blocks, (near, here, out_sum, grad_sum, scratch, rows) = refs[:count], refs[count:]
     size = near.shape[0] // 2
-    for at, scale, out in ((0, mix, out_sum), (size, None, grad_sum)):
+    for which, scale, out in ((0, mix, out_sum), (1, None, grad_sum)):
 
         def put(cut, total):
             out[:, cut] = total
 
-        first = [part(block, at, size) for block in blocks]
-        last = [part(near, at, size), part(here, at, size)]
+        first = [part(both, 0, size) for both in returned_parts(size, early, blocks, which)]
+        last = [part(near, which * size, size), part(here, which * size, size)]
         token_sums(subs, place, scale, scratch, rows, first + [None] * count + last, put)
 
 
@@ -434,7 +456,8 @@
     halves_of_output(devices, subs, step, scratch, False, term, keep_other, send_other)
 
 
-def backward_own_kernel(devices, subs, step, pre_gate, pre_up, w_gate, w_up, keep_own, send_own, scratch):
+def backward_own_kernel(devices, subs, step, pre_gate, pre_up, w_gate, w_up, keep_own, *refs):
+    send_own, scratch = list(refs[:-1]), refs[-1]
     own, _ = half_starts(subs * LANES)
     term = input_term(step, pre_gate, pre_up, w_gate, w_up, own)
     halves_of_output(devices, subs, step, scratch, True, term, keep_own, send_own)
@@ -612,6 +635,8 @@
         flops=2 * half_flops,
     )
     out_terms = (out_own, out_other, swap(send_other), swap(send_own))
+    (early,) = call(functools.partial(early_kernel, size), [lines(2)], out_terms)
+    (early,) = exchange([early], masks, devices)
     g_full, pre_gate, pre_up, dx_other, send_other = call(
         functools.partial(backward_kernel, devices, subs, step),
         [vmem((rows, width), low)] + [vmem((rows, lanes), low)] * 2 + [terms[1], terms[3]],
@@ -620,18 +645,18 @@
         flops=4 * half_flops,
     )
     came_own = swap(send_other)
-    dx_own, send_own = call(
+    dx_own, *send_own = call(
         functools.partial(backward_own_kernel, devices, subs, step),
-        [terms[0], terms[2]],
+        [terms[0]] + [lines_in_vmem(1)] * count,
         (pre_gate, pre_up, w_gate, w_up),
         scratch=spread_scratch,
         flops=2 * half_flops,
     )
-    dx_terms = (dx_own, dx_other, came_own, swap(send_own))
+    dx_terms = (dx_own, dx_other, came_own, *[swap(value) for value in send_own])
     *leaving, back, kept = call(
-        functools.partial(leave_kernel, size),
-        [lines(4)] * count + [lines(2)] * 2,
-        (*out_terms, *dx_terms),
+        functools.partial(leave_kernel, size, count),
+        [lines(2)] + [lines(4)] * (count - 1) + [lines(2)] * 2,
+        (*out_terms, *dx_terms, early),
     )
     returned = exchange(leaving, masks, devices)
     back = exchange_near(back, devices)
@@ -653,12 +678,14 @@
         traffic=sum(w.size * 2 for w in weights),
         limit=32,
     )
-    (sharing,) = call(functools.partial(share_kernel, size), [lines(2 * count)], (*returned, back, written))
+    (sharing,) = call(
+        functools.partial(share_kernel, size, count), [lines(2 * count)], (early, *returned, back, written)
+    )
     shared = swap(sharing)
     sums = call(
         functools.partial(join_kernel, count, subs),
         [vmem((tok_dev, sub_width), full)] * 2,
-        (place, mix, *returned, back, kept),
+        (place, mix, early, *returned, back, kept),
         scratch=spread_scratch + [pltpu.VMEM((rows, sub_width), low)],
         flops=4 * rows * tok_dev * sub_width,
     )

time: 56.8 us -> 59.2 us (1.042)
  starting transfers between devices: 15.6 us -> 20.2 us
  waiting for transfers between devices: 15.6 us -> 13.3 us
    ppermute x6 -> x7, starting transfers between devices: 10.5 us -> 14.3 us  [exchange(): arrived.append(lax.ppermute(block, ('expert', 'ffn'), pairs))]
    ppermute x6 -> x7, waiting for transfers between devices: 7.05 us -> 5.41 us  [exchange(): arrived.append(lax.ppermute(block, ('expert', 'ffn'), pairs))]
    ppermute x8 -> x10, starting transfers between devices: 2.5 us -> 3.58 us  [swap(): return lax.ppermute(value, 'ffn', [(0, 1), (1, 0)])]
    ppermute x8 -> x10, waiting for transfers between devices: 3.96 us -> 3.38 us  [swap(): return lax.ppermute(value, 'ffn', [(0, 1), (1, 0)])]
    pallas_call x13 -> x14, Pallas kernels: 24.7 us -> 24.7 us  [call(): pl.pallas_call(kernel, out_shape=tuple(out_shape), in_specs=[pl.BlockSpec...]
  transfers between devices with their start and end apart: 16 -> 19, of which waited for: 9 -> 10; matrix products, arithmetic and copies ran while one was open for 0% -> 0% of each run, Pallas kernels for 37% -> 36%
where the time goes in v12:
time: 59.2 us; the launch traced here: 59.1 us
  Pallas kernels  24.7 us (42%)
  starting transfers between devices  20.2 us (34%)
  waiting for transfers between devices  13.3 us (22%)
  between operations  0.82 us (1%)
    pallas_call x14, Pallas kernels, call(): pl.pallas_call(kernel, out_shape=tuple(out_shape), in_specs=[pl.BlockSpec...  24.7 us
    ppermute x7, starting transfers between devices, exchange(): arrived.append(lax.ppermute(block, ('expert', 'ffn'), pairs))  14.3 us
    ppermute x7, waiting for transfers between devices, exchange(): arrived.append(lax.ppermute(block, ('expert', 'ffn'), pairs))  5.41 us
    ppermute x2, waiting for transfers between devices, exchange_near(): return lax.ppermute(block, 'expert', [(i, i ^ 1) for i in range(devices)])  4.55 us
    ppermute x10, starting transfers between devices, swap(): return lax.ppermute(value, 'ffn', [(0, 1), (1, 0)])  3.58 us
    ppermute x10, waiting for transfers between devices, swap(): return lax.ppermute(value, 'ffn', [(0, 1), (1, 0)])  3.38 us
    ppermute x2, starting transfers between devices, exchange_near(): return lax.ppermute(block, 'expert', [(i, i ^ 1) for i in range(devices)])  2.4 us
  transfers between devices with their start and end apart: 19, of which 10 were waited for; matrix products, arithmetic and copies ran while one was open for 0% of the time, Pallas kernels for 36%

profile of v12, /device:TPU:0, one launch (start us, length us, event | category | flops | bytes accessed | tf_op | source)
XLA Modules:
  0.0 59.1 jit_solution(8019761928536785931)
XLA Ops:
  0.7 2.1 %shard_map.110 = (bf16[432,128]{1,0:T(8,128)(2,1)S(1)}, bf16[432,128]{1,0:T(8,128)(2,1)S(1)}, bf16[288,128]{1,0:T(8,128)(2,1)S(1)}, bf16[288,128]{1,0:T(8,128)(2...) custom-call(s32[8,128]{1,0:T(8,128)} %bitcast.8, ...), custom_call_target="tpu_custom_call" | custom-call | bytes 1048576 | tf_op jit(solution)/shard_map/pallas_call | solution.py:132
  2.7 0.5 collective-permute-start
  3.3 1.1 %collective-permute-done.swapped = bf16[864,128]{1,0:T(8,128)(2,1)S(1)} collective-permute-done((bf16[864,128]{1,0:T(8,128)(2,1)S(1)}, bf16[864,128]{1,0:T(8,128)(2,1)S(1)}, u32[]{:S(2)}, u32[]{:S(2)}) %collective-permute-start) | collective-permute-done | bytes 221216 | tf_op jit(solution)/shard_map/ppermute | solution.py:554
  4.4 4.0 %collective-permute-start.1 = (bf16[576,128]{1,0:T(8,128)(2,1)S(1)}, bf16[576,128]{1,0:T(8,128)(2,1)S(1)}, u32[]{:S(2)}, u32[]{:S(2)}) collective-permute-start(bf16[576,128]{1,0:T(8,128)(2,1)S(1)} %get-tuple-element.52), channel_id=1, source_target_pairs={{0,8},{1,11},{2,10},{3,9},{4,12},{5,15},{6,14},{7,13},{8,0},{9,3},... | collective-permute-start | bytes 442376 | tf_op jit(solution)/shard_map/ppermute | solution.py:545
  8.4 1.3 %collective-permute-start.2 = (bf16[576,128]{1,0:T(8,128)(2,1)S(1)}, bf16[576,128]{1,0:T(8,128)(2,1)S(1)}, u32[]{:S(2)}, u32[]{:S(2)}) collective-permute-start(bf16[576,128]{1,0:T(8,128)(2,1)S(1)} %get-tuple-element.53), channel_id=1, source_target_pairs={{0,12},{1,15},{2,14},{3,13},{4,8},{5,11},{6,10},{7,9},{8,4},{9,7},... | collective-permute-start | bytes 442376 | tf_op jit(solution)/shard_map/ppermute | solution.py:545
  9.8 0.2 collective-permute-start.3
  10.0 1.5 %collective-permute-start.4 = (bf16[288,128]{1,0:T(8,128)(2,1)S(1)}, bf16[288,128]{1,0:T(8,128)(2,1)S(1)}, u32[]{:S(2)}, u32[]{:S(2)}) collective-permute-start(bf16[288,128]{1,0:T(8,128)(2,1)S(1)} %get-tuple-element.55), channel_id=1, source_target_pairs={{0,2},{2,0},{4,6},{6,4},{8,10},{10,8},{12,14},{14,12},{1,3},{3,1},... | collective-permute-start | bytes 221192 | tf_op jit(solution)/shard_map/ppermute | solution.py:550
  11.5 4.5 %collective-permute-done.4.refs_3_ = bf16[288,128]{1,0:T(8,128)(2,1)S(1)} collective-permute-done((bf16[288,128]{1,0:T(8,128)(2,1)S(1)}, bf16[288,128]{1,0:T(8,128)(2,1)S(1)}, u32[]{:S(2)}, u32[]{:S(2)}) %collective-permute-start.4) | collective-permute-done | bytes 73760 | tf_op jit(solution)/shard_map/ppermute | solution.py:550
  16.1 3.2 %collective-permute-done.1.refs_0_ = bf16[576,128]{1,0:T(8,128)(2,1)S(1)} collective-permute-done((bf16[576,128]{1,0:T(8,128)(2,1)S(1)}, bf16[576,128]{1,0:T(8,128)(2,1)S(1)}, u32[]{:S(2)}, u32[]{:S(2)}) %collective-permute-start.1) | collective-permute-done | bytes 147488 | tf_op jit(solution)/shard_map/ppermute | solution.py:545
  19.2 1.8 %collective-permute-done.3.refs_2_ = bf16[576,128]{1,0:T(8,128)(2,1)S(1)} collective-permute-done((bf16[576,128]{1,0:T(8,128)(2,1)S(1)}, bf16[576,128]{1,0:T(8,128)(2,1)S(1)}, u32[]{:S(2)}, u32[]{:S(2)}) %collective-permute-start.3) | collective-permute-done | bytes 147488 | tf_op jit(solution)/shard_map/ppermute | solution.py:545
  21.1 0.6 %collective-permute-start.5 = (bf16[1152,128]{1,0:T(8,128)(2,1)S(1)}, bf16[1152,128]{1,0:T(8,128)(2,1)S(1)}, u32[]{:S(2)}, u32[]{:S(2)}) collective-permute-start(bf16[1152,128]{1,0:T(8,128)(2,1)S(1)} %shard_map.112.x_sent), channel_id=1, source_target_pairs={{0,1},{1,0},{2,3},{3,2},{4,5},{5,4},{6,7},{7,6},{8,9},{9,8},{10,11... | collective-permute-start | bytes 884744 | tf_op jit(solution)/shard_map/ppermute | solution.py:554
  21.8 1.1 %collective-permute-done.5.x_swapped = bf16[1152,128]{1,0:T(8,128)(2,1)S(1)} collective-permute-done((bf16[1152,128]{1,0:T(8,128)(2,1)S(1)}, bf16[1152,128]{1,0:T(8,128)(2,1)S(1)}, u32[]{:S(2)}, u32[]{:S(2)}) %collective-permute-start.5) | collective-permute-done | bytes 294944 | tf_op jit(solution)/shard_map/ppermute | solution.py:554
  22.9 2.7 %shard_map.113 = (bf16[72,4096]{1,0:T(8,128)(2,1)S(1)}, bf16[72,768]{1,0:T(8,128)(2,1)S(1)}, bf16[72,768]{1,0:T(8,128)(2,1)S(1)}, bf16[72,768]{1,0:T(8,128)(2,1)S(1)}) custom-call(bf16[1152,128]{1,0:T(8,128)(2,1)S(1)} %shard_map.112.x_sent, bf16[1152,128]{1,0:T(8,128)(2,1)S(1)} %collective-permute-done.5.x_swapped, bf16[1,4096,768]{2,1,0:T(8,128)(2,1)S(1)} %bitcast.3, ...), custom_call_target="tpu_custom_call" | custom-call | flops 905969664 | tf_op jit(solution)/shard_map/pallas_call | solution.py:132
  25.6 1.4 %shard_map.114 = (f32[720,128]{1,0:T(8,128)S(1)}, f32[432,128]{1,0:T(8,128)S(1)}, bf16[432,128]{1,0:T(8,128)(2,1)S(1)}, bf16[720,128]{1,0:T(8,128)(2,1)S(1)}) custom-call(bf16[72,768]{1,0:T(8,128)(2,1)S(1)} %get-tuple-element.57.hidden, bf16[1,768,4096]{2,1,0:T(8,128)(2,1)S(1)} %bitcast.7), custom_call_target="tpu_custom_call" | custom-call | flops 452984832 | tf_op jit(solution)/shard_map/pallas_call | solution.py:132
  27.0 0.5 collective-permute-start.6
  27.6 4.9 %shard_map.117 = (bf16[72,4096]{1,0:T(8,128)(2,1)S(1)}, bf16[72,768]{1,0:T(8,128)(2,1)S(1)}, bf16[72,768]{1,0:T(8,128)(2,1)S(1)}, f32[432,128]{1,0:T(8,128)S(1)}, bf16[720,128]{1,0:T(8,128)(2,1)S(1)}) custom-call(bf16[1152,128]{1,0:T(8,128)(2,1)S(1)} %shard_map.116.g_sent, bf16[1152,128]{1,0:T(8,128)(2,1)S(1)} %collective-permute-done.9.g_swapped, ...), custom_call_target="tpu_custom_call" | custom-call | flops 905969664 | tf_op jit(solution)/shard_map/pallas_call | solution.py:132
  32.5 0.5 collective-permute-start.10
  33.0 4.2 %collective-permute-start.8 = (bf16[288,128]{1,0:T(8,128)(2,1)S(1)}, bf16[288,128]{1,0:T(8,128)(2,1)S(1)}, u32[]{:S(2)}, u32[]{:S(2)}) collective-permute-start(bf16[288,128]{1,0:T(8,128)(2,1)S(1)} %shard_map.115), channel_id=1, source_target_pairs={{0,8},{1,11},{2,10},{3,9},{4,12},{5,15},{6,14},{7,13},{8,0},{9,3},... | collective-permute-start | bytes 221192 | tf_op jit(solution)/shard_map/ppermute | solution.py:545
  37.2 2.1 %shard_map.118 = (f32[720,128]{1,0:T(8,128)S(1)}, bf16[144,128]{1,0:T(8,128)(2,1)S(1)}, bf16[144,128]{1,0:T(8,128)(2,1)S(1)}, bf16[144,128]{1,0:T(8,128)(2,1)S(1)}) custom-call(bf16[72,768]{1,0:T(8,128)(2,1)S(1)} %get-tuple-element.64.pre_gate, bf16[72,768]{1,0:T(8,128)(2,1)S(1)} %get-tuple-element.65.pre_up, bf16[1,4096,768]{2,1,0:T(8,128)(2,1)S(1)} %bitcast.3, ...), custom_call_target="tpu_custom_call" | custom-call | flops 452984832 | tf_op jit(solution)/shard_map/pallas_call | solution.py:132
  39.3 0.5 collective-permute-start.11
  39.8 0.4 collective-permute-start.13
  40.3 0.4 collective-permute-done.11.refs_7_
  40.6 0.3 collective-permute-done.12.refs_8_
  41.1 0.4 collective-permute-done.8.refs_10_.early
  41.7 2.7 %collective-permute-start.15 = (bf16[576,128]{1,0:T(8,128)(2,1)S(1)}, bf16[576,128]{1,0:T(8,128)(2,1)S(1)}, u32[]{:S(2)}, u32[]{:S(2)}) collective-permute-start(bf16[576,128]{1,0:T(8,128)(2,1)S(1)} %get-tuple-element.73), channel_id=1, source_target_pairs={{0,12},{1,15},{2,14},{3,13},{4,8},{5,11},{6,10},{7,9},{8,4},{9,7},... | collective-permute-start | bytes 442376 | tf_op jit(solution)/shard_map/ppermute | solution.py:545
  44.4 1.7 %collective-permute-start.14 = (bf16[288,128]{1,0:T(8,128)(2,1)S(1)}, bf16[288,128]{1,0:T(8,128)(2,1)S(1)}, u32[]{:S(2)}, u32[]{:S(2)}) collective-permute-start(bf16[288,128]{1,0:T(8,128)(2,1)S(1)} %get-tuple-element.72), channel_id=1, source_target_pairs={{0,8},{1,11},{2,10},{3,9},{4,12},{5,15},{6,14},{7,13},{8,0},{9,3},... | collective-permute-start | bytes 221192 | tf_op jit(solution)/shard_map/ppermute | solution.py:545
  46.1 0.9 %collective-permute-start.17 = (bf16[288,128]{1,0:T(8,128)(2,1)S(1)}, bf16[288,128]{1,0:T(8,128)(2,1)S(1)}, u32[]{:S(2)}, u32[]{:S(2)}) collective-permute-start(bf16[288,128]{1,0:T(8,128)(2,1)S(1)} %get-tuple-element.75), channel_id=1, source_target_pairs={{0,2},{2,0},{4,6},{6,4},{8,10},{10,8},{12,14},{14,12},{1,3},{3,1},... | collective-permute-start | bytes 221192 | tf_op jit(solution)/shard_map/ppermute | solution.py:550
  47.0 9.1 %shard_map.120 = (bf16[1,4096,768]{2,1,0:T(8,128)(2,1)}, bf16[1,4096,768]{2,1,0:T(8,128)(2,1)}, bf16[1,768,4096]{2,1,0:T(8,128)(2,1)}, f32[8,128]{1,0:T(8,128)S(1)}) custom-call(bf16[72,4096]{1,0:T(8,128)(2,1)S(1)} %get-tuple-element.76.x, bf16[72,4096]{1,0:T(8,128)(2,1)S(1)} %get-tuple-element.77.g, bf16[72,768]{1,0:T(8,128)(2,1)S(1)} %get-tuple-element.57.hidden, ...), custom_call_target="tpu_custom_call" | custom-call | flops 1358954496 | bytes 18874368 | tf_op jit(solution)/shard_map/pallas_call | solution.py:132
  56.2 0.3 collective-permute-start.18
  56.5 0.9 %shard_map.122 = (f32[128,2048]{1,0:T(8,128)S(1)}, f32[128,2048]{1,0:T(8,128)S(1)}) custom-call(bf16[72,128]{1,0:T(8,128)(2,1)S(1)} %get-tuple-element.79.place, f32[72,128]{1,0:T(8,128)S(1)} %get-tuple-element.80.mix, bf16[288,128]{1,0:T(8,128)(2,1)S(1)} %collective-permute-done.8.refs_10_.early, bf16[288,128]{1,0:T(8,128)(2,1)S(1)} %collective-permute-done.14.refs_0_, ...), custom_call_target="tpu_custom_call" | custom-call | flops 75497472 | tf_op jit(solution)/shard_map/pallas_call | solution.py:132
  57.4 0.3 collective-permute-done.18.shared
  57.7 1.4 %shard_map.123 = (bf16[128,2048]{1,0:T(8,128)(2,1)}, bf16[128,2048]{1,0:T(8,128)(2,1)}) custom-call(bf16[27,128]{1,0:T(8,128)(2,1)S(1)} %get-tuple-element.47.place, f32[27,128]{1,0:T(8,128)S(1)} %get-tuple-element.48.mix, bf16[864,128]{1,0:T(8,128)(2,1)S(1)} %collective-permute-done.18.shared, f32[128,2048]{1,0:T(8,128)S(1)} %get-tuple-element.82.out_sum, ...), custom_call_target="tpu_custom_call" | custom-call | bytes 2097152 | tf_op jit(solution)/shard_map/pallas_call | solution.py:132
  (35 shorter events, 0.7 us)
Async XLA Ops:
  0.6 22.2 %slice-start = ((s8[6291456]{0:T(1024)(128)(4,1)}), s8[4194304]{0:T(1024)(128)(4,1)S(1)}, s32[]{:S(2)}) async-start(s8[6291456]{0:T(1024)(128)(4,1)} %bitcast.2), calls=%async_computation | async-start | bytes 8388608
  0.6 22.2 %slice-start.2 = ((s8[6291456]{0:T(1024)(128)(4,1)}), s8[4194304]{0:T(1024)(128)(4,1)S(1)}, s32[]{:S(2)}) async-start(s8[6291456]{0:T(1024)(128)(4,1)} %bitcast.4), calls=%async_computation.2 | async-start | bytes 8388608
  2.7 1.6 %collective-permute-start = (bf16[864,128]{1,0:T(8,128)(2,1)S(1)}, bf16[864,128]{1,0:T(8,128)(2,1)S(1)}, u32[]{:S(2)}, u32[]{:S(2)}) collective-permute-start(bf16[864,128]{1,0:T(8,128)(2,1)S(1)} %get-tuple-element.51), channel_id=1, source_target_pairs={{0,1},{1,0},{2,3},{3,2},{4,5},{5,4},{6,7},{7,6},{8,9},{9,8},{10,11... | collective-permute-start | bytes 663560 | tf_op jit(solution)/shard_map/ppermute | solution.py:554
  4.4 18.5 %slice-start.1 = ((s8[6291456]{0:T(1024)(128)(4,1)}), s8[2097152]{0:T(1024)(128)(4,1)S(1)}, s32[]{:S(2)}) async-start(s8[6291456]{0:T(1024)(128)(4,1)} %bitcast.2), calls=%async_computation.1 | async-start | bytes 4194304
  4.4 18.5 %slice-start.3 = ((s8[6291456]{0:T(1024)(128)(4,1)}), s8[2097152]{0:T(1024)(128)(4,1)S(1)}, s32[]{:S(2)}) async-start(s8[6291456]{0:T(1024)(128)(4,1)} %bitcast.4), calls=%async_computation.3 | async-start | bytes 4194304
  4.4 14.8 %collective-permute-start.1 = (bf16[576,128]{1,0:T(8,128)(2,1)S(1)}, bf16[576,128]{1,0:T(8,128)(2,1)S(1)}, u32[]{:S(2)}, u32[]{:S(2)}) collective-permute-start(bf16[576,128]{1,0:T(8,128)(2,1)S(1)} %get-tuple-element.52), channel_id=1, source_target_pairs={{0,8},{1,11},{2,10},{3,9},{4,12},{5,15},{6,14},{7,13},{8,0},{9,3},... | collective-permute-start | bytes 442376 | tf_op jit(solution)/shard_map/ppermute | solution.py:545
  8.4 10.8 %collective-permute-start.2 = (bf16[576,128]{1,0:T(8,128)(2,1)S(1)}, bf16[576,128]{1,0:T(8,128)(2,1)S(1)}, u32[]{:S(2)}, u32[]{:S(2)}) collective-permute-start(bf16[576,128]{1,0:T(8,128)(2,1)S(1)} %get-tuple-element.53), channel_id=1, source_target_pairs={{0,12},{1,15},{2,14},{3,13},{4,8},{5,11},{6,10},{7,9},{8,4},{9,7},... | collective-permute-start | bytes 442376 | tf_op jit(solution)/shard_map/ppermute | solution.py:545
  9.8 11.3 %collective-permute-start.3 = (bf16[576,128]{1,0:T(8,128)(2,1)S(1)}, bf16[576,128]{1,0:T(8,128)(2,1)S(1)}, u32[]{:S(2)}, u32[]{:S(2)}) collective-permute-start(bf16[576,128]{1,0:T(8,128)(2,1)S(1)} %get-tuple-element.54), channel_id=1, source_target_pairs={{0,4},{1,7},{2,6},{3,5},{4,0},{5,3},{6,2},{7,1},{8,12},{9,15},{10,... | collective-permute-start | bytes 442376 | tf_op jit(solution)/shard_map/ppermute | solution.py:545
  10.0 6.0 %collective-permute-start.4 = (bf16[288,128]{1,0:T(8,128)(2,1)S(1)}, bf16[288,128]{1,0:T(8,128)(2,1)S(1)}, u32[]{:S(2)}, u32[]{:S(2)}) collective-permute-start(bf16[288,128]{1,0:T(8,128)(2,1)S(1)} %get-tuple-element.55), channel_id=1, source_target_pairs={{0,2},{2,0},{4,6},{6,4},{8,10},{10,8},{12,14},{14,12},{1,3},{3,1},... | collective-permute-start | bytes 221192 | tf_op jit(solution)/shard_map/ppermute | solution.py:550
  21.1 1.8 %collective-permute-start.5 = (bf16[1152,128]{1,0:T(8,128)(2,1)S(1)}, bf16[1152,128]{1,0:T(8,128)(2,1)S(1)}, u32[]{:S(2)}, u32[]{:S(2)}) collective-permute-start(bf16[1152,128]{1,0:T(8,128)(2,1)S(1)} %shard_map.112.x_sent), channel_id=1, source_target_pairs={{0,1},{1,0},{2,3},{3,2},{4,5},{5,4},{6,7},{7,6},{8,9},{9,8},{10,11... | collective-permute-start | bytes 884744 | tf_op jit(solution)/shard_map/ppermute | solution.py:554
  21.7 4.0 %slice-start.4 = ((s8[6291456]{0:T(1024)(128)(4,1)}), s8[4194304]{0:T(1024)(128)(4,1)S(1)}, s32[]{:S(2)}) async-start(s8[6291456]{0:T(1024)(128)(4,1)} %bitcast.6), calls=%async_computation.4 | async-start | bytes 8388608
  21.7 4.0 %slice-start.5 = ((s8[6291456]{0:T(1024)(128)(4,1)}), s8[2097152]{0:T(1024)(128)(4,1)S(1)}, s32[]{:S(2)}) async-start(s8[6291456]{0:T(1024)(128)(4,1)} %bitcast.6), calls=%async_computation.5 | async-start | bytes 4194304
  21.7 5.9 %collective-permute-start.9 = (bf16[1152,128]{1,0:T(8,128)(2,1)S(1)}, bf16[1152,128]{1,0:T(8,128)(2,1)S(1)}, u32[]{:S(2)}, u32[]{:S(2)}) collective-permute-start(bf16[1152,128]{1,0:T(8,128)(2,1)S(1)} %shard_map.116.g_sent), channel_id=1, source_target_pairs={{0,1},{1,0},{2,3},{3,2},{4,5},{5,4},{6,7},{7,6},{8,9},{9,8},{10,11... | collective-permute-start | bytes 884744 | tf_op jit(solution)/shard_map/ppermute | solution.py:554
  27.0 5.9 %collective-permute-start.6 = (bf16[720,128]{1,0:T(8,128)(2,1)S(1)}, bf16[720,128]{1,0:T(8,128)(2,1)S(1)}, u32[]{:S(2)}, u32[]{:S(2)}) collective-permute-start(bf16[720,128]{1,0:T(8,128)(2,1)S(1)} %get-tuple-element.60), channel_id=1, source_target_pairs={{0,1},{1,0},{2,3},{3,2},{4,5},{5,4},{6,7},{7,6},{8,9},{9,8},{10,11... | collective-permute-start | bytes 552968 | tf_op jit(solution)/shard_map/ppermute | solution.py:554
  27.5 5.4 %collective-permute-start.7 = (bf16[432,128]{1,0:T(8,128)(2,1)S(1)}, bf16[432,128]{1,0:T(8,128)(2,1)S(1)}, u32[]{:S(2)}, u32[]{:S(2)}) collective-permute-start(bf16[432,128]{1,0:T(8,128)(2,1)S(1)} %get-tuple-element.61), channel_id=1, source_target_pairs={{0,1},{1,0},{2,3},{3,2},{4,5},{5,4},{6,7},{7,6},{8,9},{9,8},{10,11... | collective-permute-start | bytes 331784 | tf_op jit(solution)/shard_map/ppermute | solution.py:554
  32.5 8.6 %collective-permute-start.10 = (bf16[720,128]{1,0:T(8,128)(2,1)S(1)}, bf16[720,128]{1,0:T(8,128)(2,1)S(1)}, u32[]{:S(2)}, u32[]{:S(2)}) collective-permute-start(bf16[720,128]{1,0:T(8,128)(2,1)S(1)} %get-tuple-element.68), channel_id=1, source_target_pairs={{0,1},{1,0},{2,3},{3,2},{4,5},{5,4},{6,7},{7,6},{8,9},{9,8},{10,11... | collective-permute-start | bytes 552968 | tf_op jit(solution)/shard_map/ppermute | solution.py:554
  33.0 8.6 %collective-permute-start.8 = (bf16[288,128]{1,0:T(8,128)(2,1)S(1)}, bf16[288,128]{1,0:T(8,128)(2,1)S(1)}, u32[]{:S(2)}, u32[]{:S(2)}) collective-permute-start(bf16[288,128]{1,0:T(8,128)(2,1)S(1)} %shard_map.115), channel_id=1, source_target_pairs={{0,8},{1,11},{2,10},{3,9},{4,12},{5,15},{6,14},{7,13},{8,0},{9,3},... | collective-permute-start | bytes 221192 | tf_op jit(solution)/shard_map/ppermute | solution.py:545
  39.3 1.4 %collective-permute-start.11 = (bf16[144,128]{1,0:T(8,128)(2,1)S(1)}, bf16[144,128]{1,0:T(8,128)(2,1)S(1)}, u32[]{:S(2)}, u32[]{:S(2)}) collective-permute-start(bf16[144,128]{1,0:T(8,128)(2,1)S(1)} %get-tuple-element.69), channel_id=1, source_target_pairs={{0,1},{1,0},{2,3},{3,2},{4,5},{5,4},{6,7},{7,6},{8,9},{9,8},{10,11... | collective-permute-start | bytes 110600 | tf_op jit(solution)/shard_map/ppermute | solution.py:554
  39.8 1.2 %collective-permute-start.12 = (bf16[144,128]{1,0:T(8,128)(2,1)S(1)}, bf16[144,128]{1,0:T(8,128)(2,1)S(1)}, u32[]{:S(2)}, u32[]{:S(2)}) collective-permute-start(bf16[144,128]{1,0:T(8,128)(2,1)S(1)} %get-tuple-element.70), channel_id=1, source_target_pairs={{0,1},{1,0},{2,3},{3,2},{4,5},{5,4},{6,7},{7,6},{8,9},{9,8},{10,11... | collective-permute-start | bytes 110600 | tf_op jit(solution)/shard_map/ppermute | solution.py:554
  39.8 1.3 %collective-permute-start.13 = (bf16[144,128]{1,0:T(8,128)(2,1)S(1)}, bf16[144,128]{1,0:T(8,128)(2,1)S(1)}, u32[]{:S(2)}, u32[]{:S(2)}) collective-permute-start(bf16[144,128]{1,0:T(8,128)(2,1)S(1)} %get-tuple-element.71), channel_id=1, source_target_pairs={{0,1},{1,0},{2,3},{3,2},{4,5},{5,4},{6,7},{7,6},{8,9},{9,8},{10,11... | collective-permute-start | bytes 110600 | tf_op jit(solution)/shard_map/ppermute | solution.py:554
  41.7 14.5 %collective-permute-start.15 = (bf16[576,128]{1,0:T(8,128)(2,1)S(1)}, bf16[576,128]{1,0:T(8,128)(2,1)S(1)}, u32[]{:S(2)}, u32[]{:S(2)}) collective-permute-start(bf16[576,128]{1,0:T(8,128)(2,1)S(1)} %get-tuple-element.73), channel_id=1, source_target_pairs={{0,12},{1,15},{2,14},{3,13},{4,8},{5,11},{6,10},{7,9},{8,4},{9,7},... | collective-permute-start | bytes 442376 | tf_op jit(solution)/shard_map/ppermute | solution.py:545
  44.4 11.8 %collective-permute-start.16 = (bf16[576,128]{1,0:T(8,128)(2,1)S(1)}, bf16[576,128]{1,0:T(8,128)(2,1)S(1)}, u32[]{:S(2)}, u32[]{:S(2)}) collective-permute-start(bf16[576,128]{1,0:T(8,128)(2,1)S(1)} %get-tuple-element.74), channel_id=1, source_target_pairs={{0,4},{1,7},{2,6},{3,5},{4,0},{5,3},{6,2},{7,1},{8,12},{9,15},{10,... | collective-permute-start | bytes 442376 | tf_op jit(solution)/shard_map/ppermute | solution.py:545
  44.4 11.7 %collective-permute-start.14 = (bf16[288,128]{1,0:T(8,128)(2,1)S(1)}, bf16[288,128]{1,0:T(8,128)(2,1)S(1)}, u32[]{:S(2)}, u32[]{:S(2)}) collective-permute-start(bf16[288,128]{1,0:T(8,128)(2,1)S(1)} %get-tuple-element.72), channel_id=1, source_target_pairs={{0,8},{1,11},{2,10},{3,9},{4,12},{5,15},{6,14},{7,13},{8,0},{9,3},... | collective-permute-start | bytes 221192 | tf_op jit(solution)/shard_map/ppermute | solution.py:545
  46.1 10.0 %collective-permute-start.17 = (bf16[288,128]{1,0:T(8,128)(2,1)S(1)}, bf16[288,128]{1,0:T(8,128)(2,1)S(1)}, u32[]{:S(2)}, u32[]{:S(2)}) collective-permute-start(bf16[288,128]{1,0:T(8,128)(2,1)S(1)} %get-tuple-element.75), channel_id=1, source_target_pairs={{0,2},{2,0},{4,6},{6,4},{8,10},{10,8},{12,14},{14,12},{1,3},{3,1},... | collective-permute-start | bytes 221192 | tf_op jit(solution)/shard_map/ppermute | solution.py:550
  56.2 1.5 %collective-permute-start.18 = (bf16[864,128]{1,0:T(8,128)(2,1)S(1)}, bf16[864,128]{1,0:T(8,128)(2,1)S(1)}, u32[]{:S(2)}, u32[]{:S(2)}) collective-permute-start(bf16[864,128]{1,0:T(8,128)(2,1)S(1)} %shard_map.121), channel_id=1, source_target_pairs={{0,1},{1,0},{2,3},{3,2},{4,5},{5,4},{6,7},{7,6},{8,9},{9,8},{10,11... | collective-permute-start | bytes 663560 | tf_op jit(solution)/shard_map/ppermute | solution.py:554

commit v13 on v11

--- a/solution.py
+++ b/solution.py
@@ -231,24 +231,40 @@
     write(g_mine, count)
 
 
-def pack_kernel(size, x_mine, g_mine, swapped, *outs):
-    count = len(outs)
-    for j, out in enumerate(outs):
-        for i, mine in enumerate((x_mine, g_mine)):
-            part(out, 2 * i * size, size)[...] = part(mine, j * size, size)[...]
-            part(out, (2 * i + 1) * size, size)[...] = part(swapped, (i * count + j) * size, size)[...]
-
-
-def gather_kernel(size, at, *refs):
-    blocks, (near, here, out) = refs[:-3], refs[-3:]
+def pack_kernel(size, late, x_mine, g_mine, swapped, *outs):
+    count = len(outs) - len(late)
+    lates = dict(zip(late, outs[count:]))
+    for j, out in enumerate(outs[:count]):
+        places = ((out, 0), (lates.get(j, out), 0 if j in late else 2 * size))
+        for i, (mine, (to, at)) in enumerate(zip((x_mine, g_mine), places)):
+            part(to, at, size)[...] = part(mine, j * size, size)[...]
+            part(to, at + size, size)[...] = part(swapped, (i * count + j) * size, size)[...]
+    for out in lates.values():
+        rest = part(out, 2 * size, out.shape[0] - 2 * size)
+        rest[...] = jnp.zeros(rest.shape, rest.dtype)
+
+
+def gather_x_kernel(size, *refs):
+    count = (len(refs) - 3) // 2
+    blocks, (near, here), outs = refs[:count], refs[count : count + 2], refs[count + 2 :]
+    for block, out in zip(blocks, outs):
+        out[...] = part(block, 0, 2 * size)[...]
+    part(outs[-1], 0, size)[...] = part(near, 0, size)[...]
+    part(outs[-1], size, size)[...] = part(here, 0, size)[...]
+
+
+def gather_g_kernel(size, late, *refs):
+    blocks, (near, here, _, out) = refs[:-4], refs[-4:]
     for j, block in enumerate(blocks):
-        part(out, 2 * j * size, 2 * size)[...] = part(block, 2 * at, 2 * size)[...]
-    part(out, 2 * len(blocks) * size, size)[...] = part(near, at, size)[...]
-    part(out, (2 * len(blocks) + 1) * size, size)[...] = part(here, at, size)[...]
+        start = 0 if j in late else 2 * size
+        part(out, 2 * j * size, 2 * size)[...] = part(block, start, 2 * size)[...]
+    part(out, 2 * len(blocks) * size, size)[...] = part(near, size, size)[...]
+    part(out, (2 * len(blocks) + 1) * size, size)[...] = part(here, size, size)[...]
 
 
 def full_rows(devices, subs, scratch, own_sent, other_sent, out):
-    size = own_sent.shape[0] // devices
+    per = devices // len(own_sent)
+    size = own_sent[0].shape[0] // per
     count = devices // 2 - 1
     own, other = half_starts(out.shape[1] // 2)
     first, second, last = range(0, 2 * count, 2), range(1, 2 * count, 2), range(2 * count, devices)
@@ -261,7 +277,7 @@
         def put(sub, value):
             out[:, pl.ds(start + sub * LANES, LANES)] = value.astype(out.dtype)
 
-        blocks_to_rows(scratch, [part(ref, i * size, size) for ref, i in layout], put, subs)
+        blocks_to_rows(scratch, [part(refs[i // per], i % per * size, size) for refs, i in layout], put, subs)
 
 
 def split_terms(count, size, scratch, own_half, keep, send):
@@ -367,7 +383,10 @@
     split_terms(devices // 2 - 1, size, scratch, own_half, keep, send)
 
 
-def forward_kernel(devices, subs, step, x_sent, x_swapped, w_gate, w_up, x_full, gate, up, hidden, scratch):
+def forward_kernel(devices, subs, step, *refs):
+    half = devices // 2
+    x_sent, x_swapped = refs[:half], refs[half : 2 * half]
+    w_gate, w_up, x_full, gate, up, hidden, scratch = refs[2 * half :]
     full_rows(devices, subs, scratch, x_sent, x_swapped, x_full)
     for cols in pieces_of(gate.shape[1], step):
         gate_low = dot(x_full[...], w_gate[0, :, cols]).astype(jnp.bfloat16)
@@ -415,7 +434,7 @@
     scratch,
 ):
     _, other = half_starts(subs * LANES)
-    full_rows(devices, subs, scratch, g_sent, g_swapped, g_full)
+    full_rows(devices, subs, scratch, [g_sent], [g_swapped], g_full)
 
     def pull(i, carry):
         cols = chunk(i, step)
@@ -572,25 +591,27 @@
         traffic=4 * tok_dev * sub_width,
     )
     masks = even_masks(devices)
+    late = [devices // 4 - 1]
+    late_block = jax.ShapeDtypeStruct((2 * size + 16, LANES), low)
     packed = call(
-        functools.partial(pack_kernel, size),
-        [lines(4)] * count,
+        functools.partial(pack_kernel, size, late),
+        [lines(2 if j in late else 4) for j in range(count)] + [late_block] * len(late),
         (x_mine, g_mine, swap(theirs)),
         flops=24 * half_flops,
     )
-    arrived = exchange(packed, masks, devices)
+    x_arrived = exchange(packed[:count], masks, devices)
+    g_arrived = list(x_arrived)
+    for j, block in zip(late, packed[count:]):
+        (g_arrived[j],) = exchange([block], masks[j:], devices)
     near = exchange_near(near, devices)
 
     weights = (gate_weight, up_weight, down_weight)
     w_gate, w_up, w_down = [pltpu.with_memory_space_constraint(w, pltpu.VMEM) for w in weights]
 
-    def gather(at):
-        return call(functools.partial(gather_kernel, size, at), [lines(devices)], (*arrived, near, here))[0]
-
-    x_sent = gather(0)
-    x_swapped = swap(x_sent)
-    g_sent = gather(size)
-    g_swapped = swap(g_sent)
+    x_sent = call(
+        functools.partial(gather_x_kernel, size), [lines(2)] * (count + 1), (*x_arrived, near, here)
+    )
+    x_swapped = [swap(value) for value in x_sent]
     terms = [
         lines_in_vmem(count + 2, full),
         lines_in_vmem(count, full),
@@ -600,10 +621,13 @@
     x_full, gate, up, hidden = call(
         functools.partial(forward_kernel, devices, subs, step),
         [vmem((rows, width), low)] + [vmem((rows, lanes), low)] * 3,
-        (x_sent, x_swapped, w_gate, w_up),
+        (*x_sent, *x_swapped, w_gate, w_up),
         scratch=spread_scratch,
-        flops=4 * half_flops,
-    )
+    )
+    (g_sent,) = call(
+        functools.partial(gather_g_kernel, size, late), [lines(devices)], (*g_arrived, near, here, hidden)
+    )
+    g_swapped = swap(g_sent)
     out_own, out_other, send_own, send_other = call(
         functools.partial(output_kernel, devices, subs, 2 * step),
         terms,

time: 56.8 us -> 55.7 us (0.981)
  waiting for transfers between devices: 15.6 us -> 8.44 us
  starting transfers between devices: 15.6 us -> 21.6 us
    ppermute x6 -> x7, starting transfers between devices: 10.5 us -> 14.9 us  [exchange(): arrived.append(lax.ppermute(block, ('expert', 'ffn'), pairs))]
    ppermute x2, waiting for transfers between devices: 4.55 us -> 0.77 us  [exchange_near(): return lax.ppermute(block, 'expert', [(i, i ^ 1) for i in range(devices)])]
    ppermute x6 -> x7, waiting for transfers between devices: 7.05 us -> 4.48 us  [exchange(): arrived.append(lax.ppermute(block, ('expert', 'ffn'), pairs))]
    ppermute x8 -> x11, starting transfers between devices: 2.5 us -> 4.12 us  [swap(): return lax.ppermute(value, 'ffn', [(0, 1), (1, 0)])]
    ppermute x8 -> x11, waiting for transfers between devices: 3.96 us -> 3.19 us  [swap(): return lax.ppermute(value, 'ffn', [(0, 1), (1, 0)])]
  transfers between devices with their start and end apart: 16 -> 20, of which waited for: 9 -> 11; matrix products, arithmetic and copies ran while one was open for 0% -> 0% of each run, Pallas kernels for 37% -> 38%
where the time goes in v13:
time: 55.7 us; the launch traced here: 55.6 us
  Pallas kernels  24.7 us (44%)
  starting transfers between devices  21.6 us (39%)
  waiting for transfers between devices  8.44 us (15%)
  between operations  0.79 us (1%)
    pallas_call x13, Pallas kernels, call(): pl.pallas_call(kernel, out_shape=tuple(out_shape), in_specs=[pl.BlockSpec...  24.7 us
    ppermute x7, starting transfers between devices, exchange(): arrived.append(lax.ppermute(block, ('expert', 'ffn'), pairs))  14.9 us
    ppermute x7, waiting for transfers between devices, exchange(): arrived.append(lax.ppermute(block, ('expert', 'ffn'), pairs))  4.48 us
    ppermute x11, starting transfers between devices, swap(): return lax.ppermute(value, 'ffn', [(0, 1), (1, 0)])  4.12 us
    ppermute x11, waiting for transfers between devices, swap(): return lax.ppermute(value, 'ffn', [(0, 1), (1, 0)])  3.19 us
    ppermute x2, starting transfers between devices, exchange_near(): return lax.ppermute(block, 'expert', [(i, i ^ 1) for i in range(devices)])  2.63 us
  transfers between devices with their start and end apart: 20, of which 11 were waited for; matrix products, arithmetic and copies ran while one was open for 0% of the time, Pallas kernels for 38%

profile of v13, /device:TPU:0, one launch (start us, length us, event | category | flops | bytes accessed | tf_op | source)
XLA Modules:
  0.0 55.6 jit_solution(3832374499238922633)
XLA Ops:
  0.7 2.1 %shard_map.110 = (bf16[432,128]{1,0:T(8,128)(2,1)S(1)}, bf16[432,128]{1,0:T(8,128)(2,1)S(1)}, bf16[288,128]{1,0:T(8,128)(2,1)S(1)}, bf16[288,128]{1,0:T(8,128)(2...) custom-call(s32[8,128]{1,0:T(8,128)} %bitcast.8, ...), custom_call_target="tpu_custom_call" | custom-call | bytes 1048576 | tf_op jit(solution)/shard_map/pallas_call | solution.py:132
  2.7 0.5 collective-permute-start
  3.3 1.1 %collective-permute-done.swapped = bf16[864,128]{1,0:T(8,128)(2,1)S(1)} collective-permute-done((bf16[864,128]{1,0:T(8,128)(2,1)S(1)}, bf16[864,128]{1,0:T(8,128)(2,1)S(1)}, u32[]{:S(2)}, u32[]{:S(2)}) %collective-permute-start) | collective-permute-done | bytes 221216 | tf_op jit(solution)/shard_map/ppermute | solution.py:550
  4.4 4.0 %collective-permute-start.1 = (bf16[576,128]{1,0:T(8,128)(2,1)S(1)}, bf16[576,128]{1,0:T(8,128)(2,1)S(1)}, u32[]{:S(2)}, u32[]{:S(2)}) collective-permute-start(bf16[576,128]{1,0:T(8,128)(2,1)S(1)} %get-tuple-element.55), channel_id=1, source_target_pairs={{0,8},{1,11},{2,10},{3,9},{4,12},{5,15},{6,14},{7,13},{8,0},{9,3},... | collective-permute-start | bytes 442376 | tf_op jit(solution)/shard_map/ppermute | solution.py:541
  8.4 1.6 %collective-permute-start.3 = (bf16[576,128]{1,0:T(8,128)(2,1)S(1)}, bf16[576,128]{1,0:T(8,128)(2,1)S(1)}, u32[]{:S(2)}, u32[]{:S(2)}) collective-permute-start(bf16[576,128]{1,0:T(8,128)(2,1)S(1)} %get-tuple-element.57), channel_id=1, source_target_pairs={{0,4},{1,7},{2,6},{3,5},{4,0},{5,3},{6,2},{7,1},{8,12},{9,15},{10,... | collective-permute-start | bytes 442376 | tf_op jit(solution)/shard_map/ppermute | solution.py:541
  10.0 1.5 %collective-permute-start.4 = (bf16[288,128]{1,0:T(8,128)(2,1)S(1)}, bf16[288,128]{1,0:T(8,128)(2,1)S(1)}, u32[]{:S(2)}, u32[]{:S(2)}) collective-permute-start(bf16[288,128]{1,0:T(8,128)(2,1)S(1)} %get-tuple-element.58), channel_id=1, source_target_pairs={{0,2},{2,0},{4,6},{6,4},{8,10},{10,8},{12,14},{14,12},{1,3},{3,1},... | collective-permute-start | bytes 221192 | tf_op jit(solution)/shard_map/ppermute | solution.py:546
  11.5 0.2 collective-permute-start.2
  11.7 3.6 %collective-permute-start.11 = (bf16[304,128]{1,0:T(8,128)(2,1)S(1)}, bf16[304,128]{1,0:T(8,128)(2,1)S(1)}, u32[]{:S(2)}, u32[]{:S(2)}) collective-permute-start(bf16[304,128]{1,0:T(8,128)(2,1)S(1)} %get-tuple-element.69), channel_id=1, source_target_pairs={{0,12},{1,15},{2,14},{3,13},{4,8},{5,11},{6,10},{7,9},{8,4},{9,7},... | collective-permute-start | bytes 233480 | tf_op jit(solution)/shard_map/ppermute | solution.py:541
  15.3 0.8 %collective-permute-done.4.refs_3_ = bf16[288,128]{1,0:T(8,128)(2,1)S(1)} collective-permute-done((bf16[288,128]{1,0:T(8,128)(2,1)S(1)}, bf16[288,128]{1,0:T(8,128)(2,1)S(1)}, u32[]{:S(2)}, u32[]{:S(2)}) %collective-permute-start.4) | collective-permute-done | bytes 73760 | tf_op jit(solution)/shard_map/ppermute | solution.py:546
  16.1 3.2 %collective-permute-done.2.refs_1_ = bf16[288,128]{1,0:T(8,128)(2,1)S(1)} collective-permute-done((bf16[288,128]{1,0:T(8,128)(2,1)S(1)}, bf16[288,128]{1,0:T(8,128)(2,1)S(1)}, u32[]{:S(2)}, u32[]{:S(2)}) %collective-permute-start.2) | collective-permute-done | bytes 73760 | tf_op jit(solution)/shard_map/ppermute | solution.py:541
  19.4 0.5 collective-permute-start.6
  20.0 0.4 collective-permute-start.8
  20.4 0.2 collective-permute-done.5.refs_4_
  20.8 0.4 collective-permute-done.7.refs_6_
  21.3 2.7 %shard_map.113 = (bf16[72,4096]{1,0:T(8,128)(2,1)S(1)}, bf16[72,768]{1,0:T(8,128)(2,1)S(1)}, bf16[72,768]{1,0:T(8,128)(2,1)S(1)}, bf16[72,768]{1,0:T(8,128)(2,1)S(1)}) custom-call(bf16[288,128]{1,0:T(8,128)(2,1)S(1)} %get-tuple-element.60.refs_0_, bf16[288,128]{1,0:T(8,128)(2,1)S(1)} %get-tuple-element.61.refs_1_, ...), custom_call_target="tpu_custom_call" | custom-call | tf_op jit(solution)/shard_map/pallas_call | solution.py:132
  24.1 0.4 collective-permute-start.12
  24.5 1.4 %shard_map.114 = (f32[720,128]{1,0:T(8,128)S(1)}, f32[432,128]{1,0:T(8,128)S(1)}, bf16[432,128]{1,0:T(8,128)(2,1)S(1)}, bf16[720,128]{1,0:T(8,128)(2,1)S(1)}) custom-call(bf16[72,768]{1,0:T(8,128)(2,1)S(1)} %get-tuple-element.64.hidden.refs_5_, bf16[1,768,4096]{2,1,0:T(8,128)(2,1)S(1)} %bitcast.7), custom_call_target="tpu_custom_call" | custom-call | flops 452984832 | tf_op jit(solution)/shard_map/pallas_call | solution.py:132
  25.9 0.2 collective-permute-start.9
  26.1 4.9 %shard_map.116 = (bf16[72,4096]{1,0:T(8,128)(2,1)S(1)}, bf16[72,768]{1,0:T(8,128)(2,1)S(1)}, bf16[72,768]{1,0:T(8,128)(2,1)S(1)}, f32[432,128]{1,0:T(8,128)S(1)}, bf16[720,128]{1,0:T(8,128)(2,1)S(1)}) custom-call(bf16[1152,128]{1,0:T(8,128)(2,1)S(1)} %shard_map.115.g_sent, bf16[1152,128]{1,0:T(8,128)(2,1)S(1)} %collective-permute-done.12.g_swapped, ...), custom_call_target="tpu_custom_call" | custom-call | flops 905969664 | tf_op jit(solution)/shard_map/pallas_call | solution.py:132
  31.0 0.4 collective-permute-start.13
  31.6 2.1 %shard_map.117 = (f32[720,128]{1,0:T(8,128)S(1)}, bf16[432,128]{1,0:T(8,128)(2,1)S(1)}) custom-call(bf16[72,768]{1,0:T(8,128)(2,1)S(1)} %get-tuple-element.72.pre_gate, bf16[72,768]{1,0:T(8,128)(2,1)S(1)} %get-tuple-element.73.pre_up, bf16[1,4096,768]{2,1,0:T(8,128)(2,1)S(1)} %bitcast.3, bf16[1,4096,768]{2,1,0:T(8,128)(2,1)S(1)} %bitcast.5), custom_call_target="tpu_custom_call" | custom-call | flops 452984832 | tf_op jit(solution)/shard_map/pallas_call | solution.py:132
  33.7 0.4 collective-permute-start.14
  34.1 1.0 %collective-permute-done.14.refs_7_ = bf16[432,128]{1,0:T(8,128)(2,1)S(1)} collective-permute-done((bf16[432,128]{1,0:T(8,128)(2,1)S(1)}, bf16[432,128]{1,0:T(8,128)(2,1)S(1)}, u32[]{:S(2)}, u32[]{:S(2)}) %collective-permute-start.14) | collective-permute-done | bytes 110624 | tf_op jit(solution)/shard_map/ppermute | solution.py:550
  35.2 4.8 %collective-permute-start.15 = (bf16[576,128]{1,0:T(8,128)(2,1)S(1)}, bf16[576,128]{1,0:T(8,128)(2,1)S(1)}, u32[]{:S(2)}, u32[]{:S(2)}) collective-permute-start(bf16[576,128]{1,0:T(8,128)(2,1)S(1)} %get-tuple-element.78), channel_id=1, source_target_pairs={{0,8},{1,11},{2,10},{3,9},{4,12},{5,15},{6,14},{7,13},{8,0},{9,3},... | collective-permute-start | bytes 442376 | tf_op jit(solution)/shard_map/ppermute | solution.py:541
  40.0 0.4 collective-permute-start.16
  40.7 1.1 %collective-permute-start.18 = (bf16[288,128]{1,0:T(8,128)(2,1)S(1)}, bf16[288,128]{1,0:T(8,128)(2,1)S(1)}, u32[]{:S(2)}, u32[]{:S(2)}) collective-permute-start(bf16[288,128]{1,0:T(8,128)(2,1)S(1)} %get-tuple-element.81), channel_id=1, source_target_pairs={{0,2},{2,0},{4,6},{6,4},{8,10},{10,8},{12,14},{14,12},{1,3},{3,1},... | collective-permute-start | bytes 221192 | tf_op jit(solution)/shard_map/ppermute | solution.py:546
  41.8 9.1 %shard_map.119 = (bf16[1,4096,768]{2,1,0:T(8,128)(2,1)}, bf16[1,4096,768]{2,1,0:T(8,128)(2,1)}, bf16[1,768,4096]{2,1,0:T(8,128)(2,1)}, f32[8,128]{1,0:T(8,128)S(1)}) custom-call(bf16[72,4096]{1,0:T(8,128)(2,1)S(1)} %get-tuple-element.82.x, bf16[72,4096]{1,0:T(8,128)(2,1)S(1)} %get-tuple-element.83.g, bf16[72,768]{1,0:T(8,128)(2,1)S(1)} %get-tuple-element.64.hidden.refs_5_, ...), custom_call_target="tpu_custom_call" | custom-call | flops 1358954496 | bytes 18874368 | tf_op jit(solution)/shard_map/pallas_call | solution.py:132
  51.1 1.1 %collective-permute-done.17.refs_2_ = bf16[576,128]{1,0:T(8,128)(2,1)S(1)} collective-permute-done((bf16[576,128]{1,0:T(8,128)(2,1)S(1)}, bf16[576,128]{1,0:T(8,128)(2,1)S(1)}, u32[]{:S(2)}, u32[]{:S(2)}) %collective-permute-start.17) | collective-permute-done | bytes 147488 | tf_op jit(solution)/shard_map/ppermute | solution.py:541
  52.2 0.9 %collective-permute-start.19 = (bf16[864,128]{1,0:T(8,128)(2,1)S(1)}, bf16[864,128]{1,0:T(8,128)(2,1)S(1)}, u32[]{:S(2)}, u32[]{:S(2)}) collective-permute-start(bf16[864,128]{1,0:T(8,128)(2,1)S(1)} %shard_map.120), channel_id=1, source_target_pairs={{0,1},{1,0},{2,3},{3,2},{4,5},{5,4},{6,7},{7,6},{8,9},{9,8},{10,11... | collective-permute-start | bytes 663560 | tf_op jit(solution)/shard_map/ppermute | solution.py:550
  53.1 0.9 %shard_map.121 = (f32[128,2048]{1,0:T(8,128)S(1)}, f32[128,2048]{1,0:T(8,128)S(1)}) custom-call(bf16[72,128]{1,0:T(8,128)(2,1)S(1)} %get-tuple-element.85.place, f32[72,128]{1,0:T(8,128)S(1)} %get-tuple-element.86.mix, bf16[576,128]{1,0:T(8,128)(2,1)S(1)} %collective-permute-done.15.refs_0_, bf16[576,128]{1,0:T(8,128)(2,1)S(1)} %collective-permute-done.16.refs_1_, ...), custom_call_target="tpu_custom_call" | custom-call | flops 75497472 | tf_op jit(solution)/shard_map/pallas_call | solution.py:132
  54.0 0.2 collective-permute-done.19.shared
  54.2 1.4 %shard_map.122 = (bf16[128,2048]{1,0:T(8,128)(2,1)}, bf16[128,2048]{1,0:T(8,128)(2,1)}) custom-call(bf16[27,128]{1,0:T(8,128)(2,1)S(1)} %get-tuple-element.50.place, f32[27,128]{1,0:T(8,128)S(1)} %get-tuple-element.51.mix, bf16[864,128]{1,0:T(8,128)(2,1)S(1)} %collective-permute-done.19.shared, f32[128,2048]{1,0:T(8,128)S(1)} %get-tuple-element.88.out_sum, ...), custom_call_target="tpu_custom_call" | custom-call | bytes 2097152 | tf_op jit(solution)/shard_map/pallas_call | solution.py:132
  (36 shorter events, 1.3 us)
Async XLA Ops:
  0.6 20.7 %slice-start = ((s8[6291456]{0:T(1024)(128)(4,1)}), s8[4194304]{0:T(1024)(128)(4,1)S(1)}, s32[]{:S(2)}) async-start(s8[6291456]{0:T(1024)(128)(4,1)} %bitcast.2), calls=%async_computation | async-start | bytes 8388608
  0.6 20.7 %slice-start.2 = ((s8[6291456]{0:T(1024)(128)(4,1)}), s8[4194304]{0:T(1024)(128)(4,1)S(1)}, s32[]{:S(2)}) async-start(s8[6291456]{0:T(1024)(128)(4,1)} %bitcast.4), calls=%async_computation.2 | async-start | bytes 8388608
  2.7 1.6 %collective-permute-start = (bf16[864,128]{1,0:T(8,128)(2,1)S(1)}, bf16[864,128]{1,0:T(8,128)(2,1)S(1)}, u32[]{:S(2)}, u32[]{:S(2)}) collective-permute-start(bf16[864,128]{1,0:T(8,128)(2,1)S(1)} %get-tuple-element.54), channel_id=1, source_target_pairs={{0,1},{1,0},{2,3},{3,2},{4,5},{5,4},{6,7},{7,6},{8,9},{9,8},{10,11... | collective-permute-start | bytes 663560 | tf_op jit(solution)/shard_map/ppermute | solution.py:550
  4.4 16.9 %slice-start.1 = ((s8[6291456]{0:T(1024)(128)(4,1)}), s8[2097152]{0:T(1024)(128)(4,1)S(1)}, s32[]{:S(2)}) async-start(s8[6291456]{0:T(1024)(128)(4,1)} %bitcast.2), calls=%async_computation.1 | async-start | bytes 4194304
  4.4 16.9 %slice-start.3 = ((s8[6291456]{0:T(1024)(128)(4,1)}), s8[2097152]{0:T(1024)(128)(4,1)S(1)}, s32[]{:S(2)}) async-start(s8[6291456]{0:T(1024)(128)(4,1)} %bitcast.4), calls=%async_computation.3 | async-start | bytes 4194304
  4.4 14.9 %collective-permute-start.1 = (bf16[576,128]{1,0:T(8,128)(2,1)S(1)}, bf16[576,128]{1,0:T(8,128)(2,1)S(1)}, u32[]{:S(2)}, u32[]{:S(2)}) collective-permute-start(bf16[576,128]{1,0:T(8,128)(2,1)S(1)} %get-tuple-element.55), channel_id=1, source_target_pairs={{0,8},{1,11},{2,10},{3,9},{4,12},{5,15},{6,14},{7,13},{8,0},{9,3},... | collective-permute-start | bytes 442376 | tf_op jit(solution)/shard_map/ppermute | solution.py:541
  8.4 10.8 %collective-permute-start.3 = (bf16[576,128]{1,0:T(8,128)(2,1)S(1)}, bf16[576,128]{1,0:T(8,128)(2,1)S(1)}, u32[]{:S(2)}, u32[]{:S(2)}) collective-permute-start(bf16[576,128]{1,0:T(8,128)(2,1)S(1)} %get-tuple-element.57), channel_id=1, source_target_pairs={{0,4},{1,7},{2,6},{3,5},{4,0},{5,3},{6,2},{7,1},{8,12},{9,15},{10,... | collective-permute-start | bytes 442376 | tf_op jit(solution)/shard_map/ppermute | solution.py:541
  10.0 6.1 %collective-permute-start.4 = (bf16[288,128]{1,0:T(8,128)(2,1)S(1)}, bf16[288,128]{1,0:T(8,128)(2,1)S(1)}, u32[]{:S(2)}, u32[]{:S(2)}) collective-permute-start(bf16[288,128]{1,0:T(8,128)(2,1)S(1)} %get-tuple-element.58), channel_id=1, source_target_pairs={{0,2},{2,0},{4,6},{6,4},{8,10},{10,8},{12,14},{14,12},{1,3},{3,1},... | collective-permute-start | bytes 221192 | tf_op jit(solution)/shard_map/ppermute | solution.py:546
  11.5 7.8 %collective-permute-start.2 = (bf16[288,128]{1,0:T(8,128)(2,1)S(1)}, bf16[288,128]{1,0:T(8,128)(2,1)S(1)}, u32[]{:S(2)}, u32[]{:S(2)}) collective-permute-start(bf16[288,128]{1,0:T(8,128)(2,1)S(1)} %get-tuple-element.56), channel_id=1, source_target_pairs={{0,12},{1,15},{2,14},{3,13},{4,8},{5,11},{6,10},{7,9},{8,4},{9,7},... | collective-permute-start | bytes 221192 | tf_op jit(solution)/shard_map/ppermute | solution.py:541
  11.7 12.3 %collective-permute-start.11 = (bf16[304,128]{1,0:T(8,128)(2,1)S(1)}, bf16[304,128]{1,0:T(8,128)(2,1)S(1)}, u32[]{:S(2)}, u32[]{:S(2)}) collective-permute-start(bf16[304,128]{1,0:T(8,128)(2,1)S(1)} %get-tuple-element.69), channel_id=1, source_target_pairs={{0,12},{1,15},{2,14},{3,13},{4,8},{5,11},{6,10},{7,9},{8,4},{9,7},... | collective-permute-start | bytes 233480 | tf_op jit(solution)/shard_map/ppermute | solution.py:541
  19.3 1.3 %collective-permute-start.5 = (bf16[288,128]{1,0:T(8,128)(2,1)S(1)}, bf16[288,128]{1,0:T(8,128)(2,1)S(1)}, u32[]{:S(2)}, u32[]{:S(2)}) collective-permute-start(bf16[288,128]{1,0:T(8,128)(2,1)S(1)} %get-tuple-element.60.refs_0_), channel_id=1, source_target_pairs={{0,1},{1,0},{2,3},{3,2},{4,5},{5,4},{6,7},{7,6},{8,9},{9,8},{10,11... | collective-permute-start | bytes 221192 | tf_op jit(solution)/shard_map/ppermute | solution.py:550
  19.4 1.4 %collective-permute-start.6 = (bf16[288,128]{1,0:T(8,128)(2,1)S(1)}, bf16[288,128]{1,0:T(8,128)(2,1)S(1)}, u32[]{:S(2)}, u32[]{:S(2)}) collective-permute-start(bf16[288,128]{1,0:T(8,128)(2,1)S(1)} %get-tuple-element.61.refs_1_), channel_id=1, source_target_pairs={{0,1},{1,0},{2,3},{3,2},{4,5},{5,4},{6,7},{7,6},{8,9},{9,8},{10,11... | collective-permute-start | bytes 221192 | tf_op jit(solution)/shard_map/ppermute | solution.py:550
  19.9 1.3 %collective-permute-start.7 = (bf16[288,128]{1,0:T(8,128)(2,1)S(1)}, bf16[288,128]{1,0:T(8,128)(2,1)S(1)}, u32[]{:S(2)}, u32[]{:S(2)}) collective-permute-start(bf16[288,128]{1,0:T(8,128)(2,1)S(1)} %get-tuple-element.62.refs_2_), channel_id=1, source_target_pairs={{0,1},{1,0},{2,3},{3,2},{4,5},{5,4},{6,7},{7,6},{8,9},{9,8},{10,11... | collective-permute-start | bytes 221192 | tf_op jit(solution)/shard_map/ppermute | solution.py:550
  20.0 4.5 %slice-start.4 = ((s8[6291456]{0:T(1024)(128)(4,1)}), s8[4194304]{0:T(1024)(128)(4,1)S(1)}, s32[]{:S(2)}) async-start(s8[6291456]{0:T(1024)(128)(4,1)} %bitcast.6), calls=%async_computation.4 | async-start | bytes 8388608
  20.0 4.5 %slice-start.5 = ((s8[6291456]{0:T(1024)(128)(4,1)}), s8[2097152]{0:T(1024)(128)(4,1)S(1)}, s32[]{:S(2)}) async-start(s8[6291456]{0:T(1024)(128)(4,1)} %bitcast.6), calls=%async_computation.5 | async-start | bytes 4194304
  20.0 1.3 %collective-permute-start.8 = (bf16[288,128]{1,0:T(8,128)(2,1)S(1)}, bf16[288,128]{1,0:T(8,128)(2,1)S(1)}, u32[]{:S(2)}, u32[]{:S(2)}) collective-permute-start(bf16[288,128]{1,0:T(8,128)(2,1)S(1)} %get-tuple-element.63.refs_3_), channel_id=1, source_target_pairs={{0,1},{1,0},{2,3},{3,2},{4,5},{5,4},{6,7},{7,6},{8,9},{9,8},{10,11... | collective-permute-start | bytes 221192 | tf_op jit(solution)/shard_map/ppermute | solution.py:550
  24.1 2.0 %collective-permute-start.12 = (bf16[1152,128]{1,0:T(8,128)(2,1)S(1)}, bf16[1152,128]{1,0:T(8,128)(2,1)S(1)}, u32[]{:S(2)}, u32[]{:S(2)}) collective-permute-start(bf16[1152,128]{1,0:T(8,128)(2,1)S(1)} %shard_map.115.g_sent), channel_id=1, source_target_pairs={{0,1},{1,0},{2,3},{3,2},{4,5},{5,4},{6,7},{7,6},{8,9},{9,8},{10,11... | collective-permute-start | bytes 884744 | tf_op jit(solution)/shard_map/ppermute | solution.py:550
  25.9 8.2 %collective-permute-start.9 = (bf16[720,128]{1,0:T(8,128)(2,1)S(1)}, bf16[720,128]{1,0:T(8,128)(2,1)S(1)}, u32[]{:S(2)}, u32[]{:S(2)}) collective-permute-start(bf16[720,128]{1,0:T(8,128)(2,1)S(1)} %get-tuple-element.67), channel_id=1, source_target_pairs={{0,1},{1,0},{2,3},{3,2},{4,5},{5,4},{6,7},{7,6},{8,9},{9,8},{10,11... | collective-permute-start | bytes 552968 | tf_op jit(solution)/shard_map/ppermute | solution.py:550
  31.0 4.1 %collective-permute-start.13 = (bf16[720,128]{1,0:T(8,128)(2,1)S(1)}, bf16[720,128]{1,0:T(8,128)(2,1)S(1)}, u32[]{:S(2)}, u32[]{:S(2)}) collective-permute-start(bf16[720,128]{1,0:T(8,128)(2,1)S(1)} %get-tuple-element.76), channel_id=1, source_target_pairs={{0,1},{1,0},{2,3},{3,2},{4,5},{5,4},{6,7},{7,6},{8,9},{9,8},{10,11... | collective-permute-start | bytes 552968 | tf_op jit(solution)/shard_map/ppermute | solution.py:550
  31.4 2.7 %collective-permute-start.10 = (bf16[432,128]{1,0:T(8,128)(2,1)S(1)}, bf16[432,128]{1,0:T(8,128)(2,1)S(1)}, u32[]{:S(2)}, u32[]{:S(2)}) collective-permute-start(bf16[432,128]{1,0:T(8,128)(2,1)S(1)} %get-tuple-element.68), channel_id=1, source_target_pairs={{0,1},{1,0},{2,3},{3,2},{4,5},{5,4},{6,7},{7,6},{8,9},{9,8},{10,11... | collective-permute-start | bytes 331784 | tf_op jit(solution)/shard_map/ppermute | solution.py:550
  33.7 1.4 %collective-permute-start.14 = (bf16[432,128]{1,0:T(8,128)(2,1)S(1)}, bf16[432,128]{1,0:T(8,128)(2,1)S(1)}, u32[]{:S(2)}, u32[]{:S(2)}) collective-permute-start(bf16[432,128]{1,0:T(8,128)(2,1)S(1)} %get-tuple-element.77), channel_id=1, source_target_pairs={{0,1},{1,0},{2,3},{3,2},{4,5},{5,4},{6,7},{7,6},{8,9},{9,8},{10,11... | collective-permute-start | bytes 331784 | tf_op jit(solution)/shard_map/ppermute | solution.py:550
  35.2 15.9 %collective-permute-start.15 = (bf16[576,128]{1,0:T(8,128)(2,1)S(1)}, bf16[576,128]{1,0:T(8,128)(2,1)S(1)}, u32[]{:S(2)}, u32[]{:S(2)}) collective-permute-start(bf16[576,128]{1,0:T(8,128)(2,1)S(1)} %get-tuple-element.78), channel_id=1, source_target_pairs={{0,8},{1,11},{2,10},{3,9},{4,12},{5,15},{6,14},{7,13},{8,0},{9,3},... | collective-permute-start | bytes 442376 | tf_op jit(solution)/shard_map/ppermute | solution.py:541
  40.0 11.1 %collective-permute-start.16 = (bf16[576,128]{1,0:T(8,128)(2,1)S(1)}, bf16[576,128]{1,0:T(8,128)(2,1)S(1)}, u32[]{:S(2)}, u32[]{:S(2)}) collective-permute-start(bf16[576,128]{1,0:T(8,128)(2,1)S(1)} %get-tuple-element.79), channel_id=1, source_target_pairs={{0,12},{1,15},{2,14},{3,13},{4,8},{5,11},{6,10},{7,9},{8,4},{9,7},... | collective-permute-start | bytes 442376 | tf_op jit(solution)/shard_map/ppermute | solution.py:541
  40.5 11.7 %collective-permute-start.17 = (bf16[576,128]{1,0:T(8,128)(2,1)S(1)}, bf16[576,128]{1,0:T(8,128)(2,1)S(1)}, u32[]{:S(2)}, u32[]{:S(2)}) collective-permute-start(bf16[576,128]{1,0:T(8,128)(2,1)S(1)} %get-tuple-element.80), channel_id=1, source_target_pairs={{0,4},{1,7},{2,6},{3,5},{4,0},{5,3},{6,2},{7,1},{8,12},{9,15},{10,... | collective-permute-start | bytes 442376 | tf_op jit(solution)/shard_map/ppermute | solution.py:541
  40.7 10.2 %collective-permute-start.18 = (bf16[288,128]{1,0:T(8,128)(2,1)S(1)}, bf16[288,128]{1,0:T(8,128)(2,1)S(1)}, u32[]{:S(2)}, u32[]{:S(2)}) collective-permute-start(bf16[288,128]{1,0:T(8,128)(2,1)S(1)} %get-tuple-element.81), channel_id=1, source_target_pairs={{0,2},{2,0},{4,6},{6,4},{8,10},{10,8},{12,14},{14,12},{1,3},{3,1},... | collective-permute-start | bytes 221192 | tf_op jit(solution)/shard_map/ppermute | solution.py:546
  52.2 2.0 %collective-permute-start.19 = (bf16[864,128]{1,0:T(8,128)(2,1)S(1)}, bf16[864,128]{1,0:T(8,128)(2,1)S(1)}, u32[]{:S(2)}, u32[]{:S(2)}) collective-permute-start(bf16[864,128]{1,0:T(8,128)(2,1)S(1)} %shard_map.120), channel_id=1, source_target_pairs={{0,1},{1,0},{2,3},{3,2},{4,5},{5,4},{6,7},{7,6},{8,9},{9,8},{10,11... | collective-permute-start | bytes 663560 | tf_op jit(solution)/shard_map/ppermute | solution.py:550

commit v14 on v13

--- a/solution.py
+++ b/solution.py
@@ -161,7 +161,7 @@
 
 
 def even_masks(count):
-    return [*range(count // 2, count, 2), *range(2, count // 2, 2)]
+    return [*reversed(range(count // 2, count, 2)), *range(2, count // 2, 2)]
 
 
 def route_kernel(devices, capacity, subs, ids_in, weight_in, x_in, g_in, *refs):
@@ -239,7 +239,7 @@
         for i, (mine, (to, at)) in enumerate(zip((x_mine, g_mine), places)):
             part(to, at, size)[...] = part(mine, j * size, size)[...]
             part(to, at + size, size)[...] = part(swapped, (i * count + j) * size, size)[...]
-    for out in lates.values():
+    for out in [*lates.values(), *[outs[j] for j in late]]:
         rest = part(out, 2 * size, out.shape[0] - 2 * size)
         rest[...] = jnp.zeros(rest.shape, rest.dtype)
 
@@ -595,7 +595,7 @@
     late_block = jax.ShapeDtypeStruct((2 * size + 16, LANES), low)
     packed = call(
         functools.partial(pack_kernel, size, late),
-        [lines(2 if j in late else 4) for j in range(count)] + [late_block] * len(late),
+        [late_block if j in late else lines(4) for j in range(count)] + [late_block] * len(late),
         (x_mine, g_mine, swap(theirs)),
         flops=24 * half_flops,
     )

time: 55.7 us -> 55.8 us (level)
  waiting for transfers between devices: 8.44 us -> 11.3 us
  starting transfers between devices: 21.6 us -> 18.8 us
    ppermute x7, starting transfers between devices: 14.9 us -> 12.3 us  [exchange(): arrived.append(lax.ppermute(block, ('expert', 'ffn'), pairs))]
    ppermute x7, waiting for transfers between devices: 4.48 us -> 5.91 us  [exchange(): arrived.append(lax.ppermute(block, ('expert', 'ffn'), pairs))]
    ppermute x2, waiting for transfers between devices: 0.77 us -> 1.89 us  [exchange_near(): return lax.ppermute(block, 'expert', [(i, i ^ 1) for i in range(devices)])]
    ppermute x11, starting transfers between devices: 4.12 us -> 3.36 us  [swap(): return lax.ppermute(value, 'ffn', [(0, 1), (1, 0)])]
    ppermute x2, starting transfers between devices: 2.63 us -> 3.19 us  [exchange_near(): return lax.ppermute(block, 'expert', [(i, i ^ 1) for i in range(devices)])]
  transfers between devices with their start and end apart: 20 -> 20, of which waited for: 11 -> 9; matrix products, arithmetic and copies ran while one was open for 0% -> 0% of each run, Pallas kernels for 38% -> 38%
where the time goes in v14:
time: 55.8 us; the launch traced here: 55.7 us
  Pallas kernels  24.7 us (44%)
  starting transfers between devices  18.8 us (34%)
  waiting for transfers between devices  11.3 us (20%)
  between operations  0.81 us (1%)
    pallas_call x13, Pallas kernels, call(): pl.pallas_call(kernel, out_shape=tuple(out_shape), in_specs=[pl.BlockSpec...  24.7 us
    ppermute x7, starting transfers between devices, exchange(): arrived.append(lax.ppermute(block, ('expert', 'ffn'), pairs))  12.3 us
    ppermute x7, waiting for transfers between devices, exchange(): arrived.append(lax.ppermute(block, ('expert', 'ffn'), pairs))  5.91 us
    ppermute x11, waiting for transfers between devices, swap(): return lax.ppermute(value, 'ffn', [(0, 1), (1, 0)])  3.52 us
    ppermute x11, starting transfers between devices, swap(): return lax.ppermute(value, 'ffn', [(0, 1), (1, 0)])  3.36 us
    ppermute x2, starting transfers between devices, exchange_near(): return lax.ppermute(block, 'expert', [(i, i ^ 1) for i in range(devices)])  3.19 us
    ppermute x2, waiting for transfers between devices, exchange_near(): return lax.ppermute(block, 'expert', [(i, i ^ 1) for i in range(devices)])  1.89 us
  transfers between devices with their start and end apart: 20, of which 9 were waited for; matrix products, arithmetic and copies ran while one was open for 0% of the time, Pallas kernels for 38%

profile of v14, /device:TPU:0, one launch (start us, length us, event | category | flops | bytes accessed | tf_op | source)
XLA Modules:
  0.0 55.7 jit_solution(12089240191887031386)
XLA Ops:
  0.7 2.1 %shard_map.110 = (bf16[432,128]{1,0:T(8,128)(2,1)S(1)}, bf16[432,128]{1,0:T(8,128)(2,1)S(1)}, bf16[288,128]{1,0:T(8,128)(2,1)S(1)}, bf16[288,128]{1,0:T(8,128)(2...) custom-call(s32[8,128]{1,0:T(8,128)} %bitcast.8, ...), custom_call_target="tpu_custom_call" | custom-call | bytes 1048576 | tf_op jit(solution)/shard_map/pallas_call | solution.py:132
  2.7 0.5 collective-permute-start
  3.3 1.1 %collective-permute-done.swapped = bf16[864,128]{1,0:T(8,128)(2,1)S(1)} collective-permute-done((bf16[864,128]{1,0:T(8,128)(2,1)S(1)}, bf16[864,128]{1,0:T(8,128)(2,1)S(1)}, u32[]{:S(2)}, u32[]{:S(2)}) %collective-permute-start) | collective-permute-done | bytes 221216 | tf_op jit(solution)/shard_map/ppermute | solution.py:550
  4.4 5.0 %collective-permute-start.1 = (bf16[576,128]{1,0:T(8,128)(2,1)S(1)}, bf16[576,128]{1,0:T(8,128)(2,1)S(1)}, u32[]{:S(2)}, u32[]{:S(2)}) collective-permute-start(bf16[576,128]{1,0:T(8,128)(2,1)S(1)} %get-tuple-element.55), channel_id=1, source_target_pairs={{0,12},{1,15},{2,14},{3,13},{4,8},{5,11},{6,10},{7,9},{8,4},{9,7},... | collective-permute-start | bytes 442376 | tf_op jit(solution)/shard_map/ppermute | solution.py:541
  9.5 0.6 %collective-permute-start.2 = (bf16[304,128]{1,0:T(8,128)(2,1)S(1)}, bf16[304,128]{1,0:T(8,128)(2,1)S(1)}, u32[]{:S(2)}, u32[]{:S(2)}) collective-permute-start(bf16[304,128]{1,0:T(8,128)(2,1)S(1)} %get-tuple-element.56), channel_id=1, source_target_pairs={{0,8},{1,11},{2,10},{3,9},{4,12},{5,15},{6,14},{7,13},{8,0},{9,3},... | collective-permute-start | bytes 233480 | tf_op jit(solution)/shard_map/ppermute | solution.py:541
  10.1 1.6 %collective-permute-start.4 = (bf16[288,128]{1,0:T(8,128)(2,1)S(1)}, bf16[288,128]{1,0:T(8,128)(2,1)S(1)}, u32[]{:S(2)}, u32[]{:S(2)}) collective-permute-start(bf16[288,128]{1,0:T(8,128)(2,1)S(1)} %get-tuple-element.58), channel_id=1, source_target_pairs={{0,2},{2,0},{4,6},{6,4},{8,10},{10,8},{12,14},{14,12},{1,3},{3,1},... | collective-permute-start | bytes 221192 | tf_op jit(solution)/shard_map/ppermute | solution.py:546
  11.7 2.1 %collective-permute-start.11 = (bf16[304,128]{1,0:T(8,128)(2,1)S(1)}, bf16[304,128]{1,0:T(8,128)(2,1)S(1)}, u32[]{:S(2)}, u32[]{:S(2)}) collective-permute-start(bf16[304,128]{1,0:T(8,128)(2,1)S(1)} %get-tuple-element.69), channel_id=1, source_target_pairs={{0,8},{1,11},{2,10},{3,9},{4,12},{5,15},{6,14},{7,13},{8,0},{9,3},... | collective-permute-start | bytes 233480 | tf_op jit(solution)/shard_map/ppermute | solution.py:541
  13.9 1.9 %collective-permute-done.4.refs_3_ = bf16[288,128]{1,0:T(8,128)(2,1)S(1)} collective-permute-done((bf16[288,128]{1,0:T(8,128)(2,1)S(1)}, bf16[288,128]{1,0:T(8,128)(2,1)S(1)}, u32[]{:S(2)}, u32[]{:S(2)}) %collective-permute-start.4) | collective-permute-done | bytes 73760 | tf_op jit(solution)/shard_map/ppermute | solution.py:546
  15.8 5.9 %collective-permute-done.2.refs_1_ = bf16[304,128]{1,0:T(8,128)(2,1)S(1)} collective-permute-done((bf16[304,128]{1,0:T(8,128)(2,1)S(1)}, bf16[304,128]{1,0:T(8,128)(2,1)S(1)}, u32[]{:S(2)}, u32[]{:S(2)}) %collective-permute-start.2) | collective-permute-done | bytes 77856 | tf_op jit(solution)/shard_map/ppermute | solution.py:541
  21.8 0.5 collective-permute-start.6
  22.3 0.4 collective-permute-start.8
  22.8 0.2 collective-permute-done.5.refs_4_
  23.0 0.2 collective-permute-done.6.refs_5_
  23.2 0.4 collective-permute-done.7.refs_6_
  23.5 0.2 collective-permute-done.8.refs_7_
  23.7 2.7 %shard_map.113 = (bf16[72,4096]{1,0:T(8,128)(2,1)S(1)}, bf16[72,768]{1,0:T(8,128)(2,1)S(1)}, bf16[72,768]{1,0:T(8,128)(2,1)S(1)}, bf16[72,768]{1,0:T(8,128)(2,1)S(1)}) custom-call(bf16[288,128]{1,0:T(8,128)(2,1)S(1)} %get-tuple-element.60.refs_0_, bf16[288,128]{1,0:T(8,128)(2,1)S(1)} %get-tuple-element.61.refs_1_, ...), custom_call_target="tpu_custom_call" | custom-call | tf_op jit(solution)/shard_map/pallas_call | solution.py:132
  26.5 0.4 collective-permute-start.12
  26.9 1.4 %shard_map.114 = (f32[720,128]{1,0:T(8,128)S(1)}, f32[432,128]{1,0:T(8,128)S(1)}, bf16[432,128]{1,0:T(8,128)(2,1)S(1)}, bf16[720,128]{1,0:T(8,128)(2,1)S(1)}) custom-call(bf16[72,768]{1,0:T(8,128)(2,1)S(1)} %get-tuple-element.64.hidden.refs_5_, bf16[1,768,4096]{2,1,0:T(8,128)(2,1)S(1)} %bitcast.7), custom_call_target="tpu_custom_call" | custom-call | flops 452984832 | tf_op jit(solution)/shard_map/pallas_call | solution.py:132
  28.3 0.2 collective-permute-start.9
  28.5 4.9 %shard_map.116 = (bf16[72,4096]{1,0:T(8,128)(2,1)S(1)}, bf16[72,768]{1,0:T(8,128)(2,1)S(1)}, bf16[72,768]{1,0:T(8,128)(2,1)S(1)}, f32[432,128]{1,0:T(8,128)S(1)}, bf16[720,128]{1,0:T(8,128)(2,1)S(1)}) custom-call(bf16[1152,128]{1,0:T(8,128)(2,1)S(1)} %shard_map.115.g_sent, bf16[1152,128]{1,0:T(8,128)(2,1)S(1)} %collective-permute-done.12.g_swapped, ...), custom_call_target="tpu_custom_call" | custom-call | flops 905969664 | tf_op jit(solution)/shard_map/pallas_call | solution.py:132
  33.4 0.4 collective-permute-start.13
  34.0 2.1 %shard_map.117 = (f32[720,128]{1,0:T(8,128)S(1)}, bf16[432,128]{1,0:T(8,128)(2,1)S(1)}) custom-call(bf16[72,768]{1,0:T(8,128)(2,1)S(1)} %get-tuple-element.72.pre_gate, bf16[72,768]{1,0:T(8,128)(2,1)S(1)} %get-tuple-element.73.pre_up, bf16[1,4096,768]{2,1,0:T(8,128)(2,1)S(1)} %bitcast.3, bf16[1,4096,768]{2,1,0:T(8,128)(2,1)S(1)} %bitcast.5), custom_call_target="tpu_custom_call" | custom-call | flops 452984832 | tf_op jit(solution)/shard_map/pallas_call | solution.py:132
  36.1 0.4 collective-permute-start.14
  36.5 1.0 %collective-permute-done.14.refs_7_ = bf16[432,128]{1,0:T(8,128)(2,1)S(1)} collective-permute-done((bf16[432,128]{1,0:T(8,128)(2,1)S(1)}, bf16[432,128]{1,0:T(8,128)(2,1)S(1)}, u32[]{:S(2)}, u32[]{:S(2)}) %collective-permute-start.14) | collective-permute-done | bytes 110624 | tf_op jit(solution)/shard_map/ppermute | solution.py:550
  37.6 0.3 collective-permute-start.15
  37.9 0.2 collective-permute-start.16
  38.0 4.0 %collective-permute-start.17 = (bf16[576,128]{1,0:T(8,128)(2,1)S(1)}, bf16[576,128]{1,0:T(8,128)(2,1)S(1)}, u32[]{:S(2)}, u32[]{:S(2)}) collective-permute-start(bf16[576,128]{1,0:T(8,128)(2,1)S(1)} %get-tuple-element.80), channel_id=1, source_target_pairs={{0,4},{1,7},{2,6},{3,5},{4,0},{5,3},{6,2},{7,1},{8,12},{9,15},{10,... | collective-permute-start | bytes 442376 | tf_op jit(solution)/shard_map/ppermute | solution.py:541
  42.0 1.6 %collective-permute-start.18 = (bf16[288,128]{1,0:T(8,128)(2,1)S(1)}, bf16[288,128]{1,0:T(8,128)(2,1)S(1)}, u32[]{:S(2)}, u32[]{:S(2)}) collective-permute-start(bf16[288,128]{1,0:T(8,128)(2,1)S(1)} %get-tuple-element.81), channel_id=1, source_target_pairs={{0,2},{2,0},{4,6},{6,4},{8,10},{10,8},{12,14},{14,12},{1,3},{3,1},... | collective-permute-start | bytes 221192 | tf_op jit(solution)/shard_map/ppermute | solution.py:546
  43.6 9.1 %shard_map.119 = (bf16[1,4096,768]{2,1,0:T(8,128)(2,1)}, bf16[1,4096,768]{2,1,0:T(8,128)(2,1)}, bf16[1,768,4096]{2,1,0:T(8,128)(2,1)}, f32[8,128]{1,0:T(8,128)S(1)}) custom-call(bf16[72,4096]{1,0:T(8,128)(2,1)S(1)} %get-tuple-element.82.x, bf16[72,4096]{1,0:T(8,128)(2,1)S(1)} %get-tuple-element.83.g, bf16[72,768]{1,0:T(8,128)(2,1)S(1)} %get-tuple-element.64.hidden.refs_5_, ...), custom_call_target="tpu_custom_call" | custom-call | flops 1358954496 | bytes 18874368 | tf_op jit(solution)/shard_map/pallas_call | solution.py:132
  52.9 0.9 %shard_map.121 = (f32[128,2048]{1,0:T(8,128)S(1)}, f32[128,2048]{1,0:T(8,128)S(1)}) custom-call(bf16[72,128]{1,0:T(8,128)(2,1)S(1)} %get-tuple-element.85.place, f32[72,128]{1,0:T(8,128)S(1)} %get-tuple-element.86.mix, bf16[576,128]{1,0:T(8,128)(2,1)S(1)} %collective-permute-done.15.refs_0_, bf16[576,128]{1,0:T(8,128)(2,1)S(1)} %collective-permute-done.16.refs_1_, ...), custom_call_target="tpu_custom_call" | custom-call | flops 75497472 | tf_op jit(solution)/shard_map/pallas_call | solution.py:132
  53.8 0.5 collective-permute-done.19.shared
  54.3 1.4 %shard_map.122 = (bf16[128,2048]{1,0:T(8,128)(2,1)}, bf16[128,2048]{1,0:T(8,128)(2,1)}) custom-call(bf16[27,128]{1,0:T(8,128)(2,1)S(1)} %get-tuple-element.50.place, f32[27,128]{1,0:T(8,128)S(1)} %get-tuple-element.51.mix, bf16[864,128]{1,0:T(8,128)(2,1)S(1)} %collective-permute-done.19.shared, f32[128,2048]{1,0:T(8,128)S(1)} %get-tuple-element.88.out_sum, ...), custom_call_target="tpu_custom_call" | custom-call | bytes 2097152 | tf_op jit(solution)/shard_map/pallas_call | solution.py:132
  (36 shorter events, 0.7 us)
Async XLA Ops:
  0.6 23.1 %slice-start = ((s8[6291456]{0:T(1024)(128)(4,1)}), s8[4194304]{0:T(1024)(128)(4,1)S(1)}, s32[]{:S(2)}) async-start(s8[6291456]{0:T(1024)(128)(4,1)} %bitcast.2), calls=%async_computation | async-start | bytes 8388608
  0.6 23.0 %slice-start.2 = ((s8[6291456]{0:T(1024)(128)(4,1)}), s8[4194304]{0:T(1024)(128)(4,1)S(1)}, s32[]{:S(2)}) async-start(s8[6291456]{0:T(1024)(128)(4,1)} %bitcast.4), calls=%async_computation.2 | async-start | bytes 8388608
  2.7 1.6 %collective-permute-start = (bf16[864,128]{1,0:T(8,128)(2,1)S(1)}, bf16[864,128]{1,0:T(8,128)(2,1)S(1)}, u32[]{:S(2)}, u32[]{:S(2)}) collective-permute-start(bf16[864,128]{1,0:T(8,128)(2,1)S(1)} %get-tuple-element.54), channel_id=1, source_target_pairs={{0,1},{1,0},{2,3},{3,2},{4,5},{5,4},{6,7},{7,6},{8,9},{9,8},{10,11... | collective-permute-start | bytes 663560 | tf_op jit(solution)/shard_map/ppermute | solution.py:550
  4.4 19.3 %slice-start.1 = ((s8[6291456]{0:T(1024)(128)(4,1)}), s8[2097152]{0:T(1024)(128)(4,1)S(1)}, s32[]{:S(2)}) async-start(s8[6291456]{0:T(1024)(128)(4,1)} %bitcast.2), calls=%async_computation.1 | async-start | bytes 4194304
  4.4 19.3 %slice-start.3 = ((s8[6291456]{0:T(1024)(128)(4,1)}), s8[2097152]{0:T(1024)(128)(4,1)S(1)}, s32[]{:S(2)}) async-start(s8[6291456]{0:T(1024)(128)(4,1)} %bitcast.4), calls=%async_computation.3 | async-start | bytes 4194304
  4.4 17.2 %collective-permute-start.1 = (bf16[576,128]{1,0:T(8,128)(2,1)S(1)}, bf16[576,128]{1,0:T(8,128)(2,1)S(1)}, u32[]{:S(2)}, u32[]{:S(2)}) collective-permute-start(bf16[576,128]{1,0:T(8,128)(2,1)S(1)} %get-tuple-element.55), channel_id=1, source_target_pairs={{0,12},{1,15},{2,14},{3,13},{4,8},{5,11},{6,10},{7,9},{8,4},{9,7},... | collective-permute-start | bytes 442376 | tf_op jit(solution)/shard_map/ppermute | solution.py:541
  9.4 12.2 %collective-permute-start.3 = (bf16[576,128]{1,0:T(8,128)(2,1)S(1)}, bf16[576,128]{1,0:T(8,128)(2,1)S(1)}, u32[]{:S(2)}, u32[]{:S(2)}) collective-permute-start(bf16[576,128]{1,0:T(8,128)(2,1)S(1)} %get-tuple-element.57), channel_id=1, source_target_pairs={{0,4},{1,7},{2,6},{3,5},{4,0},{5,3},{6,2},{7,1},{8,12},{9,15},{10,... | collective-permute-start | bytes 442376 | tf_op jit(solution)/shard_map/ppermute | solution.py:541
  9.5 12.2 %collective-permute-start.2 = (bf16[304,128]{1,0:T(8,128)(2,1)S(1)}, bf16[304,128]{1,0:T(8,128)(2,1)S(1)}, u32[]{:S(2)}, u32[]{:S(2)}) collective-permute-start(bf16[304,128]{1,0:T(8,128)(2,1)S(1)} %get-tuple-element.56), channel_id=1, source_target_pairs={{0,8},{1,11},{2,10},{3,9},{4,12},{5,15},{6,14},{7,13},{8,0},{9,3},... | collective-permute-start | bytes 233480 | tf_op jit(solution)/shard_map/ppermute | solution.py:541
  10.1 5.7 %collective-permute-start.4 = (bf16[288,128]{1,0:T(8,128)(2,1)S(1)}, bf16[288,128]{1,0:T(8,128)(2,1)S(1)}, u32[]{:S(2)}, u32[]{:S(2)}) collective-permute-start(bf16[288,128]{1,0:T(8,128)(2,1)S(1)} %get-tuple-element.58), channel_id=1, source_target_pairs={{0,2},{2,0},{4,6},{6,4},{8,10},{10,8},{12,14},{14,12},{1,3},{3,1},... | collective-permute-start | bytes 221192 | tf_op jit(solution)/shard_map/ppermute | solution.py:546
  11.7 14.7 %collective-permute-start.11 = (bf16[304,128]{1,0:T(8,128)(2,1)S(1)}, bf16[304,128]{1,0:T(8,128)(2,1)S(1)}, u32[]{:S(2)}, u32[]{:S(2)}) collective-permute-start(bf16[304,128]{1,0:T(8,128)(2,1)S(1)} %get-tuple-element.69), channel_id=1, source_target_pairs={{0,8},{1,11},{2,10},{3,9},{4,12},{5,15},{6,14},{7,13},{8,0},{9,3},... | collective-permute-start | bytes 233480 | tf_op jit(solution)/shard_map/ppermute | solution.py:541
  21.7 1.3 %collective-permute-start.5 = (bf16[288,128]{1,0:T(8,128)(2,1)S(1)}, bf16[288,128]{1,0:T(8,128)(2,1)S(1)}, u32[]{:S(2)}, u32[]{:S(2)}) collective-permute-start(bf16[288,128]{1,0:T(8,128)(2,1)S(1)} %get-tuple-element.60.refs_0_), channel_id=1, source_target_pairs={{0,1},{1,0},{2,3},{3,2},{4,5},{5,4},{6,7},{7,6},{8,9},{9,8},{10,11... | collective-permute-start | bytes 221192 | tf_op jit(solution)/shard_map/ppermute | solution.py:550
  21.8 1.4 %collective-permute-start.6 = (bf16[288,128]{1,0:T(8,128)(2,1)S(1)}, bf16[288,128]{1,0:T(8,128)(2,1)S(1)}, u32[]{:S(2)}, u32[]{:S(2)}) collective-permute-start(bf16[288,128]{1,0:T(8,128)(2,1)S(1)} %get-tuple-element.61.refs_1_), channel_id=1, source_target_pairs={{0,1},{1,0},{2,3},{3,2},{4,5},{5,4},{6,7},{7,6},{8,9},{9,8},{10,11... | collective-permute-start | bytes 221192 | tf_op jit(solution)/shard_map/ppermute | solution.py:550
  22.3 1.3 %collective-permute-start.7 = (bf16[288,128]{1,0:T(8,128)(2,1)S(1)}, bf16[288,128]{1,0:T(8,128)(2,1)S(1)}, u32[]{:S(2)}, u32[]{:S(2)}) collective-permute-start(bf16[288,128]{1,0:T(8,128)(2,1)S(1)} %get-tuple-element.62.refs_2_), channel_id=1, source_target_pairs={{0,1},{1,0},{2,3},{3,2},{4,5},{5,4},{6,7},{7,6},{8,9},{9,8},{10,11... | collective-permute-start | bytes 221192 | tf_op jit(solution)/shard_map/ppermute | solution.py:550
  22.3 4.6 %slice-start.4 = ((s8[6291456]{0:T(1024)(128)(4,1)}), s8[4194304]{0:T(1024)(128)(4,1)S(1)}, s32[]{:S(2)}) async-start(s8[6291456]{0:T(1024)(128)(4,1)} %bitcast.6), calls=%async_computation.4 | async-start | bytes 8388608
  22.3 4.6 %slice-start.5 = ((s8[6291456]{0:T(1024)(128)(4,1)}), s8[2097152]{0:T(1024)(128)(4,1)S(1)}, s32[]{:S(2)}) async-start(s8[6291456]{0:T(1024)(128)(4,1)} %bitcast.6), calls=%async_computation.5 | async-start | bytes 4194304
  22.3 1.3 %collective-permute-start.8 = (bf16[288,128]{1,0:T(8,128)(2,1)S(1)}, bf16[288,128]{1,0:T(8,128)(2,1)S(1)}, u32[]{:S(2)}, u32[]{:S(2)}) collective-permute-start(bf16[288,128]{1,0:T(8,128)(2,1)S(1)} %get-tuple-element.63.refs_3_), channel_id=1, source_target_pairs={{0,1},{1,0},{2,3},{3,2},{4,5},{5,4},{6,7},{7,6},{8,9},{9,8},{10,11... | collective-permute-start | bytes 221192 | tf_op jit(solution)/shard_map/ppermute | solution.py:550
  26.5 2.0 %collective-permute-start.12 = (bf16[1152,128]{1,0:T(8,128)(2,1)S(1)}, bf16[1152,128]{1,0:T(8,128)(2,1)S(1)}, u32[]{:S(2)}, u32[]{:S(2)}) collective-permute-start(bf16[1152,128]{1,0:T(8,128)(2,1)S(1)} %shard_map.115.g_sent), channel_id=1, source_target_pairs={{0,1},{1,0},{2,3},{3,2},{4,5},{5,4},{6,7},{7,6},{8,9},{9,8},{10,11... | collective-permute-start | bytes 884744 | tf_op jit(solution)/shard_map/ppermute | solution.py:550
  28.3 8.2 %collective-permute-start.9 = (bf16[720,128]{1,0:T(8,128)(2,1)S(1)}, bf16[720,128]{1,0:T(8,128)(2,1)S(1)}, u32[]{:S(2)}, u32[]{:S(2)}) collective-permute-start(bf16[720,128]{1,0:T(8,128)(2,1)S(1)} %get-tuple-element.67), channel_id=1, source_target_pairs={{0,1},{1,0},{2,3},{3,2},{4,5},{5,4},{6,7},{7,6},{8,9},{9,8},{10,11... | collective-permute-start | bytes 552968 | tf_op jit(solution)/shard_map/ppermute | solution.py:550
  33.4 4.1 %collective-permute-start.13 = (bf16[720,128]{1,0:T(8,128)(2,1)S(1)}, bf16[720,128]{1,0:T(8,128)(2,1)S(1)}, u32[]{:S(2)}, u32[]{:S(2)}) collective-permute-start(bf16[720,128]{1,0:T(8,128)(2,1)S(1)} %get-tuple-element.76), channel_id=1, source_target_pairs={{0,1},{1,0},{2,3},{3,2},{4,5},{5,4},{6,7},{7,6},{8,9},{9,8},{10,11... | collective-permute-start | bytes 552968 | tf_op jit(solution)/shard_map/ppermute | solution.py:550
  33.8 2.7 %collective-permute-start.10 = (bf16[432,128]{1,0:T(8,128)(2,1)S(1)}, bf16[432,128]{1,0:T(8,128)(2,1)S(1)}, u32[]{:S(2)}, u32[]{:S(2)}) collective-permute-start(bf16[432,128]{1,0:T(8,128)(2,1)S(1)} %get-tuple-element.68), channel_id=1, source_target_pairs={{0,1},{1,0},{2,3},{3,2},{4,5},{5,4},{6,7},{7,6},{8,9},{9,8},{10,11... | collective-permute-start | bytes 331784 | tf_op jit(solution)/shard_map/ppermute | solution.py:550
  36.1 1.4 %collective-permute-start.14 = (bf16[432,128]{1,0:T(8,128)(2,1)S(1)}, bf16[432,128]{1,0:T(8,128)(2,1)S(1)}, u32[]{:S(2)}, u32[]{:S(2)}) collective-permute-start(bf16[432,128]{1,0:T(8,128)(2,1)S(1)} %get-tuple-element.77), channel_id=1, source_target_pairs={{0,1},{1,0},{2,3},{3,2},{4,5},{5,4},{6,7},{7,6},{8,9},{9,8},{10,11... | collective-permute-start | bytes 331784 | tf_op jit(solution)/shard_map/ppermute | solution.py:550
  37.6 15.1 %collective-permute-start.15 = (bf16[576,128]{1,0:T(8,128)(2,1)S(1)}, bf16[576,128]{1,0:T(8,128)(2,1)S(1)}, u32[]{:S(2)}, u32[]{:S(2)}) collective-permute-start(bf16[576,128]{1,0:T(8,128)(2,1)S(1)} %get-tuple-element.78), channel_id=1, source_target_pairs={{0,12},{1,15},{2,14},{3,13},{4,8},{5,11},{6,10},{7,9},{8,4},{9,7},... | collective-permute-start | bytes 442376 | tf_op jit(solution)/shard_map/ppermute | solution.py:541
  37.9 14.9 %collective-permute-start.16 = (bf16[576,128]{1,0:T(8,128)(2,1)S(1)}, bf16[576,128]{1,0:T(8,128)(2,1)S(1)}, u32[]{:S(2)}, u32[]{:S(2)}) collective-permute-start(bf16[576,128]{1,0:T(8,128)(2,1)S(1)} %get-tuple-element.79), channel_id=1, source_target_pairs={{0,8},{1,11},{2,10},{3,9},{4,12},{5,15},{6,14},{7,13},{8,0},{9,3},... | collective-permute-start | bytes 442376 | tf_op jit(solution)/shard_map/ppermute | solution.py:541
  38.0 14.7 %collective-permute-start.17 = (bf16[576,128]{1,0:T(8,128)(2,1)S(1)}, bf16[576,128]{1,0:T(8,128)(2,1)S(1)}, u32[]{:S(2)}, u32[]{:S(2)}) collective-permute-start(bf16[576,128]{1,0:T(8,128)(2,1)S(1)} %get-tuple-element.80), channel_id=1, source_target_pairs={{0,4},{1,7},{2,6},{3,5},{4,0},{5,3},{6,2},{7,1},{8,12},{9,15},{10,... | collective-permute-start | bytes 442376 | tf_op jit(solution)/shard_map/ppermute | solution.py:541
  42.0 10.7 %collective-permute-start.18 = (bf16[288,128]{1,0:T(8,128)(2,1)S(1)}, bf16[288,128]{1,0:T(8,128)(2,1)S(1)}, u32[]{:S(2)}, u32[]{:S(2)}) collective-permute-start(bf16[288,128]{1,0:T(8,128)(2,1)S(1)} %get-tuple-element.81), channel_id=1, source_target_pairs={{0,2},{2,0},{4,6},{6,4},{8,10},{10,8},{12,14},{14,12},{1,3},{3,1},... | collective-permute-start | bytes 221192 | tf_op jit(solution)/shard_map/ppermute | solution.py:546
  52.8 1.5 %collective-permute-start.19 = (bf16[864,128]{1,0:T(8,128)(2,1)S(1)}, bf16[864,128]{1,0:T(8,128)(2,1)S(1)}, u32[]{:S(2)}, u32[]{:S(2)}) collective-permute-start(bf16[864,128]{1,0:T(8,128)(2,1)S(1)} %shard_map.120), channel_id=1, source_target_pairs={{0,1},{1,0},{2,3},{3,2},{4,5},{5,4},{6,7},{7,6},{8,9},{9,8},{10,11... | collective-permute-start | bytes 663560 | tf_op jit(solution)/shard_map/ppermute | solution.py:550

commit v15 on v14

--- a/solution.py
+++ b/solution.py
@@ -291,7 +291,7 @@
 
 
 def leave_kernel(size, *refs):
-    terms, outs = (refs[:4], refs[4:8]), refs[8:]
+    terms, outs = (refs[:4], refs[4:8]), refs[9:]
     count = len(outs) - 2
     for at, (keep_own, keep_other, came_own, came_other) in zip((0, size), terms):
 
@@ -467,28 +467,36 @@
     return [slice(at, min(at + size, total)) for at in range(0, total, size)]
 
 
+def first_chunk_kernel(hidden, g, turned, out):
+    turned[...] = flip(hidden[...]).astype(turned.dtype)
+    for cut in pieces_of(out.shape[1], 256):
+        out[:, cut] = dot(turned[...], g[:, cut]).astype(out.dtype)
+
+
 def gradient_kernel(
     step,
     x,
     g,
-    hidden,
+    hidden_turned,
+    first,
     pre_gate,
     pre_up,
     grad_gate,
     grad_up,
     grad_down,
     written,
-    flipped,
     turned,
     tall,
     wide,
     tall_sems,
     wide_sems,
+    first_sem,
 ):
+    width, lanes = x.shape[1], hidden_turned.shape[0]
+    count = width // step
     written[...] = jnp.zeros_like(written)
-    width, lanes = x.shape[1], hidden.shape[1]
-    count = width // step
-    flipped[...] = flip(hidden[...]).astype(flipped.dtype)
+    first_copy = pltpu.make_async_copy(first, grad_down.at[0, :, 0:step], first_sem)
+    first_copy.start()
 
     def wide_copy(i, slot):
         return pltpu.make_async_copy(wide.at[slot], grad_down.at[0, :, chunk(i, step)], wide_sems.at[slot])
@@ -499,18 +507,17 @@
     def down(i, carry):
         slot = i % 2
 
-        @pl.when(i >= 2)
+        @pl.when(i >= 3)
         def _():
             wide_copy(i - 2, slot).wait()
 
         for cut in pieces_of(step, 256):
             right = g[:, chunk(i, step)][:, cut]
-            for high in pieces_of(lanes, 256):
-                wide[slot, high, cut] = dot(flipped[high, :], right).astype(wide.dtype)
+            wide[slot, :, cut] = dot(hidden_turned[...], right).astype(wide.dtype)
         wide_copy(i, slot).start()
         return carry
 
-    lax.fori_loop(0, count, down, 0)
+    lax.fori_loop(1, count, down, 0)
 
     def inputs(i, carry):
         slot = i % 2
@@ -522,14 +529,16 @@
                 tall_copy(which, out, i - 2, slot).wait()
 
             for cut in pieces_of(lanes, 256):
-                for high in pieces_of(step, 256):
+                for high in pieces_of(step, 512):
                     tall[which, slot, high, cut] = dot(turned[high, :], right[:, cut]).astype(tall.dtype)
             tall_copy(which, out, i, slot).start()
         return carry
 
     lax.fori_loop(0, count, inputs, 0)
+    first_copy.wait()
+    for i in range(max(1, count - 2), count):
+        wide_copy(i, i % 2).wait()
     for i in range(max(0, count - 2), count):
-        wide_copy(i, i % 2).wait()
         tall_copy(0, grad_gate, i, i % 2).wait()
         tall_copy(1, grad_up, i, i % 2).wait()
 
@@ -591,7 +600,7 @@
         traffic=4 * tok_dev * sub_width,
     )
     masks = even_masks(devices)
-    late = [devices // 4 - 1]
+    late = [0]
     late_block = jax.ShapeDtypeStruct((2 * size + 16, LANES), low)
     packed = call(
         functools.partial(pack_kernel, size, late),
@@ -652,26 +661,32 @@
         flops=2 * half_flops,
     )
     dx_terms = (dx_own, dx_other, came_own, swap(send_own))
+    cut = 1024 if width % 1024 == 0 else width
+    hidden_turned, first = call(
+        first_chunk_kernel,
+        [vmem((lanes, rows), low), vmem((lanes, cut), low)],
+        (hidden, g_full),
+        flops=2 * half_flops * cut // width,
+    )
     *leaving, back, kept = call(
         functools.partial(leave_kernel, size),
         [lines(4)] * count + [lines(2)] * 2,
-        (*out_terms, *dx_terms),
+        (*out_terms, *dx_terms, first),
     )
     returned = exchange(leaving, masks, devices)
     back = exchange_near(back, devices)
-    cut = 1024 if width % 1024 == 0 else width
     grad_gate, grad_up, grad_down, written = call(
         functools.partial(gradient_kernel, cut),
         [jax.ShapeDtypeStruct(w.shape, low) for w in weights] + [vmem((8, LANES), full)],
-        (x_full, g_full, hidden, pre_gate, pre_up),
+        (x_full, g_full, hidden_turned, first, pre_gate, pre_up),
         out_spaces=[pl.ANY] * 3 + [pltpu.VMEM],
         scratch=[
-            pltpu.VMEM((lanes, rows), low),
             pltpu.VMEM((cut, rows), low),
             pltpu.VMEM((2, 2, cut, lanes), low),
             pltpu.VMEM((2, lanes, cut), low),
             pltpu.SemaphoreType.DMA((2, 2)),
             pltpu.SemaphoreType.DMA((2,)),
+            pltpu.SemaphoreType.DMA,
         ],
         flops=6 * half_flops,
         traffic=sum(w.size * 2 for w in weights),

time: 55.8 us -> 56.4 us (1.011)
  starting transfers between devices: 18.8 us -> 20.9 us
  waiting for transfers between devices: 11.3 us -> 9.93 us
    ppermute x7, starting transfers between devices: 12.3 us -> 14.7 us  [exchange(): arrived.append(lax.ppermute(block, ('expert', 'ffn'), pairs))]
    ppermute x2, waiting for transfers between devices: 1.89 us -> 0.82 us  [exchange_near(): return lax.ppermute(block, 'expert', [(i, i ^ 1) for i in range(devices)])]
    ppermute x11, waiting for transfers between devices: 3.52 us -> 2.85 us  [swap(): return lax.ppermute(value, 'ffn', [(0, 1), (1, 0)])]
    pallas_call x13 -> x14, Pallas kernels: 24.7 us -> 24.6 us  [call(): pl.pallas_call(kernel, out_shape=tuple(out_shape), in_specs=[pl.BlockSpec...]
  transfers between devices with their start and end apart: 20 -> 20, of which waited for: 9 -> 10; matrix products, arithmetic and copies ran while one was open for 0% -> 0% of each run, Pallas kernels for 38% -> 37%
where the time goes in v15:
time: 56.4 us; the launch traced here: 56.3 us
  Pallas kernels  24.6 us (44%)
  starting transfers between devices  20.9 us (37%)
  waiting for transfers between devices  9.93 us (18%)
  between operations  0.82 us (1%)
    pallas_call x14, Pallas kernels, call(): pl.pallas_call(kernel, out_shape=tuple(out_shape), in_specs=[pl.BlockSpec...  24.6 us
    ppermute x7, starting transfers between devices, exchange(): arrived.append(lax.ppermute(block, ('expert', 'ffn'), pairs))  14.7 us
    ppermute x7, waiting for transfers between devices, exchange(): arrived.append(lax.ppermute(block, ('expert', 'ffn'), pairs))  6.27 us
    ppermute x11, starting transfers between devices, swap(): return lax.ppermute(value, 'ffn', [(0, 1), (1, 0)])  3.38 us
    ppermute x11, waiting for transfers between devices, swap(): return lax.ppermute(value, 'ffn', [(0, 1), (1, 0)])  2.85 us
    ppermute x2, starting transfers between devices, exchange_near(): return lax.ppermute(block, 'expert', [(i, i ^ 1) for i in range(devices)])  2.82 us
  transfers between devices with their start and end apart: 20, of which 10 were waited for; matrix products, arithmetic and copies ran while one was open for 0% of the time, Pallas kernels for 37%

profile of v15, /device:TPU:0, one launch (start us, length us, event | category | flops | bytes accessed | tf_op | source)
XLA Modules:
  0.0 56.3 jit_solution(13096747399298451427)
XLA Ops:
  0.7 2.1 %shard_map.110 = (bf16[432,128]{1,0:T(8,128)(2,1)S(1)}, bf16[432,128]{1,0:T(8,128)(2,1)S(1)}, bf16[288,128]{1,0:T(8,128)(2,1)S(1)}, bf16[288,128]{1,0:T(8,128)(2...) custom-call(s32[8,128]{1,0:T(8,128)} %bitcast.8, ...), custom_call_target="tpu_custom_call" | custom-call | bytes 1048576 | tf_op jit(solution)/shard_map/pallas_call | solution.py:132
  2.7 0.5 collective-permute-start
  3.3 1.1 %collective-permute-done.swapped = bf16[864,128]{1,0:T(8,128)(2,1)S(1)} collective-permute-done((bf16[864,128]{1,0:T(8,128)(2,1)S(1)}, bf16[864,128]{1,0:T(8,128)(2,1)S(1)}, u32[]{:S(2)}, u32[]{:S(2)}) %collective-permute-start) | collective-permute-done | bytes 221216 | tf_op jit(solution)/shard_map/ppermute | solution.py:559
  4.4 4.0 %collective-permute-start.2 = (bf16[576,128]{1,0:T(8,128)(2,1)S(1)}, bf16[576,128]{1,0:T(8,128)(2,1)S(1)}, u32[]{:S(2)}, u32[]{:S(2)}) collective-permute-start(bf16[576,128]{1,0:T(8,128)(2,1)S(1)} %get-tuple-element.58), channel_id=1, source_target_pairs={{0,8},{1,11},{2,10},{3,9},{4,12},{5,15},{6,14},{7,13},{8,0},{9,3},... | collective-permute-start | bytes 442376 | tf_op jit(solution)/shard_map/ppermute | solution.py:550
  8.4 1.6 %collective-permute-start.3 = (bf16[576,128]{1,0:T(8,128)(2,1)S(1)}, bf16[576,128]{1,0:T(8,128)(2,1)S(1)}, u32[]{:S(2)}, u32[]{:S(2)}) collective-permute-start(bf16[576,128]{1,0:T(8,128)(2,1)S(1)} %get-tuple-element.59), channel_id=1, source_target_pairs={{0,4},{1,7},{2,6},{3,5},{4,0},{5,3},{6,2},{7,1},{8,12},{9,15},{10,... | collective-permute-start | bytes 442376 | tf_op jit(solution)/shard_map/ppermute | solution.py:550
  10.0 1.7 %collective-permute-start.4 = (bf16[288,128]{1,0:T(8,128)(2,1)S(1)}, bf16[288,128]{1,0:T(8,128)(2,1)S(1)}, u32[]{:S(2)}, u32[]{:S(2)}) collective-permute-start(bf16[288,128]{1,0:T(8,128)(2,1)S(1)} %get-tuple-element.60), channel_id=1, source_target_pairs={{0,2},{2,0},{4,6},{6,4},{8,10},{10,8},{12,14},{14,12},{1,3},{3,1},... | collective-permute-start | bytes 221192 | tf_op jit(solution)/shard_map/ppermute | solution.py:555
  11.7 3.6 %collective-permute-start.11 = (bf16[304,128]{1,0:T(8,128)(2,1)S(1)}, bf16[304,128]{1,0:T(8,128)(2,1)S(1)}, u32[]{:S(2)}, u32[]{:S(2)}) collective-permute-start(bf16[304,128]{1,0:T(8,128)(2,1)S(1)} %get-tuple-element.71), channel_id=1, source_target_pairs={{0,12},{1,15},{2,14},{3,13},{4,8},{5,11},{6,10},{7,9},{8,4},{9,7},... | collective-permute-start | bytes 233480 | tf_op jit(solution)/shard_map/ppermute | solution.py:550
  15.3 0.8 %collective-permute-done.4.refs_3_ = bf16[288,128]{1,0:T(8,128)(2,1)S(1)} collective-permute-done((bf16[288,128]{1,0:T(8,128)(2,1)S(1)}, bf16[288,128]{1,0:T(8,128)(2,1)S(1)}, u32[]{:S(2)}, u32[]{:S(2)}) %collective-permute-start.4) | collective-permute-done | bytes 73760 | tf_op jit(solution)/shard_map/ppermute | solution.py:555
  16.1 3.2 %collective-permute-done.1.refs_0_ = bf16[304,128]{1,0:T(8,128)(2,1)S(1)} collective-permute-done((bf16[304,128]{1,0:T(8,128)(2,1)S(1)}, bf16[304,128]{1,0:T(8,128)(2,1)S(1)}, u32[]{:S(2)}, u32[]{:S(2)}) %collective-permute-start.1) | collective-permute-done | bytes 77856 | tf_op jit(solution)/shard_map/ppermute | solution.py:550
  19.5 0.5 collective-permute-start.6
  20.1 0.4 collective-permute-start.8
  20.5 0.2 collective-permute-done.5.refs_4_
  20.9 0.4 collective-permute-done.7.refs_6_
  21.4 2.7 %shard_map.113 = (bf16[72,4096]{1,0:T(8,128)(2,1)S(1)}, bf16[72,768]{1,0:T(8,128)(2,1)S(1)}, bf16[72,768]{1,0:T(8,128)(2,1)S(1)}, bf16[72,768]{1,0:T(8,128)(2,1)S(1)}) custom-call(bf16[288,128]{1,0:T(8,128)(2,1)S(1)} %get-tuple-element.62.refs_0_, bf16[288,128]{1,0:T(8,128)(2,1)S(1)} %get-tuple-element.63.refs_1_, ...), custom_call_target="tpu_custom_call" | custom-call | tf_op jit(solution)/shard_map/pallas_call | solution.py:132
  24.2 0.4 collective-permute-start.12
  24.6 1.4 %shard_map.114 = (f32[720,128]{1,0:T(8,128)S(1)}, f32[432,128]{1,0:T(8,128)S(1)}, bf16[432,128]{1,0:T(8,128)(2,1)S(1)}, bf16[720,128]{1,0:T(8,128)(2,1)S(1)}) custom-call(bf16[72,768]{1,0:T(8,128)(2,1)S(1)} %get-tuple-element.66.hidden.refs_5_, bf16[1,768,4096]{2,1,0:T(8,128)(2,1)S(1)} %bitcast.7), custom_call_target="tpu_custom_call" | custom-call | flops 452984832 | tf_op jit(solution)/shard_map/pallas_call | solution.py:132
  26.0 0.2 collective-permute-start.9
  26.2 4.9 %shard_map.116 = (bf16[72,4096]{1,0:T(8,128)(2,1)S(1)}, bf16[72,768]{1,0:T(8,128)(2,1)S(1)}, bf16[72,768]{1,0:T(8,128)(2,1)S(1)}, f32[432,128]{1,0:T(8,128)S(1)}, bf16[720,128]{1,0:T(8,128)(2,1)S(1)}) custom-call(bf16[1152,128]{1,0:T(8,128)(2,1)S(1)} %shard_map.115.g_sent, bf16[1152,128]{1,0:T(8,128)(2,1)S(1)} %collective-permute-done.12.g_swapped, ...), custom_call_target="tpu_custom_call" | custom-call | flops 905969664 | tf_op jit(solution)/shard_map/pallas_call | solution.py:132
  31.1 0.4 collective-permute-start.13
  31.6 2.1 %shard_map.117 = (f32[720,128]{1,0:T(8,128)S(1)}, bf16[432,128]{1,0:T(8,128)(2,1)S(1)}) custom-call(bf16[72,768]{1,0:T(8,128)(2,1)S(1)} %get-tuple-element.74.pre_gate, bf16[72,768]{1,0:T(8,128)(2,1)S(1)} %get-tuple-element.75.pre_up, bf16[1,4096,768]{2,1,0:T(8,128)(2,1)S(1)} %bitcast.3, bf16[1,4096,768]{2,1,0:T(8,128)(2,1)S(1)} %bitcast.5), custom_call_target="tpu_custom_call" | custom-call | flops 452984832 | tf_op jit(solution)/shard_map/pallas_call | solution.py:132
  33.7 0.4 collective-permute-start.14
  34.2 0.6 %shard_map.118 = (bf16[768,72]{1,0:T(8,128)(2,1)S(1)}, bf16[768,1024]{1,0:T(8,128)(2,1)S(1)}) custom-call(bf16[72,768]{1,0:T(8,128)(2,1)S(1)} %get-tuple-element.66.hidden.refs_5_, bf16[72,4096]{1,0:T(8,128)(2,1)S(1)} %get-tuple-element.80.g), custom_call_target="tpu_custom_call" | custom-call | flops 113246208 | tf_op jit(solution)/shard_map/pallas_call | solution.py:132
  34.9 0.3 collective-permute-done.14.refs_7_
  35.3 2.5 %collective-permute-start.15 = (bf16[576,128]{1,0:T(8,128)(2,1)S(1)}, bf16[576,128]{1,0:T(8,128)(2,1)S(1)}, u32[]{:S(2)}, u32[]{:S(2)}) collective-permute-start(bf16[576,128]{1,0:T(8,128)(2,1)S(1)} %get-tuple-element.82), channel_id=1, source_target_pairs={{0,12},{1,15},{2,14},{3,13},{4,8},{5,11},{6,10},{7,9},{8,4},{9,7},... | collective-permute-start | bytes 442376 | tf_op jit(solution)/shard_map/ppermute | solution.py:550
  37.8 2.5 %collective-permute-start.16 = (bf16[576,128]{1,0:T(8,128)(2,1)S(1)}, bf16[576,128]{1,0:T(8,128)(2,1)S(1)}, u32[]{:S(2)}, u32[]{:S(2)}) collective-permute-start(bf16[576,128]{1,0:T(8,128)(2,1)S(1)} %get-tuple-element.83), channel_id=1, source_target_pairs={{0,8},{1,11},{2,10},{3,9},{4,12},{5,15},{6,14},{7,13},{8,0},{9,3},... | collective-permute-start | bytes 442376 | tf_op jit(solution)/shard_map/ppermute | solution.py:550
  40.3 0.5 collective-permute-start.17
  40.8 1.1 %collective-permute-start.18 = (bf16[288,128]{1,0:T(8,128)(2,1)S(1)}, bf16[288,128]{1,0:T(8,128)(2,1)S(1)}, u32[]{:S(2)}, u32[]{:S(2)}) collective-permute-start(bf16[288,128]{1,0:T(8,128)(2,1)S(1)} %get-tuple-element.85), channel_id=1, source_target_pairs={{0,2},{2,0},{4,6},{6,4},{8,10},{10,8},{12,14},{14,12},{1,3},{3,1},... | collective-permute-start | bytes 221192 | tf_op jit(solution)/shard_map/ppermute | solution.py:555
  41.9 8.4 %shard_map.120 = (bf16[1,4096,768]{2,1,0:T(8,128)(2,1)}, bf16[1,4096,768]{2,1,0:T(8,128)(2,1)}, bf16[1,768,4096]{2,1,0:T(8,128)(2,1)}, f32[8,128]{1,0:T(8,128)S(1)}) custom-call(bf16[72,4096]{1,0:T(8,128)(2,1)S(1)} %get-tuple-element.86.x, bf16[72,4096]{1,0:T(8,128)(2,1)S(1)} %get-tuple-element.80.g, bf16[768,72]{1,0:T(8,128)(2,1)S(1)} %get-tuple-element.87.hidden_turned, ...), custom_call_target="tpu_custom_call" | custom-call | flops 1358954496 | bytes 18874368 | tf_op jit(solution)/shard_map/pallas_call | solution.py:132
  50.3 3.0 %collective-permute-done.16.refs_1_ = bf16[576,128]{1,0:T(8,128)(2,1)S(1)} collective-permute-done((bf16[576,128]{1,0:T(8,128)(2,1)S(1)}, bf16[576,128]{1,0:T(8,128)(2,1)S(1)}, u32[]{:S(2)}, u32[]{:S(2)}) %collective-permute-start.16) | collective-permute-done | bytes 147488 | tf_op jit(solution)/shard_map/ppermute | solution.py:550
  53.5 0.9 %shard_map.122 = (f32[128,2048]{1,0:T(8,128)S(1)}, f32[128,2048]{1,0:T(8,128)S(1)}) custom-call(bf16[72,128]{1,0:T(8,128)(2,1)S(1)} %get-tuple-element.89.place, f32[72,128]{1,0:T(8,128)S(1)} %get-tuple-element.90.mix, bf16[576,128]{1,0:T(8,128)(2,1)S(1)} %collective-permute-done.15.refs_0_, bf16[576,128]{1,0:T(8,128)(2,1)S(1)} %collective-permute-done.16.refs_1_, ...), custom_call_target="tpu_custom_call" | custom-call | flops 75497472 | tf_op jit(solution)/shard_map/pallas_call | solution.py:132
  54.4 0.5 collective-permute-done.19.shared
  54.9 1.4 %shard_map.123 = (bf16[128,2048]{1,0:T(8,128)(2,1)}, bf16[128,2048]{1,0:T(8,128)(2,1)}) custom-call(bf16[27,128]{1,0:T(8,128)(2,1)S(1)} %get-tuple-element.52.place, f32[27,128]{1,0:T(8,128)S(1)} %get-tuple-element.53.mix, bf16[864,128]{1,0:T(8,128)(2,1)S(1)} %collective-permute-done.19.shared, f32[128,2048]{1,0:T(8,128)S(1)} %get-tuple-element.92.out_sum, ...), custom_call_target="tpu_custom_call" | custom-call | bytes 2097152 | tf_op jit(solution)/shard_map/pallas_call | solution.py:132
  (37 shorter events, 1.0 us)
Async XLA Ops:
  0.6 20.8 %slice-start = ((s8[6291456]{0:T(1024)(128)(4,1)}), s8[4194304]{0:T(1024)(128)(4,1)S(1)}, s32[]{:S(2)}) async-start(s8[6291456]{0:T(1024)(128)(4,1)} %bitcast.2), calls=%async_computation | async-start | bytes 8388608
  0.6 20.8 %slice-start.2 = ((s8[6291456]{0:T(1024)(128)(4,1)}), s8[4194304]{0:T(1024)(128)(4,1)S(1)}, s32[]{:S(2)}) async-start(s8[6291456]{0:T(1024)(128)(4,1)} %bitcast.4), calls=%async_computation.2 | async-start | bytes 8388608
  2.7 1.6 %collective-permute-start = (bf16[864,128]{1,0:T(8,128)(2,1)S(1)}, bf16[864,128]{1,0:T(8,128)(2,1)S(1)}, u32[]{:S(2)}, u32[]{:S(2)}) collective-permute-start(bf16[864,128]{1,0:T(8,128)(2,1)S(1)} %get-tuple-element.56), channel_id=1, source_target_pairs={{0,1},{1,0},{2,3},{3,2},{4,5},{5,4},{6,7},{7,6},{8,9},{9,8},{10,11... | collective-permute-start | bytes 663560 | tf_op jit(solution)/shard_map/ppermute | solution.py:559
  4.4 17.0 %slice-start.1 = ((s8[6291456]{0:T(1024)(128)(4,1)}), s8[2097152]{0:T(1024)(128)(4,1)S(1)}, s32[]{:S(2)}) async-start(s8[6291456]{0:T(1024)(128)(4,1)} %bitcast.2), calls=%async_computation.1 | async-start | bytes 4194304
  4.4 17.0 %slice-start.3 = ((s8[6291456]{0:T(1024)(128)(4,1)}), s8[2097152]{0:T(1024)(128)(4,1)S(1)}, s32[]{:S(2)}) async-start(s8[6291456]{0:T(1024)(128)(4,1)} %bitcast.4), calls=%async_computation.3 | async-start | bytes 4194304
  4.4 15.0 %collective-permute-start.2 = (bf16[576,128]{1,0:T(8,128)(2,1)S(1)}, bf16[576,128]{1,0:T(8,128)(2,1)S(1)}, u32[]{:S(2)}, u32[]{:S(2)}) collective-permute-start(bf16[576,128]{1,0:T(8,128)(2,1)S(1)} %get-tuple-element.58), channel_id=1, source_target_pairs={{0,8},{1,11},{2,10},{3,9},{4,12},{5,15},{6,14},{7,13},{8,0},{9,3},... | collective-permute-start | bytes 442376 | tf_op jit(solution)/shard_map/ppermute | solution.py:550
  8.4 10.9 %collective-permute-start.3 = (bf16[576,128]{1,0:T(8,128)(2,1)S(1)}, bf16[576,128]{1,0:T(8,128)(2,1)S(1)}, u32[]{:S(2)}, u32[]{:S(2)}) collective-permute-start(bf16[576,128]{1,0:T(8,128)(2,1)S(1)} %get-tuple-element.59), channel_id=1, source_target_pairs={{0,4},{1,7},{2,6},{3,5},{4,0},{5,3},{6,2},{7,1},{8,12},{9,15},{10,... | collective-permute-start | bytes 442376 | tf_op jit(solution)/shard_map/ppermute | solution.py:550
  10.0 9.3 %collective-permute-start.1 = (bf16[304,128]{1,0:T(8,128)(2,1)S(1)}, bf16[304,128]{1,0:T(8,128)(2,1)S(1)}, u32[]{:S(2)}, u32[]{:S(2)}) collective-permute-start(bf16[304,128]{1,0:T(8,128)(2,1)S(1)} %get-tuple-element.57), channel_id=1, source_target_pairs={{0,12},{1,15},{2,14},{3,13},{4,8},{5,11},{6,10},{7,9},{8,4},{9,7},... | collective-permute-start | bytes 233480 | tf_op jit(solution)/shard_map/ppermute | solution.py:550
  10.0 6.1 %collective-permute-start.4 = (bf16[288,128]{1,0:T(8,128)(2,1)S(1)}, bf16[288,128]{1,0:T(8,128)(2,1)S(1)}, u32[]{:S(2)}, u32[]{:S(2)}) collective-permute-start(bf16[288,128]{1,0:T(8,128)(2,1)S(1)} %get-tuple-element.60), channel_id=1, source_target_pairs={{0,2},{2,0},{4,6},{6,4},{8,10},{10,8},{12,14},{14,12},{1,3},{3,1},... | collective-permute-start | bytes 221192 | tf_op jit(solution)/shard_map/ppermute | solution.py:555
  11.7 12.4 %collective-permute-start.11 = (bf16[304,128]{1,0:T(8,128)(2,1)S(1)}, bf16[304,128]{1,0:T(8,128)(2,1)S(1)}, u32[]{:S(2)}, u32[]{:S(2)}) collective-permute-start(bf16[304,128]{1,0:T(8,128)(2,1)S(1)} %get-tuple-element.71), channel_id=1, source_target_pairs={{0,12},{1,15},{2,14},{3,13},{4,8},{5,11},{6,10},{7,9},{8,4},{9,7},... | collective-permute-start | bytes 233480 | tf_op jit(solution)/shard_map/ppermute | solution.py:550
  19.4 1.3 %collective-permute-start.5 = (bf16[288,128]{1,0:T(8,128)(2,1)S(1)}, bf16[288,128]{1,0:T(8,128)(2,1)S(1)}, u32[]{:S(2)}, u32[]{:S(2)}) collective-permute-start(bf16[288,128]{1,0:T(8,128)(2,1)S(1)} %get-tuple-element.62.refs_0_), channel_id=1, source_target_pairs={{0,1},{1,0},{2,3},{3,2},{4,5},{5,4},{6,7},{7,6},{8,9},{9,8},{10,11... | collective-permute-start | bytes 221192 | tf_op jit(solution)/shard_map/ppermute | solution.py:559
  19.5 1.4 %collective-permute-start.6 = (bf16[288,128]{1,0:T(8,128)(2,1)S(1)}, bf16[288,128]{1,0:T(8,128)(2,1)S(1)}, u32[]{:S(2)}, u32[]{:S(2)}) collective-permute-start(bf16[288,128]{1,0:T(8,128)(2,1)S(1)} %get-tuple-element.63.refs_1_), channel_id=1, source_target_pairs={{0,1},{1,0},{2,3},{3,2},{4,5},{5,4},{6,7},{7,6},{8,9},{9,8},{10,11... | collective-permute-start | bytes 221192 | tf_op jit(solution)/shard_map/ppermute | solution.py:559
  20.0 1.3 %collective-permute-start.7 = (bf16[288,128]{1,0:T(8,128)(2,1)S(1)}, bf16[288,128]{1,0:T(8,128)(2,1)S(1)}, u32[]{:S(2)}, u32[]{:S(2)}) collective-permute-start(bf16[288,128]{1,0:T(8,128)(2,1)S(1)} %get-tuple-element.64.refs_2_), channel_id=1, source_target_pairs={{0,1},{1,0},{2,3},{3,2},{4,5},{5,4},{6,7},{7,6},{8,9},{9,8},{10,11... | collective-permute-start | bytes 221192 | tf_op jit(solution)/shard_map/ppermute | solution.py:559
  20.0 4.6 %slice-start.4 = ((s8[6291456]{0:T(1024)(128)(4,1)}), s8[4194304]{0:T(1024)(128)(4,1)S(1)}, s32[]{:S(2)}) async-start(s8[6291456]{0:T(1024)(128)(4,1)} %bitcast.6), calls=%async_computation.4 | async-start | bytes 8388608
  20.0 4.6 %slice-start.5 = ((s8[6291456]{0:T(1024)(128)(4,1)}), s8[2097152]{0:T(1024)(128)(4,1)S(1)}, s32[]{:S(2)}) async-start(s8[6291456]{0:T(1024)(128)(4,1)} %bitcast.6), calls=%async_computation.5 | async-start | bytes 4194304
  20.1 1.3 %collective-permute-start.8 = (bf16[288,128]{1,0:T(8,128)(2,1)S(1)}, bf16[288,128]{1,0:T(8,128)(2,1)S(1)}, u32[]{:S(2)}, u32[]{:S(2)}) collective-permute-start(bf16[288,128]{1,0:T(8,128)(2,1)S(1)} %get-tuple-element.65.refs_3_), channel_id=1, source_target_pairs={{0,1},{1,0},{2,3},{3,2},{4,5},{5,4},{6,7},{7,6},{8,9},{9,8},{10,11... | collective-permute-start | bytes 221192 | tf_op jit(solution)/shard_map/ppermute | solution.py:559
  24.2 2.0 %collective-permute-start.12 = (bf16[1152,128]{1,0:T(8,128)(2,1)S(1)}, bf16[1152,128]{1,0:T(8,128)(2,1)S(1)}, u32[]{:S(2)}, u32[]{:S(2)}) collective-permute-start(bf16[1152,128]{1,0:T(8,128)(2,1)S(1)} %shard_map.115.g_sent), channel_id=1, source_target_pairs={{0,1},{1,0},{2,3},{3,2},{4,5},{5,4},{6,7},{7,6},{8,9},{9,8},{10,11... | collective-permute-start | bytes 884744 | tf_op jit(solution)/shard_map/ppermute | solution.py:559
  26.0 8.9 %collective-permute-start.9 = (bf16[720,128]{1,0:T(8,128)(2,1)S(1)}, bf16[720,128]{1,0:T(8,128)(2,1)S(1)}, u32[]{:S(2)}, u32[]{:S(2)}) collective-permute-start(bf16[720,128]{1,0:T(8,128)(2,1)S(1)} %get-tuple-element.69), channel_id=1, source_target_pairs={{0,1},{1,0},{2,3},{3,2},{4,5},{5,4},{6,7},{7,6},{8,9},{9,8},{10,11... | collective-permute-start | bytes 552968 | tf_op jit(solution)/shard_map/ppermute | solution.py:559
  31.1 4.1 %collective-permute-start.13 = (bf16[720,128]{1,0:T(8,128)(2,1)S(1)}, bf16[720,128]{1,0:T(8,128)(2,1)S(1)}, u32[]{:S(2)}, u32[]{:S(2)}) collective-permute-start(bf16[720,128]{1,0:T(8,128)(2,1)S(1)} %get-tuple-element.78), channel_id=1, source_target_pairs={{0,1},{1,0},{2,3},{3,2},{4,5},{5,4},{6,7},{7,6},{8,9},{9,8},{10,11... | collective-permute-start | bytes 552968 | tf_op jit(solution)/shard_map/ppermute | solution.py:559
  31.5 3.3 %collective-permute-start.10 = (bf16[432,128]{1,0:T(8,128)(2,1)S(1)}, bf16[432,128]{1,0:T(8,128)(2,1)S(1)}, u32[]{:S(2)}, u32[]{:S(2)}) collective-permute-start(bf16[432,128]{1,0:T(8,128)(2,1)S(1)} %get-tuple-element.70), channel_id=1, source_target_pairs={{0,1},{1,0},{2,3},{3,2},{4,5},{5,4},{6,7},{7,6},{8,9},{9,8},{10,11... | collective-permute-start | bytes 331784 | tf_op jit(solution)/shard_map/ppermute | solution.py:559
  33.7 1.4 %collective-permute-start.14 = (bf16[432,128]{1,0:T(8,128)(2,1)S(1)}, bf16[432,128]{1,0:T(8,128)(2,1)S(1)}, u32[]{:S(2)}, u32[]{:S(2)}) collective-permute-start(bf16[432,128]{1,0:T(8,128)(2,1)S(1)} %get-tuple-element.79), channel_id=1, source_target_pairs={{0,1},{1,0},{2,3},{3,2},{4,5},{5,4},{6,7},{7,6},{8,9},{9,8},{10,11... | collective-permute-start | bytes 331784 | tf_op jit(solution)/shard_map/ppermute | solution.py:559
  35.3 15.0 %collective-permute-start.15 = (bf16[576,128]{1,0:T(8,128)(2,1)S(1)}, bf16[576,128]{1,0:T(8,128)(2,1)S(1)}, u32[]{:S(2)}, u32[]{:S(2)}) collective-permute-start(bf16[576,128]{1,0:T(8,128)(2,1)S(1)} %get-tuple-element.82), channel_id=1, source_target_pairs={{0,12},{1,15},{2,14},{3,13},{4,8},{5,11},{6,10},{7,9},{8,4},{9,7},... | collective-permute-start | bytes 442376 | tf_op jit(solution)/shard_map/ppermute | solution.py:550
  37.8 15.5 %collective-permute-start.16 = (bf16[576,128]{1,0:T(8,128)(2,1)S(1)}, bf16[576,128]{1,0:T(8,128)(2,1)S(1)}, u32[]{:S(2)}, u32[]{:S(2)}) collective-permute-start(bf16[576,128]{1,0:T(8,128)(2,1)S(1)} %get-tuple-element.83), channel_id=1, source_target_pairs={{0,8},{1,11},{2,10},{3,9},{4,12},{5,15},{6,14},{7,13},{8,0},{9,3},... | collective-permute-start | bytes 442376 | tf_op jit(solution)/shard_map/ppermute | solution.py:550
  40.3 13.1 %collective-permute-start.17 = (bf16[576,128]{1,0:T(8,128)(2,1)S(1)}, bf16[576,128]{1,0:T(8,128)(2,1)S(1)}, u32[]{:S(2)}, u32[]{:S(2)}) collective-permute-start(bf16[576,128]{1,0:T(8,128)(2,1)S(1)} %get-tuple-element.84), channel_id=1, source_target_pairs={{0,4},{1,7},{2,6},{3,5},{4,0},{5,3},{6,2},{7,1},{8,12},{9,15},{10,... | collective-permute-start | bytes 442376 | tf_op jit(solution)/shard_map/ppermute | solution.py:550
  40.8 9.5 %collective-permute-start.18 = (bf16[288,128]{1,0:T(8,128)(2,1)S(1)}, bf16[288,128]{1,0:T(8,128)(2,1)S(1)}, u32[]{:S(2)}, u32[]{:S(2)}) collective-permute-start(bf16[288,128]{1,0:T(8,128)(2,1)S(1)} %get-tuple-element.85), channel_id=1, source_target_pairs={{0,2},{2,0},{4,6},{6,4},{8,10},{10,8},{12,14},{14,12},{1,3},{3,1},... | collective-permute-start | bytes 221192 | tf_op jit(solution)/shard_map/ppermute | solution.py:555
  53.4 1.5 %collective-permute-start.19 = (bf16[864,128]{1,0:T(8,128)(2,1)S(1)}, bf16[864,128]{1,0:T(8,128)(2,1)S(1)}, u32[]{:S(2)}, u32[]{:S(2)}) collective-permute-start(bf16[864,128]{1,0:T(8,128)(2,1)S(1)} %shard_map.121), channel_id=1, source_target_pairs={{0,1},{1,0},{2,3},{3,2},{4,5},{5,4},{6,7},{7,6},{8,9},{9,8},{10,11... | collective-permute-start | bytes 663560 | tf_op jit(solution)/shard_map/ppermute | solution.py:559

commit v16 on v15

--- a/solution.py
+++ b/solution.py
@@ -600,7 +600,7 @@
         traffic=4 * tok_dev * sub_width,
     )
     masks = even_masks(devices)
-    late = [0]
+    late = [devices // 4 - 1]
     late_block = jax.ShapeDtypeStruct((2 * size + 16, LANES), low)
     packed = call(
         functools.partial(pack_kernel, size, late),

time: 56.4 us -> 55.3 us (0.980)
  starting transfers between devices: 20.9 us -> 19.4 us
    ppermute x7, starting transfers between devices: 14.7 us -> 12.3 us  [exchange(): arrived.append(lax.ppermute(block, ('expert', 'ffn'), pairs))]
    ppermute x2, waiting for transfers between devices: 0.82 us -> 1.89 us  [exchange_near(): return lax.ppermute(block, 'expert', [(i, i ^ 1) for i in range(devices)])]
  transfers between devices with their start and end apart: 20 -> 20, of which waited for: 10 -> 9; matrix products, arithmetic and copies ran while one was open for 0% -> 0% of each run, Pallas kernels for 37% -> 38%
where the time goes in v16:
time: 55.3 us; the launch traced here: 55.2 us
  Pallas kernels  24.6 us (44%)
  starting transfers between devices  19.4 us (35%)
  waiting for transfers between devices  10.3 us (19%)
  between operations  0.84 us (2%)
    pallas_call x14, Pallas kernels, call(): pl.pallas_call(kernel, out_shape=tuple(out_shape), in_specs=[pl.BlockSpec...  24.6 us
    ppermute x7, starting transfers between devices, exchange(): arrived.append(lax.ppermute(block, ('expert', 'ffn'), pairs))  12.3 us
    ppermute x7, waiting for transfers between devices, exchange(): arrived.append(lax.ppermute(block, ('expert', 'ffn'), pairs))  5.91 us
    ppermute x11, starting transfers between devices, swap(): return lax.ppermute(value, 'ffn', [(0, 1), (1, 0)])  3.89 us
    ppermute x2, starting transfers between devices, exchange_near(): return lax.ppermute(block, 'expert', [(i, i ^ 1) for i in range(devices)])  3.19 us
    ppermute x11, waiting for transfers between devices, swap(): return lax.ppermute(value, 'ffn', [(0, 1), (1, 0)])  2.53 us
    ppermute x2, waiting for transfers between devices, exchange_near(): return lax.ppermute(block, 'expert', [(i, i ^ 1) for i in range(devices)])  1.89 us
  transfers between devices with their start and end apart: 20, of which 9 were waited for; matrix products, arithmetic and copies ran while one was open for 0% of the time, Pallas kernels for 38%

profile of v16, /device:TPU:0, one launch (start us, length us, event | category | flops | bytes accessed | tf_op | source)
XLA Modules:
  0.0 55.2 jit_solution(12295464649946518513)
XLA Ops:
  0.7 2.1 %shard_map.110 = (bf16[432,128]{1,0:T(8,128)(2,1)S(1)}, bf16[432,128]{1,0:T(8,128)(2,1)S(1)}, bf16[288,128]{1,0:T(8,128)(2,1)S(1)}, bf16[288,128]{1,0:T(8,128)(2...) custom-call(s32[8,128]{1,0:T(8,128)} %bitcast.8, ...), custom_call_target="tpu_custom_call" | custom-call | bytes 1048576 | tf_op jit(solution)/shard_map/pallas_call | solution.py:132
  2.7 0.5 collective-permute-start
  3.3 1.1 %collective-permute-done.swapped = bf16[864,128]{1,0:T(8,128)(2,1)S(1)} collective-permute-done((bf16[864,128]{1,0:T(8,128)(2,1)S(1)}, bf16[864,128]{1,0:T(8,128)(2,1)S(1)}, u32[]{:S(2)}, u32[]{:S(2)}) %collective-permute-start) | collective-permute-done | bytes 221216 | tf_op jit(solution)/shard_map/ppermute | solution.py:559
  4.4 5.0 %collective-permute-start.1 = (bf16[576,128]{1,0:T(8,128)(2,1)S(1)}, bf16[576,128]{1,0:T(8,128)(2,1)S(1)}, u32[]{:S(2)}, u32[]{:S(2)}) collective-permute-start(bf16[576,128]{1,0:T(8,128)(2,1)S(1)} %get-tuple-element.57), channel_id=1, source_target_pairs={{0,12},{1,15},{2,14},{3,13},{4,8},{5,11},{6,10},{7,9},{8,4},{9,7},... | collective-permute-start | bytes 442376 | tf_op jit(solution)/shard_map/ppermute | solution.py:550
  9.5 0.6 %collective-permute-start.2 = (bf16[304,128]{1,0:T(8,128)(2,1)S(1)}, bf16[304,128]{1,0:T(8,128)(2,1)S(1)}, u32[]{:S(2)}, u32[]{:S(2)}) collective-permute-start(bf16[304,128]{1,0:T(8,128)(2,1)S(1)} %get-tuple-element.58), channel_id=1, source_target_pairs={{0,8},{1,11},{2,10},{3,9},{4,12},{5,15},{6,14},{7,13},{8,0},{9,3},... | collective-permute-start | bytes 233480 | tf_op jit(solution)/shard_map/ppermute | solution.py:550
  10.1 1.6 %collective-permute-start.4 = (bf16[288,128]{1,0:T(8,128)(2,1)S(1)}, bf16[288,128]{1,0:T(8,128)(2,1)S(1)}, u32[]{:S(2)}, u32[]{:S(2)}) collective-permute-start(bf16[288,128]{1,0:T(8,128)(2,1)S(1)} %get-tuple-element.60), channel_id=1, source_target_pairs={{0,2},{2,0},{4,6},{6,4},{8,10},{10,8},{12,14},{14,12},{1,3},{3,1},... | collective-permute-start | bytes 221192 | tf_op jit(solution)/shard_map/ppermute | solution.py:555
  11.7 2.1 %collective-permute-start.11 = (bf16[304,128]{1,0:T(8,128)(2,1)S(1)}, bf16[304,128]{1,0:T(8,128)(2,1)S(1)}, u32[]{:S(2)}, u32[]{:S(2)}) collective-permute-start(bf16[304,128]{1,0:T(8,128)(2,1)S(1)} %get-tuple-element.71), channel_id=1, source_target_pairs={{0,8},{1,11},{2,10},{3,9},{4,12},{5,15},{6,14},{7,13},{8,0},{9,3},... | collective-permute-start | bytes 233480 | tf_op jit(solution)/shard_map/ppermute | solution.py:550
  13.9 1.9 %collective-permute-done.4.refs_3_ = bf16[288,128]{1,0:T(8,128)(2,1)S(1)} collective-permute-done((bf16[288,128]{1,0:T(8,128)(2,1)S(1)}, bf16[288,128]{1,0:T(8,128)(2,1)S(1)}, u32[]{:S(2)}, u32[]{:S(2)}) %collective-permute-start.4) | collective-permute-done | bytes 73760 | tf_op jit(solution)/shard_map/ppermute | solution.py:555
  15.8 5.9 %collective-permute-done.2.refs_1_ = bf16[304,128]{1,0:T(8,128)(2,1)S(1)} collective-permute-done((bf16[304,128]{1,0:T(8,128)(2,1)S(1)}, bf16[304,128]{1,0:T(8,128)(2,1)S(1)}, u32[]{:S(2)}, u32[]{:S(2)}) %collective-permute-start.2) | collective-permute-done | bytes 77856 | tf_op jit(solution)/shard_map/ppermute | solution.py:550
  21.8 0.5 collective-permute-start.6
  22.3 0.4 collective-permute-start.8
  22.8 0.2 collective-permute-done.5.refs_4_
  23.2 0.4 collective-permute-done.7.refs_6_
  23.7 2.7 %shard_map.113 = (bf16[72,4096]{1,0:T(8,128)(2,1)S(1)}, bf16[72,768]{1,0:T(8,128)(2,1)S(1)}, bf16[72,768]{1,0:T(8,128)(2,1)S(1)}, bf16[72,768]{1,0:T(8,128)(2,1)S(1)}) custom-call(bf16[288,128]{1,0:T(8,128)(2,1)S(1)} %get-tuple-element.62.refs_0_, bf16[288,128]{1,0:T(8,128)(2,1)S(1)} %get-tuple-element.63.refs_1_, ...), custom_call_target="tpu_custom_call" | custom-call | tf_op jit(solution)/shard_map/pallas_call | solution.py:132
  26.5 0.4 collective-permute-start.12
  26.9 1.4 %shard_map.114 = (f32[720,128]{1,0:T(8,128)S(1)}, f32[432,128]{1,0:T(8,128)S(1)}, bf16[432,128]{1,0:T(8,128)(2,1)S(1)}, bf16[720,128]{1,0:T(8,128)(2,1)S(1)}) custom-call(bf16[72,768]{1,0:T(8,128)(2,1)S(1)} %get-tuple-element.66.hidden.refs_5_, bf16[1,768,4096]{2,1,0:T(8,128)(2,1)S(1)} %bitcast.7), custom_call_target="tpu_custom_call" | custom-call | flops 452984832 | tf_op jit(solution)/shard_map/pallas_call | solution.py:132
  28.3 0.2 collective-permute-start.9
  28.5 4.9 %shard_map.116 = (bf16[72,4096]{1,0:T(8,128)(2,1)S(1)}, bf16[72,768]{1,0:T(8,128)(2,1)S(1)}, bf16[72,768]{1,0:T(8,128)(2,1)S(1)}, f32[432,128]{1,0:T(8,128)S(1)}, bf16[720,128]{1,0:T(8,128)(2,1)S(1)}) custom-call(bf16[1152,128]{1,0:T(8,128)(2,1)S(1)} %shard_map.115.g_sent, bf16[1152,128]{1,0:T(8,128)(2,1)S(1)} %collective-permute-done.12.g_swapped, ...), custom_call_target="tpu_custom_call" | custom-call | flops 905969664 | tf_op jit(solution)/shard_map/pallas_call | solution.py:132
  33.4 0.4 collective-permute-start.13
  34.0 2.1 %shard_map.117 = (f32[720,128]{1,0:T(8,128)S(1)}, bf16[432,128]{1,0:T(8,128)(2,1)S(1)}) custom-call(bf16[72,768]{1,0:T(8,128)(2,1)S(1)} %get-tuple-element.74.pre_gate, bf16[72,768]{1,0:T(8,128)(2,1)S(1)} %get-tuple-element.75.pre_up, bf16[1,4096,768]{2,1,0:T(8,128)(2,1)S(1)} %bitcast.3, bf16[1,4096,768]{2,1,0:T(8,128)(2,1)S(1)} %bitcast.5), custom_call_target="tpu_custom_call" | custom-call | flops 452984832 | tf_op jit(solution)/shard_map/pallas_call | solution.py:132
  36.1 0.4 collective-permute-start.14
  36.5 0.6 %shard_map.118 = (bf16[768,72]{1,0:T(8,128)(2,1)S(1)}, bf16[768,1024]{1,0:T(8,128)(2,1)S(1)}) custom-call(bf16[72,768]{1,0:T(8,128)(2,1)S(1)} %get-tuple-element.66.hidden.refs_5_, bf16[72,4096]{1,0:T(8,128)(2,1)S(1)} %get-tuple-element.80.g), custom_call_target="tpu_custom_call" | custom-call | flops 113246208 | tf_op jit(solution)/shard_map/pallas_call | solution.py:132
  37.2 0.3 collective-permute-done.14.refs_7_
  37.6 0.3 collective-permute-start.15
  37.9 0.2 collective-permute-start.16
  38.0 4.0 %collective-permute-start.17 = (bf16[576,128]{1,0:T(8,128)(2,1)S(1)}, bf16[576,128]{1,0:T(8,128)(2,1)S(1)}, u32[]{:S(2)}, u32[]{:S(2)}) collective-permute-start(bf16[576,128]{1,0:T(8,128)(2,1)S(1)} %get-tuple-element.84), channel_id=1, source_target_pairs={{0,4},{1,7},{2,6},{3,5},{4,0},{5,3},{6,2},{7,1},{8,12},{9,15},{10,... | collective-permute-start | bytes 442376 | tf_op jit(solution)/shard_map/ppermute | solution.py:550
  42.0 1.6 %collective-permute-start.18 = (bf16[288,128]{1,0:T(8,128)(2,1)S(1)}, bf16[288,128]{1,0:T(8,128)(2,1)S(1)}, u32[]{:S(2)}, u32[]{:S(2)}) collective-permute-start(bf16[288,128]{1,0:T(8,128)(2,1)S(1)} %get-tuple-element.85), channel_id=1, source_target_pairs={{0,2},{2,0},{4,6},{6,4},{8,10},{10,8},{12,14},{14,12},{1,3},{3,1},... | collective-permute-start | bytes 221192 | tf_op jit(solution)/shard_map/ppermute | solution.py:555
  43.6 8.4 %shard_map.120 = (bf16[1,4096,768]{2,1,0:T(8,128)(2,1)}, bf16[1,4096,768]{2,1,0:T(8,128)(2,1)}, bf16[1,768,4096]{2,1,0:T(8,128)(2,1)}, f32[8,128]{1,0:T(8,128)S(1)}) custom-call(bf16[72,4096]{1,0:T(8,128)(2,1)S(1)} %get-tuple-element.86.x, bf16[72,4096]{1,0:T(8,128)(2,1)S(1)} %get-tuple-element.80.g, bf16[768,72]{1,0:T(8,128)(2,1)S(1)} %get-tuple-element.87.hidden_turned, ...), custom_call_target="tpu_custom_call" | custom-call | flops 1358954496 | bytes 18874368 | tf_op jit(solution)/shard_map/pallas_call | solution.py:132
  52.1 0.6 %collective-permute-start.19 = (bf16[864,128]{1,0:T(8,128)(2,1)S(1)}, bf16[864,128]{1,0:T(8,128)(2,1)S(1)}, u32[]{:S(2)}, u32[]{:S(2)}) collective-permute-start(bf16[864,128]{1,0:T(8,128)(2,1)S(1)} %shard_map.121), channel_id=1, source_target_pairs={{0,1},{1,0},{2,3},{3,2},{4,5},{5,4},{6,7},{7,6},{8,9},{9,8},{10,11... | collective-permute-start | bytes 663560 | tf_op jit(solution)/shard_map/ppermute | solution.py:559
  52.7 0.9 %shard_map.122 = (f32[128,2048]{1,0:T(8,128)S(1)}, f32[128,2048]{1,0:T(8,128)S(1)}) custom-call(bf16[72,128]{1,0:T(8,128)(2,1)S(1)} %get-tuple-element.89.place, f32[72,128]{1,0:T(8,128)S(1)} %get-tuple-element.90.mix, bf16[576,128]{1,0:T(8,128)(2,1)S(1)} %collective-permute-done.15.refs_0_, bf16[576,128]{1,0:T(8,128)(2,1)S(1)} %collective-permute-done.16.refs_1_, ...), custom_call_target="tpu_custom_call" | custom-call | flops 75497472 | tf_op jit(solution)/shard_map/pallas_call | solution.py:132
  53.6 0.2 collective-permute-done.19.shared
  53.8 1.4 %shard_map.123 = (bf16[128,2048]{1,0:T(8,128)(2,1)}, bf16[128,2048]{1,0:T(8,128)(2,1)}) custom-call(bf16[27,128]{1,0:T(8,128)(2,1)S(1)} %get-tuple-element.52.place, f32[27,128]{1,0:T(8,128)S(1)} %get-tuple-element.53.mix, bf16[864,128]{1,0:T(8,128)(2,1)S(1)} %collective-permute-done.19.shared, f32[128,2048]{1,0:T(8,128)S(1)} %get-tuple-element.92.out_sum, ...), custom_call_target="tpu_custom_call" | custom-call | bytes 2097152 | tf_op jit(solution)/shard_map/pallas_call | solution.py:132
  (37 shorter events, 0.9 us)
Async XLA Ops:
  0.6 23.1 %slice-start = ((s8[6291456]{0:T(1024)(128)(4,1)}), s8[4194304]{0:T(1024)(128)(4,1)S(1)}, s32[]{:S(2)}) async-start(s8[6291456]{0:T(1024)(128)(4,1)} %bitcast.2), calls=%async_computation | async-start | bytes 8388608
  0.6 23.0 %slice-start.2 = ((s8[6291456]{0:T(1024)(128)(4,1)}), s8[4194304]{0:T(1024)(128)(4,1)S(1)}, s32[]{:S(2)}) async-start(s8[6291456]{0:T(1024)(128)(4,1)} %bitcast.4), calls=%async_computation.2 | async-start | bytes 8388608
  2.7 1.6 %collective-permute-start = (bf16[864,128]{1,0:T(8,128)(2,1)S(1)}, bf16[864,128]{1,0:T(8,128)(2,1)S(1)}, u32[]{:S(2)}, u32[]{:S(2)}) collective-permute-start(bf16[864,128]{1,0:T(8,128)(2,1)S(1)} %get-tuple-element.56), channel_id=1, source_target_pairs={{0,1},{1,0},{2,3},{3,2},{4,5},{5,4},{6,7},{7,6},{8,9},{9,8},{10,11... | collective-permute-start | bytes 663560 | tf_op jit(solution)/shard_map/ppermute | solution.py:559
  4.4 19.3 %slice-start.1 = ((s8[6291456]{0:T(1024)(128)(4,1)}), s8[2097152]{0:T(1024)(128)(4,1)S(1)}, s32[]{:S(2)}) async-start(s8[6291456]{0:T(1024)(128)(4,1)} %bitcast.2), calls=%async_computation.1 | async-start | bytes 4194304
  4.4 19.3 %slice-start.3 = ((s8[6291456]{0:T(1024)(128)(4,1)}), s8[2097152]{0:T(1024)(128)(4,1)S(1)}, s32[]{:S(2)}) async-start(s8[6291456]{0:T(1024)(128)(4,1)} %bitcast.4), calls=%async_computation.3 | async-start | bytes 4194304
  4.4 17.2 %collective-permute-start.1 = (bf16[576,128]{1,0:T(8,128)(2,1)S(1)}, bf16[576,128]{1,0:T(8,128)(2,1)S(1)}, u32[]{:S(2)}, u32[]{:S(2)}) collective-permute-start(bf16[576,128]{1,0:T(8,128)(2,1)S(1)} %get-tuple-element.57), channel_id=1, source_target_pairs={{0,12},{1,15},{2,14},{3,13},{4,8},{5,11},{6,10},{7,9},{8,4},{9,7},... | collective-permute-start | bytes 442376 | tf_op jit(solution)/shard_map/ppermute | solution.py:550
  9.4 12.2 %collective-permute-start.3 = (bf16[576,128]{1,0:T(8,128)(2,1)S(1)}, bf16[576,128]{1,0:T(8,128)(2,1)S(1)}, u32[]{:S(2)}, u32[]{:S(2)}) collective-permute-start(bf16[576,128]{1,0:T(8,128)(2,1)S(1)} %get-tuple-element.59), channel_id=1, source_target_pairs={{0,4},{1,7},{2,6},{3,5},{4,0},{5,3},{6,2},{7,1},{8,12},{9,15},{10,... | collective-permute-start | bytes 442376 | tf_op jit(solution)/shard_map/ppermute | solution.py:550
  9.5 12.2 %collective-permute-start.2 = (bf16[304,128]{1,0:T(8,128)(2,1)S(1)}, bf16[304,128]{1,0:T(8,128)(2,1)S(1)}, u32[]{:S(2)}, u32[]{:S(2)}) collective-permute-start(bf16[304,128]{1,0:T(8,128)(2,1)S(1)} %get-tuple-element.58), channel_id=1, source_target_pairs={{0,8},{1,11},{2,10},{3,9},{4,12},{5,15},{6,14},{7,13},{8,0},{9,3},... | collective-permute-start | bytes 233480 | tf_op jit(solution)/shard_map/ppermute | solution.py:550
  10.1 5.7 %collective-permute-start.4 = (bf16[288,128]{1,0:T(8,128)(2,1)S(1)}, bf16[288,128]{1,0:T(8,128)(2,1)S(1)}, u32[]{:S(2)}, u32[]{:S(2)}) collective-permute-start(bf16[288,128]{1,0:T(8,128)(2,1)S(1)} %get-tuple-element.60), channel_id=1, source_target_pairs={{0,2},{2,0},{4,6},{6,4},{8,10},{10,8},{12,14},{14,12},{1,3},{3,1},... | collective-permute-start | bytes 221192 | tf_op jit(solution)/shard_map/ppermute | solution.py:555
  11.7 14.7 %collective-permute-start.11 = (bf16[304,128]{1,0:T(8,128)(2,1)S(1)}, bf16[304,128]{1,0:T(8,128)(2,1)S(1)}, u32[]{:S(2)}, u32[]{:S(2)}) collective-permute-start(bf16[304,128]{1,0:T(8,128)(2,1)S(1)} %get-tuple-element.71), channel_id=1, source_target_pairs={{0,8},{1,11},{2,10},{3,9},{4,12},{5,15},{6,14},{7,13},{8,0},{9,3},... | collective-permute-start | bytes 233480 | tf_op jit(solution)/shard_map/ppermute | solution.py:550
  21.7 1.3 %collective-permute-start.5 = (bf16[288,128]{1,0:T(8,128)(2,1)S(1)}, bf16[288,128]{1,0:T(8,128)(2,1)S(1)}, u32[]{:S(2)}, u32[]{:S(2)}) collective-permute-start(bf16[288,128]{1,0:T(8,128)(2,1)S(1)} %get-tuple-element.62.refs_0_), channel_id=1, source_target_pairs={{0,1},{1,0},{2,3},{3,2},{4,5},{5,4},{6,7},{7,6},{8,9},{9,8},{10,11... | collective-permute-start | bytes 221192 | tf_op jit(solution)/shard_map/ppermute | solution.py:559
  21.8 1.4 %collective-permute-start.6 = (bf16[288,128]{1,0:T(8,128)(2,1)S(1)}, bf16[288,128]{1,0:T(8,128)(2,1)S(1)}, u32[]{:S(2)}, u32[]{:S(2)}) collective-permute-start(bf16[288,128]{1,0:T(8,128)(2,1)S(1)} %get-tuple-element.63.refs_1_), channel_id=1, source_target_pairs={{0,1},{1,0},{2,3},{3,2},{4,5},{5,4},{6,7},{7,6},{8,9},{9,8},{10,11... | collective-permute-start | bytes 221192 | tf_op jit(solution)/shard_map/ppermute | solution.py:559
  22.3 1.3 %collective-permute-start.7 = (bf16[288,128]{1,0:T(8,128)(2,1)S(1)}, bf16[288,128]{1,0:T(8,128)(2,1)S(1)}, u32[]{:S(2)}, u32[]{:S(2)}) collective-permute-start(bf16[288,128]{1,0:T(8,128)(2,1)S(1)} %get-tuple-element.64.refs_2_), channel_id=1, source_target_pairs={{0,1},{1,0},{2,3},{3,2},{4,5},{5,4},{6,7},{7,6},{8,9},{9,8},{10,11... | collective-permute-start | bytes 221192 | tf_op jit(solution)/shard_map/ppermute | solution.py:559
  22.3 4.6 %slice-start.4 = ((s8[6291456]{0:T(1024)(128)(4,1)}), s8[4194304]{0:T(1024)(128)(4,1)S(1)}, s32[]{:S(2)}) async-start(s8[6291456]{0:T(1024)(128)(4,1)} %bitcast.6), calls=%async_computation.4 | async-start | bytes 8388608
  22.3 4.6 %slice-start.5 = ((s8[6291456]{0:T(1024)(128)(4,1)}), s8[2097152]{0:T(1024)(128)(4,1)S(1)}, s32[]{:S(2)}) async-start(s8[6291456]{0:T(1024)(128)(4,1)} %bitcast.6), calls=%async_computation.5 | async-start | bytes 4194304
  22.3 1.3 %collective-permute-start.8 = (bf16[288,128]{1,0:T(8,128)(2,1)S(1)}, bf16[288,128]{1,0:T(8,128)(2,1)S(1)}, u32[]{:S(2)}, u32[]{:S(2)}) collective-permute-start(bf16[288,128]{1,0:T(8,128)(2,1)S(1)} %get-tuple-element.65.refs_3_), channel_id=1, source_target_pairs={{0,1},{1,0},{2,3},{3,2},{4,5},{5,4},{6,7},{7,6},{8,9},{9,8},{10,11... | collective-permute-start | bytes 221192 | tf_op jit(solution)/shard_map/ppermute | solution.py:559
  26.5 2.0 %collective-permute-start.12 = (bf16[1152,128]{1,0:T(8,128)(2,1)S(1)}, bf16[1152,128]{1,0:T(8,128)(2,1)S(1)}, u32[]{:S(2)}, u32[]{:S(2)}) collective-permute-start(bf16[1152,128]{1,0:T(8,128)(2,1)S(1)} %shard_map.115.g_sent), channel_id=1, source_target_pairs={{0,1},{1,0},{2,3},{3,2},{4,5},{5,4},{6,7},{7,6},{8,9},{9,8},{10,11... | collective-permute-start | bytes 884744 | tf_op jit(solution)/shard_map/ppermute | solution.py:559
  28.3 8.9 %collective-permute-start.9 = (bf16[720,128]{1,0:T(8,128)(2,1)S(1)}, bf16[720,128]{1,0:T(8,128)(2,1)S(1)}, u32[]{:S(2)}, u32[]{:S(2)}) collective-permute-start(bf16[720,128]{1,0:T(8,128)(2,1)S(1)} %get-tuple-element.69), channel_id=1, source_target_pairs={{0,1},{1,0},{2,3},{3,2},{4,5},{5,4},{6,7},{7,6},{8,9},{9,8},{10,11... | collective-permute-start | bytes 552968 | tf_op jit(solution)/shard_map/ppermute | solution.py:559
  33.4 4.1 %collective-permute-start.13 = (bf16[720,128]{1,0:T(8,128)(2,1)S(1)}, bf16[720,128]{1,0:T(8,128)(2,1)S(1)}, u32[]{:S(2)}, u32[]{:S(2)}) collective-permute-start(bf16[720,128]{1,0:T(8,128)(2,1)S(1)} %get-tuple-element.78), channel_id=1, source_target_pairs={{0,1},{1,0},{2,3},{3,2},{4,5},{5,4},{6,7},{7,6},{8,9},{9,8},{10,11... | collective-permute-start | bytes 552968 | tf_op jit(solution)/shard_map/ppermute | solution.py:559
  33.8 3.3 %collective-permute-start.10 = (bf16[432,128]{1,0:T(8,128)(2,1)S(1)}, bf16[432,128]{1,0:T(8,128)(2,1)S(1)}, u32[]{:S(2)}, u32[]{:S(2)}) collective-permute-start(bf16[432,128]{1,0:T(8,128)(2,1)S(1)} %get-tuple-element.70), channel_id=1, source_target_pairs={{0,1},{1,0},{2,3},{3,2},{4,5},{5,4},{6,7},{7,6},{8,9},{9,8},{10,11... | collective-permute-start | bytes 331784 | tf_op jit(solution)/shard_map/ppermute | solution.py:559
  36.1 1.4 %collective-permute-start.14 = (bf16[432,128]{1,0:T(8,128)(2,1)S(1)}, bf16[432,128]{1,0:T(8,128)(2,1)S(1)}, u32[]{:S(2)}, u32[]{:S(2)}) collective-permute-start(bf16[432,128]{1,0:T(8,128)(2,1)S(1)} %get-tuple-element.79), channel_id=1, source_target_pairs={{0,1},{1,0},{2,3},{3,2},{4,5},{5,4},{6,7},{7,6},{8,9},{9,8},{10,11... | collective-permute-start | bytes 331784 | tf_op jit(solution)/shard_map/ppermute | solution.py:559
  37.6 14.4 %collective-permute-start.15 = (bf16[576,128]{1,0:T(8,128)(2,1)S(1)}, bf16[576,128]{1,0:T(8,128)(2,1)S(1)}, u32[]{:S(2)}, u32[]{:S(2)}) collective-permute-start(bf16[576,128]{1,0:T(8,128)(2,1)S(1)} %get-tuple-element.82), channel_id=1, source_target_pairs={{0,12},{1,15},{2,14},{3,13},{4,8},{5,11},{6,10},{7,9},{8,4},{9,7},... | collective-permute-start | bytes 442376 | tf_op jit(solution)/shard_map/ppermute | solution.py:550
  37.9 14.2 %collective-permute-start.16 = (bf16[576,128]{1,0:T(8,128)(2,1)S(1)}, bf16[576,128]{1,0:T(8,128)(2,1)S(1)}, u32[]{:S(2)}, u32[]{:S(2)}) collective-permute-start(bf16[576,128]{1,0:T(8,128)(2,1)S(1)} %get-tuple-element.83), channel_id=1, source_target_pairs={{0,8},{1,11},{2,10},{3,9},{4,12},{5,15},{6,14},{7,13},{8,0},{9,3},... | collective-permute-start | bytes 442376 | tf_op jit(solution)/shard_map/ppermute | solution.py:550
  38.0 14.0 %collective-permute-start.17 = (bf16[576,128]{1,0:T(8,128)(2,1)S(1)}, bf16[576,128]{1,0:T(8,128)(2,1)S(1)}, u32[]{:S(2)}, u32[]{:S(2)}) collective-permute-start(bf16[576,128]{1,0:T(8,128)(2,1)S(1)} %get-tuple-element.84), channel_id=1, source_target_pairs={{0,4},{1,7},{2,6},{3,5},{4,0},{5,3},{6,2},{7,1},{8,12},{9,15},{10,... | collective-permute-start | bytes 442376 | tf_op jit(solution)/shard_map/ppermute | solution.py:550
  42.0 10.0 %collective-permute-start.18 = (bf16[288,128]{1,0:T(8,128)(2,1)S(1)}, bf16[288,128]{1,0:T(8,128)(2,1)S(1)}, u32[]{:S(2)}, u32[]{:S(2)}) collective-permute-start(bf16[288,128]{1,0:T(8,128)(2,1)S(1)} %get-tuple-element.85), channel_id=1, source_target_pairs={{0,2},{2,0},{4,6},{6,4},{8,10},{10,8},{12,14},{14,12},{1,3},{3,1},... | collective-permute-start | bytes 221192 | tf_op jit(solution)/shard_map/ppermute | solution.py:555
  52.1 1.7 %collective-permute-start.19 = (bf16[864,128]{1,0:T(8,128)(2,1)S(1)}, bf16[864,128]{1,0:T(8,128)(2,1)S(1)}, u32[]{:S(2)}, u32[]{:S(2)}) collective-permute-start(bf16[864,128]{1,0:T(8,128)(2,1)S(1)} %shard_map.121), channel_id=1, source_target_pairs={{0,1},{1,0},{2,3},{3,2},{4,5},{5,4},{6,7},{7,6},{8,9},{9,8},{10,11... | collective-permute-start | bytes 663560 | tf_op jit(solution)/shard_map/ppermute | solution.py:559

commit v17 on v16

--- a/solution.py
+++ b/solution.py
@@ -498,26 +498,14 @@
     first_copy = pltpu.make_async_copy(first, grad_down.at[0, :, 0:step], first_sem)
     first_copy.start()
 
-    def wide_copy(i, slot):
-        return pltpu.make_async_copy(wide.at[slot], grad_down.at[0, :, chunk(i, step)], wide_sems.at[slot])
+    cuts = pieces_of(step, 256)
+
+    def wide_copy(i, slot, n):
+        there = pl.ds(pl.multiple_of(i * step, step) + cuts[n].start, cuts[n].stop - cuts[n].start)
+        return pltpu.make_async_copy(wide.at[slot, :, cuts[n]], grad_down.at[0, :, there], wide_sems.at[slot, n])
 
     def tall_copy(which, out, i, slot):
         return pltpu.make_async_copy(tall.at[which, slot], out.at[0, chunk(i, step), :], tall_sems.at[which, slot])
-
-    def down(i, carry):
-        slot = i % 2
-
-        @pl.when(i >= 3)
-        def _():
-            wide_copy(i - 2, slot).wait()
-
-        for cut in pieces_of(step, 256):
-            right = g[:, chunk(i, step)][:, cut]
-            wide[slot, :, cut] = dot(hidden_turned[...], right).astype(wide.dtype)
-        wide_copy(i, slot).start()
-        return carry
-
-    lax.fori_loop(1, count, down, 0)
 
     def inputs(i, carry):
         slot = i % 2
@@ -529,15 +517,32 @@
                 tall_copy(which, out, i - 2, slot).wait()
 
             for cut in pieces_of(lanes, 256):
-                for high in pieces_of(step, 512):
+                for high in pieces_of(step, 1024):
                     tall[which, slot, high, cut] = dot(turned[high, :], right[:, cut]).astype(tall.dtype)
             tall_copy(which, out, i, slot).start()
         return carry
 
     lax.fori_loop(0, count, inputs, 0)
+
+    def down(i, carry):
+        slot = i % 2
+
+        @pl.when(i >= 3)
+        def _():
+            for n in range(len(cuts)):
+                wide_copy(i - 2, slot, n).wait()
+
+        for n, cut in enumerate(cuts):
+            right = g[:, chunk(i, step)][:, cut]
+            wide[slot, :, cut] = dot(hidden_turned[...], right).astype(wide.dtype)
+            wide_copy(i, slot, n).start()
+        return carry
+
+    lax.fori_loop(1, count, down, 0)
     first_copy.wait()
     for i in range(max(1, count - 2), count):
-        wide_copy(i, i % 2).wait()
+        for n in range(len(cuts)):
+            wide_copy(i, i % 2, n).wait()
     for i in range(max(0, count - 2), count):
         tall_copy(0, grad_gate, i, i % 2).wait()
         tall_copy(1, grad_up, i, i % 2).wait()
@@ -685,7 +690,7 @@
             pltpu.VMEM((2, 2, cut, lanes), low),
             pltpu.VMEM((2, lanes, cut), low),
             pltpu.SemaphoreType.DMA((2, 2)),
-            pltpu.SemaphoreType.DMA((2,)),
+            pltpu.SemaphoreType.DMA((2, -(-cut // 256))),
             pltpu.SemaphoreType.DMA,
         ],
         flops=6 * half_flops,

time: 55.3 us -> 55.9 us (1.011)
  Pallas kernels: 24.6 us -> 25.4 us
  starting transfers between devices: 19.4 us -> 18.8 us
    pallas_call x14, Pallas kernels: 24.6 us -> 25.4 us  [call(): pl.pallas_call(kernel, out_shape=tuple(out_shape), in_specs=[pl.BlockSpec...]
  transfers between devices with their start and end apart: 20 -> 20, of which waited for: 9 -> 9; matrix products, arithmetic and copies ran while one was open for 0% -> 0% of each run, Pallas kernels for 38% -> 39%
where the time goes in v17:
time: 55.9 us; the launch traced here: 55.8 us
  Pallas kernels  25.4 us (45%)
  starting transfers between devices  18.8 us (34%)
  waiting for transfers between devices  10.7 us (19%)
  between operations  0.84 us (2%)
    pallas_call x14, Pallas kernels, call(): pl.pallas_call(kernel, out_shape=tuple(out_shape), in_specs=[pl.BlockSpec...  25.4 us
    ppermute x7, starting transfers between devices, exchange(): arrived.append(lax.ppermute(block, ('expert', 'ffn'), pairs))  12.3 us
    ppermute x7, waiting for transfers between devices, exchange(): arrived.append(lax.ppermute(block, ('expert', 'ffn'), pairs))  5.91 us
    ppermute x11, starting transfers between devices, swap(): return lax.ppermute(value, 'ffn', [(0, 1), (1, 0)])  3.37 us
    ppermute x2, starting transfers between devices, exchange_near(): return lax.ppermute(block, 'expert', [(i, i ^ 1) for i in range(devices)])  3.19 us
    ppermute x11, waiting for transfers between devices, swap(): return lax.ppermute(value, 'ffn', [(0, 1), (1, 0)])  2.86 us
    ppermute x2, waiting for transfers between devices, exchange_near(): return lax.ppermute(block, 'expert', [(i, i ^ 1) for i in range(devices)])  1.89 us
  transfers between devices with their start and end apart: 20, of which 9 were waited for; matrix products, arithmetic and copies ran while one was open for 0% of the time, Pallas kernels for 39%

profile of v17, /device:TPU:0, one launch (start us, length us, event | category | flops | bytes accessed | tf_op | source)
XLA Modules:
  0.0 55.8 jit_solution(177044167484346519)
XLA Ops:
  0.7 2.1 %shard_map.110 = (bf16[432,128]{1,0:T(8,128)(2,1)S(1)}, bf16[432,128]{1,0:T(8,128)(2,1)S(1)}, bf16[288,128]{1,0:T(8,128)(2,1)S(1)}, bf16[288,128]{1,0:T(8,128)(2...) custom-call(s32[8,128]{1,0:T(8,128)} %bitcast.8, ...), custom_call_target="tpu_custom_call" | custom-call | bytes 1048576 | tf_op jit(solution)/shard_map/pallas_call | solution.py:132
  2.7 0.5 collective-permute-start
  3.3 1.1 %collective-permute-done.swapped = bf16[864,128]{1,0:T(8,128)(2,1)S(1)} collective-permute-done((bf16[864,128]{1,0:T(8,128)(2,1)S(1)}, bf16[864,128]{1,0:T(8,128)(2,1)S(1)}, u32[]{:S(2)}, u32[]{:S(2)}) %collective-permute-start) | collective-permute-done | bytes 221216 | tf_op jit(solution)/shard_map/ppermute | solution.py:564
  4.4 5.0 %collective-permute-start.1 = (bf16[576,128]{1,0:T(8,128)(2,1)S(1)}, bf16[576,128]{1,0:T(8,128)(2,1)S(1)}, u32[]{:S(2)}, u32[]{:S(2)}) collective-permute-start(bf16[576,128]{1,0:T(8,128)(2,1)S(1)} %get-tuple-element.57), channel_id=1, source_target_pairs={{0,12},{1,15},{2,14},{3,13},{4,8},{5,11},{6,10},{7,9},{8,4},{9,7},... | collective-permute-start | bytes 442376 | tf_op jit(solution)/shard_map/ppermute | solution.py:555
  9.5 0.6 %collective-permute-start.2 = (bf16[304,128]{1,0:T(8,128)(2,1)S(1)}, bf16[304,128]{1,0:T(8,128)(2,1)S(1)}, u32[]{:S(2)}, u32[]{:S(2)}) collective-permute-start(bf16[304,128]{1,0:T(8,128)(2,1)S(1)} %get-tuple-element.58), channel_id=1, source_target_pairs={{0,8},{1,11},{2,10},{3,9},{4,12},{5,15},{6,14},{7,13},{8,0},{9,3},... | collective-permute-start | bytes 233480 | tf_op jit(solution)/shard_map/ppermute | solution.py:555
  10.1 1.6 %collective-permute-start.4 = (bf16[288,128]{1,0:T(8,128)(2,1)S(1)}, bf16[288,128]{1,0:T(8,128)(2,1)S(1)}, u32[]{:S(2)}, u32[]{:S(2)}) collective-permute-start(bf16[288,128]{1,0:T(8,128)(2,1)S(1)} %get-tuple-element.60), channel_id=1, source_target_pairs={{0,2},{2,0},{4,6},{6,4},{8,10},{10,8},{12,14},{14,12},{1,3},{3,1},... | collective-permute-start | bytes 221192 | tf_op jit(solution)/shard_map/ppermute | solution.py:560
  11.7 2.1 %collective-permute-start.11 = (bf16[304,128]{1,0:T(8,128)(2,1)S(1)}, bf16[304,128]{1,0:T(8,128)(2,1)S(1)}, u32[]{:S(2)}, u32[]{:S(2)}) collective-permute-start(bf16[304,128]{1,0:T(8,128)(2,1)S(1)} %get-tuple-element.71), channel_id=1, source_target_pairs={{0,8},{1,11},{2,10},{3,9},{4,12},{5,15},{6,14},{7,13},{8,0},{9,3},... | collective-permute-start | bytes 233480 | tf_op jit(solution)/shard_map/ppermute | solution.py:555
  13.9 1.9 %collective-permute-done.4.refs_3_ = bf16[288,128]{1,0:T(8,128)(2,1)S(1)} collective-permute-done((bf16[288,128]{1,0:T(8,128)(2,1)S(1)}, bf16[288,128]{1,0:T(8,128)(2,1)S(1)}, u32[]{:S(2)}, u32[]{:S(2)}) %collective-permute-start.4) | collective-permute-done | bytes 73760 | tf_op jit(solution)/shard_map/ppermute | solution.py:560
  15.8 5.9 %collective-permute-done.2.refs_1_ = bf16[304,128]{1,0:T(8,128)(2,1)S(1)} collective-permute-done((bf16[304,128]{1,0:T(8,128)(2,1)S(1)}, bf16[304,128]{1,0:T(8,128)(2,1)S(1)}, u32[]{:S(2)}, u32[]{:S(2)}) %collective-permute-start.2) | collective-permute-done | bytes 77856 | tf_op jit(solution)/shard_map/ppermute | solution.py:555
  21.8 0.5 collective-permute-start.6
  22.3 0.4 collective-permute-start.8
  22.8 0.2 collective-permute-done.5.refs_4_
  23.2 0.4 collective-permute-done.7.refs_6_
  23.5 0.2 collective-permute-done.8.refs_7_
  23.7 2.7 %shard_map.113 = (bf16[72,4096]{1,0:T(8,128)(2,1)S(1)}, bf16[72,768]{1,0:T(8,128)(2,1)S(1)}, bf16[72,768]{1,0:T(8,128)(2,1)S(1)}, bf16[72,768]{1,0:T(8,128)(2,1)S(1)}) custom-call(bf16[288,128]{1,0:T(8,128)(2,1)S(1)} %get-tuple-element.62.refs_0_, bf16[288,128]{1,0:T(8,128)(2,1)S(1)} %get-tuple-element.63.refs_1_, ...), custom_call_target="tpu_custom_call" | custom-call | tf_op jit(solution)/shard_map/pallas_call | solution.py:132
  26.5 0.4 collective-permute-start.12
  26.9 1.4 %shard_map.114 = (f32[720,128]{1,0:T(8,128)S(1)}, f32[432,128]{1,0:T(8,128)S(1)}, bf16[432,128]{1,0:T(8,128)(2,1)S(1)}, bf16[720,128]{1,0:T(8,128)(2,1)S(1)}) custom-call(bf16[72,768]{1,0:T(8,128)(2,1)S(1)} %get-tuple-element.66.hidden.refs_5_, bf16[1,768,4096]{2,1,0:T(8,128)(2,1)S(1)} %bitcast.7), custom_call_target="tpu_custom_call" | custom-call | flops 452984832 | tf_op jit(solution)/shard_map/pallas_call | solution.py:132
  28.3 0.2 collective-permute-start.9
  28.5 4.9 %shard_map.116 = (bf16[72,4096]{1,0:T(8,128)(2,1)S(1)}, bf16[72,768]{1,0:T(8,128)(2,1)S(1)}, bf16[72,768]{1,0:T(8,128)(2,1)S(1)}, f32[432,128]{1,0:T(8,128)S(1)}, bf16[720,128]{1,0:T(8,128)(2,1)S(1)}) custom-call(bf16[1152,128]{1,0:T(8,128)(2,1)S(1)} %shard_map.115.g_sent, bf16[1152,128]{1,0:T(8,128)(2,1)S(1)} %collective-permute-done.12.g_swapped, ...), custom_call_target="tpu_custom_call" | custom-call | flops 905969664 | tf_op jit(solution)/shard_map/pallas_call | solution.py:132
  33.4 0.4 collective-permute-start.13
  34.0 2.1 %shard_map.117 = (f32[720,128]{1,0:T(8,128)S(1)}, bf16[432,128]{1,0:T(8,128)(2,1)S(1)}) custom-call(bf16[72,768]{1,0:T(8,128)(2,1)S(1)} %get-tuple-element.74.pre_gate, bf16[72,768]{1,0:T(8,128)(2,1)S(1)} %get-tuple-element.75.pre_up, bf16[1,4096,768]{2,1,0:T(8,128)(2,1)S(1)} %bitcast.3, bf16[1,4096,768]{2,1,0:T(8,128)(2,1)S(1)} %bitcast.5), custom_call_target="tpu_custom_call" | custom-call | flops 452984832 | tf_op jit(solution)/shard_map/pallas_call | solution.py:132
  36.1 0.4 collective-permute-start.14
  36.5 0.6 %shard_map.118 = (bf16[768,72]{1,0:T(8,128)(2,1)S(1)}, bf16[768,1024]{1,0:T(8,128)(2,1)S(1)}) custom-call(bf16[72,768]{1,0:T(8,128)(2,1)S(1)} %get-tuple-element.66.hidden.refs_5_, bf16[72,4096]{1,0:T(8,128)(2,1)S(1)} %get-tuple-element.80.g), custom_call_target="tpu_custom_call" | custom-call | flops 113246208 | tf_op jit(solution)/shard_map/pallas_call | solution.py:132
  37.2 0.3 collective-permute-done.14.refs_7_
  37.6 0.3 collective-permute-start.15
  37.9 0.2 collective-permute-start.16
  38.0 4.0 %collective-permute-start.17 = (bf16[576,128]{1,0:T(8,128)(2,1)S(1)}, bf16[576,128]{1,0:T(8,128)(2,1)S(1)}, u32[]{:S(2)}, u32[]{:S(2)}) collective-permute-start(bf16[576,128]{1,0:T(8,128)(2,1)S(1)} %get-tuple-element.84), channel_id=1, source_target_pairs={{0,4},{1,7},{2,6},{3,5},{4,0},{5,3},{6,2},{7,1},{8,12},{9,15},{10,... | collective-permute-start | bytes 442376 | tf_op jit(solution)/shard_map/ppermute | solution.py:555
  42.0 1.6 %collective-permute-start.18 = (bf16[288,128]{1,0:T(8,128)(2,1)S(1)}, bf16[288,128]{1,0:T(8,128)(2,1)S(1)}, u32[]{:S(2)}, u32[]{:S(2)}) collective-permute-start(bf16[288,128]{1,0:T(8,128)(2,1)S(1)} %get-tuple-element.85), channel_id=1, source_target_pairs={{0,2},{2,0},{4,6},{6,4},{8,10},{10,8},{12,14},{14,12},{1,3},{3,1},... | collective-permute-start | bytes 221192 | tf_op jit(solution)/shard_map/ppermute | solution.py:560
  43.6 9.2 %shard_map.120 = (bf16[1,4096,768]{2,1,0:T(8,128)(2,1)}, bf16[1,4096,768]{2,1,0:T(8,128)(2,1)}, bf16[1,768,4096]{2,1,0:T(8,128)(2,1)}, f32[8,128]{1,0:T(8,128)S(1)}) custom-call(bf16[72,4096]{1,0:T(8,128)(2,1)S(1)} %get-tuple-element.86.x, bf16[72,4096]{1,0:T(8,128)(2,1)S(1)} %get-tuple-element.80.g, bf16[768,72]{1,0:T(8,128)(2,1)S(1)} %get-tuple-element.87.hidden_turned, ...), custom_call_target="tpu_custom_call" | custom-call | flops 1358954496 | bytes 18874368 | tf_op jit(solution)/shard_map/pallas_call | solution.py:132
  53.0 0.9 %shard_map.122 = (f32[128,2048]{1,0:T(8,128)S(1)}, f32[128,2048]{1,0:T(8,128)S(1)}) custom-call(bf16[72,128]{1,0:T(8,128)(2,1)S(1)} %get-tuple-element.89.place, f32[72,128]{1,0:T(8,128)S(1)} %get-tuple-element.90.mix, bf16[576,128]{1,0:T(8,128)(2,1)S(1)} %collective-permute-done.15.refs_0_, bf16[576,128]{1,0:T(8,128)(2,1)S(1)} %collective-permute-done.16.refs_1_, ...), custom_call_target="tpu_custom_call" | custom-call | flops 75497472 | tf_op jit(solution)/shard_map/pallas_call | solution.py:132
  53.8 0.5 collective-permute-done.19.shared
  54.4 1.4 %shard_map.123 = (bf16[128,2048]{1,0:T(8,128)(2,1)}, bf16[128,2048]{1,0:T(8,128)(2,1)}) custom-call(bf16[27,128]{1,0:T(8,128)(2,1)S(1)} %get-tuple-element.52.place, f32[27,128]{1,0:T(8,128)S(1)} %get-tuple-element.53.mix, bf16[864,128]{1,0:T(8,128)(2,1)S(1)} %collective-permute-done.19.shared, f32[128,2048]{1,0:T(8,128)S(1)} %get-tuple-element.92.out_sum, ...), custom_call_target="tpu_custom_call" | custom-call | bytes 2097152 | tf_op jit(solution)/shard_map/pallas_call | solution.py:132
  (37 shorter events, 0.8 us)
Async XLA Ops:
  0.6 23.1 %slice-start = ((s8[6291456]{0:T(1024)(128)(4,1)}), s8[4194304]{0:T(1024)(128)(4,1)S(1)}, s32[]{:S(2)}) async-start(s8[6291456]{0:T(1024)(128)(4,1)} %bitcast.2), calls=%async_computation | async-start | bytes 8388608
  0.6 23.0 %slice-start.2 = ((s8[6291456]{0:T(1024)(128)(4,1)}), s8[4194304]{0:T(1024)(128)(4,1)S(1)}, s32[]{:S(2)}) async-start(s8[6291456]{0:T(1024)(128)(4,1)} %bitcast.4), calls=%async_computation.2 | async-start | bytes 8388608
  2.7 1.6 %collective-permute-start = (bf16[864,128]{1,0:T(8,128)(2,1)S(1)}, bf16[864,128]{1,0:T(8,128)(2,1)S(1)}, u32[]{:S(2)}, u32[]{:S(2)}) collective-permute-start(bf16[864,128]{1,0:T(8,128)(2,1)S(1)} %get-tuple-element.56), channel_id=1, source_target_pairs={{0,1},{1,0},{2,3},{3,2},{4,5},{5,4},{6,7},{7,6},{8,9},{9,8},{10,11... | collective-permute-start | bytes 663560 | tf_op jit(solution)/shard_map/ppermute | solution.py:564
  4.4 19.3 %slice-start.1 = ((s8[6291456]{0:T(1024)(128)(4,1)}), s8[2097152]{0:T(1024)(128)(4,1)S(1)}, s32[]{:S(2)}) async-start(s8[6291456]{0:T(1024)(128)(4,1)} %bitcast.2), calls=%async_computation.1 | async-start | bytes 4194304
  4.4 19.3 %slice-start.3 = ((s8[6291456]{0:T(1024)(128)(4,1)}), s8[2097152]{0:T(1024)(128)(4,1)S(1)}, s32[]{:S(2)}) async-start(s8[6291456]{0:T(1024)(128)(4,1)} %bitcast.4), calls=%async_computation.3 | async-start | bytes 4194304
  4.4 17.2 %collective-permute-start.1 = (bf16[576,128]{1,0:T(8,128)(2,1)S(1)}, bf16[576,128]{1,0:T(8,128)(2,1)S(1)}, u32[]{:S(2)}, u32[]{:S(2)}) collective-permute-start(bf16[576,128]{1,0:T(8,128)(2,1)S(1)} %get-tuple-element.57), channel_id=1, source_target_pairs={{0,12},{1,15},{2,14},{3,13},{4,8},{5,11},{6,10},{7,9},{8,4},{9,7},... | collective-permute-start | bytes 442376 | tf_op jit(solution)/shard_map/ppermute | solution.py:555
  9.4 12.2 %collective-permute-start.3 = (bf16[576,128]{1,0:T(8,128)(2,1)S(1)}, bf16[576,128]{1,0:T(8,128)(2,1)S(1)}, u32[]{:S(2)}, u32[]{:S(2)}) collective-permute-start(bf16[576,128]{1,0:T(8,128)(2,1)S(1)} %get-tuple-element.59), channel_id=1, source_target_pairs={{0,4},{1,7},{2,6},{3,5},{4,0},{5,3},{6,2},{7,1},{8,12},{9,15},{10,... | collective-permute-start | bytes 442376 | tf_op jit(solution)/shard_map/ppermute | solution.py:555
  9.5 12.2 %collective-permute-start.2 = (bf16[304,128]{1,0:T(8,128)(2,1)S(1)}, bf16[304,128]{1,0:T(8,128)(2,1)S(1)}, u32[]{:S(2)}, u32[]{:S(2)}) collective-permute-start(bf16[304,128]{1,0:T(8,128)(2,1)S(1)} %get-tuple-element.58), channel_id=1, source_target_pairs={{0,8},{1,11},{2,10},{3,9},{4,12},{5,15},{6,14},{7,13},{8,0},{9,3},... | collective-permute-start | bytes 233480 | tf_op jit(solution)/shard_map/ppermute | solution.py:555
  10.1 5.7 %collective-permute-start.4 = (bf16[288,128]{1,0:T(8,128)(2,1)S(1)}, bf16[288,128]{1,0:T(8,128)(2,1)S(1)}, u32[]{:S(2)}, u32[]{:S(2)}) collective-permute-start(bf16[288,128]{1,0:T(8,128)(2,1)S(1)} %get-tuple-element.60), channel_id=1, source_target_pairs={{0,2},{2,0},{4,6},{6,4},{8,10},{10,8},{12,14},{14,12},{1,3},{3,1},... | collective-permute-start | bytes 221192 | tf_op jit(solution)/shard_map/ppermute | solution.py:560
  11.7 14.7 %collective-permute-start.11 = (bf16[304,128]{1,0:T(8,128)(2,1)S(1)}, bf16[304,128]{1,0:T(8,128)(2,1)S(1)}, u32[]{:S(2)}, u32[]{:S(2)}) collective-permute-start(bf16[304,128]{1,0:T(8,128)(2,1)S(1)} %get-tuple-element.71), channel_id=1, source_target_pairs={{0,8},{1,11},{2,10},{3,9},{4,12},{5,15},{6,14},{7,13},{8,0},{9,3},... | collective-permute-start | bytes 233480 | tf_op jit(solution)/shard_map/ppermute | solution.py:555
  21.7 1.3 %collective-permute-start.5 = (bf16[288,128]{1,0:T(8,128)(2,1)S(1)}, bf16[288,128]{1,0:T(8,128)(2,1)S(1)}, u32[]{:S(2)}, u32[]{:S(2)}) collective-permute-start(bf16[288,128]{1,0:T(8,128)(2,1)S(1)} %get-tuple-element.62.refs_0_), channel_id=1, source_target_pairs={{0,1},{1,0},{2,3},{3,2},{4,5},{5,4},{6,7},{7,6},{8,9},{9,8},{10,11... | collective-permute-start | bytes 221192 | tf_op jit(solution)/shard_map/ppermute | solution.py:564
  21.8 1.4 %collective-permute-start.6 = (bf16[288,128]{1,0:T(8,128)(2,1)S(1)}, bf16[288,128]{1,0:T(8,128)(2,1)S(1)}, u32[]{:S(2)}, u32[]{:S(2)}) collective-permute-start(bf16[288,128]{1,0:T(8,128)(2,1)S(1)} %get-tuple-element.63.refs_1_), channel_id=1, source_target_pairs={{0,1},{1,0},{2,3},{3,2},{4,5},{5,4},{6,7},{7,6},{8,9},{9,8},{10,11... | collective-permute-start | bytes 221192 | tf_op jit(solution)/shard_map/ppermute | solution.py:564
  22.3 1.3 %collective-permute-start.7 = (bf16[288,128]{1,0:T(8,128)(2,1)S(1)}, bf16[288,128]{1,0:T(8,128)(2,1)S(1)}, u32[]{:S(2)}, u32[]{:S(2)}) collective-permute-start(bf16[288,128]{1,0:T(8,128)(2,1)S(1)} %get-tuple-element.64.refs_2_), channel_id=1, source_target_pairs={{0,1},{1,0},{2,3},{3,2},{4,5},{5,4},{6,7},{7,6},{8,9},{9,8},{10,11... | collective-permute-start | bytes 221192 | tf_op jit(solution)/shard_map/ppermute | solution.py:564
  22.3 4.6 %slice-start.4 = ((s8[6291456]{0:T(1024)(128)(4,1)}), s8[4194304]{0:T(1024)(128)(4,1)S(1)}, s32[]{:S(2)}) async-start(s8[6291456]{0:T(1024)(128)(4,1)} %bitcast.6), calls=%async_computation.4 | async-start | bytes 8388608
  22.3 4.6 %slice-start.5 = ((s8[6291456]{0:T(1024)(128)(4,1)}), s8[2097152]{0:T(1024)(128)(4,1)S(1)}, s32[]{:S(2)}) async-start(s8[6291456]{0:T(1024)(128)(4,1)} %bitcast.6), calls=%async_computation.5 | async-start | bytes 4194304
  22.3 1.3 %collective-permute-start.8 = (bf16[288,128]{1,0:T(8,128)(2,1)S(1)}, bf16[288,128]{1,0:T(8,128)(2,1)S(1)}, u32[]{:S(2)}, u32[]{:S(2)}) collective-permute-start(bf16[288,128]{1,0:T(8,128)(2,1)S(1)} %get-tuple-element.65.refs_3_), channel_id=1, source_target_pairs={{0,1},{1,0},{2,3},{3,2},{4,5},{5,4},{6,7},{7,6},{8,9},{9,8},{10,11... | collective-permute-start | bytes 221192 | tf_op jit(solution)/shard_map/ppermute | solution.py:564
  26.5 2.0 %collective-permute-start.12 = (bf16[1152,128]{1,0:T(8,128)(2,1)S(1)}, bf16[1152,128]{1,0:T(8,128)(2,1)S(1)}, u32[]{:S(2)}, u32[]{:S(2)}) collective-permute-start(bf16[1152,128]{1,0:T(8,128)(2,1)S(1)} %shard_map.115.g_sent), channel_id=1, source_target_pairs={{0,1},{1,0},{2,3},{3,2},{4,5},{5,4},{6,7},{7,6},{8,9},{9,8},{10,11... | collective-permute-start | bytes 884744 | tf_op jit(solution)/shard_map/ppermute | solution.py:564
  28.3 8.9 %collective-permute-start.9 = (bf16[720,128]{1,0:T(8,128)(2,1)S(1)}, bf16[720,128]{1,0:T(8,128)(2,1)S(1)}, u32[]{:S(2)}, u32[]{:S(2)}) collective-permute-start(bf16[720,128]{1,0:T(8,128)(2,1)S(1)} %get-tuple-element.69), channel_id=1, source_target_pairs={{0,1},{1,0},{2,3},{3,2},{4,5},{5,4},{6,7},{7,6},{8,9},{9,8},{10,11... | collective-permute-start | bytes 552968 | tf_op jit(solution)/shard_map/ppermute | solution.py:564
  33.4 4.1 %collective-permute-start.13 = (bf16[720,128]{1,0:T(8,128)(2,1)S(1)}, bf16[720,128]{1,0:T(8,128)(2,1)S(1)}, u32[]{:S(2)}, u32[]{:S(2)}) collective-permute-start(bf16[720,128]{1,0:T(8,128)(2,1)S(1)} %get-tuple-element.78), channel_id=1, source_target_pairs={{0,1},{1,0},{2,3},{3,2},{4,5},{5,4},{6,7},{7,6},{8,9},{9,8},{10,11... | collective-permute-start | bytes 552968 | tf_op jit(solution)/shard_map/ppermute | solution.py:564
  33.8 3.3 %collective-permute-start.10 = (bf16[432,128]{1,0:T(8,128)(2,1)S(1)}, bf16[432,128]{1,0:T(8,128)(2,1)S(1)}, u32[]{:S(2)}, u32[]{:S(2)}) collective-permute-start(bf16[432,128]{1,0:T(8,128)(2,1)S(1)} %get-tuple-element.70), channel_id=1, source_target_pairs={{0,1},{1,0},{2,3},{3,2},{4,5},{5,4},{6,7},{7,6},{8,9},{9,8},{10,11... | collective-permute-start | bytes 331784 | tf_op jit(solution)/shard_map/ppermute | solution.py:564
  36.1 1.4 %collective-permute-start.14 = (bf16[432,128]{1,0:T(8,128)(2,1)S(1)}, bf16[432,128]{1,0:T(8,128)(2,1)S(1)}, u32[]{:S(2)}, u32[]{:S(2)}) collective-permute-start(bf16[432,128]{1,0:T(8,128)(2,1)S(1)} %get-tuple-element.79), channel_id=1, source_target_pairs={{0,1},{1,0},{2,3},{3,2},{4,5},{5,4},{6,7},{7,6},{8,9},{9,8},{10,11... | collective-permute-start | bytes 331784 | tf_op jit(solution)/shard_map/ppermute | solution.py:564
  37.6 15.2 %collective-permute-start.15 = (bf16[576,128]{1,0:T(8,128)(2,1)S(1)}, bf16[576,128]{1,0:T(8,128)(2,1)S(1)}, u32[]{:S(2)}, u32[]{:S(2)}) collective-permute-start(bf16[576,128]{1,0:T(8,128)(2,1)S(1)} %get-tuple-element.82), channel_id=1, source_target_pairs={{0,12},{1,15},{2,14},{3,13},{4,8},{5,11},{6,10},{7,9},{8,4},{9,7},... | collective-permute-start | bytes 442376 | tf_op jit(solution)/shard_map/ppermute | solution.py:555
  37.9 14.9 %collective-permute-start.16 = (bf16[576,128]{1,0:T(8,128)(2,1)S(1)}, bf16[576,128]{1,0:T(8,128)(2,1)S(1)}, u32[]{:S(2)}, u32[]{:S(2)}) collective-permute-start(bf16[576,128]{1,0:T(8,128)(2,1)S(1)} %get-tuple-element.83), channel_id=1, source_target_pairs={{0,8},{1,11},{2,10},{3,9},{4,12},{5,15},{6,14},{7,13},{8,0},{9,3},... | collective-permute-start | bytes 442376 | tf_op jit(solution)/shard_map/ppermute | solution.py:555
  38.0 14.8 %collective-permute-start.17 = (bf16[576,128]{1,0:T(8,128)(2,1)S(1)}, bf16[576,128]{1,0:T(8,128)(2,1)S(1)}, u32[]{:S(2)}, u32[]{:S(2)}) collective-permute-start(bf16[576,128]{1,0:T(8,128)(2,1)S(1)} %get-tuple-element.84), channel_id=1, source_target_pairs={{0,4},{1,7},{2,6},{3,5},{4,0},{5,3},{6,2},{7,1},{8,12},{9,15},{10,... | collective-permute-start | bytes 442376 | tf_op jit(solution)/shard_map/ppermute | solution.py:555
  42.0 10.7 %collective-permute-start.18 = (bf16[288,128]{1,0:T(8,128)(2,1)S(1)}, bf16[288,128]{1,0:T(8,128)(2,1)S(1)}, u32[]{:S(2)}, u32[]{:S(2)}) collective-permute-start(bf16[288,128]{1,0:T(8,128)(2,1)S(1)} %get-tuple-element.85), channel_id=1, source_target_pairs={{0,2},{2,0},{4,6},{6,4},{8,10},{10,8},{12,14},{14,12},{1,3},{3,1},... | collective-permute-start | bytes 221192 | tf_op jit(solution)/shard_map/ppermute | solution.py:560
  52.8 1.5 %collective-permute-start.19 = (bf16[864,128]{1,0:T(8,128)(2,1)S(1)}, bf16[864,128]{1,0:T(8,128)(2,1)S(1)}, u32[]{:S(2)}, u32[]{:S(2)}) collective-permute-start(bf16[864,128]{1,0:T(8,128)(2,1)S(1)} %shard_map.121), channel_id=1, source_target_pairs={{0,1},{1,0},{2,3},{3,2},{4,5},{5,4},{6,7},{7,6},{8,9},{9,8},{10,11... | collective-permute-start | bytes 663560 | tf_op jit(solution)/shard_map/ppermute | solution.py:564

commit v18 on v17

--- a/solution.py
+++ b/solution.py
@@ -517,7 +517,7 @@
                 tall_copy(which, out, i - 2, slot).wait()
 
             for cut in pieces_of(lanes, 256):
-                for high in pieces_of(step, 1024):
+                for high in pieces_of(step, 512):
                     tall[which, slot, high, cut] = dot(turned[high, :], right[:, cut]).astype(tall.dtype)
             tall_copy(which, out, i, slot).start()
         return carry

time: 55.9 us -> 55.3 us (0.989)
  Pallas kernels: 25.4 us -> 24.4 us
  starting transfers between devices: 18.8 us -> 19.5 us
    pallas_call x14, Pallas kernels: 25.4 us -> 24.4 us  [call(): pl.pallas_call(kernel, out_shape=tuple(out_shape), in_specs=[pl.BlockSpec...]
    ppermute x11, starting transfers between devices: 3.37 us -> 4.03 us  [swap(): return lax.ppermute(value, 'ffn', [(0, 1), (1, 0)])]
  transfers between devices with their start and end apart: 20 -> 20, of which waited for: 9 -> 10; matrix products, arithmetic and copies ran while one was open for 0% -> 0% of each run, Pallas kernels for 39% -> 38%
where the time goes in v18:
time: 55.3 us; the launch traced here: 55.2 us
  Pallas kernels  24.4 us (44%)
  starting transfers between devices  19.5 us (35%)
  waiting for transfers between devices  10.5 us (19%)
  between operations  0.82 us (1%)
    pallas_call x14, Pallas kernels, call(): pl.pallas_call(kernel, out_shape=tuple(out_shape), in_specs=[pl.BlockSpec...  24.4 us
    ppermute x7, starting transfers between devices, exchange(): arrived.append(lax.ppermute(block, ('expert', 'ffn'), pairs))  12.3 us
    ppermute x7, waiting for transfers between devices, exchange(): arrived.append(lax.ppermute(block, ('expert', 'ffn'), pairs))  6.04 us
    ppermute x11, starting transfers between devices, swap(): return lax.ppermute(value, 'ffn', [(0, 1), (1, 0)])  4.03 us
    ppermute x2, starting transfers between devices, exchange_near(): return lax.ppermute(block, 'expert', [(i, i ^ 1) for i in range(devices)])  3.19 us
    ppermute x11, waiting for transfers between devices, swap(): return lax.ppermute(value, 'ffn', [(0, 1), (1, 0)])  2.53 us
    ppermute x2, waiting for transfers between devices, exchange_near(): return lax.ppermute(block, 'expert', [(i, i ^ 1) for i in range(devices)])  1.89 us
  transfers between devices with their start and end apart: 20, of which 10 were waited for; matrix products, arithmetic and copies ran while one was open for 0% of the time, Pallas kernels for 38%

profile of v18, /device:TPU:0, one launch (start us, length us, event | category | flops | bytes accessed | tf_op | source)
XLA Modules:
  0.0 55.2 jit_solution(10229417134583769948)
XLA Ops:
  0.7 2.1 %shard_map.110 = (bf16[432,128]{1,0:T(8,128)(2,1)S(1)}, bf16[432,128]{1,0:T(8,128)(2,1)S(1)}, bf16[288,128]{1,0:T(8,128)(2,1)S(1)}, bf16[288,128]{1,0:T(8,128)(2...) custom-call(s32[8,128]{1,0:T(8,128)} %bitcast.8, ...), custom_call_target="tpu_custom_call" | custom-call | bytes 1048576 | tf_op jit(solution)/shard_map/pallas_call | solution.py:132
  2.7 0.5 collective-permute-start
  3.3 1.1 %collective-permute-done.swapped = bf16[864,128]{1,0:T(8,128)(2,1)S(1)} collective-permute-done((bf16[864,128]{1,0:T(8,128)(2,1)S(1)}, bf16[864,128]{1,0:T(8,128)(2,1)S(1)}, u32[]{:S(2)}, u32[]{:S(2)}) %collective-permute-start) | collective-permute-done | bytes 221216 | tf_op jit(solution)/shard_map/ppermute | solution.py:564
  4.4 5.0 %collective-permute-start.1 = (bf16[576,128]{1,0:T(8,128)(2,1)S(1)}, bf16[576,128]{1,0:T(8,128)(2,1)S(1)}, u32[]{:S(2)}, u32[]{:S(2)}) collective-permute-start(bf16[576,128]{1,0:T(8,128)(2,1)S(1)} %get-tuple-element.57), channel_id=1, source_target_pairs={{0,12},{1,15},{2,14},{3,13},{4,8},{5,11},{6,10},{7,9},{8,4},{9,7},... | collective-permute-start | bytes 442376 | tf_op jit(solution)/shard_map/ppermute | solution.py:555
  9.5 0.6 %collective-permute-start.2 = (bf16[304,128]{1,0:T(8,128)(2,1)S(1)}, bf16[304,128]{1,0:T(8,128)(2,1)S(1)}, u32[]{:S(2)}, u32[]{:S(2)}) collective-permute-start(bf16[304,128]{1,0:T(8,128)(2,1)S(1)} %get-tuple-element.58), channel_id=1, source_target_pairs={{0,8},{1,11},{2,10},{3,9},{4,12},{5,15},{6,14},{7,13},{8,0},{9,3},... | collective-permute-start | bytes 233480 | tf_op jit(solution)/shard_map/ppermute | solution.py:555
  10.1 1.6 %collective-permute-start.4 = (bf16[288,128]{1,0:T(8,128)(2,1)S(1)}, bf16[288,128]{1,0:T(8,128)(2,1)S(1)}, u32[]{:S(2)}, u32[]{:S(2)}) collective-permute-start(bf16[288,128]{1,0:T(8,128)(2,1)S(1)} %get-tuple-element.60), channel_id=1, source_target_pairs={{0,2},{2,0},{4,6},{6,4},{8,10},{10,8},{12,14},{14,12},{1,3},{3,1},... | collective-permute-start | bytes 221192 | tf_op jit(solution)/shard_map/ppermute | solution.py:560
  11.7 2.1 %collective-permute-start.11 = (bf16[304,128]{1,0:T(8,128)(2,1)S(1)}, bf16[304,128]{1,0:T(8,128)(2,1)S(1)}, u32[]{:S(2)}, u32[]{:S(2)}) collective-permute-start(bf16[304,128]{1,0:T(8,128)(2,1)S(1)} %get-tuple-element.71), channel_id=1, source_target_pairs={{0,8},{1,11},{2,10},{3,9},{4,12},{5,15},{6,14},{7,13},{8,0},{9,3},... | collective-permute-start | bytes 233480 | tf_op jit(solution)/shard_map/ppermute | solution.py:555
  13.9 1.9 %collective-permute-done.4.refs_3_ = bf16[288,128]{1,0:T(8,128)(2,1)S(1)} collective-permute-done((bf16[288,128]{1,0:T(8,128)(2,1)S(1)}, bf16[288,128]{1,0:T(8,128)(2,1)S(1)}, u32[]{:S(2)}, u32[]{:S(2)}) %collective-permute-start.4) | collective-permute-done | bytes 73760 | tf_op jit(solution)/shard_map/ppermute | solution.py:560
  15.8 5.9 %collective-permute-done.2.refs_1_ = bf16[304,128]{1,0:T(8,128)(2,1)S(1)} collective-permute-done((bf16[304,128]{1,0:T(8,128)(2,1)S(1)}, bf16[304,128]{1,0:T(8,128)(2,1)S(1)}, u32[]{:S(2)}, u32[]{:S(2)}) %collective-permute-start.2) | collective-permute-done | bytes 77856 | tf_op jit(solution)/shard_map/ppermute | solution.py:555
  21.8 0.5 collective-permute-start.6
  22.3 0.4 collective-permute-start.8
  22.8 0.2 collective-permute-done.5.refs_4_
  23.2 0.4 collective-permute-done.7.refs_6_
  23.7 2.7 %shard_map.113 = (bf16[72,4096]{1,0:T(8,128)(2,1)S(1)}, bf16[72,768]{1,0:T(8,128)(2,1)S(1)}, bf16[72,768]{1,0:T(8,128)(2,1)S(1)}, bf16[72,768]{1,0:T(8,128)(2,1)S(1)}) custom-call(bf16[288,128]{1,0:T(8,128)(2,1)S(1)} %get-tuple-element.62.refs_0_, bf16[288,128]{1,0:T(8,128)(2,1)S(1)} %get-tuple-element.63.refs_1_, ...), custom_call_target="tpu_custom_call" | custom-call | tf_op jit(solution)/shard_map/pallas_call | solution.py:132
  26.5 0.4 collective-permute-start.12
  26.9 1.4 %shard_map.114 = (f32[720,128]{1,0:T(8,128)S(1)}, f32[432,128]{1,0:T(8,128)S(1)}, bf16[432,128]{1,0:T(8,128)(2,1)S(1)}, bf16[720,128]{1,0:T(8,128)(2,1)S(1)}) custom-call(bf16[72,768]{1,0:T(8,128)(2,1)S(1)} %get-tuple-element.66.hidden.refs_5_, bf16[1,768,4096]{2,1,0:T(8,128)(2,1)S(1)} %bitcast.7), custom_call_target="tpu_custom_call" | custom-call | flops 452984832 | tf_op jit(solution)/shard_map/pallas_call | solution.py:132
  28.3 0.2 collective-permute-start.9
  28.5 4.9 %shard_map.116 = (bf16[72,4096]{1,0:T(8,128)(2,1)S(1)}, bf16[72,768]{1,0:T(8,128)(2,1)S(1)}, bf16[72,768]{1,0:T(8,128)(2,1)S(1)}, f32[432,128]{1,0:T(8,128)S(1)}, bf16[720,128]{1,0:T(8,128)(2,1)S(1)}) custom-call(bf16[1152,128]{1,0:T(8,128)(2,1)S(1)} %shard_map.115.g_sent, bf16[1152,128]{1,0:T(8,128)(2,1)S(1)} %collective-permute-done.12.g_swapped, ...), custom_call_target="tpu_custom_call" | custom-call | flops 905969664 | tf_op jit(solution)/shard_map/pallas_call | solution.py:132
  33.4 0.4 collective-permute-start.13
  34.0 2.1 %shard_map.117 = (f32[720,128]{1,0:T(8,128)S(1)}, bf16[432,128]{1,0:T(8,128)(2,1)S(1)}) custom-call(bf16[72,768]{1,0:T(8,128)(2,1)S(1)} %get-tuple-element.74.pre_gate, bf16[72,768]{1,0:T(8,128)(2,1)S(1)} %get-tuple-element.75.pre_up, bf16[1,4096,768]{2,1,0:T(8,128)(2,1)S(1)} %bitcast.3, bf16[1,4096,768]{2,1,0:T(8,128)(2,1)S(1)} %bitcast.5), custom_call_target="tpu_custom_call" | custom-call | flops 452984832 | tf_op jit(solution)/shard_map/pallas_call | solution.py:132
  36.1 0.4 collective-permute-start.14
  36.5 0.6 %shard_map.118 = (bf16[768,72]{1,0:T(8,128)(2,1)S(1)}, bf16[768,1024]{1,0:T(8,128)(2,1)S(1)}) custom-call(bf16[72,768]{1,0:T(8,128)(2,1)S(1)} %get-tuple-element.66.hidden.refs_5_, bf16[72,4096]{1,0:T(8,128)(2,1)S(1)} %get-tuple-element.80.g), custom_call_target="tpu_custom_call" | custom-call | flops 113246208 | tf_op jit(solution)/shard_map/pallas_call | solution.py:132
  37.2 0.3 collective-permute-done.14.refs_7_
  37.6 0.3 collective-permute-start.15
  37.9 0.2 collective-permute-start.16
  38.0 4.0 %collective-permute-start.17 = (bf16[576,128]{1,0:T(8,128)(2,1)S(1)}, bf16[576,128]{1,0:T(8,128)(2,1)S(1)}, u32[]{:S(2)}, u32[]{:S(2)}) collective-permute-start(bf16[576,128]{1,0:T(8,128)(2,1)S(1)} %get-tuple-element.84), channel_id=1, source_target_pairs={{0,4},{1,7},{2,6},{3,5},{4,0},{5,3},{6,2},{7,1},{8,12},{9,15},{10,... | collective-permute-start | bytes 442376 | tf_op jit(solution)/shard_map/ppermute | solution.py:555
  42.0 1.6 %collective-permute-start.18 = (bf16[288,128]{1,0:T(8,128)(2,1)S(1)}, bf16[288,128]{1,0:T(8,128)(2,1)S(1)}, u32[]{:S(2)}, u32[]{:S(2)}) collective-permute-start(bf16[288,128]{1,0:T(8,128)(2,1)S(1)} %get-tuple-element.85), channel_id=1, source_target_pairs={{0,2},{2,0},{4,6},{6,4},{8,10},{10,8},{12,14},{14,12},{1,3},{3,1},... | collective-permute-start | bytes 221192 | tf_op jit(solution)/shard_map/ppermute | solution.py:560
  43.6 8.1 %shard_map.120 = (bf16[1,4096,768]{2,1,0:T(8,128)(2,1)}, bf16[1,4096,768]{2,1,0:T(8,128)(2,1)}, bf16[1,768,4096]{2,1,0:T(8,128)(2,1)}, f32[8,128]{1,0:T(8,128)S(1)}) custom-call(bf16[72,4096]{1,0:T(8,128)(2,1)S(1)} %get-tuple-element.86.x, bf16[72,4096]{1,0:T(8,128)(2,1)S(1)} %get-tuple-element.80.g, bf16[768,72]{1,0:T(8,128)(2,1)S(1)} %get-tuple-element.87.hidden_turned, ...), custom_call_target="tpu_custom_call" | custom-call | flops 1358954496 | bytes 18874368 | tf_op jit(solution)/shard_map/pallas_call | solution.py:132
  51.9 0.8 %collective-permute-start.19 = (bf16[864,128]{1,0:T(8,128)(2,1)S(1)}, bf16[864,128]{1,0:T(8,128)(2,1)S(1)}, u32[]{:S(2)}, u32[]{:S(2)}) collective-permute-start(bf16[864,128]{1,0:T(8,128)(2,1)S(1)} %shard_map.121), channel_id=1, source_target_pairs={{0,1},{1,0},{2,3},{3,2},{4,5},{5,4},{6,7},{7,6},{8,9},{9,8},{10,11... | collective-permute-start | bytes 663560 | tf_op jit(solution)/shard_map/ppermute | solution.py:564
  52.7 0.9 %shard_map.122 = (f32[128,2048]{1,0:T(8,128)S(1)}, f32[128,2048]{1,0:T(8,128)S(1)}) custom-call(bf16[72,128]{1,0:T(8,128)(2,1)S(1)} %get-tuple-element.89.place, f32[72,128]{1,0:T(8,128)S(1)} %get-tuple-element.90.mix, bf16[576,128]{1,0:T(8,128)(2,1)S(1)} %collective-permute-done.15.refs_0_, bf16[576,128]{1,0:T(8,128)(2,1)S(1)} %collective-permute-done.16.refs_1_, ...), custom_call_target="tpu_custom_call" | custom-call | flops 75497472 | tf_op jit(solution)/shard_map/pallas_call | solution.py:132
  53.6 0.2 collective-permute-done.19.shared
  53.8 1.4 %shard_map.123 = (bf16[128,2048]{1,0:T(8,128)(2,1)}, bf16[128,2048]{1,0:T(8,128)(2,1)}) custom-call(bf16[27,128]{1,0:T(8,128)(2,1)S(1)} %get-tuple-element.52.place, f32[27,128]{1,0:T(8,128)S(1)} %get-tuple-element.53.mix, bf16[864,128]{1,0:T(8,128)(2,1)S(1)} %collective-permute-done.19.shared, f32[128,2048]{1,0:T(8,128)S(1)} %get-tuple-element.92.out_sum, ...), custom_call_target="tpu_custom_call" | custom-call | bytes 2097152 | tf_op jit(solution)/shard_map/pallas_call | solution.py:132
  (37 shorter events, 1.0 us)
Async XLA Ops:
  0.6 23.1 %slice-start = ((s8[6291456]{0:T(1024)(128)(4,1)}), s8[4194304]{0:T(1024)(128)(4,1)S(1)}, s32[]{:S(2)}) async-start(s8[6291456]{0:T(1024)(128)(4,1)} %bitcast.2), calls=%async_computation | async-start | bytes 8388608
  0.6 23.0 %slice-start.2 = ((s8[6291456]{0:T(1024)(128)(4,1)}), s8[4194304]{0:T(1024)(128)(4,1)S(1)}, s32[]{:S(2)}) async-start(s8[6291456]{0:T(1024)(128)(4,1)} %bitcast.4), calls=%async_computation.2 | async-start | bytes 8388608
  2.7 1.6 %collective-permute-start = (bf16[864,128]{1,0:T(8,128)(2,1)S(1)}, bf16[864,128]{1,0:T(8,128)(2,1)S(1)}, u32[]{:S(2)}, u32[]{:S(2)}) collective-permute-start(bf16[864,128]{1,0:T(8,128)(2,1)S(1)} %get-tuple-element.56), channel_id=1, source_target_pairs={{0,1},{1,0},{2,3},{3,2},{4,5},{5,4},{6,7},{7,6},{8,9},{9,8},{10,11... | collective-permute-start | bytes 663560 | tf_op jit(solution)/shard_map/ppermute | solution.py:564
  4.4 19.3 %slice-start.1 = ((s8[6291456]{0:T(1024)(128)(4,1)}), s8[2097152]{0:T(1024)(128)(4,1)S(1)}, s32[]{:S(2)}) async-start(s8[6291456]{0:T(1024)(128)(4,1)} %bitcast.2), calls=%async_computation.1 | async-start | bytes 4194304
  4.4 19.3 %slice-start.3 = ((s8[6291456]{0:T(1024)(128)(4,1)}), s8[2097152]{0:T(1024)(128)(4,1)S(1)}, s32[]{:S(2)}) async-start(s8[6291456]{0:T(1024)(128)(4,1)} %bitcast.4), calls=%async_computation.3 | async-start | bytes 4194304
  4.4 17.2 %collective-permute-start.1 = (bf16[576,128]{1,0:T(8,128)(2,1)S(1)}, bf16[576,128]{1,0:T(8,128)(2,1)S(1)}, u32[]{:S(2)}, u32[]{:S(2)}) collective-permute-start(bf16[576,128]{1,0:T(8,128)(2,1)S(1)} %get-tuple-element.57), channel_id=1, source_target_pairs={{0,12},{1,15},{2,14},{3,13},{4,8},{5,11},{6,10},{7,9},{8,4},{9,7},... | collective-permute-start | bytes 442376 | tf_op jit(solution)/shard_map/ppermute | solution.py:555
  9.4 12.2 %collective-permute-start.3 = (bf16[576,128]{1,0:T(8,128)(2,1)S(1)}, bf16[576,128]{1,0:T(8,128)(2,1)S(1)}, u32[]{:S(2)}, u32[]{:S(2)}) collective-permute-start(bf16[576,128]{1,0:T(8,128)(2,1)S(1)} %get-tuple-element.59), channel_id=1, source_target_pairs={{0,4},{1,7},{2,6},{3,5},{4,0},{5,3},{6,2},{7,1},{8,12},{9,15},{10,... | collective-permute-start | bytes 442376 | tf_op jit(solution)/shard_map/ppermute | solution.py:555
  9.5 12.2 %collective-permute-start.2 = (bf16[304,128]{1,0:T(8,128)(2,1)S(1)}, bf16[304,128]{1,0:T(8,128)(2,1)S(1)}, u32[]{:S(2)}, u32[]{:S(2)}) collective-permute-start(bf16[304,128]{1,0:T(8,128)(2,1)S(1)} %get-tuple-element.58), channel_id=1, source_target_pairs={{0,8},{1,11},{2,10},{3,9},{4,12},{5,15},{6,14},{7,13},{8,0},{9,3},... | collective-permute-start | bytes 233480 | tf_op jit(solution)/shard_map/ppermute | solution.py:555
  10.1 5.7 %collective-permute-start.4 = (bf16[288,128]{1,0:T(8,128)(2,1)S(1)}, bf16[288,128]{1,0:T(8,128)(2,1)S(1)}, u32[]{:S(2)}, u32[]{:S(2)}) collective-permute-start(bf16[288,128]{1,0:T(8,128)(2,1)S(1)} %get-tuple-element.60), channel_id=1, source_target_pairs={{0,2},{2,0},{4,6},{6,4},{8,10},{10,8},{12,14},{14,12},{1,3},{3,1},... | collective-permute-start | bytes 221192 | tf_op jit(solution)/shard_map/ppermute | solution.py:560
  11.7 14.7 %collective-permute-start.11 = (bf16[304,128]{1,0:T(8,128)(2,1)S(1)}, bf16[304,128]{1,0:T(8,128)(2,1)S(1)}, u32[]{:S(2)}, u32[]{:S(2)}) collective-permute-start(bf16[304,128]{1,0:T(8,128)(2,1)S(1)} %get-tuple-element.71), channel_id=1, source_target_pairs={{0,8},{1,11},{2,10},{3,9},{4,12},{5,15},{6,14},{7,13},{8,0},{9,3},... | collective-permute-start | bytes 233480 | tf_op jit(solution)/shard_map/ppermute | solution.py:555
  21.7 1.3 %collective-permute-start.5 = (bf16[288,128]{1,0:T(8,128)(2,1)S(1)}, bf16[288,128]{1,0:T(8,128)(2,1)S(1)}, u32[]{:S(2)}, u32[]{:S(2)}) collective-permute-start(bf16[288,128]{1,0:T(8,128)(2,1)S(1)} %get-tuple-element.62.refs_0_), channel_id=1, source_target_pairs={{0,1},{1,0},{2,3},{3,2},{4,5},{5,4},{6,7},{7,6},{8,9},{9,8},{10,11... | collective-permute-start | bytes 221192 | tf_op jit(solution)/shard_map/ppermute | solution.py:564
  21.8 1.4 %collective-permute-start.6 = (bf16[288,128]{1,0:T(8,128)(2,1)S(1)}, bf16[288,128]{1,0:T(8,128)(2,1)S(1)}, u32[]{:S(2)}, u32[]{:S(2)}) collective-permute-start(bf16[288,128]{1,0:T(8,128)(2,1)S(1)} %get-tuple-element.63.refs_1_), channel_id=1, source_target_pairs={{0,1},{1,0},{2,3},{3,2},{4,5},{5,4},{6,7},{7,6},{8,9},{9,8},{10,11... | collective-permute-start | bytes 221192 | tf_op jit(solution)/shard_map/ppermute | solution.py:564
  22.3 1.3 %collective-permute-start.7 = (bf16[288,128]{1,0:T(8,128)(2,1)S(1)}, bf16[288,128]{1,0:T(8,128)(2,1)S(1)}, u32[]{:S(2)}, u32[]{:S(2)}) collective-permute-start(bf16[288,128]{1,0:T(8,128)(2,1)S(1)} %get-tuple-element.64.refs_2_), channel_id=1, source_target_pairs={{0,1},{1,0},{2,3},{3,2},{4,5},{5,4},{6,7},{7,6},{8,9},{9,8},{10,11... | collective-permute-start | bytes 221192 | tf_op jit(solution)/shard_map/ppermute | solution.py:564
  22.3 4.6 %slice-start.4 = ((s8[6291456]{0:T(1024)(128)(4,1)}), s8[4194304]{0:T(1024)(128)(4,1)S(1)}, s32[]{:S(2)}) async-start(s8[6291456]{0:T(1024)(128)(4,1)} %bitcast.6), calls=%async_computation.4 | async-start | bytes 8388608
  22.3 4.6 %slice-start.5 = ((s8[6291456]{0:T(1024)(128)(4,1)}), s8[2097152]{0:T(1024)(128)(4,1)S(1)}, s32[]{:S(2)}) async-start(s8[6291456]{0:T(1024)(128)(4,1)} %bitcast.6), calls=%async_computation.5 | async-start | bytes 4194304
  22.3 1.3 %collective-permute-start.8 = (bf16[288,128]{1,0:T(8,128)(2,1)S(1)}, bf16[288,128]{1,0:T(8,128)(2,1)S(1)}, u32[]{:S(2)}, u32[]{:S(2)}) collective-permute-start(bf16[288,128]{1,0:T(8,128)(2,1)S(1)} %get-tuple-element.65.refs_3_), channel_id=1, source_target_pairs={{0,1},{1,0},{2,3},{3,2},{4,5},{5,4},{6,7},{7,6},{8,9},{9,8},{10,11... | collective-permute-start | bytes 221192 | tf_op jit(solution)/shard_map/ppermute | solution.py:564
  26.5 2.0 %collective-permute-start.12 = (bf16[1152,128]{1,0:T(8,128)(2,1)S(1)}, bf16[1152,128]{1,0:T(8,128)(2,1)S(1)}, u32[]{:S(2)}, u32[]{:S(2)}) collective-permute-start(bf16[1152,128]{1,0:T(8,128)(2,1)S(1)} %shard_map.115.g_sent), channel_id=1, source_target_pairs={{0,1},{1,0},{2,3},{3,2},{4,5},{5,4},{6,7},{7,6},{8,9},{9,8},{10,11... | collective-permute-start | bytes 884744 | tf_op jit(solution)/shard_map/ppermute | solution.py:564
  28.3 8.9 %collective-permute-start.9 = (bf16[720,128]{1,0:T(8,128)(2,1)S(1)}, bf16[720,128]{1,0:T(8,128)(2,1)S(1)}, u32[]{:S(2)}, u32[]{:S(2)}) collective-permute-start(bf16[720,128]{1,0:T(8,128)(2,1)S(1)} %get-tuple-element.69), channel_id=1, source_target_pairs={{0,1},{1,0},{2,3},{3,2},{4,5},{5,4},{6,7},{7,6},{8,9},{9,8},{10,11... | collective-permute-start | bytes 552968 | tf_op jit(solution)/shard_map/ppermute | solution.py:564
  33.4 4.1 %collective-permute-start.13 = (bf16[720,128]{1,0:T(8,128)(2,1)S(1)}, bf16[720,128]{1,0:T(8,128)(2,1)S(1)}, u32[]{:S(2)}, u32[]{:S(2)}) collective-permute-start(bf16[720,128]{1,0:T(8,128)(2,1)S(1)} %get-tuple-element.78), channel_id=1, source_target_pairs={{0,1},{1,0},{2,3},{3,2},{4,5},{5,4},{6,7},{7,6},{8,9},{9,8},{10,11... | collective-permute-start | bytes 552968 | tf_op jit(solution)/shard_map/ppermute | solution.py:564
  33.8 3.3 %collective-permute-start.10 = (bf16[432,128]{1,0:T(8,128)(2,1)S(1)}, bf16[432,128]{1,0:T(8,128)(2,1)S(1)}, u32[]{:S(2)}, u32[]{:S(2)}) collective-permute-start(bf16[432,128]{1,0:T(8,128)(2,1)S(1)} %get-tuple-element.70), channel_id=1, source_target_pairs={{0,1},{1,0},{2,3},{3,2},{4,5},{5,4},{6,7},{7,6},{8,9},{9,8},{10,11... | collective-permute-start | bytes 331784 | tf_op jit(solution)/shard_map/ppermute | solution.py:564
  36.1 1.4 %collective-permute-start.14 = (bf16[432,128]{1,0:T(8,128)(2,1)S(1)}, bf16[432,128]{1,0:T(8,128)(2,1)S(1)}, u32[]{:S(2)}, u32[]{:S(2)}) collective-permute-start(bf16[432,128]{1,0:T(8,128)(2,1)S(1)} %get-tuple-element.79), channel_id=1, source_target_pairs={{0,1},{1,0},{2,3},{3,2},{4,5},{5,4},{6,7},{7,6},{8,9},{9,8},{10,11... | collective-permute-start | bytes 331784 | tf_op jit(solution)/shard_map/ppermute | solution.py:564
  37.6 14.2 %collective-permute-start.15 = (bf16[576,128]{1,0:T(8,128)(2,1)S(1)}, bf16[576,128]{1,0:T(8,128)(2,1)S(1)}, u32[]{:S(2)}, u32[]{:S(2)}) collective-permute-start(bf16[576,128]{1,0:T(8,128)(2,1)S(1)} %get-tuple-element.82), channel_id=1, source_target_pairs={{0,12},{1,15},{2,14},{3,13},{4,8},{5,11},{6,10},{7,9},{8,4},{9,7},... | collective-permute-start | bytes 442376 | tf_op jit(solution)/shard_map/ppermute | solution.py:555
  37.9 14.0 %collective-permute-start.16 = (bf16[576,128]{1,0:T(8,128)(2,1)S(1)}, bf16[576,128]{1,0:T(8,128)(2,1)S(1)}, u32[]{:S(2)}, u32[]{:S(2)}) collective-permute-start(bf16[576,128]{1,0:T(8,128)(2,1)S(1)} %get-tuple-element.83), channel_id=1, source_target_pairs={{0,8},{1,11},{2,10},{3,9},{4,12},{5,15},{6,14},{7,13},{8,0},{9,3},... | collective-permute-start | bytes 442376 | tf_op jit(solution)/shard_map/ppermute | solution.py:555
  38.0 13.9 %collective-permute-start.17 = (bf16[576,128]{1,0:T(8,128)(2,1)S(1)}, bf16[576,128]{1,0:T(8,128)(2,1)S(1)}, u32[]{:S(2)}, u32[]{:S(2)}) collective-permute-start(bf16[576,128]{1,0:T(8,128)(2,1)S(1)} %get-tuple-element.84), channel_id=1, source_target_pairs={{0,4},{1,7},{2,6},{3,5},{4,0},{5,3},{6,2},{7,1},{8,12},{9,15},{10,... | collective-permute-start | bytes 442376 | tf_op jit(solution)/shard_map/ppermute | solution.py:555
  42.0 9.7 %collective-permute-start.18 = (bf16[288,128]{1,0:T(8,128)(2,1)S(1)}, bf16[288,128]{1,0:T(8,128)(2,1)S(1)}, u32[]{:S(2)}, u32[]{:S(2)}) collective-permute-start(bf16[288,128]{1,0:T(8,128)(2,1)S(1)} %get-tuple-element.85), channel_id=1, source_target_pairs={{0,2},{2,0},{4,6},{6,4},{8,10},{10,8},{12,14},{14,12},{1,3},{3,1},... | collective-permute-start | bytes 221192 | tf_op jit(solution)/shard_map/ppermute | solution.py:560
  51.9 1.9 %collective-permute-start.19 = (bf16[864,128]{1,0:T(8,128)(2,1)S(1)}, bf16[864,128]{1,0:T(8,128)(2,1)S(1)}, u32[]{:S(2)}, u32[]{:S(2)}) collective-permute-start(bf16[864,128]{1,0:T(8,128)(2,1)S(1)} %shard_map.121), channel_id=1, source_target_pairs={{0,1},{1,0},{2,3},{3,2},{4,5},{5,4},{6,7},{7,6},{8,9},{9,8},{10,11... | collective-permute-start | bytes 663560 | tf_op jit(solution)/shard_map/ppermute | solution.py:564

commit v19 on v18

--- a/solution.py
+++ b/solution.py
@@ -222,12 +222,16 @@
         part(here, start, size)[...] = block(2 * count + 1)
 
     copies[2].wait()
-    for sub in range(subs):
-        spread_lanes(scratch, sub, subs, dot(low, x[:, lanes_of(sub)]))
+    for cut in pieces_of(subs * LANES, 512):
+        value = dot(low, x[:, cut])
+        for i in range(value.shape[1] // LANES):
+            spread_lanes(scratch, cut.start // LANES + i, subs, value[:, lanes_of(i)])
     write(x_mine, 0)
     copies[3].wait()
-    for sub in range(subs):
-        spread_lanes(scratch, sub, subs, dot(low, g[:, lanes_of(sub)]) * row_weight)
+    for cut in pieces_of(subs * LANES, 512):
+        value = dot(low, g[:, cut])
+        for i in range(value.shape[1] // LANES):
+            spread_lanes(scratch, cut.start // LANES + i, subs, value[:, lanes_of(i)] * row_weight)
     write(g_mine, count)
 
 
@@ -350,11 +354,12 @@
 
         def put(cut, total):
             low[i, :, cut] = (before[:, cut] + total).astype(low.dtype)
+            sem = sems.at[i, cut.start // 512]
+            copies.append(pltpu.make_async_copy(low.at[i, :, cut], out.at[:, cut], sem))
+            copies[-1].start()
 
         blocks = [part(shared, 2 * j * size + at, size) for j in range(count)]
         token_sums(subs, place, scale, scratch, rows, blocks, put)
-        copies.append(pltpu.make_async_copy(low.at[i], out, sems.at[i]))
-        copies[-1].start()
     for copy in copies:
         copy.wait()
 
@@ -715,7 +720,7 @@
             pltpu.VMEM((count * size, LANES), full),
             pltpu.VMEM((other_rows, sub_width), low),
             pltpu.VMEM((2, tok_dev, sub_width), low),
-            pltpu.SemaphoreType.DMA((2,)),
+            pltpu.SemaphoreType.DMA((2, -(-sub_width // 512))),
         ],
         traffic=8 * tok_dev * sub_width,
     )

time: 55.3 us -> 55.1 us (level)
  no operation moved by 1% of the time
where the time goes in v19:
time: 55.1 us; the launch traced here: 55 us
  Pallas kernels  24.2 us (44%)
  starting transfers between devices  19.5 us (35%)
  waiting for transfers between devices  10.5 us (19%)
  between operations  0.82 us (1%)
    pallas_call x14, Pallas kernels, call(): pl.pallas_call(kernel, out_shape=tuple(out_shape), in_specs=[pl.BlockSpec...  24.2 us
    ppermute x7, starting transfers between devices, exchange(): arrived.append(lax.ppermute(block, ('expert', 'ffn'), pairs))  12.3 us
    ppermute x7, waiting for transfers between devices, exchange(): arrived.append(lax.ppermute(block, ('expert', 'ffn'), pairs))  6.07 us
    ppermute x11, starting transfers between devices, swap(): return lax.ppermute(value, 'ffn', [(0, 1), (1, 0)])  4.03 us
    ppermute x2, starting transfers between devices, exchange_near(): return lax.ppermute(block, 'expert', [(i, i ^ 1) for i in range(devices)])  3.19 us
    ppermute x11, waiting for transfers between devices, swap(): return lax.ppermute(value, 'ffn', [(0, 1), (1, 0)])  2.53 us
    ppermute x2, waiting for transfers between devices, exchange_near(): return lax.ppermute(block, 'expert', [(i, i ^ 1) for i in range(devices)])  1.88 us
  transfers between devices with their start and end apart: 20, of which 10 were waited for; matrix products, arithmetic and copies ran while one was open for 0% of the time, Pallas kernels for 38%

profile of v19, /device:TPU:0, one launch (start us, length us, event | category | flops | bytes accessed | tf_op | source)
XLA Modules:
  0.0 55.0 jit_solution(6276254203092959918)
XLA Ops:
  0.7 1.9 %shard_map.110 = (bf16[432,128]{1,0:T(8,128)(2,1)S(1)}, bf16[432,128]{1,0:T(8,128)(2,1)S(1)}, bf16[288,128]{1,0:T(8,128)(2,1)S(1)}, bf16[288,128]{1,0:T(8,128)(2...) custom-call(s32[8,128]{1,0:T(8,128)} %bitcast.8, ...), custom_call_target="tpu_custom_call" | custom-call | bytes 1048576 | tf_op jit(solution)/shard_map/pallas_call | solution.py:132
  2.6 0.5 collective-permute-start
  3.1 1.1 %collective-permute-done.swapped = bf16[864,128]{1,0:T(8,128)(2,1)S(1)} collective-permute-done((bf16[864,128]{1,0:T(8,128)(2,1)S(1)}, bf16[864,128]{1,0:T(8,128)(2,1)S(1)}, u32[]{:S(2)}, u32[]{:S(2)}) %collective-permute-start) | collective-permute-done | bytes 221216 | tf_op jit(solution)/shard_map/ppermute | solution.py:569
  4.3 5.0 %collective-permute-start.1 = (bf16[576,128]{1,0:T(8,128)(2,1)S(1)}, bf16[576,128]{1,0:T(8,128)(2,1)S(1)}, u32[]{:S(2)}, u32[]{:S(2)}) collective-permute-start(bf16[576,128]{1,0:T(8,128)(2,1)S(1)} %get-tuple-element.57), channel_id=1, source_target_pairs={{0,12},{1,15},{2,14},{3,13},{4,8},{5,11},{6,10},{7,9},{8,4},{9,7},... | collective-permute-start | bytes 442376 | tf_op jit(solution)/shard_map/ppermute | solution.py:560
  9.3 0.6 %collective-permute-start.2 = (bf16[304,128]{1,0:T(8,128)(2,1)S(1)}, bf16[304,128]{1,0:T(8,128)(2,1)S(1)}, u32[]{:S(2)}, u32[]{:S(2)}) collective-permute-start(bf16[304,128]{1,0:T(8,128)(2,1)S(1)} %get-tuple-element.58), channel_id=1, source_target_pairs={{0,8},{1,11},{2,10},{3,9},{4,12},{5,15},{6,14},{7,13},{8,0},{9,3},... | collective-permute-start | bytes 233480 | tf_op jit(solution)/shard_map/ppermute | solution.py:560
  9.9 1.6 %collective-permute-start.4 = (bf16[288,128]{1,0:T(8,128)(2,1)S(1)}, bf16[288,128]{1,0:T(8,128)(2,1)S(1)}, u32[]{:S(2)}, u32[]{:S(2)}) collective-permute-start(bf16[288,128]{1,0:T(8,128)(2,1)S(1)} %get-tuple-element.60), channel_id=1, source_target_pairs={{0,2},{2,0},{4,6},{6,4},{8,10},{10,8},{12,14},{14,12},{1,3},{3,1},... | collective-permute-start | bytes 221192 | tf_op jit(solution)/shard_map/ppermute | solution.py:565
  11.6 2.1 %collective-permute-start.11 = (bf16[304,128]{1,0:T(8,128)(2,1)S(1)}, bf16[304,128]{1,0:T(8,128)(2,1)S(1)}, u32[]{:S(2)}, u32[]{:S(2)}) collective-permute-start(bf16[304,128]{1,0:T(8,128)(2,1)S(1)} %get-tuple-element.71), channel_id=1, source_target_pairs={{0,8},{1,11},{2,10},{3,9},{4,12},{5,15},{6,14},{7,13},{8,0},{9,3},... | collective-permute-start | bytes 233480 | tf_op jit(solution)/shard_map/ppermute | solution.py:560
  13.7 1.9 %collective-permute-done.4.refs_3_ = bf16[288,128]{1,0:T(8,128)(2,1)S(1)} collective-permute-done((bf16[288,128]{1,0:T(8,128)(2,1)S(1)}, bf16[288,128]{1,0:T(8,128)(2,1)S(1)}, u32[]{:S(2)}, u32[]{:S(2)}) %collective-permute-start.4) | collective-permute-done | bytes 73760 | tf_op jit(solution)/shard_map/ppermute | solution.py:565
  15.6 5.9 %collective-permute-done.2.refs_1_ = bf16[304,128]{1,0:T(8,128)(2,1)S(1)} collective-permute-done((bf16[304,128]{1,0:T(8,128)(2,1)S(1)}, bf16[304,128]{1,0:T(8,128)(2,1)S(1)}, u32[]{:S(2)}, u32[]{:S(2)}) %collective-permute-start.2) | collective-permute-done | bytes 77856 | tf_op jit(solution)/shard_map/ppermute | solution.py:560
  21.6 0.5 collective-permute-start.6
  22.2 0.4 collective-permute-start.8
  22.6 0.2 collective-permute-done.5.refs_4_
  23.0 0.4 collective-permute-done.7.refs_6_
  23.6 2.7 %shard_map.113 = (bf16[72,4096]{1,0:T(8,128)(2,1)S(1)}, bf16[72,768]{1,0:T(8,128)(2,1)S(1)}, bf16[72,768]{1,0:T(8,128)(2,1)S(1)}, bf16[72,768]{1,0:T(8,128)(2,1)S(1)}) custom-call(bf16[288,128]{1,0:T(8,128)(2,1)S(1)} %get-tuple-element.62.refs_0_, bf16[288,128]{1,0:T(8,128)(2,1)S(1)} %get-tuple-element.63.refs_1_, ...), custom_call_target="tpu_custom_call" | custom-call | tf_op jit(solution)/shard_map/pallas_call | solution.py:132
  26.3 0.4 collective-permute-start.12
  26.8 1.4 %shard_map.114 = (f32[720,128]{1,0:T(8,128)S(1)}, f32[432,128]{1,0:T(8,128)S(1)}, bf16[432,128]{1,0:T(8,128)(2,1)S(1)}, bf16[720,128]{1,0:T(8,128)(2,1)S(1)}) custom-call(bf16[72,768]{1,0:T(8,128)(2,1)S(1)} %get-tuple-element.66.hidden.refs_5_, bf16[1,768,4096]{2,1,0:T(8,128)(2,1)S(1)} %bitcast.7), custom_call_target="tpu_custom_call" | custom-call | flops 452984832 | tf_op jit(solution)/shard_map/pallas_call | solution.py:132
  28.1 0.2 collective-permute-start.9
  28.3 4.9 %shard_map.116 = (bf16[72,4096]{1,0:T(8,128)(2,1)S(1)}, bf16[72,768]{1,0:T(8,128)(2,1)S(1)}, bf16[72,768]{1,0:T(8,128)(2,1)S(1)}, f32[432,128]{1,0:T(8,128)S(1)}, bf16[720,128]{1,0:T(8,128)(2,1)S(1)}) custom-call(bf16[1152,128]{1,0:T(8,128)(2,1)S(1)} %shard_map.115.g_sent, bf16[1152,128]{1,0:T(8,128)(2,1)S(1)} %collective-permute-done.12.g_swapped, ...), custom_call_target="tpu_custom_call" | custom-call | flops 905969664 | tf_op jit(solution)/shard_map/pallas_call | solution.py:132
  33.2 0.4 collective-permute-start.13
  33.8 2.1 %shard_map.117 = (f32[720,128]{1,0:T(8,128)S(1)}, bf16[432,128]{1,0:T(8,128)(2,1)S(1)}) custom-call(bf16[72,768]{1,0:T(8,128)(2,1)S(1)} %get-tuple-element.74.pre_gate, bf16[72,768]{1,0:T(8,128)(2,1)S(1)} %get-tuple-element.75.pre_up, bf16[1,4096,768]{2,1,0:T(8,128)(2,1)S(1)} %bitcast.3, bf16[1,4096,768]{2,1,0:T(8,128)(2,1)S(1)} %bitcast.5), custom_call_target="tpu_custom_call" | custom-call | flops 452984832 | tf_op jit(solution)/shard_map/pallas_call | solution.py:132
  35.9 0.4 collective-permute-start.14
  36.3 0.6 %shard_map.118 = (bf16[768,72]{1,0:T(8,128)(2,1)S(1)}, bf16[768,1024]{1,0:T(8,128)(2,1)S(1)}) custom-call(bf16[72,768]{1,0:T(8,128)(2,1)S(1)} %get-tuple-element.66.hidden.refs_5_, bf16[72,4096]{1,0:T(8,128)(2,1)S(1)} %get-tuple-element.80.g), custom_call_target="tpu_custom_call" | custom-call | flops 113246208 | tf_op jit(solution)/shard_map/pallas_call | solution.py:132
  37.0 0.3 collective-permute-done.14.refs_7_
  37.4 0.3 collective-permute-start.15
  37.7 0.2 collective-permute-start.16
  37.9 4.0 %collective-permute-start.17 = (bf16[576,128]{1,0:T(8,128)(2,1)S(1)}, bf16[576,128]{1,0:T(8,128)(2,1)S(1)}, u32[]{:S(2)}, u32[]{:S(2)}) collective-permute-start(bf16[576,128]{1,0:T(8,128)(2,1)S(1)} %get-tuple-element.84), channel_id=1, source_target_pairs={{0,4},{1,7},{2,6},{3,5},{4,0},{5,3},{6,2},{7,1},{8,12},{9,15},{10,... | collective-permute-start | bytes 442376 | tf_op jit(solution)/shard_map/ppermute | solution.py:560
  41.9 1.6 %collective-permute-start.18 = (bf16[288,128]{1,0:T(8,128)(2,1)S(1)}, bf16[288,128]{1,0:T(8,128)(2,1)S(1)}, u32[]{:S(2)}, u32[]{:S(2)}) collective-permute-start(bf16[288,128]{1,0:T(8,128)(2,1)S(1)} %get-tuple-element.85), channel_id=1, source_target_pairs={{0,2},{2,0},{4,6},{6,4},{8,10},{10,8},{12,14},{14,12},{1,3},{3,1},... | collective-permute-start | bytes 221192 | tf_op jit(solution)/shard_map/ppermute | solution.py:565
  43.4 8.1 %shard_map.120 = (bf16[1,4096,768]{2,1,0:T(8,128)(2,1)}, bf16[1,4096,768]{2,1,0:T(8,128)(2,1)}, bf16[1,768,4096]{2,1,0:T(8,128)(2,1)}, f32[8,128]{1,0:T(8,128)S(1)}) custom-call(bf16[72,4096]{1,0:T(8,128)(2,1)S(1)} %get-tuple-element.86.x, bf16[72,4096]{1,0:T(8,128)(2,1)S(1)} %get-tuple-element.80.g, bf16[768,72]{1,0:T(8,128)(2,1)S(1)} %get-tuple-element.87.hidden_turned, ...), custom_call_target="tpu_custom_call" | custom-call | flops 1358954496 | bytes 18874368 | tf_op jit(solution)/shard_map/pallas_call | solution.py:132
  51.8 0.8 %collective-permute-start.19 = (bf16[864,128]{1,0:T(8,128)(2,1)S(1)}, bf16[864,128]{1,0:T(8,128)(2,1)S(1)}, u32[]{:S(2)}, u32[]{:S(2)}) collective-permute-start(bf16[864,128]{1,0:T(8,128)(2,1)S(1)} %shard_map.121), channel_id=1, source_target_pairs={{0,1},{1,0},{2,3},{3,2},{4,5},{5,4},{6,7},{7,6},{8,9},{9,8},{10,11... | collective-permute-start | bytes 663560 | tf_op jit(solution)/shard_map/ppermute | solution.py:569
  52.5 0.9 %shard_map.122 = (f32[128,2048]{1,0:T(8,128)S(1)}, f32[128,2048]{1,0:T(8,128)S(1)}) custom-call(bf16[72,128]{1,0:T(8,128)(2,1)S(1)} %get-tuple-element.89.place, f32[72,128]{1,0:T(8,128)S(1)} %get-tuple-element.90.mix, bf16[576,128]{1,0:T(8,128)(2,1)S(1)} %collective-permute-done.15.refs_0_, bf16[576,128]{1,0:T(8,128)(2,1)S(1)} %collective-permute-done.16.refs_1_, ...), custom_call_target="tpu_custom_call" | custom-call | flops 75497472 | tf_op jit(solution)/shard_map/pallas_call | solution.py:132
  53.4 0.2 collective-permute-done.19.shared
  53.7 1.3 %shard_map.123 = (bf16[128,2048]{1,0:T(8,128)(2,1)}, bf16[128,2048]{1,0:T(8,128)(2,1)}) custom-call(bf16[27,128]{1,0:T(8,128)(2,1)S(1)} %get-tuple-element.52.place, f32[27,128]{1,0:T(8,128)S(1)} %get-tuple-element.53.mix, bf16[864,128]{1,0:T(8,128)(2,1)S(1)} %collective-permute-done.19.shared, f32[128,2048]{1,0:T(8,128)S(1)} %get-tuple-element.92.out_sum, ...), custom_call_target="tpu_custom_call" | custom-call | bytes 2097152 | tf_op jit(solution)/shard_map/pallas_call | solution.py:132
  (37 shorter events, 1.0 us)
Async XLA Ops:
  0.6 22.9 %slice-start = ((s8[6291456]{0:T(1024)(128)(4,1)}), s8[4194304]{0:T(1024)(128)(4,1)S(1)}, s32[]{:S(2)}) async-start(s8[6291456]{0:T(1024)(128)(4,1)} %bitcast.2), calls=%async_computation | async-start | bytes 8388608
  0.6 22.9 %slice-start.2 = ((s8[6291456]{0:T(1024)(128)(4,1)}), s8[4194304]{0:T(1024)(128)(4,1)S(1)}, s32[]{:S(2)}) async-start(s8[6291456]{0:T(1024)(128)(4,1)} %bitcast.4), calls=%async_computation.2 | async-start | bytes 8388608
  2.6 1.6 %collective-permute-start = (bf16[864,128]{1,0:T(8,128)(2,1)S(1)}, bf16[864,128]{1,0:T(8,128)(2,1)S(1)}, u32[]{:S(2)}, u32[]{:S(2)}) collective-permute-start(bf16[864,128]{1,0:T(8,128)(2,1)S(1)} %get-tuple-element.56), channel_id=1, source_target_pairs={{0,1},{1,0},{2,3},{3,2},{4,5},{5,4},{6,7},{7,6},{8,9},{9,8},{10,11... | collective-permute-start | bytes 663560 | tf_op jit(solution)/shard_map/ppermute | solution.py:569
  4.2 19.3 %slice-start.1 = ((s8[6291456]{0:T(1024)(128)(4,1)}), s8[2097152]{0:T(1024)(128)(4,1)S(1)}, s32[]{:S(2)}) async-start(s8[6291456]{0:T(1024)(128)(4,1)} %bitcast.2), calls=%async_computation.1 | async-start | bytes 4194304
  4.2 19.3 %slice-start.3 = ((s8[6291456]{0:T(1024)(128)(4,1)}), s8[2097152]{0:T(1024)(128)(4,1)S(1)}, s32[]{:S(2)}) async-start(s8[6291456]{0:T(1024)(128)(4,1)} %bitcast.4), calls=%async_computation.3 | async-start | bytes 4194304
  4.3 17.2 %collective-permute-start.1 = (bf16[576,128]{1,0:T(8,128)(2,1)S(1)}, bf16[576,128]{1,0:T(8,128)(2,1)S(1)}, u32[]{:S(2)}, u32[]{:S(2)}) collective-permute-start(bf16[576,128]{1,0:T(8,128)(2,1)S(1)} %get-tuple-element.57), channel_id=1, source_target_pairs={{0,12},{1,15},{2,14},{3,13},{4,8},{5,11},{6,10},{7,9},{8,4},{9,7},... | collective-permute-start | bytes 442376 | tf_op jit(solution)/shard_map/ppermute | solution.py:560
  9.3 12.2 %collective-permute-start.3 = (bf16[576,128]{1,0:T(8,128)(2,1)S(1)}, bf16[576,128]{1,0:T(8,128)(2,1)S(1)}, u32[]{:S(2)}, u32[]{:S(2)}) collective-permute-start(bf16[576,128]{1,0:T(8,128)(2,1)S(1)} %get-tuple-element.59), channel_id=1, source_target_pairs={{0,4},{1,7},{2,6},{3,5},{4,0},{5,3},{6,2},{7,1},{8,12},{9,15},{10,... | collective-permute-start | bytes 442376 | tf_op jit(solution)/shard_map/ppermute | solution.py:560
  9.3 12.2 %collective-permute-start.2 = (bf16[304,128]{1,0:T(8,128)(2,1)S(1)}, bf16[304,128]{1,0:T(8,128)(2,1)S(1)}, u32[]{:S(2)}, u32[]{:S(2)}) collective-permute-start(bf16[304,128]{1,0:T(8,128)(2,1)S(1)} %get-tuple-element.58), channel_id=1, source_target_pairs={{0,8},{1,11},{2,10},{3,9},{4,12},{5,15},{6,14},{7,13},{8,0},{9,3},... | collective-permute-start | bytes 233480 | tf_op jit(solution)/shard_map/ppermute | solution.py:560
  9.9 5.7 %collective-permute-start.4 = (bf16[288,128]{1,0:T(8,128)(2,1)S(1)}, bf16[288,128]{1,0:T(8,128)(2,1)S(1)}, u32[]{:S(2)}, u32[]{:S(2)}) collective-permute-start(bf16[288,128]{1,0:T(8,128)(2,1)S(1)} %get-tuple-element.60), channel_id=1, source_target_pairs={{0,2},{2,0},{4,6},{6,4},{8,10},{10,8},{12,14},{14,12},{1,3},{3,1},... | collective-permute-start | bytes 221192 | tf_op jit(solution)/shard_map/ppermute | solution.py:565
  11.6 14.7 %collective-permute-start.11 = (bf16[304,128]{1,0:T(8,128)(2,1)S(1)}, bf16[304,128]{1,0:T(8,128)(2,1)S(1)}, u32[]{:S(2)}, u32[]{:S(2)}) collective-permute-start(bf16[304,128]{1,0:T(8,128)(2,1)S(1)} %get-tuple-element.71), channel_id=1, source_target_pairs={{0,8},{1,11},{2,10},{3,9},{4,12},{5,15},{6,14},{7,13},{8,0},{9,3},... | collective-permute-start | bytes 233480 | tf_op jit(solution)/shard_map/ppermute | solution.py:560
  21.5 1.3 %collective-permute-start.5 = (bf16[288,128]{1,0:T(8,128)(2,1)S(1)}, bf16[288,128]{1,0:T(8,128)(2,1)S(1)}, u32[]{:S(2)}, u32[]{:S(2)}) collective-permute-start(bf16[288,128]{1,0:T(8,128)(2,1)S(1)} %get-tuple-element.62.refs_0_), channel_id=1, source_target_pairs={{0,1},{1,0},{2,3},{3,2},{4,5},{5,4},{6,7},{7,6},{8,9},{9,8},{10,11... | collective-permute-start | bytes 221192 | tf_op jit(solution)/shard_map/ppermute | solution.py:569
  21.6 1.4 %collective-permute-start.6 = (bf16[288,128]{1,0:T(8,128)(2,1)S(1)}, bf16[288,128]{1,0:T(8,128)(2,1)S(1)}, u32[]{:S(2)}, u32[]{:S(2)}) collective-permute-start(bf16[288,128]{1,0:T(8,128)(2,1)S(1)} %get-tuple-element.63.refs_1_), channel_id=1, source_target_pairs={{0,1},{1,0},{2,3},{3,2},{4,5},{5,4},{6,7},{7,6},{8,9},{9,8},{10,11... | collective-permute-start | bytes 221192 | tf_op jit(solution)/shard_map/ppermute | solution.py:569
  22.1 1.3 %collective-permute-start.7 = (bf16[288,128]{1,0:T(8,128)(2,1)S(1)}, bf16[288,128]{1,0:T(8,128)(2,1)S(1)}, u32[]{:S(2)}, u32[]{:S(2)}) collective-permute-start(bf16[288,128]{1,0:T(8,128)(2,1)S(1)} %get-tuple-element.64.refs_2_), channel_id=1, source_target_pairs={{0,1},{1,0},{2,3},{3,2},{4,5},{5,4},{6,7},{7,6},{8,9},{9,8},{10,11... | collective-permute-start | bytes 221192 | tf_op jit(solution)/shard_map/ppermute | solution.py:569
  22.2 4.6 %slice-start.4 = ((s8[6291456]{0:T(1024)(128)(4,1)}), s8[4194304]{0:T(1024)(128)(4,1)S(1)}, s32[]{:S(2)}) async-start(s8[6291456]{0:T(1024)(128)(4,1)} %bitcast.6), calls=%async_computation.4 | async-start | bytes 8388608
  22.2 4.6 %slice-start.5 = ((s8[6291456]{0:T(1024)(128)(4,1)}), s8[2097152]{0:T(1024)(128)(4,1)S(1)}, s32[]{:S(2)}) async-start(s8[6291456]{0:T(1024)(128)(4,1)} %bitcast.6), calls=%async_computation.5 | async-start | bytes 4194304
  22.2 1.3 %collective-permute-start.8 = (bf16[288,128]{1,0:T(8,128)(2,1)S(1)}, bf16[288,128]{1,0:T(8,128)(2,1)S(1)}, u32[]{:S(2)}, u32[]{:S(2)}) collective-permute-start(bf16[288,128]{1,0:T(8,128)(2,1)S(1)} %get-tuple-element.65.refs_3_), channel_id=1, source_target_pairs={{0,1},{1,0},{2,3},{3,2},{4,5},{5,4},{6,7},{7,6},{8,9},{9,8},{10,11... | collective-permute-start | bytes 221192 | tf_op jit(solution)/shard_map/ppermute | solution.py:569
  26.3 2.0 %collective-permute-start.12 = (bf16[1152,128]{1,0:T(8,128)(2,1)S(1)}, bf16[1152,128]{1,0:T(8,128)(2,1)S(1)}, u32[]{:S(2)}, u32[]{:S(2)}) collective-permute-start(bf16[1152,128]{1,0:T(8,128)(2,1)S(1)} %shard_map.115.g_sent), channel_id=1, source_target_pairs={{0,1},{1,0},{2,3},{3,2},{4,5},{5,4},{6,7},{7,6},{8,9},{9,8},{10,11... | collective-permute-start | bytes 884744 | tf_op jit(solution)/shard_map/ppermute | solution.py:569
  28.1 8.9 %collective-permute-start.9 = (bf16[720,128]{1,0:T(8,128)(2,1)S(1)}, bf16[720,128]{1,0:T(8,128)(2,1)S(1)}, u32[]{:S(2)}, u32[]{:S(2)}) collective-permute-start(bf16[720,128]{1,0:T(8,128)(2,1)S(1)} %get-tuple-element.69), channel_id=1, source_target_pairs={{0,1},{1,0},{2,3},{3,2},{4,5},{5,4},{6,7},{7,6},{8,9},{9,8},{10,11... | collective-permute-start | bytes 552968 | tf_op jit(solution)/shard_map/ppermute | solution.py:569
  33.2 4.1 %collective-permute-start.13 = (bf16[720,128]{1,0:T(8,128)(2,1)S(1)}, bf16[720,128]{1,0:T(8,128)(2,1)S(1)}, u32[]{:S(2)}, u32[]{:S(2)}) collective-permute-start(bf16[720,128]{1,0:T(8,128)(2,1)S(1)} %get-tuple-element.78), channel_id=1, source_target_pairs={{0,1},{1,0},{2,3},{3,2},{4,5},{5,4},{6,7},{7,6},{8,9},{9,8},{10,11... | collective-permute-start | bytes 552968 | tf_op jit(solution)/shard_map/ppermute | solution.py:569
  33.7 3.3 %collective-permute-start.10 = (bf16[432,128]{1,0:T(8,128)(2,1)S(1)}, bf16[432,128]{1,0:T(8,128)(2,1)S(1)}, u32[]{:S(2)}, u32[]{:S(2)}) collective-permute-start(bf16[432,128]{1,0:T(8,128)(2,1)S(1)} %get-tuple-element.70), channel_id=1, source_target_pairs={{0,1},{1,0},{2,3},{3,2},{4,5},{5,4},{6,7},{7,6},{8,9},{9,8},{10,11... | collective-permute-start | bytes 331784 | tf_op jit(solution)/shard_map/ppermute | solution.py:569
  35.9 1.4 %collective-permute-start.14 = (bf16[432,128]{1,0:T(8,128)(2,1)S(1)}, bf16[432,128]{1,0:T(8,128)(2,1)S(1)}, u32[]{:S(2)}, u32[]{:S(2)}) collective-permute-start(bf16[432,128]{1,0:T(8,128)(2,1)S(1)} %get-tuple-element.79), channel_id=1, source_target_pairs={{0,1},{1,0},{2,3},{3,2},{4,5},{5,4},{6,7},{7,6},{8,9},{9,8},{10,11... | collective-permute-start | bytes 331784 | tf_op jit(solution)/shard_map/ppermute | solution.py:569
  37.4 14.2 %collective-permute-start.15 = (bf16[576,128]{1,0:T(8,128)(2,1)S(1)}, bf16[576,128]{1,0:T(8,128)(2,1)S(1)}, u32[]{:S(2)}, u32[]{:S(2)}) collective-permute-start(bf16[576,128]{1,0:T(8,128)(2,1)S(1)} %get-tuple-element.82), channel_id=1, source_target_pairs={{0,12},{1,15},{2,14},{3,13},{4,8},{5,11},{6,10},{7,9},{8,4},{9,7},... | collective-permute-start | bytes 442376 | tf_op jit(solution)/shard_map/ppermute | solution.py:560
  37.7 14.0 %collective-permute-start.16 = (bf16[576,128]{1,0:T(8,128)(2,1)S(1)}, bf16[576,128]{1,0:T(8,128)(2,1)S(1)}, u32[]{:S(2)}, u32[]{:S(2)}) collective-permute-start(bf16[576,128]{1,0:T(8,128)(2,1)S(1)} %get-tuple-element.83), channel_id=1, source_target_pairs={{0,8},{1,11},{2,10},{3,9},{4,12},{5,15},{6,14},{7,13},{8,0},{9,3},... | collective-permute-start | bytes 442376 | tf_op jit(solution)/shard_map/ppermute | solution.py:560
  37.9 13.9 %collective-permute-start.17 = (bf16[576,128]{1,0:T(8,128)(2,1)S(1)}, bf16[576,128]{1,0:T(8,128)(2,1)S(1)}, u32[]{:S(2)}, u32[]{:S(2)}) collective-permute-start(bf16[576,128]{1,0:T(8,128)(2,1)S(1)} %get-tuple-element.84), channel_id=1, source_target_pairs={{0,4},{1,7},{2,6},{3,5},{4,0},{5,3},{6,2},{7,1},{8,12},{9,15},{10,... | collective-permute-start | bytes 442376 | tf_op jit(solution)/shard_map/ppermute | solution.py:560
  41.9 9.7 %collective-permute-start.18 = (bf16[288,128]{1,0:T(8,128)(2,1)S(1)}, bf16[288,128]{1,0:T(8,128)(2,1)S(1)}, u32[]{:S(2)}, u32[]{:S(2)}) collective-permute-start(bf16[288,128]{1,0:T(8,128)(2,1)S(1)} %get-tuple-element.85), channel_id=1, source_target_pairs={{0,2},{2,0},{4,6},{6,4},{8,10},{10,8},{12,14},{14,12},{1,3},{3,1},... | collective-permute-start | bytes 221192 | tf_op jit(solution)/shard_map/ppermute | solution.py:565
  51.8 1.9 %collective-permute-start.19 = (bf16[864,128]{1,0:T(8,128)(2,1)S(1)}, bf16[864,128]{1,0:T(8,128)(2,1)S(1)}, u32[]{:S(2)}, u32[]{:S(2)}) collective-permute-start(bf16[864,128]{1,0:T(8,128)(2,1)S(1)} %shard_map.121), channel_id=1, source_target_pairs={{0,1},{1,0},{2,3},{3,2},{4,5},{5,4},{6,7},{7,6},{8,9},{9,8},{10,11... | collective-permute-start | bytes 663560 | tf_op jit(solution)/shard_map/ppermute | solution.py:569
